TPU v7x, 32 devices: a whole 2x2x4 slice. The times are simulated.
32 devices in a mesh: angle: 2 (over x), gx: 4 (over y, core), gy: 4 (over z).
Axes of the slice: x: 2, y: 2, z: 4, core: 2. Of those that a mesh axis runs over, the one named last changes fastest.
Arguments:
- forward_fields: float32 [2, 12, 32, 64, 128], P('angle', None, 'gx', 'gy'), may hold values from -6 to 6
- adjoint_fields: float32 [2, 12, 32, 64, 128], P('angle', None, 'gx', 'gy'), may hold values from -6 to 6
- forward_spectrum: float32 [2, 6, 32, 64, 128], P('angle', None, 'gx', 'gy'), may hold values from -6 to 6
- adjoint_spectrum: float32 [2, 6, 32, 64, 128], P('angle', None, 'gx', 'gy'), may hold values from -6 to 6
- permittivity: float32 [32, 64, 128], P('gx', 'gy'), may hold values from 1 to 12
- phase_table: float32 [2, 2], replicated, may hold values from -3.140625 to 3.140625
- angle_index: int32 [2], P('angle'), may hold values from 0 to 1, each once
- design_tiles: int32 [4], replicated, may hold values from 0 to 15, as said below
Outputs:
- forward_transform: float32 [2, 6, 32, 64, 128], P('angle', None, 'gx', 'gy')
- adjoint_transform: float32 [2, 6, 32, 64, 128], P('angle', None, 'gx', 'gy')
- gradient: float32 [32, 64, 128], P('gx', 'gy', 'angle')
Inputs may be any that keep to these rules, and one draw needn't show every extreme that they name: `angle_index`: every row of phase_table is used by exactly one angle. `design_tiles`: 4 distinct tile numbers; tiles 0 and 15 are always among them.
All inputs are finite; a program needn't handle non-finite values.
Results may differ from a plain program's by a relative error of at most 0.0001.
Values sent between devices are 32-bit elements; how exact they have to be, the bound alone decides.
No kernel may reach another device: no remote copies, remote signals or barrier semaphores. Data moves between devices by JAX's collectives and lax.ppermute only.
A program may use at most 64 MiB of HBM per device.

v0:
```python
import math

import jax
import jax.numpy as jnp
from jax import lax
from jax.sharding import PartitionSpec as P

STEPS = 3


courant = 0.5
omega_step = 0.7


def padded_2(shard, sides, width):
    for axis, dim in sides:
        size, length = (lax.axis_size(axis), shard.shape[dim])
        up = [(i, (i + 1) % size) for i in range(size)]
        down = [(j, i) for i, j in up]
        last = lax.slice_in_dim(shard, length - width, length, axis=dim)
        first = lax.slice_in_dim(shard, 0, width, axis=dim)
        before = lax.ppermute(last, axis, up)
        after = lax.ppermute(first, axis, down)
        shard = jnp.concatenate([before, shard, after], axis=dim)
    return shard


def rotate_runs(pair, cosine, sine):
    sine_full = sine.reshape((2,) + (1,) * (pair.ndim - 2))
    real_part = pair[:, 0]
    imag_part = pair[:, 1]
    return jnp.stack(
        [real_part * cosine - imag_part * sine_full, real_part * sine_full + imag_part * cosine],
        axis=1,
    )


def next_depth(field):
    return jnp.concatenate([field[..., 1:], jnp.zeros_like(field[..., :1])], axis=-1)


def prev_depth(field):
    return jnp.concatenate([jnp.zeros_like(field[..., :1]), field[..., :-1]], axis=-1)


def next_local(field, axis):
    count = field.shape[axis]
    upper = lax.slice_in_dim(field, 1, count, 1, axis)
    pad_zero = jnp.zeros_like(lax.slice_in_dim(field, 0, 1, 1, axis))
    return jnp.concatenate([upper, pad_zero], axis=axis)


def prev_local(field, axis):
    count = field.shape[axis]
    lower = lax.slice_in_dim(field, 0, count - 1, 1, axis)
    pad_zero = jnp.zeros_like(lax.slice_in_dim(field, 0, 1, 1, axis))
    return jnp.concatenate([pad_zero, lower], axis=axis)


def local_curl_forward(efield):
    comp_x = efield[:, :, 0]
    comp_y = efield[:, :, 1]
    comp_z = efield[:, :, 2]
    dz_dy = next_local(comp_z, 3) - comp_z
    dy_dz = next_depth(comp_y) - comp_y
    dx_dz = next_depth(comp_x) - comp_x
    dz_dx = next_local(comp_z, 2) - comp_z
    dy_dx = next_local(comp_y, 2) - comp_y
    dx_dy = next_local(comp_x, 3) - comp_x
    return jnp.stack([dz_dy - dy_dz, dx_dz - dz_dx, dy_dx - dx_dy], axis=2)


def local_curl_backward(hfield):
    comp_x = hfield[:, :, 0]
    comp_y = hfield[:, :, 1]
    comp_z = hfield[:, :, 2]
    first = comp_z - prev_local(comp_z, 3) - (comp_y - prev_depth(comp_y))
    second = comp_x - prev_depth(comp_x) - (comp_z - prev_local(comp_z, 2))
    third = comp_y - prev_local(comp_y, 2) - (comp_x - prev_local(comp_x, 3))
    return jnp.stack([first, second, third], axis=2)


def rim_turns(count, inner, place, last):
    rows = jnp.arange(count + 2 * inner)
    below = jnp.where((place == 0) & (rows < inner), -1.0, 0.0)
    above = jnp.where((place == last) & (rows >= inner + count), 1.0, 0.0)
    return (below + above).astype(jnp.float32)


def deep_advance(fields, spectrum, permittivity, angle_x, angle_y, run_sign):
    runs, planes, size_x, size_y, depth = fields.shape
    stacked = jnp.concatenate(
        [fields.reshape((runs * planes, size_x, size_y, depth)), permittivity[None]], axis=0
    )
    padded = padded_2(stacked, (("gx", 1), ("gy", 2)), STEPS)
    wide_x = size_x + 2 * STEPS
    wide_y = size_y + 2 * STEPS
    perm_pad = padded[runs * planes]
    field_pad = padded[: runs * planes].reshape((runs, 2, 2, 3, wide_x, wide_y, depth))
    turn_x = rim_turns(size_x, STEPS, lax.axis_index("gx"), lax.axis_size("gx") - 1)
    turn_y = rim_turns(size_y, STEPS, lax.axis_index("gy"), lax.axis_size("gy") - 1)
    turn = run_sign[:, None, None] * (
        angle_x * turn_x[None, :, None] + angle_y * turn_y[None, None, :]
    )
    cos_turn = jnp.cos(turn)[:, None, None, :, :, None]
    sin_turn = jnp.sin(turn)[:, None, None, :, :, None]
    real_part = field_pad[:, :, 0]
    imag_part = field_pad[:, :, 1]
    turned = jnp.stack(
        [real_part * cos_turn - imag_part * sin_turn, real_part * sin_turn + imag_part * cos_turn],
        axis=2,
    )
    efield = turned[:, 0]
    hfield = turned[:, 1]
    coef = courant / perm_pad
    for step in range(STEPS):
        hfield = hfield - courant * local_curl_forward(efield)
        efield = efield + coef * local_curl_backward(hfield)
        theta = omega_step * (step + 1)
        inner = efield[:, :, :, STEPS : STEPS + size_x, STEPS : STEPS + size_y]
        spectrum = spectrum + rotate_runs(
            inner, math.cos(theta), jnp.full((2,), math.sin(theta), jnp.float32)
        )
    return spectrum


def shards(
    forward_fields,
    adjoint_fields,
    forward_spectrum,
    adjoint_spectrum,
    permittivity,
    phase_table,
    angle_index,
    design_tiles,
):
    cells = forward_fields.shape[2:]
    fields = jnp.concatenate([forward_fields, adjoint_fields], axis=0)
    spectrum = jnp.concatenate([forward_spectrum, adjoint_spectrum], axis=0).reshape(
        (2, 2, 3) + cells
    )
    table_rows = phase_table.shape[0]
    picked = (jnp.arange(table_rows) == angle_index[0]).astype(jnp.float32)
    angle_x = jnp.sum(picked * phase_table[:, 0])
    angle_y = jnp.sum(picked * phase_table[:, 1])
    run_sign = jnp.array([1.0, -1.0], jnp.float32)
    spectrum = deep_advance(fields, spectrum, permittivity, angle_x, angle_y, run_sign)
    local_term = jnp.sum(spectrum[0, 0] * spectrum[1, 0] - spectrum[0, 1] * spectrum[1, 1], axis=0)
    own_tile = lax.axis_index("gx") * lax.axis_size("gy") + lax.axis_index("gy")
    chosen = jnp.any(design_tiles == own_tile)
    local_term = jnp.where(chosen, local_term, jnp.zeros_like(local_term))
    groups = lax.axis_size("angle")
    whole = lax.psum(local_term, "angle")
    share = whole.shape[2] // groups
    summed = lax.dynamic_slice_in_dim(whole, lax.axis_index("angle") * share, share, 2)
    gradient = summed * (1.0 / groups)
    forward_out = spectrum[0].reshape((1, 6) + cells)
    adjoint_out = spectrum[1].reshape((1, 6) + cells)
    return (forward_out, adjoint_out, gradient)


def solution(mesh):
    in_specs = (
        P("angle", None, "gx", "gy", None),
        P("angle", None, "gx", "gy", None),
        P("angle", None, "gx", "gy", None),
        P("angle", None, "gx", "gy", None),
        P("gx", "gy", None),
        P(),
        P("angle"),
        P(),
    )
    out_specs = (
        P("angle", None, "gx", "gy", None),
        P("angle", None, "gx", "gy", None),
        P("gx", "gy", "angle"),
    )
    return jax.shard_map(shards, mesh=mesh, in_specs=in_specs, out_specs=out_specs, check_vma=False)
```

profile of v0, /device:TPU:0, one launch (start us, length us, event | category | flops | bytes accessed | tf_op | source)
XLA Modules:
  0.0 102.0 jit_solution(16161755186824042370)
XLA Ops:
  7.2 1.5 %pad_maximum_fusion.2 = f32[2,12,8,16,128]{4,3,2,1,0:T(8,128)S(1)} fusion(f32[1,12,8,16,128]{4,3,2,1,0:T(8,128)} %param.10, f32[1,12,8,16,128]{4,3,2,1,0:T(8,128)} %param.9), kind=kLoop, calls=%fused_computation.21 | loop fusion | flops 393216 | bytes 3145728 | tf_op jit(solution)/shard_map/concatenate | solution.py:138
  8.8 0.9 pad_maximum_fusion.11
  9.7 0.5 collective-permute-start
  10.2 2.0 %collective-permute-start.1 = (f32[25,3,16,128]{3,2,1,0:T(8,128)S(1)}, f32[25,3,16,128]{3,2,1,0:T(8,128)S(1)}, u32[]{:S(2)}, u32[]{:S(2)}) collective-permute-start(f32[25,3,16,128]{3,2,1,0:T(8,128)S(1)} %get-tuple-element.54), channel_id=1, source_target_pairs={{4,0},{8,4},{12,8},{0,12},{5,1},{9,5},{13,9},{1,13},{6,2},{10,6},{... | collective-permute-start | bytes 1843208 | tf_op jit(solution)/shard_map/ppermute | solution.py:23
  13.0 0.6 fusion.12
  13.6 0.7 fusion.17
  14.2 0.6 compare_reduce_fusion
  14.9 1.2 %pad_maximum_fusion.3 = f32[2,6,8,16,128]{4,3,2,1,0:T(8,128)S(1)} fusion(f32[1,6,8,16,128]{4,3,2,1,0:T(8,128)} %param.12, f32[1,6,8,16,128]{4,3,2,1,0:T(8,128)} %param.11), kind=kLoop, calls=%fused_computation.22 | loop fusion | flops 196608 | bytes 1572864 | tf_op jit(solution)/shard_map/concatenate | solution.py:139
  16.0 8.2 %collective-permute-done = f32[25,3,16,128]{3,2,1,0:T(8,128)S(1)} collective-permute-done((f32[25,3,16,128]{3,2,1,0:T(8,128)}, f32[25,3,16,128]{3,2,1,0:T(8,128)S(1)}, u32[]{:S(2)}, u32[]{:S(2)}) %collective-permute-start) | collective-permute-done | bytes 614432 | tf_op jit(solution)/shard_map/ppermute | solution.py:22
  24.3 1.9 %collective-permute-done.1 = f32[25,3,16,128]{3,2,1,0:T(8,128)S(1)} collective-permute-done((f32[25,3,16,128]{3,2,1,0:T(8,128)S(1)}, f32[25,3,16,128]{3,2,1,0:T(8,128)S(1)}, u32[]{:S(2)}, u32[]{:S(2)}) %collective-permute-start.1) | collective-permute-done | bytes 614432 | tf_op jit(solution)/shard_map/ppermute | solution.py:23
  26.5 2.0 %collective-permute-start.2 = (f32[25,14,3,128]{3,1,2,0:T(8,128)S(1)}, f32[25,14,3,128]{3,1,2,0:T(8,128)S(1)}, u32[]{:S(2)}, u32[]{:S(2)}) collective-permute-start(f32[25,14,3,128]{3,1,2,0:T(8,128)S(1)} %copy.38), channel_id=1, source_target_pairs={{0,1},{1,2},{2,3},{3,0},{4,5},{5,6},{6,7},{7,4},{8,9},{9,10},{10,1... | collective-permute-start | bytes 1612808 | tf_op jit(solution)/shard_map/ppermute | solution.py:22
  28.6 2.1 %collective-permute-start.3 = (f32[25,14,3,128]{3,1,2,0:T(8,128)S(1)}, f32[25,14,3,128]{3,1,2,0:T(8,128)S(1)}, u32[]{:S(2)}, u32[]{:S(2)}) collective-permute-start(f32[25,14,3,128]{3,1,2,0:T(8,128)S(1)} %copy.39), channel_id=1, source_target_pairs={{1,0},{2,1},{3,2},{0,3},{5,4},{6,5},{7,6},{4,7},{9,8},{10,9},{11,1... | collective-permute-start | bytes 1612808 | tf_op jit(solution)/shard_map/ppermute | solution.py:23
  30.7 0.7 fusion.16
  31.6 13.8 %collective-permute-done.2 = f32[25,14,3,128]{3,1,2,0:T(8,128)S(1)} collective-permute-done((f32[25,14,3,128]{3,1,2,0:T(8,128)S(1)}, f32[25,14,3,128]{3,1,2,0:T(8,128)S(1)}, u32[]{:S(2)}, u32[]{:S(2)}) %collective-permute-start.2) | collective-permute-done | bytes 537632 | tf_op jit(solution)/shard_map/ppermute | solution.py:22
  45.6 12.5 %collective-permute-done.3 = f32[25,14,3,128]{3,1,2,0:T(8,128)S(1)} collective-permute-done((f32[25,14,3,128]{3,1,2,0:T(8,128)S(1)}, f32[25,14,3,128]{3,1,2,0:T(8,128)S(1)}, u32[]{:S(2)}, u32[]{:S(2)}) %collective-permute-start.3) | collective-permute-done | bytes 537632 | tf_op jit(solution)/shard_map/ppermute | solution.py:23
  58.4 1.7 %pad_maximum_fusion = f32[25,14,22,128]{3,2,1,0:T(8,128)S(1)} fusion(f32[25,14,3,128]{3,2,1,0:T(4,128)S(1)} %copy.41, f32[25,3,16,128]{3,2,1,0:T(8,128)S(1)} %collective-permute-done.1, f32[1,8,16,128]{3,2,1,0:T(8,128)S(1)} %bitcast.196, f32[24,8,16,128]{3,2,1,0:T(8,128)S(1)} %bitcast.178, f32[25,3,16,128]{3,2,1,0:T(8,128)S(1)} %collective-permute-done, ...), kind=kLoop, calls=%fused_computation | loop fusion | flops 4928000 | bytes 7884800 | tf_op jit(solution)/shard_map/concatenate | solution.py:24
  60.4 0.3 fusion.18
  60.7 0.5 multiply_subtract_fusion
  62.3 0.4 subtract_bitcast_fusion.17
  62.7 0.3 fusion.3
  63.3 0.7 subtract_bitcast_fusion.14
  65.1 0.4 subtract_bitcast_fusion.11
  66.0 0.6 subtract_bitcast_fusion.8
  66.6 0.5 fusion.6
  68.3 0.3 subtract_bitcast_fusion.5
  68.6 0.4 fusion.7
  69.3 0.7 subtract_bitcast_fusion.2
  70.0 0.7 fusion.8
  71.2 1.3 %broadcast_select_fusion = f32[8,16,128]{2,1,0:T(8,128)} fusion(f32[8,16,128]{2,1,0:T(8,128)S(1)} %fusion.10, pred[]{:T(512)} %compare_reduce_fusion), kind=kLoop, calls=%fused_computation.83 | loop fusion | flops 16384 | bytes 131073 | tf_op jit(solution)/shard_map/jit(_where)/select_n | solution.py:151
  72.5 1.0 fusion.19
  73.5 20.1 %all-reduce.38.cloned.1.call-done = f32[8,16,128]{2,1,0:T(8,128)} async-done(((f32[8,16,128]{2,1,0:T(8,128)}), f32[8,16,128]{2,1,0:T(8,128)}) %all-reduce.38.cloned.1.call-update) | async-done | bytes 65552 | tf_op jit(solution)/shard_map/psum | solution.py:153
  93.6 1.6 %dynamic-slice_multiply_fusion = f32[8,16,64]{2,1,0:T(8,128)} fusion(f32[8,16,128]{2,1,0:T(8,128)} %all-reduce.38.cloned.1.call-done, s32[]{:T(128)S(6)} %select_n.47), kind=kLoop, calls=%fused_computation.82 | loop fusion | flops 8192 | bytes 65540 | tf_op jit(solution)/shard_map/mul | solution.py:156
  (58 shorter events, 6.2 us)
Async XLA Ops:
  7.2 1.6 %copy-start = (f32[8,16,128]{2,1,0:T(8,128)S(1)}, f32[8,16,128]{2,1,0:T(8,128)}, u32[]{:S(2)}) copy-start(f32[8,16,128]{2,1,0:T(8,128)} %param.13) | copy-start | bytes 196612
  7.2 86.4 %all-reduce.38.cloned.1.call-start = ((), (), s32[]{:S(2)}) async-start(), calls=%async_computation | async-start | bytes 131072 | tf_op jit(solution)/shard_map/psum | solution.py:153
  8.7 4.0 %copy-start.1 = (f32[2,2]{1,0:T(2,128)S(1)}, f32[2,2]{1,0:T(2,128)}, u32[]{:S(2)}) copy-start(f32[2,2]{1,0:T(2,128)} %param.14) | copy-start | bytes 52
  8.7 5.5 %copy-start.3 = (s32[4]{0:T(128)S(1)}, s32[4]{0:T(128)}, u32[]{:S(2)}) copy-start(s32[4]{0:T(128)} %param.16) | copy-start | bytes 52
  9.7 14.6 %collective-permute-start = (f32[25,3,16,128]{3,2,1,0:T(8,128)}, f32[25,3,16,128]{3,2,1,0:T(8,128)S(1)}, u32[]{:S(2)}, u32[]{:S(2)}) collective-permute-start(f32[25,3,16,128]{3,2,1,0:T(8,128)} %get-tuple-element.53), channel_id=1, source_target_pairs={{0,4},{4,8},{8,12},{12,0},{1,5},{5,9},{9,13},{13,1},{2,6},{6,10},{... | collective-permute-start | bytes 1843208 | tf_op jit(solution)/shard_map/ppermute | solution.py:22
  10.2 16.0 %collective-permute-start.1 = (f32[25,3,16,128]{3,2,1,0:T(8,128)S(1)}, f32[25,3,16,128]{3,2,1,0:T(8,128)S(1)}, u32[]{:S(2)}, u32[]{:S(2)}) collective-permute-start(f32[25,3,16,128]{3,2,1,0:T(8,128)S(1)} %get-tuple-element.54), channel_id=1, source_target_pairs={{4,0},{8,4},{12,8},{0,12},{5,1},{9,5},{13,9},{1,13},{6,2},{10,6},{... | collective-permute-start | bytes 1843208 | tf_op jit(solution)/shard_map/ppermute | solution.py:23
  26.4 5.0 %copy-start.2 = (f32[2]{0:T(128)S(1)}, f32[2]{0:T(128)}, u32[]{:S(2)}) copy-start(f32[2]{0:T(128)} %constant.22.clone) | copy-start | bytes 28
  26.5 18.8 %collective-permute-start.2 = (f32[25,14,3,128]{3,1,2,0:T(8,128)S(1)}, f32[25,14,3,128]{3,1,2,0:T(8,128)S(1)}, u32[]{:S(2)}, u32[]{:S(2)}) collective-permute-start(f32[25,14,3,128]{3,1,2,0:T(8,128)S(1)} %copy.38), channel_id=1, source_target_pairs={{0,1},{1,2},{2,3},{3,0},{4,5},{5,6},{6,7},{7,4},{8,9},{9,10},{10,1... | collective-permute-start | bytes 1612808 | tf_op jit(solution)/shard_map/ppermute | solution.py:22
  28.6 29.5 %collective-permute-start.3 = (f32[25,14,3,128]{3,1,2,0:T(8,128)S(1)}, f32[25,14,3,128]{3,1,2,0:T(8,128)S(1)}, u32[]{:S(2)}, u32[]{:S(2)}) collective-permute-start(f32[25,14,3,128]{3,1,2,0:T(8,128)S(1)} %copy.39), channel_id=1, source_target_pairs={{1,0},{2,1},{3,2},{0,3},{5,4},{6,5},{7,6},{4,7},{9,8},{10,9},{11,1... | collective-permute-start | bytes 1612808 | tf_op jit(solution)/shard_map/ppermute | solution.py:23
Sparse Core Ops, SparseCore 0:
  72.6 20.8 all-reduce.37
where the time goes:
time: 102 us
  waiting for transfers between devices  56.5 us (55%)
  other arithmetic  18.3 us (18%)
  between operations  15.1 us (15%)
  starting transfers between devices  6.56 us (6%)
  local copies, waits for them, and re-layouts  5.53 us (5%)
    ppermute x2, waiting for transfers between devices, padded_2(): before = lax.ppermute(last, axis, up)  22 us
    psum x1, waiting for transfers between devices, shards(): whole = lax.psum(local_term, 'angle')  20.1 us
    ppermute x2, waiting for transfers between devices, padded_2(): after = lax.ppermute(first, axis, down)  14.4 us
    ppermute x2, starting transfers between devices, padded_2(): after = lax.ppermute(first, axis, down)  4.05 us
    ppermute x2, starting transfers between devices, padded_2(): before = lax.ppermute(last, axis, up)  2.47 us
    another operation x3, other arithmetic, local_curl_backward(): return jnp.stack([first, second, third], axis=2)  2.08 us
  transfers between devices with their start and end apart: 5, of which 5 were waited for; matrix products, arithmetic and copies ran while one was open for 5% of the time, Pallas kernels for 0%

commit v1 on v0

v1 whole, which is shorter than its diff:
```python
import functools
import math

import jax
import jax.numpy as jnp
from jax import lax
from jax.experimental import pallas as pl
from jax.experimental.pallas import tpu as pltpu
from jax.sharding import PartitionSpec as P

STEPS = 3
SUB = 8

courant = 0.5
omega_step = 0.7

VMEM = pl.BlockSpec(memory_space=pltpu.VMEM)
SMEM = pl.BlockSpec(memory_space=pltpu.SMEM)
ANY = pl.BlockSpec(memory_space=pl.ANY)


def moved(cells, dx, dy):
    return {(x + dx, y + dy) for x, y in cells}


def cone(nx, ny):
    block = {(x, y) for x in range(nx) for y in range(ny)}
    ex, ey, ez = block, block, block
    hx, hy, hz, eps = set(), set(), set(), set()
    for _ in range(STEPS):
        eps = eps | ex | ey | ez
        hx, hy, hz = (
            hx | ey | ez | moved(ez, 0, -1),
            hy | ex | ez | moved(ez, -1, 0),
            hz | ex | moved(ex, 0, -1) | ey | moved(ey, -1, 0),
        )
        ex, ey, ez = (
            ex | hy | hz | moved(hz, 0, 1),
            ey | hx | hz | moved(hz, 1, 0),
            ez | hx | moved(hx, 0, 1) | hy | moved(hy, 1, 0),
        )
    return (ex, ey, ez), (hx, hy, hz), eps


PLANES = [(run, kind, part, comp) for run in (0, 1) for kind in (0, 1) for comp in (0, 1, 2) for part in (0, 1)]


class Plan:
    def __init__(self, nx, ny):
        efield, hfield, eps = cone(nx, ny)
        self.nx, self.ny = nx, ny

        def cells(plane):
            if plane is None:
                return eps
            return (efield, hfield)[plane[1]][plane[3]]

        planes = PLANES + [None]
        self.x_low, self.x_high, self.y_low, self.y_high = [], [], [], []
        for plane in planes:
            need = cells(plane)
            self.x_low += [(plane, x) for x in range(-STEPS, 0) if any((x, y) in need for y in range(ny))]
            self.x_high += [(plane, x) for x in range(nx, nx + STEPS) if any((x, y) in need for y in range(ny))]
            self.y_low += [(plane, y) for y in range(-STEPS, 0) if any((x, y) in need for x in range(nx))]
            self.y_high += [(plane, y) for y in range(ny, ny + STEPS) if any((x, y) in need for x in range(nx))]
        self.corner_low, self.corner_high = [], []
        for out, layers in ((self.corner_low, range(-STEPS, 0)), (self.corner_high, range(nx, nx + STEPS))):
            for rows in (range(-STEPS, 0), range(ny, ny + STEPS)):
                for plane in planes:
                    need = cells(plane)
                    out += [(plane, x, y) for x in layers for y in rows if (x, y) in need]


def row_of(plane, nx, ny, x, y):
    _, kind, part, comp = plane
    return ((kind * 6 + part * 3 + comp) * nx + x) * ny + y


def pack_kernel(plan, fwd, adj, eps, x_up, x_down, z_up, z_down):
    nx, ny = plan.nx, plan.ny

    def source(plane, x, y):
        if plane is None:
            return eps, x * ny + y
        return (fwd, adj)[plane[0]], row_of(plane, nx, ny, x, y)

    for entries, shift, out in ((plan.y_low, ny, z_up), (plan.y_high, -ny, z_down)):
        for i, (plane, y) in enumerate(entries):
            ref, row = source(plane, 0, y + shift)
            out[pl.ds(i * nx, nx), :] = ref[pl.ds(row, nx, stride=ny), :]
    for entries, shift, out in ((plan.x_low, nx, x_up), (plan.x_high, -nx, x_down)):
        for i, (plane, x) in enumerate(entries):
            ref, row = source(plane, x + shift, 0)
            out[pl.ds(i * ny, ny), :] = ref[pl.ds(row, ny), :]


def corner_kernel(plan, z_low, z_high, c_up, c_down):
    nx, ny = plan.nx, plan.ny
    low = {entry: i for i, entry in enumerate(plan.y_low)}
    high = {entry: i for i, entry in enumerate(plan.y_high)}
    for entries, shift, out in ((plan.corner_low, nx, c_up), (plan.corner_high, -nx, c_down)):
        for i, (plane, x, y) in enumerate(entries):
            ref, at = (z_low, low[plane, y]) if y < 0 else (z_high, high[plane, y])
            out[pl.ds(i, 1), :] = ref[pl.ds(at * nx + x + shift, 1), :]


def turned(real, imag, cosine, sine):
    return real * cosine - imag * sine, real * sine + imag * cosine


def advance_kernel(plan, groups, fwd, adj, spec_f, spec_a, eps, x_low, x_high, z_low, z_high, c_low, c_high,
                   table, index, tiles, out_f, out_a, parts, state, coef, turns):
    nx, ny = plan.nx, plan.ny
    wide_x, ring = nx + 2 * STEPS, ny + SUB

    def base(level, kind, run, part, comp):
        return (((level * 2 + kind) * 2 + run) * 6 + part * 3 + comp) * wide_x * ring

    def place(plane, x, y):
        start = 0 if plane is None else base(0, plane[1], plane[0], plane[2], plane[3])
        return (coef if plane is None else state), start + (x + STEPS) * ring + y % ring

    for run, ref in enumerate((fwd, adj)):
        for kind in (0, 1):
            for part in (0, 1):
                for comp in (0, 1, 2):
                    for x in range(nx):
                        source = row_of((run, kind, part, comp), nx, ny, x, 0)
                        target = base(0, kind, run, part, comp) + (x + STEPS) * ring
                        state[pl.ds(target, ny), :] = ref[pl.ds(source, ny), :]
    for x in range(nx):
        coef[pl.ds((x + STEPS) * ring, ny), :] = eps[pl.ds(x * ny, ny), :]

    row = index[0]
    phi_x, phi_y = table[row, 0], table[row, 1]
    at_x, at_y = lax.axis_index("gx"), lax.axis_index("gy")
    none = jnp.float32(0.0)
    ax_low = jnp.where(at_x == 0, -phi_x, none)
    ax_high = jnp.where(at_x == lax.axis_size("gx") - 1, phi_x, none)
    ay_low = jnp.where(at_y == 0, -phi_y, none)
    ay_high = jnp.where(at_y == lax.axis_size("gy") - 1, phi_y, none)
    sub = lax.broadcasted_iota(jnp.int32, (SUB, 128), 0)
    angles = jnp.zeros((SUB, 128), jnp.float32)
    for i, angle in enumerate((ax_low, ax_high, ay_low, ay_high, ax_low + ay_low, ax_low + ay_high,
                               ax_high + ay_low, ax_high + ay_high)):
        angles = jnp.where(sub == i, angle, angles)
    turns[pl.ds(0, SUB), :] = jnp.cos(angles)
    turns[pl.ds(SUB, SUB), :] = jnp.sin(angles)

    def turn(i, run):
        cosine = turns[pl.ds(i, 1), :]
        sine = turns[pl.ds(SUB + i, 1), :]
        return cosine, (sine if run == 0 else -sine)

    for which, entries, ref in ((0, plan.x_low, x_low), (1, plan.x_high, x_high)):
        at = {entry: i for i, entry in enumerate(entries)}
        for (plane, x), i in at.items():
            if plane is None:
                target, row = place(plane, x, 0)
                target[pl.ds(row, ny), :] = ref[pl.ds(i * ny, ny), :]
            elif plane[2] == 0:
                twin = plane[:2] + (1,) + plane[3:]
                cosine, sine = turn(which, plane[0])
                real, imag = turned(ref[pl.ds(i * ny, ny), :], ref[pl.ds(at[twin, x] * ny, ny), :], cosine, sine)
                state[pl.ds(place(plane, x, 0)[1], ny), :] = real
                state[pl.ds(place(twin, x, 0)[1], ny), :] = imag
    for which, entries, ref in ((2, plan.y_low, z_low), (3, plan.y_high, z_high)):
        at = {entry: i for i, entry in enumerate(entries)}
        for (plane, y), i in at.items():
            if plane is None:
                target, row = place(plane, 0, y)
                target[pl.ds(row, nx, stride=ring), :] = ref[pl.ds(i * nx, nx), :]
            elif plane[2] == 0:
                twin = plane[:2] + (1,) + plane[3:]
                cosine, sine = turn(which, plane[0])
                real, imag = turned(ref[pl.ds(i * nx, nx), :], ref[pl.ds(at[twin, y] * nx, nx), :], cosine, sine)
                state[pl.ds(place(plane, 0, y)[1], nx, stride=ring), :] = real
                state[pl.ds(place(twin, 0, y)[1], nx, stride=ring), :] = imag
    for which, entries, ref in ((4, plan.corner_low, c_low), (6, plan.corner_high, c_high)):
        at = {entry: i for i, entry in enumerate(entries)}
        for (plane, x, y), i in at.items():
            target, row = place(plane, x, y)
            if plane is None:
                target[pl.ds(row, 1), :] = ref[pl.ds(i, 1), :]
            elif plane[2] == 0:
                twin = plane[:2] + (1,) + plane[3:]
                cosine, sine = turn(which + (y >= 0), plane[0])
                real, imag = turned(ref[pl.ds(i, 1), :], ref[pl.ds(at[twin, x, y], 1), :], cosine, sine)
                state[pl.ds(row, 1), :] = real
                state[pl.ds(place(twin, x, y)[1], 1), :] = imag

    @pl.loop(0, wide_x)
    def _(x):
        rows = pl.ds(pl.multiple_of(x * ring, SUB), ring)
        coef[rows, :] = (0.5 * courant) / coef[rows, :]

    lane = lax.broadcasted_iota(jnp.int32, (ring, 128), 1)
    first, last = lane == 0, lane == 127

    def next_z(value):
        return jnp.where(last, 0.0, pltpu.roll(value, 127, 1))

    def prev_z(value):
        return jnp.where(first, 0.0, pltpu.roll(value, 1, 1))

    def next_y(value):
        return pltpu.roll(value, ring - 1, 0)

    def prev_y(value):
        return pltpu.roll(value, 1, 0)

    for step in range(STEPS):

        def rows(level, kind, run, part, comp, x):
            return pl.ds(pl.multiple_of(base(level, kind, run, part, comp) + x * ring, SUB), ring)

        def get(level, kind, run, part, comp, x):
            return state[rows(level, kind, run, part, comp, x), :]

        def update_h(run, part, x):
            ex, ey, ez = (get(step, 0, run, part, comp, x) for comp in range(3))
            ey_x, ez_x = get(step, 0, run, part, 1, x + 1), get(step, 0, run, part, 2, x + 1)
            hx, hy, hz = (get(step, 1, run, part, comp, x) for comp in range(3))
            if step == 0:
                hx, hy, hz = hx + hx, hy + hy, hz + hz
            hx = hx - ((next_y(ez) - ez) - (next_z(ey) - ey))
            hy = hy - ((next_z(ex) - ex) - (ez_x - ez))
            hz = hz - ((ey_x - ey) - (next_y(ex) - ex))
            for comp, value in enumerate((hx, hy, hz)):
                state[rows(step + 1, 1, run, part, comp, x), :] = value
            return (ex, ey, ez), (hx, hy, hz)

        def update_e(run, part, x, efield, hfield):
            ex, ey, ez = efield
            hx, hy, hz = hfield
            hy_x, hz_x = get(step + 1, 1, run, part, 1, x - 1), get(step + 1, 1, run, part, 2, x - 1)
            scale = coef[pl.ds(pl.multiple_of(x * ring, SUB), ring), :]
            ex = ex + scale * ((hz - prev_y(hz)) - (hy - prev_z(hy)))
            ey = ey + scale * ((hx - prev_z(hx)) - (hz - hz_x))
            ez = ez + scale * ((hy - hy_x) - (hx - prev_y(hx)))
            for comp, value in enumerate((ex, ey, ez)):
                state[rows(step + 1, 0, run, part, comp, x), :] = value

        for run in (0, 1):
            for part in (0, 1):
                update_h(run, part, step)

        @pl.loop(step + 1, wide_x - step - 1)
        def _(x):
            for run in (0, 1):
                for part in (0, 1):
                    efield, hfield = update_h(run, part, x)
                    update_e(run, part, x, efield, hfield)

    own_tile = at_x * lax.axis_size("gy") + at_y
    chosen = tiles[0] == own_tile
    for i in range(1, tiles.shape[0]):
        chosen = jnp.logical_or(chosen, tiles[i] == own_tile)
    weight = jnp.where(chosen, jnp.float32(1.0 / groups), none)
    share = parts.shape[2]
    shift = lax.rem(groups - lax.axis_index("angle"), groups) * share

    @pl.loop(0, nx * (ny // SUB))
    def _(i):
        x, tile = i // (ny // SUB), lax.rem(i, ny // SUB)
        total = jnp.zeros((SUB, 128), jnp.float32)
        for comp in range(3):
            ends = []
            for run, (spec, out) in enumerate(((spec_f, out_f), (spec_a, out_a))):
                at = [pl.ds(pl.multiple_of(((part * 3 + comp) * nx + x) * ny + tile * SUB, SUB), SUB) for part in (0, 1)]
                real, imag = spec[at[0], :], spec[at[1], :]
                for step in range(STEPS):
                    theta = omega_step * (step + 1)
                    efield = [
                        state[pl.ds(pl.multiple_of(base(step + 1, 0, run, part, comp) + (x + STEPS) * ring + tile * SUB, SUB), SUB), :]
                        for part in (0, 1)
                    ]
                    more = turned(efield[0], efield[1], math.cos(theta), math.sin(theta))
                    real, imag = real + more[0], imag + more[1]
                out[at[0], :], out[at[1], :] = real, imag
                ends.append((real, imag))
            total = total + (ends[0][0] * ends[1][0] - ends[0][1] * ends[1][1])
        total = pltpu.roll(total * weight, shift, 1)
        for k in range(groups):
            parts[k, pl.ds(pl.multiple_of(i * SUB, SUB), SUB), :] = total[:, k * share : (k + 1) * share]


def ring_pairs(axis, offset):
    size = lax.axis_size(axis)
    return [(i, (i + offset) % size) for i in range(size)]


def shards(
    forward_fields,
    adjoint_fields,
    forward_spectrum,
    adjoint_spectrum,
    permittivity,
    phase_table,
    angle_index,
    design_tiles,
):
    nx, ny, depth = permittivity.shape
    plan = Plan(nx, ny)
    groups = lax.axis_size("angle")
    wide_x, ring = nx + 2 * STEPS, ny + SUB

    def rows(array):
        return array.reshape((-1, depth))

    def lines(count):
        return jax.ShapeDtypeStruct((count, depth), jnp.float32)

    fwd, adj, eps = rows(forward_fields), rows(adjoint_fields), rows(permittivity)
    params = pltpu.CompilerParams(vmem_limit_bytes=40 * 2**20)
    with jax.named_scope("pack_faces"):
        x_up, x_down, z_up, z_down = pl.pallas_call(
            functools.partial(pack_kernel, plan),
            out_shape=(
                lines(len(plan.x_low) * ny),
                lines(len(plan.x_high) * ny),
                lines(len(plan.y_low) * nx),
                lines(len(plan.y_high) * nx),
            ),
            in_specs=[VMEM] * 3,
            out_specs=[VMEM] * 4,
            compiler_params=params,
        )(fwd, adj, eps)
    with jax.named_scope("send_faces"):
        z_low = lax.ppermute(z_up, "gy", ring_pairs("gy", 1))
        z_high = lax.ppermute(z_down, "gy", ring_pairs("gy", -1))
        x_low = lax.ppermute(x_up, "gx", ring_pairs("gx", 1))
        x_high = lax.ppermute(x_down, "gx", ring_pairs("gx", -1))
    with jax.named_scope("relay_corners"):
        c_up, c_down = pl.pallas_call(
            functools.partial(corner_kernel, plan),
            out_shape=(lines(-(-len(plan.corner_low) // SUB) * SUB), lines(-(-len(plan.corner_high) // SUB) * SUB)),
            in_specs=[VMEM] * 2,
            out_specs=[VMEM] * 2,
            compiler_params=params,
        )(z_low, z_high)
        c_low = lax.ppermute(c_up, "gx", ring_pairs("gx", 1))
        c_high = lax.ppermute(c_down, "gx", ring_pairs("gx", -1))
    with jax.named_scope("advance"):
        out_f, out_a, parts = pl.pallas_call(
            functools.partial(advance_kernel, plan, groups),
            out_shape=(
                lines(6 * nx * ny),
                lines(6 * nx * ny),
                jax.ShapeDtypeStruct((groups, nx * ny, depth // groups), jnp.float32),
            ),
            in_specs=[VMEM] * 11 + [SMEM] * 3,
            out_specs=[VMEM] * 3,
            scratch_shapes=[
                pltpu.VMEM(((STEPS + 1) * 24 * wide_x * ring, depth), jnp.float32),
                pltpu.VMEM((wide_x * ring, depth), jnp.float32),
                pltpu.VMEM((2 * SUB, depth), jnp.float32),
            ],
            compiler_params=params,
        )(fwd, adj, rows(forward_spectrum), rows(adjoint_spectrum), eps, x_low, x_high, z_low, z_high, c_low, c_high,
          phase_table, angle_index, design_tiles)
    with jax.named_scope("sum_angles"):
        gradient = parts[0]
        for k in range(1, groups):
            gradient = gradient + lax.ppermute(parts[k], "angle", ring_pairs("angle", k))
    return (
        out_f.reshape(forward_spectrum.shape),
        out_a.reshape(adjoint_spectrum.shape),
        gradient.reshape((nx, ny, depth // groups)),
    )


def solution(mesh):
    in_specs = (
        P("angle", None, "gx", "gy", None),
        P("angle", None, "gx", "gy", None),
        P("angle", None, "gx", "gy", None),
        P("angle", None, "gx", "gy", None),
        P("gx", "gy", None),
        P(),
        P("angle"),
        P(),
    )
    out_specs = (
        P("angle", None, "gx", "gy", None),
        P("angle", None, "gx", "gy", None),
        P("gx", "gy", "angle"),
    )
    return jax.shard_map(shards, mesh=mesh, in_specs=in_specs, out_specs=out_specs, check_vma=False)
```

time: 102 us -> 42.4 us (0.42)
  waiting for transfers between devices: 56.5 us -> 15.9 us
  other arithmetic: 18.3 us -> 0.64 us
  between operations: 15.1 us -> 1.36 us
  Pallas kernels: 0 us -> 10.3 us
  starting transfers between devices: 6.56 us -> 10.2 us
  local copies, waits for them, and re-layouts: 5.53 us -> 3.76 us
    ppermute x4 -> x7, waiting for transfers between devices: 36.3 us -> 15.9 us  [the longest x1 11.4 us: shards(): z_high = lax.ppermute(z_down, 'gy', ring_pairs('gy', -1))]
    psum x1 -> x0, waiting for transfers between devices: 20.1 us -> none  [shards(): whole = lax.psum(local_term, 'angle')]
    pallas_call x0 -> x3, Pallas kernels: none -> 10.3 us  [the longest x1 10 us: shards(): pl.pallas_call(functools.partial(advance_kernel, plan, groups), out_shape...]
    concatenate x3 -> x0, other arithmetic: 4.4 us -> none  [the longest x1 1.74 us: padded_2(): shard = jnp.concatenate([before, shard, after], axis=dim)]
    slice x30 -> x0, local copies, waits for them, and re-layouts: 4.14 us -> none  [the longest x6 1.46 us: next_depth(): field[..., 1:]]
    unnamed x8 -> x16, local copies, waits for them, and re-layouts: 0.02 us -> 3.75 us
    ppermute x4 -> x7, starting transfers between devices: 6.52 us -> 10.2 us  [the longest x1 2.3 us: shards(): z_low = lax.ppermute(z_up, 'gy', ring_pairs('gy', 1))]
    another operation x6 -> x0, other arithmetic: 3.21 us -> none  [the longest x3 2.08 us: local_curl_backward(): return jnp.stack([first, second, third], axis=2)]
  transfers between devices with their start and end apart: 5 -> 7, of which waited for: 5 -> 4; matrix products, arithmetic and copies ran while one was open for 5% -> 0% of each run, Pallas kernels for 0% -> 0%
where the time goes in v1:
time: 42.4 us; the launch traced here: 42.1 us
  waiting for transfers between devices  15.9 us (38%)
  Pallas kernels  10.3 us (24%)
  starting transfers between devices  10.2 us (24%)
  local copies, waits for them, and re-layouts  3.76 us (9%)
  between operations  1.36 us (3%)
  other arithmetic  0.64 us (2%)
    ppermute x1, waiting for transfers between devices, shards(): z_high = lax.ppermute(z_down, 'gy', ring_pairs('gy', -1))  11.4 us
    pallas_call x1, Pallas kernels, shards(): pl.pallas_call(functools.partial(advance_kernel, plan, groups), out_shape...  10 us
    unnamed x16, local copies, waits for them, and re-layouts  3.75 us
    ppermute x1, waiting for transfers between devices, shards(): lax.ppermute(parts[k], 'angle', ring_pairs('angle', k))  2.98 us
    ppermute x1, starting transfers between devices, shards(): z_low = lax.ppermute(z_up, 'gy', ring_pairs('gy', 1))  2.3 us
    ppermute x1, starting transfers between devices, shards(): z_high = lax.ppermute(z_down, 'gy', ring_pairs('gy', -1))  2.03 us
    ppermute x1, starting transfers between devices, shards(): x_high = lax.ppermute(x_down, 'gx', ring_pairs('gx', -1))  2.02 us
    ppermute x1, starting transfers between devices, shards(): c_high = lax.ppermute(c_down, 'gx', ring_pairs('gx', -1))  1.73 us
  transfers between devices with their start and end apart: 7, of which 4 were waited for; matrix products, arithmetic and copies ran while one was open for 0% of the time, Pallas kernels for 0%

profile of v1, /device:TPU:0, one launch (start us, length us, event | category | flops | bytes accessed | tf_op | source)
XLA Modules:
  0.0 42.1 jit_solution(17787292074036804359)
XLA Ops:
  0.6 0.0 copy-start
  0.6 1.1 %copy-done = f32[1,12,8,16,128]{4,3,2,1,0:T(8,128)S(1)} copy-done((f32[1,12,8,16,128]{4,3,2,1,0:T(8,128)S(1)}, f32[1,12,8,16,128]{4,3,2,1,0:T(8,128)}, u32[]{:S(2)}) %copy-start) | copy-done | bytes 786456
  1.8 0.0 copy-start.2
  1.8 1.1 %copy-done.2 = f32[1,12,8,16,128]{4,3,2,1,0:T(8,128)S(1)} copy-done((f32[1,12,8,16,128]{4,3,2,1,0:T(8,128)S(1)}, f32[1,12,8,16,128]{4,3,2,1,0:T(8,128)}, u32[]{:S(2)}) %copy-start.2) | copy-done | bytes 786456
  2.9 0.0 copy-start.5
  2.9 0.8 %copy-done.5 = f32[8,16,128]{2,1,0:T(8,128)S(1)} copy-done((f32[8,16,128]{2,1,0:T(8,128)S(1)}, f32[8,16,128]{2,1,0:T(8,128)}, u32[]{:S(2)}) %copy-start.5) | copy-done | bytes 65560
  3.7 0.0 copy-start.1
  3.7 0.2 pack_faces.1
  4.0 0.0 copy-start.3
  4.0 0.5 %collective-permute-start = (f32[1120,128]{1,0:T(8,128)S(1)}, f32[1120,128]{1,0:T(8,128)S(1)}, u32[]{:S(2)}, u32[]{:S(2)}) collective-permute-start(f32[1120,128]{1,0:T(8,128)S(1)} %get-tuple-element.12), channel_id=1, source_target_pairs={{0,4},{4,8},{8,12},{12,0},{1,5},{5,9},{9,13},{13,1},{2,6},{6,10},{... | collective-permute-start | bytes 1720328 | tf_op jit(solution)/shard_map/send_faces/ppermute | solution.py:332
  4.5 2.0 %collective-permute-start.1 = (f32[928,128]{1,0:T(8,128)S(1)}, f32[928,128]{1,0:T(8,128)S(1)}, u32[]{:S(2)}, u32[]{:S(2)}) collective-permute-start(f32[928,128]{1,0:T(8,128)S(1)} %get-tuple-element.13), channel_id=1, source_target_pairs={{0,12},{4,0},{8,4},{12,8},{1,13},{5,1},{9,5},{13,9},{2,14},{6,2},{... | collective-permute-start | bytes 1425416 | tf_op jit(solution)/shard_map/send_faces/ppermute | solution.py:333
  6.5 2.3 %collective-permute-start.2 = (f32[560,128]{1,0:T(8,128)S(1)}, f32[560,128]{1,0:T(8,128)S(1)}, u32[]{:S(2)}, u32[]{:S(2)}) collective-permute-start(f32[560,128]{1,0:T(8,128)S(1)} %get-tuple-element.14), channel_id=1, source_target_pairs={{0,1},{1,2},{2,3},{3,0},{4,5},{5,6},{6,7},{7,4},{8,9},{9,10},{10,1... | collective-permute-start | bytes 860168 | tf_op jit(solution)/shard_map/send_faces/ppermute | solution.py:330
  8.8 2.0 %collective-permute-start.3 = (f32[464,128]{1,0:T(8,128)S(1)}, f32[464,128]{1,0:T(8,128)S(1)}, u32[]{:S(2)}, u32[]{:S(2)}) collective-permute-start(f32[464,128]{1,0:T(8,128)S(1)} %get-tuple-element.15), channel_id=1, source_target_pairs={{0,3},{1,0},{2,1},{3,2},{4,7},{5,4},{6,5},{7,6},{8,11},{9,8},{10,9... | collective-permute-start | bytes 712712 | tf_op jit(solution)/shard_map/send_faces/ppermute | solution.py:331
  10.8 11.4 %collective-permute-done.3.z_high = f32[464,128]{1,0:T(8,128)S(1)} collective-permute-done((f32[464,128]{1,0:T(8,128)S(1)}, f32[464,128]{1,0:T(8,128)S(1)}, u32[]{:S(2)}, u32[]{:S(2)}) %collective-permute-start.3) | collective-permute-done | bytes 237600 | tf_op jit(solution)/shard_map/send_faces/ppermute | solution.py:331
  22.3 0.0 collective-permute-done.2.z_low
  22.3 0.1 relay_corners.1
  22.3 0.1 collective-permute-start.4
  22.4 1.7 %collective-permute-start.5 = (f32[128,128]{1,0:T(8,128)S(1)}, f32[128,128]{1,0:T(8,128)S(1)}, u32[]{:S(2)}, u32[]{:S(2)}) collective-permute-start(f32[128,128]{1,0:T(8,128)S(1)} %get-tuple-element.17), channel_id=1, source_target_pairs={{0,12},{4,0},{8,4},{12,8},{1,13},{5,1},{9,5},{13,9},{2,14},{6,2},{... | collective-permute-start | bytes 196616 | tf_op jit(solution)/shard_map/relay_corners/ppermute | solution.py:343
  24.8 1.3 %collective-permute-done.5.c_high = f32[128,128]{1,0:T(8,128)S(1)} collective-permute-done((f32[128,128]{1,0:T(8,128)S(1)}, f32[128,128]{1,0:T(8,128)S(1)}, u32[]{:S(2)}, u32[]{:S(2)}) %collective-permute-start.5) | collective-permute-done | bytes 65568 | tf_op jit(solution)/shard_map/relay_corners/ppermute | solution.py:343
  26.1 0.2 collective-permute-done.4.c_low
  26.3 0.0 collective-permute-done.1.x_high
  26.3 0.0 collective-permute-done.x_low
  26.3 0.0 copy-start.7
  26.3 0.0 copy-done.1
  26.3 0.0 copy-done.4
  26.3 0.0 copy-done.3
  26.3 0.6 %copy-done.6 = f32[2,2]{1,0:T(2,128)S(1)} copy-done((f32[2,2]{1,0:T(2,128)S(1)}, f32[2,2]{1,0:T(2,128)}, u32[]{:S(2)}) %copy-start.6) | copy-done | bytes 40
  27.0 0.0 copy-done.7
  27.0 10.0 %advance.1 = (f32[768,128]{1,0:T(8,128)}, f32[768,128]{1,0:T(8,128)}, f32[2,128,64]{2,1,0:T(8,128)S(1)}) custom-call(f32[1536,128]{1,0:T(8,128)S(1)} %bitcast.13, f32[1536,128]{1,0:T(8,128)S(1)} %bitcast.15, f32[768,128]{1,0:T(8,128)S(1)} %bitcast.16, f32[768,128]{1,0:T(8,128)S(1)} %bitcast.17, f32[128,128]{1,0:T(8,128)S(1)} %bitcast.19, ...), custom_call_target="tpu_custom_call" | custom-call | tf_op jit(solution)/shard_map/advance/pallas_call | solution.py:345
  37.0 1.5 %collective-permute-start.6 = (f32[128,64]{1,0:T(8,128)S(1)}, f32[128,64]{1,0:T(8,128)S(1)}, u32[]{:S(2)}, u32[]{:S(2)}) collective-permute-start(f32[128,64]{1,0:T(8,128)S(1)} %slice_bitcast_fusion), channel_id=1, source_target_pairs={{0,16},{16,0},{1,17},{17,1},{2,18},{18,2},{3,19},{19,3},{4,20},{20... | collective-permute-start | bytes 98312 | tf_op jit(solution)/shard_map/sum_angles/ppermute | solution.py:365
  38.5 3.0 %collective-permute-done.6 = f32[128,64]{1,0:T(8,128)S(1)} collective-permute-done((f32[128,64]{1,0:T(8,128)S(1)}, f32[128,64]{1,0:T(8,128)S(1)}, u32[]{:S(2)}, u32[]{:S(2)}) %collective-permute-start.6) | collective-permute-done | bytes 32800 | tf_op jit(solution)/shard_map/sum_angles/ppermute | solution.py:365
  41.5 0.6 %bitcast_add_fusion = f32[128,64]{1,0:T(8,128)} fusion(f32[128,64]{1,0:T(8,128)S(1)} %collective-permute-done.6, f32[2,128,64]{2,1,0:T(8,128)S(1)} %get-tuple-element.20), kind=kLoop, calls=%fused_computation | loop fusion | flops 8192 | bytes 98304 | tf_op jit(solution)/shard_map/sum_angles/add | solution.py:365
  (3 shorter events, 0.0 us)
Async XLA Ops:
  0.6 1.1 %copy-start = (f32[1,12,8,16,128]{4,3,2,1,0:T(8,128)S(1)}, f32[1,12,8,16,128]{4,3,2,1,0:T(8,128)}, u32[]{:S(2)}) copy-start(f32[1,12,8,16,128]{4,3,2,1,0:T(8,128)} %param.8) | copy-start | bytes 2359300
  1.8 1.1 %copy-start.2 = (f32[1,12,8,16,128]{4,3,2,1,0:T(8,128)S(1)}, f32[1,12,8,16,128]{4,3,2,1,0:T(8,128)}, u32[]{:S(2)}) copy-start(f32[1,12,8,16,128]{4,3,2,1,0:T(8,128)} %param.9) | copy-start | bytes 2359300
  2.9 0.8 %copy-start.5 = (f32[8,16,128]{2,1,0:T(8,128)S(1)}, f32[8,16,128]{2,1,0:T(8,128)}, u32[]{:S(2)}) copy-start(f32[8,16,128]{2,1,0:T(8,128)} %param.12) | copy-start | bytes 196612
  3.7 22.6 %copy-start.1 = (f32[1,12,8,16,128]{4,3,2,1,0:T(8,128)S(1)}, f32[1,12,8,16,128]{4,3,2,1,0:T(8,128)}, u32[]{:S(2)}) copy-start(f32[1,12,8,16,128]{4,3,2,1,0:T(8,128)} %param.8) | copy-start | bytes 2359300
  3.7 22.6 %copy-start.4 = (f32[1,6,8,16,128]{4,3,2,1,0:T(8,128)S(1)}, f32[1,6,8,16,128]{4,3,2,1,0:T(8,128)}, u32[]{:S(2)}) copy-start(f32[1,6,8,16,128]{4,3,2,1,0:T(8,128)} %param.11) | copy-start | bytes 1179652
  4.0 22.3 %copy-start.3 = (f32[1,6,8,16,128]{4,3,2,1,0:T(8,128)S(1)}, f32[1,6,8,16,128]{4,3,2,1,0:T(8,128)}, u32[]{:S(2)}) copy-start(f32[1,6,8,16,128]{4,3,2,1,0:T(8,128)} %param.10) | copy-start | bytes 1179652
  4.0 22.3 %collective-permute-start = (f32[1120,128]{1,0:T(8,128)S(1)}, f32[1120,128]{1,0:T(8,128)S(1)}, u32[]{:S(2)}, u32[]{:S(2)}) collective-permute-start(f32[1120,128]{1,0:T(8,128)S(1)} %get-tuple-element.12), channel_id=1, source_target_pairs={{0,4},{4,8},{8,12},{12,0},{1,5},{5,9},{9,13},{13,1},{2,6},{6,10},{... | collective-permute-start | bytes 1720328 | tf_op jit(solution)/shard_map/send_faces/ppermute | solution.py:332
  4.5 21.8 %collective-permute-start.1 = (f32[928,128]{1,0:T(8,128)S(1)}, f32[928,128]{1,0:T(8,128)S(1)}, u32[]{:S(2)}, u32[]{:S(2)}) collective-permute-start(f32[928,128]{1,0:T(8,128)S(1)} %get-tuple-element.13), channel_id=1, source_target_pairs={{0,12},{4,0},{8,4},{12,8},{1,13},{5,1},{9,5},{13,9},{2,14},{6,2},{... | collective-permute-start | bytes 1425416 | tf_op jit(solution)/shard_map/send_faces/ppermute | solution.py:333
  6.5 15.7 %collective-permute-start.2 = (f32[560,128]{1,0:T(8,128)S(1)}, f32[560,128]{1,0:T(8,128)S(1)}, u32[]{:S(2)}, u32[]{:S(2)}) collective-permute-start(f32[560,128]{1,0:T(8,128)S(1)} %get-tuple-element.14), channel_id=1, source_target_pairs={{0,1},{1,2},{2,3},{3,0},{4,5},{5,6},{6,7},{7,4},{8,9},{9,10},{10,1... | collective-permute-start | bytes 860168 | tf_op jit(solution)/shard_map/send_faces/ppermute | solution.py:330
  8.8 13.4 %collective-permute-start.3 = (f32[464,128]{1,0:T(8,128)S(1)}, f32[464,128]{1,0:T(8,128)S(1)}, u32[]{:S(2)}, u32[]{:S(2)}) collective-permute-start(f32[464,128]{1,0:T(8,128)S(1)} %get-tuple-element.15), channel_id=1, source_target_pairs={{0,3},{1,0},{2,1},{3,2},{4,7},{5,4},{6,5},{7,6},{8,11},{9,8},{10,9... | collective-permute-start | bytes 712712 | tf_op jit(solution)/shard_map/send_faces/ppermute | solution.py:331
  22.3 3.9 %collective-permute-start.4 = (f32[152,128]{1,0:T(8,128)S(1)}, f32[152,128]{1,0:T(8,128)S(1)}, u32[]{:S(2)}, u32[]{:S(2)}) collective-permute-start(f32[152,128]{1,0:T(8,128)S(1)} %get-tuple-element.16), channel_id=1, source_target_pairs={{0,4},{4,8},{8,12},{12,0},{1,5},{5,9},{9,13},{13,1},{2,6},{6,10},{... | collective-permute-start | bytes 233480 | tf_op jit(solution)/shard_map/relay_corners/ppermute | solution.py:342
  22.4 3.6 %collective-permute-start.5 = (f32[128,128]{1,0:T(8,128)S(1)}, f32[128,128]{1,0:T(8,128)S(1)}, u32[]{:S(2)}, u32[]{:S(2)}) collective-permute-start(f32[128,128]{1,0:T(8,128)S(1)} %get-tuple-element.17), channel_id=1, source_target_pairs={{0,12},{4,0},{8,4},{12,8},{1,13},{5,1},{9,5},{13,9},{2,14},{6,2},{... | collective-permute-start | bytes 196616 | tf_op jit(solution)/shard_map/relay_corners/ppermute | solution.py:343
  26.3 0.7 %copy-start.6 = (f32[2,2]{1,0:T(2,128)S(1)}, f32[2,2]{1,0:T(2,128)}, u32[]{:S(2)}) copy-start(f32[2,2]{1,0:T(2,128)} %table.1) | copy-start | bytes 52
  26.3 0.7 %copy-start.7 = (s32[4]{0:T(128)S(1)}, s32[4]{0:T(128)}, u32[]{:S(2)}) copy-start(s32[4]{0:T(128)} %tiles.1) | copy-start | bytes 52
  37.0 4.5 %collective-permute-start.6 = (f32[128,64]{1,0:T(8,128)S(1)}, f32[128,64]{1,0:T(8,128)S(1)}, u32[]{:S(2)}, u32[]{:S(2)}) collective-permute-start(f32[128,64]{1,0:T(8,128)S(1)} %slice_bitcast_fusion), channel_id=1, source_target_pairs={{0,16},{16,0},{1,17},{17,1},{2,18},{18,2},{3,19},{19,3},{4,20},{20... | collective-permute-start | bytes 98312 | tf_op jit(solution)/shard_map/sum_angles/ppermute | solution.py:365

commit v2 on v1

v2 whole, which is shorter than its diff:
```python
import functools
import math

import jax
import jax.numpy as jnp
from jax import lax
from jax.experimental import pallas as pl
from jax.experimental.pallas import tpu as pltpu
from jax.sharding import PartitionSpec as P

STEPS = 3
SUB = 8

courant = 0.5
omega_step = 0.7

VMEM = pl.BlockSpec(memory_space=pltpu.VMEM)
SMEM = pl.BlockSpec(memory_space=pltpu.SMEM)
HBM = pl.BlockSpec(memory_space=pltpu.HBM)


def moved(cells, dx, dy):
    return {(x + dx, y + dy) for x, y in cells}


def cone(nx, ny):
    block = {(x, y) for x in range(nx) for y in range(ny)}
    ex, ey, ez = block, block, block
    hx, hy, hz, eps = set(), set(), set(), set()
    for _ in range(STEPS):
        eps = eps | ex | ey | ez
        hx, hy, hz = (
            hx | ey | ez | moved(ez, 0, -1),
            hy | ex | ez | moved(ez, -1, 0),
            hz | ex | moved(ex, 0, -1) | ey | moved(ey, -1, 0),
        )
        ex, ey, ez = (
            ex | hy | hz | moved(hz, 0, 1),
            ey | hx | hz | moved(hz, 1, 0),
            ez | hx | moved(hx, 0, 1) | hy | moved(hy, 1, 0),
        )
    return (ex, ey, ez), (hx, hy, hz), eps


PLANES = [(run, kind, part, comp) for run in (0, 1) for kind in (0, 1) for comp in (0, 1, 2) for part in (0, 1)]


class Plan:
    def __init__(self, nx, ny):
        efield, hfield, eps = cone(nx, ny)
        self.nx, self.ny = nx, ny
        self.wide, self.ring = nx + 2 * STEPS, ny + SUB

        def cells(plane):
            if plane is None:
                return eps
            return (efield, hfield)[plane[1]][plane[3]]

        planes = PLANES + [None]
        self.x_low, self.x_high, self.y_low, self.y_high = [], [], [], []
        for plane in planes:
            need = cells(plane)
            self.x_low += [(plane, x) for x in range(-STEPS, 0) if any((x, y) in need for y in range(ny))]
            self.x_high += [(plane, x) for x in range(nx, nx + STEPS) if any((x, y) in need for y in range(ny))]
            self.y_low += [(plane, y) for y in range(-STEPS, 0) if any((x, y) in need for x in range(nx))]
            self.y_high += [(plane, y) for y in range(ny, ny + STEPS) if any((x, y) in need for x in range(nx))]
        self.corner_low, self.corner_high = [], []
        for out, layers in ((self.corner_low, range(-STEPS, 0)), (self.corner_high, range(nx, nx + STEPS))):
            for rows in (range(-STEPS, 0), range(ny, ny + STEPS)):
                for plane in planes:
                    need = cells(plane)
                    out += [(plane, x, y) for x in layers for y in rows if (x, y) in need]

    def row(self, x, y, plane=(0, 0, 0, 0)):
        run, _, part, comp = plane
        return ((run * 6 + part * 3 + comp) * self.wide + x + STEPS) * self.ring + y % self.ring


def pack_y_kernel(plan, fwd, adj, eps, e0, h0, coef, z_up, z_down, sems):
    nx, ny = plan.nx, plan.ny
    own = (pl.ds(STEPS, nx), pl.ds(0, ny), slice(None))
    copies = []
    for run, ref in enumerate((fwd, adj)):
        for kind, state in enumerate((e0, h0)):
            for i in range(6):
                copies.append(
                    pltpu.make_async_copy(ref.at[kind * 6 + i], state.at[(run * 6 + i, *own)], sems.at[len(copies)])
                )
    copies.append(pltpu.make_async_copy(eps, coef.at[own], sems.at[len(copies)]))
    for copy in copies:
        copy.start()
    for copy in copies:
        copy.wait()
    for x in range(nx):
        coef[STEPS + x, pl.ds(0, ny), :] = (0.5 * courant) / coef[STEPS + x, pl.ds(0, ny), :]
    flat = [state.reshape((-1, state.shape[-1])) for state in (e0, h0)]
    flat_coef = coef.reshape((-1, coef.shape[-1]))
    for entries, shift, out in ((plan.y_low, ny, z_up), (plan.y_high, -ny, z_down)):
        for i, (plane, y) in enumerate(entries):
            ref, row = (flat_coef, plan.row(0, y + shift)) if plane is None else (flat[plane[1]], plan.row(0, y + shift, plane))
            out[pl.ds(i * nx, nx), :] = ref[pl.ds(row, nx, stride=plan.ring), :]


def pack_x_kernel(plan, e0, h0, coef, x_up, x_down):
    nx, ny = plan.nx, plan.ny
    for entries, shift, out in ((plan.x_low, nx, x_up), (plan.x_high, -nx, x_down)):
        for i, (plane, x) in enumerate(entries):
            ref, row = (coef, plan.row(x + shift, 0)) if plane is None else ((e0, h0)[plane[1]], plan.row(x + shift, 0, plane))
            out[pl.ds(i * ny, ny), :] = ref[pl.ds(row, ny), :]


def turns_kernel(groups, table, index, tiles, turns):
    row = index[0]
    phi_x, phi_y = table[row, 0], table[row, 1]
    at_x, at_y = lax.axis_index("gx"), lax.axis_index("gy")
    none = jnp.float32(0.0)
    ax_low = jnp.where(at_x == 0, -phi_x, none)
    ax_high = jnp.where(at_x == lax.axis_size("gx") - 1, phi_x, none)
    ay_low = jnp.where(at_y == 0, -phi_y, none)
    ay_high = jnp.where(at_y == lax.axis_size("gy") - 1, phi_y, none)
    sub = lax.broadcasted_iota(jnp.int32, (SUB, turns.shape[1]), 0)
    angles = jnp.zeros(sub.shape, jnp.float32)
    for i, angle in enumerate((ax_low, ax_high, ay_low, ay_high, ax_low + ay_low, ax_low + ay_high,
                               ax_high + ay_low, ax_high + ay_high)):
        angles = jnp.where(sub == i, angle, angles)
    turns[pl.ds(0, SUB), :] = jnp.cos(angles)
    turns[pl.ds(SUB, SUB), :] = jnp.sin(angles)
    own_tile = at_x * lax.axis_size("gy") + at_y
    chosen = tiles[0] == own_tile
    for i in range(1, tiles.shape[0]):
        chosen = jnp.logical_or(chosen, tiles[i] == own_tile)
    weight = jnp.where(chosen, jnp.float32(1.0 / groups), none)
    turns[pl.ds(2 * SUB, SUB), :] = jnp.full(sub.shape, weight, jnp.float32)


def corner_kernel(plan, z_low, z_high, c_up, c_down):
    nx = plan.nx
    low = {entry: i for i, entry in enumerate(plan.y_low)}
    high = {entry: i for i, entry in enumerate(plan.y_high)}
    for entries, shift, out in ((plan.corner_low, nx, c_up), (plan.corner_high, -nx, c_down)):
        for i, (plane, x, y) in enumerate(entries):
            ref, at = (z_low, low[plane, y]) if y < 0 else (z_high, high[plane, y])
            out[pl.ds(i, 1), :] = ref[pl.ds(at * nx + x + shift, 1), :]


def turned(real, imag, cosine, sine):
    return real * cosine - imag * sine, real * sine + imag * cosine


def unpack(entries, ref, count, which, turns, target):
    at = {entry: i for i, entry in enumerate(entries)}
    for entry, i in at.items():
        plane = entry[0]
        own = ref[pl.ds(i * count, count), :]
        if plane is None:
            array, rows = target(entry)
            array[rows, :] = own
        elif plane[2] == 0:
            twin = (plane[:2] + (1,) + plane[3:], *entry[1:])
            row = which(entry)
            cosine, sine = turns[pl.ds(row, 1), :], turns[pl.ds(SUB + row, 1), :]
            if plane[0] == 1:
                sine = -sine
            real, imag = turned(own, ref[pl.ds(at[twin] * count, count), :], cosine, sine)
            for what, value in ((entry, real), (twin, imag)):
                array, rows = target(what)
                array[rows, :] = value


class Sweeps:
    def __init__(self, plan, efield, hfield, coef):
        self.plan, self.efield, self.hfield, self.coef = plan, efield, hfield, coef
        lane = lax.broadcasted_iota(jnp.int32, (plan.ring, coef.shape[1]), 1)
        self.first, self.last = lane == 0, lane == coef.shape[1] - 1

    def rows(self, group, comp, x):
        plan = self.plan
        start = (group * 3 + comp) * plan.wide * plan.ring + (x + STEPS) * plan.ring
        return pl.ds(start if isinstance(start, int) else pl.multiple_of(start, SUB), plan.ring)

    def next_z(self, value):
        return jnp.where(self.last, 0.0, pltpu.roll(value, value.shape[1] - 1, 1))

    def prev_z(self, value):
        return jnp.where(self.first, 0.0, pltpu.roll(value, 1, 1))

    def next_y(self, value):
        return pltpu.roll(value, self.plan.ring - 1, 0)

    def prev_y(self, value):
        return pltpu.roll(value, 1, 0)

    def update_h(self, step, group, x):
        efield, old, new = self.efield[step - 1], self.hfield[step - 1], self.hfield[step]
        ex, ey, ez = (efield[self.rows(group, comp, x), :] for comp in range(3))
        ey_x, ez_x = (efield[self.rows(group, comp, x + 1), :] for comp in (1, 2))
        hx, hy, hz = (old[self.rows(group, comp, x), :] for comp in range(3))
        if step == 1:
            hx, hy, hz = hx + hx, hy + hy, hz + hz
        new[self.rows(group, 0, x), :] = hx - ((self.next_y(ez) - ez) - (self.next_z(ey) - ey))
        new[self.rows(group, 1, x), :] = hy - ((self.next_z(ex) - ex) - (ez_x - ez))
        new[self.rows(group, 2, x), :] = hz - ((ey_x - ey) - (self.next_y(ex) - ex))

    def update_e(self, step, group, x):
        old, new, hfield = self.efield[step - 1], self.efield[step], self.hfield[step]
        ex, ey, ez = (old[self.rows(group, comp, x), :] for comp in range(3))
        hx, hy, hz = (hfield[self.rows(group, comp, x), :] for comp in range(3))
        hy_x, hz_x = (hfield[self.rows(group, comp, x - 1), :] for comp in (1, 2))
        scale = self.coef[self.rows(0, 0, x), :]
        new[self.rows(group, 0, x), :] = ex + scale * ((hz - self.prev_y(hz)) - (hy - self.prev_z(hy)))
        new[self.rows(group, 1, x), :] = ey + scale * ((hx - self.prev_z(hx)) - (hz - hz_x))
        new[self.rows(group, 2, x), :] = ez + scale * ((hy - hy_x) - (hx - self.prev_y(hx)))

    def both(self, step, h_layers, e_layers):
        for update, layers in ((self.update_h, h_layers), (self.update_e, e_layers)):

            @pl.loop(0, 2)
            def _(run):
                for part in (0, 1):
                    for x in layers:
                        update(step, run * 2 + part, x)


def middle_kernel(plan, e0_in, h0_in, coef_in, z_low, z_high, turns, *state):
    nx = plan.nx
    efield, hfield, coef = state[: STEPS + 1], state[STEPS + 1 : 2 * STEPS + 2], state[-1]

    def target(entry):
        plane, y = entry
        if plane is None:
            return coef, pl.ds(plan.row(0, y), nx, stride=plan.ring)
        return (efield, hfield)[plane[1]][0], pl.ds(plan.row(0, y, plane), nx, stride=plan.ring)

    unpack(plan.y_low, z_low, nx, lambda entry: 2, turns, target)
    unpack(plan.y_high, z_high, nx, lambda entry: 3, turns, target)
    sweeps = Sweeps(plan, efield, hfield, coef)
    for step in range(1, STEPS + 1):
        sweeps.both(step, range(step - 1, nx - step), range(step, nx - step))


def edges_kernel(plan, groups, *refs):
    nx, ny = plan.nx, plan.ny
    count = 2 * STEPS + 3
    x_low, x_high, c_low, c_high, turns, spec_f, spec_a = refs[count : count + 7]
    state = refs[count + 7 : 2 * count + 7]
    out_f, out_a, parts = refs[2 * count + 7 :]
    efield, hfield, coef = state[: STEPS + 1], state[STEPS + 1 : 2 * STEPS + 2], state[-1]

    def target(entry):
        plane, x = entry[:2]
        y, size = (0, ny) if len(entry) == 2 else (entry[2], 1)
        if plane is None:
            return coef, pl.ds(plan.row(x, y), size)
        return (efield, hfield)[plane[1]][0], pl.ds(plan.row(x, y, plane), size)

    unpack(plan.x_low, x_low, ny, lambda entry: 0, turns, target)
    unpack(plan.x_high, x_high, ny, lambda entry: 1, turns, target)
    unpack(plan.corner_low, c_low, 1, lambda entry: 4 + (entry[2] >= 0), turns, target)
    unpack(plan.corner_high, c_high, 1, lambda entry: 6 + (entry[2] >= 0), turns, target)
    sweeps = Sweeps(plan, efield, hfield, coef)
    for step in range(1, STEPS + 1):
        low, high = step - STEPS, nx - step
        sweeps.both(
            step,
            [*range(low - 1, step - 1), *range(high, nx + STEPS - step)],
            [*range(low, step), *range(high, nx + STEPS - step)],
        )

    share = parts.shape[2]
    shift = lax.rem(groups - lax.axis_index("angle"), groups) * share
    weight = turns[pl.ds(2 * SUB, SUB), :]
    tiles = ny // SUB

    @pl.loop(0, nx * tiles)
    def _(i):
        x, tile = i // tiles, lax.rem(i, tiles)
        total = jnp.zeros(weight.shape, jnp.float32)
        for comp in range(3):
            ends = []
            for run, (spec, out) in enumerate(((spec_f, out_f), (spec_a, out_a))):
                at = [pl.ds(pl.multiple_of(((part * 3 + comp) * nx + x) * ny + tile * SUB, SUB), SUB) for part in (0, 1)]
                real, imag = spec[at[0], :], spec[at[1], :]
                for step in range(1, STEPS + 1):
                    theta = omega_step * step
                    ends_e = [
                        efield[step][pl.ds(pl.multiple_of(plan.row(x, 0, (run, 0, part, comp)) + tile * SUB, SUB), SUB), :]
                        for part in (0, 1)
                    ]
                    more = turned(*ends_e, math.cos(theta), math.sin(theta))
                    real, imag = real + more[0], imag + more[1]
                out[at[0], :], out[at[1], :] = real, imag
                ends.append((real, imag))
            total = total + (ends[0][0] * ends[1][0] - ends[0][1] * ends[1][1])
        total = pltpu.roll(total * weight, shift, 1)
        for k in range(groups):
            parts[k, pl.ds(pl.multiple_of(i * SUB, SUB), SUB), :] = total[:, k * share : (k + 1) * share]


def write_kernel(tr_f, tr_a, out_f, out_a, sems):
    copies = []
    for source, target in ((tr_f, out_f), (tr_a, out_a)):
        for i in range(source.shape[0]):
            copies.append(pltpu.make_async_copy(source.at[i], target.at[i], sems.at[len(copies)]))
    for copy in copies:
        copy.start()
    for copy in copies:
        copy.wait()


def ring_pairs(axis, offset):
    size = lax.axis_size(axis)
    return [(i, (i + offset) % size) for i in range(size)]


def shards(
    forward_fields,
    adjoint_fields,
    forward_spectrum,
    adjoint_spectrum,
    permittivity,
    phase_table,
    angle_index,
    design_tiles,
):
    nx, ny, depth = permittivity.shape
    plan = Plan(nx, ny)
    groups = lax.axis_size("angle")
    wide, ring = plan.wide, plan.ring

    def array(*shape):
        return jax.ShapeDtypeStruct(shape, jnp.float32)

    def lines(count):
        return array(count, depth)

    def params(mib):
        return pltpu.CompilerParams(vmem_limit_bytes=mib * 2**20)

    def cost(size):
        return pl.CostEstimate(flops=size, bytes_accessed=size, transcendentals=0)

    with jax.named_scope("pack_y"):
        e0, h0, coef, z_up, z_down = pl.pallas_call(
            functools.partial(pack_y_kernel, plan),
            out_shape=(
                array(12, wide, ring, depth),
                array(12, wide, ring, depth),
                array(wide, ring, depth),
                lines(len(plan.y_low) * nx),
                lines(len(plan.y_high) * nx),
            ),
            in_specs=[HBM] * 3,
            out_specs=[VMEM] * 5,
            scratch_shapes=[pltpu.SemaphoreType.DMA((25,))],
            compiler_params=params(16),
        )(forward_fields[0], adjoint_fields[0], permittivity)
    e0, h0, coef = (state.reshape((-1, depth)) for state in (e0, h0, coef))
    with jax.named_scope("send_y"):
        z_low = lax.ppermute(z_up, "gy", ring_pairs("gy", 1))
        z_high = lax.ppermute(z_down, "gy", ring_pairs("gy", -1))
    with jax.named_scope("pack_x"):
        x_up, x_down = pl.pallas_call(
            functools.partial(pack_x_kernel, plan),
            out_shape=(lines(len(plan.x_low) * ny), lines(len(plan.x_high) * ny)),
            in_specs=[VMEM] * 3,
            out_specs=[VMEM] * 2,
            compiler_params=params(8),
            cost_estimate=cost(40 * 2**20),
        )(e0, h0, coef)
    with jax.named_scope("send_x"):
        x_low = lax.ppermute(x_up, "gx", ring_pairs("gx", 1))
        x_high = lax.ppermute(x_down, "gx", ring_pairs("gx", -1))
    with jax.named_scope("turns"):
        turns = pl.pallas_call(
            functools.partial(turns_kernel, groups),
            out_shape=lines(3 * SUB),
            in_specs=[SMEM] * 3,
            out_specs=VMEM,
            compiler_params=params(4),
        )(phase_table, angle_index, design_tiles)
    with jax.named_scope("relay_corners"):
        c_up, c_down = pl.pallas_call(
            functools.partial(corner_kernel, plan),
            out_shape=(lines(-(-len(plan.corner_low) // SUB) * SUB), lines(-(-len(plan.corner_high) // SUB) * SUB)),
            in_specs=[VMEM] * 2,
            out_specs=[VMEM] * 2,
            compiler_params=params(4),
        )(z_low, z_high)
        c_low = lax.ppermute(c_up, "gx", ring_pairs("gx", 1))
        c_high = lax.ppermute(c_down, "gx", ring_pairs("gx", -1))
    level = lines(12 * wide * ring)
    count = 2 * STEPS + 3
    levels = [level] * (count - 1) + [lines(wide * ring)]
    with jax.named_scope("middle"):
        state = pl.pallas_call(
            functools.partial(middle_kernel, plan),
            out_shape=levels,
            in_specs=[VMEM] * 6,
            out_specs=[VMEM] * count,
            input_output_aliases={0: 0, 1: STEPS + 1, 2: count - 1},
            compiler_params=params(8),
            cost_estimate=cost(20 * 2**20),
        )(e0, h0, coef, z_low, z_high, turns)
    with jax.named_scope("edges"):
        spectra = [spectrum.reshape((-1, depth)) for spectrum in (forward_spectrum, adjoint_spectrum)]
        *_, tr_f, tr_a, parts = pl.pallas_call(
            functools.partial(edges_kernel, plan, groups),
            out_shape=[*levels, lines(6 * nx * ny), lines(6 * nx * ny), array(groups, nx * ny, depth // groups)],
            in_specs=[VMEM] * (count + 7),
            out_specs=[VMEM] * (count + 3),
            input_output_aliases={i: i for i in range(count)},
            compiler_params=params(8),
        )(*state, x_low, x_high, c_low, c_high, turns, *spectra)
    with jax.named_scope("sum_angles"):
        gradient = parts[0]
        for k in range(1, groups):
            gradient = gradient + lax.ppermute(parts[k], "angle", ring_pairs("angle", k))
    with jax.named_scope("write"):
        out_f, out_a = pl.pallas_call(
            write_kernel,
            out_shape=[array(6, nx, ny, depth)] * 2,
            in_specs=[VMEM] * 2,
            out_specs=[HBM] * 2,
            scratch_shapes=[pltpu.SemaphoreType.DMA((12,))],
            compiler_params=params(4),
        )(tr_f.reshape((6, nx, ny, depth)), tr_a.reshape((6, nx, ny, depth)))
    return (
        out_f.reshape(forward_spectrum.shape),
        out_a.reshape(adjoint_spectrum.shape),
        gradient.reshape((nx, ny, depth // groups)),
    )


def solution(mesh):
    in_specs = (
        P("angle", None, "gx", "gy", None),
        P("angle", None, "gx", "gy", None),
        P("angle", None, "gx", "gy", None),
        P("angle", None, "gx", "gy", None),
        P("gx", "gy", None),
        P(),
        P("angle"),
        P(),
    )
    out_specs = (
        P("angle", None, "gx", "gy", None),
        P("angle", None, "gx", "gy", None),
        P("gx", "gy", "angle"),
    )
    return jax.shard_map(shards, mesh=mesh, in_specs=in_specs, out_specs=out_specs, check_vma=False)
```

time: 42.4 us -> 37.6 us (0.89)
  waiting for transfers between devices: 15.9 us -> 13.2 us
  Pallas kernels: 10.3 us -> 8.78 us
  local copies, waits for them, and re-layouts: 3.76 us -> 3.13 us
    pallas_call x2 -> x6, Pallas kernels: 10.3 us -> 8.7 us  [the longest x1 4.76 us: shards(): pl.pallas_call(functools.partial(edges_kernel, plan, groups), out_shape=[...]
    ppermute x1, waiting for transfers between devices: 1.25 us -> 0.01 us  [shards(): c_high = lax.ppermute(c_down, 'gx', ring_pairs('gx', -1))]
    ppermute x1, waiting for transfers between devices: 2.98 us -> 1.8 us  [shards(): lax.ppermute(parts[k], 'angle', ring_pairs('angle', k))]
    unnamed x16 -> x14, local copies, waits for them, and re-layouts: 3.75 us -> 3.12 us
  transfers between devices with their start and end apart: 7 -> 7, of which waited for: 4 -> 2; matrix products, arithmetic and copies ran while one was open for 0% -> 0% of each run, Pallas kernels for 0% -> 9%
where the time goes in v2:
time: 37.6 us; the launch traced here: 37.3 us
  waiting for transfers between devices  13.2 us (35%)
  starting transfers between devices  10.1 us (27%)
  Pallas kernels  8.78 us (23%)
  local copies, waits for them, and re-layouts  3.13 us (8%)
  between operations  1.44 us (4%)
  other arithmetic  0.64 us (2%)
    ppermute x1, waiting for transfers between devices, shards(): z_high = lax.ppermute(z_down, 'gy', ring_pairs('gy', -1))  11.4 us
    pallas_call x1, Pallas kernels, shards(): pl.pallas_call(functools.partial(edges_kernel, plan, groups), out_shape=[...  4.76 us
    unnamed x14, local copies, waits for them, and re-layouts  3.12 us
    ppermute x1, starting transfers between devices, shards(): z_low = lax.ppermute(z_up, 'gy', ring_pairs('gy', 1))  2.3 us
    ppermute x1, starting transfers between devices, shards(): z_high = lax.ppermute(z_down, 'gy', ring_pairs('gy', -1))  2.03 us
    ppermute x1, starting transfers between devices, shards(): x_high = lax.ppermute(x_down, 'gx', ring_pairs('gx', -1))  2.02 us
    ppermute x1, waiting for transfers between devices, shards(): lax.ppermute(parts[k], 'angle', ring_pairs('angle', k))  1.8 us
    ppermute x1, starting transfers between devices, shards(): c_high = lax.ppermute(c_down, 'gx', ring_pairs('gx', -1))  1.73 us
  transfers between devices with their start and end apart: 7, of which 2 were waited for; matrix products, arithmetic and copies ran while one was open for 0% of the time, Pallas kernels for 9%

profile of v2, /device:TPU:0, one launch (start us, length us, event | category | flops | bytes accessed | tf_op | source)
XLA Modules:
  0.0 37.3 jit_solution(3857043111369269871)
XLA Ops:
  0.6 0.0 copy-start
  0.6 1.1 %copy-done = f32[1,12,8,16,128]{4,3,2,1,0:T(8,128)S(1)} copy-done((f32[1,12,8,16,128]{4,3,2,1,0:T(8,128)S(1)}, f32[1,12,8,16,128]{4,3,2,1,0:T(8,128)}, u32[]{:S(2)}) %copy-start) | copy-done | bytes 786456
  1.8 1.1 %copy-done.1 = f32[1,12,8,16,128]{4,3,2,1,0:T(8,128)S(1)} copy-done((f32[1,12,8,16,128]{4,3,2,1,0:T(8,128)S(1)}, f32[1,12,8,16,128]{4,3,2,1,0:T(8,128)}, u32[]{:S(2)}) %copy-start.1) | copy-done | bytes 786456
  2.9 0.8 %copy-done.4 = f32[8,16,128]{2,1,0:T(8,128)S(1)} copy-done((f32[8,16,128]{2,1,0:T(8,128)S(1)}, f32[8,16,128]{2,1,0:T(8,128)}, u32[]{:S(2)}) %copy-start.4) | copy-done | bytes 65560
  3.7 0.6 %pack_y.1 = (f32[12,14,24,128]{3,2,1,0:T(8,128)S(1)}, f32[12,14,24,128]{3,2,1,0:T(8,128)S(1)}, f32[14,24,128]{2,1,0:T(8,128)S(1)}, f32[560,128]{1,0:T(8,128)S(1)}, f32[464,128]{1,0:T(8,128)S(1)}) custom-call(f32[12,8,16,128]{3,2,1,0:T(8,128)S(1)} %bitcast.22, f32[12,8,16,128]{3,2,1,0:T(8,128)S(1)} %bitcast.23, f32[8,16,128]{2,1,0:T(8,128)S(1)} %copy-done.4), custom_call_target="tpu_custom_call" | custom-call | tf_op jit(solution)/shard_map/pack_y/pallas_call | solution.py:343
  4.4 0.0 copy-start.5
  4.4 0.0 copy-start.6
  4.4 0.1 pack_x.1
  4.5 0.5 %collective-permute-start.2 = (f32[1120,128]{1,0:T(8,128)S(1)}, f32[1120,128]{1,0:T(8,128)S(1)}, u32[]{:S(2)}, u32[]{:S(2)}) collective-permute-start(f32[1120,128]{1,0:T(8,128)S(1)} %get-tuple-element.40), channel_id=1, source_target_pairs={{0,4},{4,8},{8,12},{12,0},{1,5},{5,9},{9,13},{13,1},{2,6},{6,10},{... | collective-permute-start | bytes 1720328 | tf_op jit(solution)/shard_map/send_x/ppermute | solution.py:371
  5.0 2.0 %collective-permute-start.3 = (f32[928,128]{1,0:T(8,128)S(1)}, f32[928,128]{1,0:T(8,128)S(1)}, u32[]{:S(2)}, u32[]{:S(2)}) collective-permute-start(f32[928,128]{1,0:T(8,128)S(1)} %get-tuple-element.41), channel_id=1, source_target_pairs={{0,12},{4,0},{8,4},{12,8},{1,13},{5,1},{9,5},{13,9},{2,14},{6,2},{... | collective-permute-start | bytes 1425416 | tf_op jit(solution)/shard_map/send_x/ppermute | solution.py:372
  7.0 2.3 %collective-permute-start = (f32[560,128]{1,0:T(8,128)S(1)}, f32[560,128]{1,0:T(8,128)S(1)}, u32[]{:S(2)}, u32[]{:S(2)}) collective-permute-start(f32[560,128]{1,0:T(8,128)S(1)} %get-tuple-element.29), channel_id=1, source_target_pairs={{0,1},{1,2},{2,3},{3,0},{4,5},{5,6},{6,7},{7,4},{8,9},{9,10},{10,1... | collective-permute-start | bytes 860168 | tf_op jit(solution)/shard_map/send_y/ppermute | solution.py:359
  9.3 2.0 %collective-permute-start.1 = (f32[464,128]{1,0:T(8,128)S(1)}, f32[464,128]{1,0:T(8,128)S(1)}, u32[]{:S(2)}, u32[]{:S(2)}) collective-permute-start(f32[464,128]{1,0:T(8,128)S(1)} %get-tuple-element.30), channel_id=1, source_target_pairs={{0,3},{1,0},{2,1},{3,2},{4,7},{5,4},{6,5},{7,6},{8,11},{9,8},{10,9... | collective-permute-start | bytes 712712 | tf_op jit(solution)/shard_map/send_y/ppermute | solution.py:360
  11.3 11.4 %collective-permute-done.1.z_high = f32[464,128]{1,0:T(8,128)S(1)} collective-permute-done((f32[464,128]{1,0:T(8,128)S(1)}, f32[464,128]{1,0:T(8,128)S(1)}, u32[]{:S(2)}, u32[]{:S(2)}) %collective-permute-start.1) | collective-permute-done | bytes 237600 | tf_op jit(solution)/shard_map/send_y/ppermute | solution.py:360
  22.7 0.0 collective-permute-done.z_low
  22.7 0.1 relay_corners.1
  22.8 0.1 collective-permute-start.4
  22.9 1.7 %collective-permute-start.5 = (f32[128,128]{1,0:T(8,128)S(1)}, f32[128,128]{1,0:T(8,128)S(1)}, u32[]{:S(2)}, u32[]{:S(2)}) collective-permute-start(f32[128,128]{1,0:T(8,128)S(1)} %get-tuple-element.43), channel_id=1, source_target_pairs={{0,12},{4,0},{8,4},{12,8},{1,13},{5,1},{9,5},{13,9},{2,14},{6,2},{... | collective-permute-start | bytes 196616 | tf_op jit(solution)/shard_map/relay_corners/ppermute | solution.py:390
  25.3 0.0 copy-done.5
  25.3 0.0 copy-done.6
  25.3 0.6 %turns.1.refs_13_ = f32[24,128]{1,0:T(8,128)S(1)} custom-call(f32[2,2]{1,0:T(2,128)S(1)} %copy-done.5, s32[1]{0:T(128)S(6)} %copy.35.index, s32[4]{0:T(128)S(1)} %copy-done.6), custom_call_target="tpu_custom_call" | custom-call | tf_op jit(solution)/shard_map/turns/pallas_call | solution.py:374
  25.9 0.0 copy-start.2
  25.9 0.0 copy-start.3
  25.9 1.7 %middle.1 = (f32[4032,128]{1,0:T(8,128)S(1)}, f32[4032,128]{1,0:T(8,128)S(1)}, f32[4032,128]{1,0:T(8,128)S(1)}, f32[4032,128]{1,0:T(8,128)S(1)}, f32[4032,128]{1...) custom-call(f32[4032,128]{1,0:T(8,128)S(1)} %bitcast.17, ...), custom_call_target="tpu_custom_call", output_to_operand_aliasing={{0}: (0, {}), {4}: (1, {}), {8}: (2, {})} | custom-call | flops 20971520 | bytes 20971520 | tf_op jit(solution)/shard_map/middle/pallas_call | solution.py:395
  27.6 0.0 collective-permute-done.5.refs_12_
  27.6 0.0 collective-permute-done.4.refs_11_
  27.6 0.0 collective-permute-done.3.refs_10_
  27.6 0.0 collective-permute-done.2.refs_9_
  27.7 4.8 %edges.1 = (f32[4032,128]{1,0:T(8,128)S(1)}, f32[4032,128]{1,0:T(8,128)S(1)}, f32[4032,128]{1,0:T(8,128)S(1)}, f32[4032,128]{1,0:T(8,128)S(1)}, f32[4032,128]{1,...) custom-call(f32[4032,128]{1,0:T(8,128)S(1)} %get-tuple-element.31.re, ...), custom_call_target="tpu_custom_call", output_to_operand_aliasing={{0}: (0, {}), {1}: (1, {}), {2}: (2, {}), {3}: (3, {}), {4}... | custom-call | tf_op jit(solution)/shard_map/edges/pallas_call | solution.py:406
  32.4 1.5 %collective-permute-start.6 = (f32[128,64]{1,0:T(8,128)S(1)}, f32[128,64]{1,0:T(8,128)S(1)}, u32[]{:S(2)}, u32[]{:S(2)}) collective-permute-start(f32[128,64]{1,0:T(8,128)S(1)} %slice_bitcast_fusion), channel_id=1, source_target_pairs={{0,16},{16,0},{1,17},{17,1},{2,18},{18,2},{3,19},{19,3},{4,20},{20... | collective-permute-start | bytes 98312 | tf_op jit(solution)/shard_map/sum_angles/ppermute | solution.py:417
  33.9 1.0 %write.1 = (f32[6,8,16,128]{3,2,1,0:T(8,128)}, f32[6,8,16,128]{3,2,1,0:T(8,128)}) custom-call(f32[6,8,16,128]{3,2,1,0:T(8,128)S(1)} %bitcast.24, f32[6,8,16,128]{3,2,1,0:T(8,128)S(1)} %bitcast.25), custom_call_target="tpu_custom_call" | custom-call | tf_op jit(solution)/shard_map/write/pallas_call | solution.py:419
  34.9 1.8 %collective-permute-done.6 = f32[128,64]{1,0:T(8,128)S(1)} collective-permute-done((f32[128,64]{1,0:T(8,128)S(1)}, f32[128,64]{1,0:T(8,128)S(1)}, u32[]{:S(2)}, u32[]{:S(2)}) %collective-permute-start.6) | collective-permute-done | bytes 32800 | tf_op jit(solution)/shard_map/sum_angles/ppermute | solution.py:417
  36.7 0.6 %bitcast_add_fusion = f32[128,64]{1,0:T(8,128)} fusion(f32[128,64]{1,0:T(8,128)S(1)} %collective-permute-done.6, f32[2,128,64]{2,1,0:T(8,128)S(1)} %get-tuple-element.48), kind=kLoop, calls=%fused_computation | loop fusion | flops 8192 | bytes 98304 | tf_op jit(solution)/shard_map/sum_angles/add | solution.py:417
  (5 shorter events, 0.0 us)
Async XLA Ops:
  0.6 1.1 %copy-start = (f32[1,12,8,16,128]{4,3,2,1,0:T(8,128)S(1)}, f32[1,12,8,16,128]{4,3,2,1,0:T(8,128)}, u32[]{:S(2)}) copy-start(f32[1,12,8,16,128]{4,3,2,1,0:T(8,128)} %param.8) | copy-start | bytes 2359300
  1.8 1.1 %copy-start.1 = (f32[1,12,8,16,128]{4,3,2,1,0:T(8,128)S(1)}, f32[1,12,8,16,128]{4,3,2,1,0:T(8,128)}, u32[]{:S(2)}) copy-start(f32[1,12,8,16,128]{4,3,2,1,0:T(8,128)} %param.9) | copy-start | bytes 2359300
  2.9 0.8 %copy-start.4 = (f32[8,16,128]{2,1,0:T(8,128)S(1)}, f32[8,16,128]{2,1,0:T(8,128)}, u32[]{:S(2)}) copy-start(f32[8,16,128]{2,1,0:T(8,128)} %eps.1) | copy-start | bytes 196612
  4.4 20.9 %copy-start.5 = (f32[2,2]{1,0:T(2,128)S(1)}, f32[2,2]{1,0:T(2,128)}, u32[]{:S(2)}) copy-start(f32[2,2]{1,0:T(2,128)} %table.1) | copy-start | bytes 52
  4.4 20.9 %copy-start.6 = (s32[4]{0:T(128)S(1)}, s32[4]{0:T(128)}, u32[]{:S(2)}) copy-start(s32[4]{0:T(128)} %tiles.1) | copy-start | bytes 52
  4.5 23.2 %collective-permute-start.2 = (f32[1120,128]{1,0:T(8,128)S(1)}, f32[1120,128]{1,0:T(8,128)S(1)}, u32[]{:S(2)}, u32[]{:S(2)}) collective-permute-start(f32[1120,128]{1,0:T(8,128)S(1)} %get-tuple-element.40), channel_id=1, source_target_pairs={{0,4},{4,8},{8,12},{12,0},{1,5},{5,9},{9,13},{13,1},{2,6},{6,10},{... | collective-permute-start | bytes 1720328 | tf_op jit(solution)/shard_map/send_x/ppermute | solution.py:371
  5.0 22.7 %collective-permute-start.3 = (f32[928,128]{1,0:T(8,128)S(1)}, f32[928,128]{1,0:T(8,128)S(1)}, u32[]{:S(2)}, u32[]{:S(2)}) collective-permute-start(f32[928,128]{1,0:T(8,128)S(1)} %get-tuple-element.41), channel_id=1, source_target_pairs={{0,12},{4,0},{8,4},{12,8},{1,13},{5,1},{9,5},{13,9},{2,14},{6,2},{... | collective-permute-start | bytes 1425416 | tf_op jit(solution)/shard_map/send_x/ppermute | solution.py:372
  7.0 15.7 %collective-permute-start = (f32[560,128]{1,0:T(8,128)S(1)}, f32[560,128]{1,0:T(8,128)S(1)}, u32[]{:S(2)}, u32[]{:S(2)}) collective-permute-start(f32[560,128]{1,0:T(8,128)S(1)} %get-tuple-element.29), channel_id=1, source_target_pairs={{0,1},{1,2},{2,3},{3,0},{4,5},{5,6},{6,7},{7,4},{8,9},{9,10},{10,1... | collective-permute-start | bytes 860168 | tf_op jit(solution)/shard_map/send_y/ppermute | solution.py:359
  9.3 13.4 %collective-permute-start.1 = (f32[464,128]{1,0:T(8,128)S(1)}, f32[464,128]{1,0:T(8,128)S(1)}, u32[]{:S(2)}, u32[]{:S(2)}) collective-permute-start(f32[464,128]{1,0:T(8,128)S(1)} %get-tuple-element.30), channel_id=1, source_target_pairs={{0,3},{1,0},{2,1},{3,2},{4,7},{5,4},{6,5},{7,6},{8,11},{9,8},{10,9... | collective-permute-start | bytes 712712 | tf_op jit(solution)/shard_map/send_y/ppermute | solution.py:360
  22.8 4.8 %collective-permute-start.4 = (f32[152,128]{1,0:T(8,128)S(1)}, f32[152,128]{1,0:T(8,128)S(1)}, u32[]{:S(2)}, u32[]{:S(2)}) collective-permute-start(f32[152,128]{1,0:T(8,128)S(1)} %get-tuple-element.42), channel_id=1, source_target_pairs={{0,4},{4,8},{8,12},{12,0},{1,5},{5,9},{9,13},{13,1},{2,6},{6,10},{... | collective-permute-start | bytes 233480 | tf_op jit(solution)/shard_map/relay_corners/ppermute | solution.py:389
  22.9 4.7 %collective-permute-start.5 = (f32[128,128]{1,0:T(8,128)S(1)}, f32[128,128]{1,0:T(8,128)S(1)}, u32[]{:S(2)}, u32[]{:S(2)}) collective-permute-start(f32[128,128]{1,0:T(8,128)S(1)} %get-tuple-element.43), channel_id=1, source_target_pairs={{0,12},{4,0},{8,4},{12,8},{1,13},{5,1},{9,5},{13,9},{2,14},{6,2},{... | collective-permute-start | bytes 196616 | tf_op jit(solution)/shard_map/relay_corners/ppermute | solution.py:390
  25.9 1.8 %copy-start.2 = (f32[1,6,8,16,128]{4,3,2,1,0:T(8,128)S(1)}, f32[1,6,8,16,128]{4,3,2,1,0:T(8,128)}, u32[]{:S(2)}) copy-start(f32[1,6,8,16,128]{4,3,2,1,0:T(8,128)} %param.10) | copy-start | bytes 1179652
  25.9 1.8 %copy-start.3 = (f32[1,6,8,16,128]{4,3,2,1,0:T(8,128)S(1)}, f32[1,6,8,16,128]{4,3,2,1,0:T(8,128)}, u32[]{:S(2)}) copy-start(f32[1,6,8,16,128]{4,3,2,1,0:T(8,128)} %param.11) | copy-start | bytes 1179652
  32.4 4.3 %collective-permute-start.6 = (f32[128,64]{1,0:T(8,128)S(1)}, f32[128,64]{1,0:T(8,128)S(1)}, u32[]{:S(2)}, u32[]{:S(2)}) collective-permute-start(f32[128,64]{1,0:T(8,128)S(1)} %slice_bitcast_fusion), channel_id=1, source_target_pairs={{0,16},{16,0},{1,17},{17,1},{2,18},{18,2},{3,19},{19,3},{4,20},{20... | collective-permute-start | bytes 98312 | tf_op jit(solution)/shard_map/sum_angles/ppermute | solution.py:417

commit v3 on v2

--- a/solution.py
+++ b/solution.py
@@ -353,7 +353,7 @@
             out_specs=[VMEM] * 5,
             scratch_shapes=[pltpu.SemaphoreType.DMA((25,))],
             compiler_params=params(16),
-        )(forward_fields[0], adjoint_fields[0], permittivity)
+        )(*(pltpu.with_memory_space_constraint(array, pltpu.HBM) for array in (forward_fields[0], adjoint_fields[0], permittivity)))
     e0, h0, coef = (state.reshape((-1, depth)) for state in (e0, h0, coef))
     with jax.named_scope("send_y"):
         z_low = lax.ppermute(z_up, "gy", ring_pairs("gy", 1))
@@ -399,7 +399,7 @@
             out_specs=[VMEM] * count,
             input_output_aliases={0: 0, 1: STEPS + 1, 2: count - 1},
             compiler_params=params(8),
-            cost_estimate=cost(20 * 2**20),
+            cost_estimate=cost(2**32),
         )(e0, h0, coef, z_low, z_high, turns)
     with jax.named_scope("edges"):
         spectra = [spectrum.reshape((-1, depth)) for spectrum in (forward_spectrum, adjoint_spectrum)]

time: 37.6 us -> 33.5 us (0.89)
  local copies, waits for them, and re-layouts: 3.13 us -> 0.02 us
  Pallas kernels: 8.78 us -> 9.92 us
  starting transfers between devices: 10.1 us -> 9.03 us
  waiting for transfers between devices: 13.2 us -> 12.3 us
    ppermute x1, waiting for transfers between devices: 11.4 us -> 8.14 us  [shards(): z_high = lax.ppermute(z_down, 'gy', ring_pairs('gy', -1))]
    unnamed x14 -> x8, local copies, waits for them, and re-layouts: 3.12 us -> 0.01 us
    ppermute x1, waiting for transfers between devices: 0.01 us -> 1.54 us  [shards(): c_low = lax.ppermute(c_up, 'gx', ring_pairs('gx', 1))]
    ppermute x1, starting transfers between devices: 1.73 us -> 0.57 us  [shards(): c_high = lax.ppermute(c_down, 'gx', ring_pairs('gx', -1))]
    pallas_call x1, Pallas kernels: 0.62 us -> 1.74 us  [shards(): pl.pallas_call(functools.partial(pack_y_kernel, plan), out_shape=(array(1...]
    ppermute x1, waiting for transfers between devices: 0.01 us -> 0.83 us  [shards(): c_high = lax.ppermute(c_down, 'gx', ring_pairs('gx', -1))]
    ppermute x1, starting transfers between devices: 2.3 us -> 3.08 us  [shards(): z_low = lax.ppermute(z_up, 'gy', ring_pairs('gy', 1))]
    ppermute x1, starting transfers between devices: 0.5 us -> 0.06 us  [shards(): x_low = lax.ppermute(x_up, 'gx', ring_pairs('gx', 1))]
  transfers between devices with their start and end apart: 7 -> 7, of which waited for: 2 -> 4; matrix products, arithmetic and copies ran while one was open for 0% -> 0% of each run, Pallas kernels for 9% -> 10%
where the time goes in v3:
time: 33.5 us; the launch traced here: 33.3 us
  waiting for transfers between devices  12.3 us (37%)
  Pallas kernels  9.92 us (30%)
  starting transfers between devices  9.03 us (27%)
  between operations  1.36 us (4%)
  other arithmetic  0.64 us (2%)
    ppermute x1, waiting for transfers between devices, shards(): z_high = lax.ppermute(z_down, 'gy', ring_pairs('gy', -1))  8.14 us
    pallas_call x1, Pallas kernels, shards(): pl.pallas_call(functools.partial(edges_kernel, plan, groups), out_shape=[...  4.78 us
    ppermute x1, starting transfers between devices, shards(): z_low = lax.ppermute(z_up, 'gy', ring_pairs('gy', 1))  3.08 us
    ppermute x1, starting transfers between devices, shards(): z_high = lax.ppermute(z_down, 'gy', ring_pairs('gy', -1))  2.09 us
    ppermute x1, waiting for transfers between devices, shards(): lax.ppermute(parts[k], 'angle', ring_pairs('angle', k))  1.79 us
    pallas_call x1, Pallas kernels, shards(): pl.pallas_call(functools.partial(pack_y_kernel, plan), out_shape=(array(1...  1.74 us
    ppermute x1, starting transfers between devices, shards(): x_high = lax.ppermute(x_down, 'gx', ring_pairs('gx', -1))  1.73 us
    pallas_call x1, Pallas kernels, shards(): pl.pallas_call(functools.partial(middle_kernel, plan), out_shape=levels,...  1.68 us
  transfers between devices with their start and end apart: 7, of which 4 were waited for; matrix products, arithmetic and copies ran while one was open for 0% of the time, Pallas kernels for 10%

profile of v3, /device:TPU:0, one launch (start us, length us, event | category | flops | bytes accessed | tf_op | source)
XLA Modules:
  0.0 33.3 jit_solution(6570818805554019759)
XLA Ops:
  0.6 1.7 %pack_y.1 = (f32[12,14,24,128]{3,2,1,0:T(8,128)S(1)}, f32[12,14,24,128]{3,2,1,0:T(8,128)S(1)}, f32[14,24,128]{2,1,0:T(8,128)S(1)}, f32[560,128]{1,0:T(8,128)S(1)}, f32[464,128]{1,0:T(8,128)S(1)}) custom-call(f32[12,8,16,128]{3,2,1,0:T(8,128)} %bitcast.26, f32[12,8,16,128]{3,2,1,0:T(8,128)} %bitcast.27, f32[8,16,128]{2,1,0:T(8,128)} %eps.1), custom_call_target="tpu_custom_call" | custom-call | tf_op jit(solution)/shard_map/pack_y/pallas_call | solution.py:343
  2.4 3.1 %collective-permute-start = (f32[560,128]{1,0:T(8,128)S(1)}, f32[560,128]{1,0:T(8,128)S(1)}, u32[]{:S(2)}, u32[]{:S(2)}) collective-permute-start(f32[560,128]{1,0:T(8,128)S(1)} %get-tuple-element.29), channel_id=1, source_target_pairs={{0,1},{1,2},{2,3},{3,0},{4,5},{5,6},{6,7},{7,4},{8,9},{9,10},{10,1... | collective-permute-start | bytes 860168 | tf_op jit(solution)/shard_map/send_y/ppermute | solution.py:359
  5.5 2.1 %collective-permute-start.1 = (f32[464,128]{1,0:T(8,128)S(1)}, f32[464,128]{1,0:T(8,128)S(1)}, u32[]{:S(2)}, u32[]{:S(2)}) collective-permute-start(f32[464,128]{1,0:T(8,128)S(1)} %get-tuple-element.30), channel_id=1, source_target_pairs={{0,3},{1,0},{2,1},{3,2},{4,7},{5,4},{6,5},{7,6},{8,11},{9,8},{10,9... | collective-permute-start | bytes 712712 | tf_op jit(solution)/shard_map/send_y/ppermute | solution.py:360
  7.5 0.0 copy-start.2
  7.5 0.0 copy-start.3
  7.5 0.1 pack_x.1
  7.6 0.1 collective-permute-start.2
  7.7 1.7 %collective-permute-start.3 = (f32[928,128]{1,0:T(8,128)S(1)}, f32[928,128]{1,0:T(8,128)S(1)}, u32[]{:S(2)}, u32[]{:S(2)}) collective-permute-start(f32[928,128]{1,0:T(8,128)S(1)} %get-tuple-element.41), channel_id=1, source_target_pairs={{0,12},{4,0},{8,4},{12,8},{1,13},{5,1},{9,5},{13,9},{2,14},{6,2},{... | collective-permute-start | bytes 1425416 | tf_op jit(solution)/shard_map/send_x/ppermute | solution.py:372
  10.1 0.0 copy-done.2
  10.1 0.0 copy-done.3
  10.1 0.6 %turns.1.refs_13_ = f32[24,128]{1,0:T(8,128)S(1)} custom-call(f32[2,2]{1,0:T(2,128)S(1)} %copy-done.2, s32[1]{0:T(128)S(6)} %copy.35.index, s32[4]{0:T(128)S(1)} %copy-done.3), custom_call_target="tpu_custom_call" | custom-call | tf_op jit(solution)/shard_map/turns/pallas_call | solution.py:374
  10.7 8.1 %collective-permute-done.1.z_high = f32[464,128]{1,0:T(8,128)S(1)} collective-permute-done((f32[464,128]{1,0:T(8,128)S(1)}, f32[464,128]{1,0:T(8,128)S(1)}, u32[]{:S(2)}, u32[]{:S(2)}) %collective-permute-start.1) | collective-permute-done | bytes 237600 | tf_op jit(solution)/shard_map/send_y/ppermute | solution.py:360
  18.8 0.0 collective-permute-done.z_low
  18.8 0.1 relay_corners.1
  18.9 0.6 %collective-permute-start.5 = (f32[128,128]{1,0:T(8,128)S(1)}, f32[128,128]{1,0:T(8,128)S(1)}, u32[]{:S(2)}, u32[]{:S(2)}) collective-permute-start(f32[128,128]{1,0:T(8,128)S(1)} %get-tuple-element.43), channel_id=1, source_target_pairs={{0,12},{4,0},{8,4},{12,8},{1,13},{5,1},{9,5},{13,9},{2,14},{6,2},{... | collective-permute-start | bytes 196616 | tf_op jit(solution)/shard_map/relay_corners/ppermute | solution.py:390
  19.5 0.0 copy-start
  19.5 0.0 copy-start.1
  19.5 0.0 collective-permute-start.4
  19.5 1.7 %middle.1 = (f32[4032,128]{1,0:T(8,128)S(1)}, f32[4032,128]{1,0:T(8,128)S(1)}, f32[4032,128]{1,0:T(8,128)S(1)}, f32[4032,128]{1,0:T(8,128)S(1)}, f32[4032,128]{1...) custom-call(f32[4032,128]{1,0:T(8,128)S(1)} %bitcast.17, ...), custom_call_target="tpu_custom_call", output_to_operand_aliasing={{0}: (0, {}), {4}: (1, {}), {8}: (2, {})} | custom-call | flops 4294967296 | bytes 4294967296 | tf_op jit(solution)/shard_map/middle/pallas_call | solution.py:395
  21.2 0.8 %collective-permute-done.5.refs_12_ = f32[128,128]{1,0:T(8,128)S(1)} collective-permute-done((f32[128,128]{1,0:T(8,128)S(1)}, f32[128,128]{1,0:T(8,128)S(1)}, u32[]{:S(2)}, u32[]{:S(2)}) %collective-permute-start.5) | collective-permute-done | bytes 65568 | tf_op jit(solution)/shard_map/relay_corners/ppermute | solution.py:390
  22.0 1.5 %collective-permute-done.4.refs_11_ = f32[152,128]{1,0:T(8,128)S(1)} collective-permute-done((f32[152,128]{1,0:T(8,128)S(1)}, f32[152,128]{1,0:T(8,128)S(1)}, u32[]{:S(2)}, u32[]{:S(2)}) %collective-permute-start.4) | collective-permute-done | bytes 77856 | tf_op jit(solution)/shard_map/relay_corners/ppermute | solution.py:389
  23.6 0.0 collective-permute-done.3.refs_10_
  23.6 0.0 collective-permute-done.2.refs_9_
  23.6 0.0 copy-done
  23.6 0.0 copy-done.1
  23.6 4.8 %edges.1 = (f32[4032,128]{1,0:T(8,128)S(1)}, f32[4032,128]{1,0:T(8,128)S(1)}, f32[4032,128]{1,0:T(8,128)S(1)}, f32[4032,128]{1,0:T(8,128)S(1)}, f32[4032,128]{1,...) custom-call(f32[4032,128]{1,0:T(8,128)S(1)} %get-tuple-element.31.re, ...), custom_call_target="tpu_custom_call", output_to_operand_aliasing={{0}: (0, {}), {1}: (1, {}), {2}: (2, {}), {3}: (3, {}), {4}... | custom-call | tf_op jit(solution)/shard_map/edges/pallas_call | solution.py:406
  28.4 1.5 %collective-permute-start.6 = (f32[128,64]{1,0:T(8,128)S(1)}, f32[128,64]{1,0:T(8,128)S(1)}, u32[]{:S(2)}, u32[]{:S(2)}) collective-permute-start(f32[128,64]{1,0:T(8,128)S(1)} %slice_bitcast_fusion), channel_id=1, source_target_pairs={{0,16},{16,0},{1,17},{17,1},{2,18},{18,2},{3,19},{19,3},{4,20},{20... | collective-permute-start | bytes 98312 | tf_op jit(solution)/shard_map/sum_angles/ppermute | solution.py:417
  29.9 1.0 %write.1 = (f32[6,8,16,128]{3,2,1,0:T(8,128)}, f32[6,8,16,128]{3,2,1,0:T(8,128)}) custom-call(f32[6,8,16,128]{3,2,1,0:T(8,128)S(1)} %bitcast.22, f32[6,8,16,128]{3,2,1,0:T(8,128)S(1)} %bitcast.23), custom_call_target="tpu_custom_call" | custom-call | tf_op jit(solution)/shard_map/write/pallas_call | solution.py:419
  30.9 1.8 %collective-permute-done.6 = f32[128,64]{1,0:T(8,128)S(1)} collective-permute-done((f32[128,64]{1,0:T(8,128)S(1)}, f32[128,64]{1,0:T(8,128)S(1)}, u32[]{:S(2)}, u32[]{:S(2)}) %collective-permute-start.6) | collective-permute-done | bytes 32800 | tf_op jit(solution)/shard_map/sum_angles/ppermute | solution.py:417
  32.6 0.6 %bitcast_add_fusion = f32[128,64]{1,0:T(8,128)} fusion(f32[128,64]{1,0:T(8,128)S(1)} %collective-permute-done.6, f32[2,128,64]{2,1,0:T(8,128)S(1)} %get-tuple-element.48), kind=kLoop, calls=%fused_computation | loop fusion | flops 8192 | bytes 98304 | tf_op jit(solution)/shard_map/sum_angles/add | solution.py:417
  (1 shorter events, 0.0 us)
Async XLA Ops:
  2.4 16.5 %collective-permute-start = (f32[560,128]{1,0:T(8,128)S(1)}, f32[560,128]{1,0:T(8,128)S(1)}, u32[]{:S(2)}, u32[]{:S(2)}) collective-permute-start(f32[560,128]{1,0:T(8,128)S(1)} %get-tuple-element.29), channel_id=1, source_target_pairs={{0,1},{1,2},{2,3},{3,0},{4,5},{5,6},{6,7},{7,4},{8,9},{9,10},{10,1... | collective-permute-start | bytes 860168 | tf_op jit(solution)/shard_map/send_y/ppermute | solution.py:359
  5.5 13.4 %collective-permute-start.1 = (f32[464,128]{1,0:T(8,128)S(1)}, f32[464,128]{1,0:T(8,128)S(1)}, u32[]{:S(2)}, u32[]{:S(2)}) collective-permute-start(f32[464,128]{1,0:T(8,128)S(1)} %get-tuple-element.30), channel_id=1, source_target_pairs={{0,3},{1,0},{2,1},{3,2},{4,7},{5,4},{6,5},{7,6},{8,11},{9,8},{10,9... | collective-permute-start | bytes 712712 | tf_op jit(solution)/shard_map/send_y/ppermute | solution.py:360
  7.5 2.5 %copy-start.2 = (f32[2,2]{1,0:T(2,128)S(1)}, f32[2,2]{1,0:T(2,128)}, u32[]{:S(2)}) copy-start(f32[2,2]{1,0:T(2,128)} %table.1) | copy-start | bytes 52
  7.5 2.5 %copy-start.3 = (s32[4]{0:T(128)S(1)}, s32[4]{0:T(128)}, u32[]{:S(2)}) copy-start(s32[4]{0:T(128)} %tiles.1) | copy-start | bytes 52
  7.6 16.0 %collective-permute-start.2 = (f32[1120,128]{1,0:T(8,128)S(1)}, f32[1120,128]{1,0:T(8,128)S(1)}, u32[]{:S(2)}, u32[]{:S(2)}) collective-permute-start(f32[1120,128]{1,0:T(8,128)S(1)} %get-tuple-element.40), channel_id=1, source_target_pairs={{0,4},{4,8},{8,12},{12,0},{1,5},{5,9},{9,13},{13,1},{2,6},{6,10},{... | collective-permute-start | bytes 1720328 | tf_op jit(solution)/shard_map/send_x/ppermute | solution.py:371
  7.7 15.9 %collective-permute-start.3 = (f32[928,128]{1,0:T(8,128)S(1)}, f32[928,128]{1,0:T(8,128)S(1)}, u32[]{:S(2)}, u32[]{:S(2)}) collective-permute-start(f32[928,128]{1,0:T(8,128)S(1)} %get-tuple-element.41), channel_id=1, source_target_pairs={{0,12},{4,0},{8,4},{12,8},{1,13},{5,1},{9,5},{13,9},{2,14},{6,2},{... | collective-permute-start | bytes 1425416 | tf_op jit(solution)/shard_map/send_x/ppermute | solution.py:372
  18.9 3.1 %collective-permute-start.5 = (f32[128,128]{1,0:T(8,128)S(1)}, f32[128,128]{1,0:T(8,128)S(1)}, u32[]{:S(2)}, u32[]{:S(2)}) collective-permute-start(f32[128,128]{1,0:T(8,128)S(1)} %get-tuple-element.43), channel_id=1, source_target_pairs={{0,12},{4,0},{8,4},{12,8},{1,13},{5,1},{9,5},{13,9},{2,14},{6,2},{... | collective-permute-start | bytes 196616 | tf_op jit(solution)/shard_map/relay_corners/ppermute | solution.py:390
  19.5 4.1 %copy-start = (f32[1,6,8,16,128]{4,3,2,1,0:T(8,128)S(1)}, f32[1,6,8,16,128]{4,3,2,1,0:T(8,128)}, u32[]{:S(2)}) copy-start(f32[1,6,8,16,128]{4,3,2,1,0:T(8,128)} %param.10) | copy-start | bytes 1179652
  19.5 4.1 %copy-start.1 = (f32[1,6,8,16,128]{4,3,2,1,0:T(8,128)S(1)}, f32[1,6,8,16,128]{4,3,2,1,0:T(8,128)}, u32[]{:S(2)}) copy-start(f32[1,6,8,16,128]{4,3,2,1,0:T(8,128)} %param.11) | copy-start | bytes 1179652
  19.5 4.1 %collective-permute-start.4 = (f32[152,128]{1,0:T(8,128)S(1)}, f32[152,128]{1,0:T(8,128)S(1)}, u32[]{:S(2)}, u32[]{:S(2)}) collective-permute-start(f32[152,128]{1,0:T(8,128)S(1)} %get-tuple-element.42), channel_id=1, source_target_pairs={{0,4},{4,8},{8,12},{12,0},{1,5},{5,9},{9,13},{13,1},{2,6},{6,10},{... | collective-permute-start | bytes 233480 | tf_op jit(solution)/shard_map/relay_corners/ppermute | solution.py:389
  28.4 4.3 %collective-permute-start.6 = (f32[128,64]{1,0:T(8,128)S(1)}, f32[128,64]{1,0:T(8,128)S(1)}, u32[]{:S(2)}, u32[]{:S(2)}) collective-permute-start(f32[128,64]{1,0:T(8,128)S(1)} %slice_bitcast_fusion), channel_id=1, source_target_pairs={{0,16},{16,0},{1,17},{17,1},{2,18},{18,2},{3,19},{19,3},{4,20},{20... | collective-permute-start | bytes 98312 | tf_op jit(solution)/shard_map/sum_angles/ppermute | solution.py:417

commit v4 on v3

v4 whole, which is shorter than its diff:
```python
import functools
import math

import jax
import jax.numpy as jnp
from jax import lax
from jax.experimental import pallas as pl
from jax.experimental.pallas import tpu as pltpu
from jax.sharding import PartitionSpec as P

STEPS = 3
SUB = 8

courant = 0.5
omega_step = 0.7

VMEM = pl.BlockSpec(memory_space=pltpu.VMEM)
SMEM = pl.BlockSpec(memory_space=pltpu.SMEM)
HBM = pl.BlockSpec(memory_space=pltpu.HBM)


def reads(node):
    kind, level, comp, x, y = node
    others = [c for c in range(3) if c != comp]
    if kind == "E":
        found = [("E", level - 1, comp, x, y), ("C", 0, 0, x, y)] + [("H", level, c, x, y) for c in others]
        if comp != 1:
            found.append(("H", level, 2 - comp, x, y - 1))
        if comp != 0:
            found.append(("H", level, 3 - comp, x - 1, y))
        return found
    found = [("H", level - 1, comp, x, y)] + [("E", level - 1, c, x, y) for c in others]
    if comp != 1:
        found.append(("E", level - 1, 2 - comp, x, y + 1))
    if comp != 0:
        found.append(("E", level - 1, 3 - comp, x + 1, y))
    return found


def wanted(nx, ny):
    def block(node):
        return node[3] // nx, node[4] // ny

    @functools.cache
    def alone(node):
        if node[1] == 0:
            return True
        return node[1] == 1 and all(block(other) == block(node) and alone(other) for other in reads(node))

    found, seen = set(), set()
    todo = [("E", STEPS, comp, x, y) for comp in range(3) for x in range(nx) for y in range(ny)]
    while todo:
        node = todo.pop()
        if node in seen:
            continue
        seen.add(node)
        if block(node) != (0, 0) and alone(node):
            found.add(node)
        elif node[1]:
            todo += reads(node)
    return found


class Message:
    def __init__(self, nodes, axis):
        self.axis, self.runs, self.at, self.size = axis, [], {}, 0
        stretches = []
        for node in sorted(nodes):
            before = list(node)
            before[3 + axis] -= 1
            if tuple(before) in nodes:
                continue
            count = 1
            while (*node[:3], node[3] + count * (axis == 0), node[4] + count * (axis == 1)) in nodes:
                count += 1
            stretches.append((count, node))
        for count, (kind, level, comp, x, y) in sorted(stretches, key=lambda item: (-item[0], item[1])):
            for run in (0, 1) if kind != "C" else (0,):
                for part in (0, 1) if kind != "C" else (0,):
                    what = (kind, level, comp, run, part)
                    self.runs.append((what, x, y, count, self.size))
                    for i in range(count):
                        self.at[what, x + i * (axis == 0), y + i * (axis == 1)] = self.size + i
                    self.size += count
        self.lines = -(-self.size // SUB) * SUB


class Plan:
    def __init__(self, nx, ny):
        self.nx, self.ny = nx, ny
        self.wide, self.ring = nx + 2 * STEPS, ny + SUB
        nodes = wanted(nx, ny)
        sides = {}
        for node in nodes:
            sides.setdefault((node[3] // nx, node[4] // ny), set()).add(node)

        def shifted(found, dx):
            return {(*node[:3], node[3] + dx, node[4]) for node in found}

        self.x_low, self.x_high = Message(sides[-1, 0], 1), Message(sides[1, 0], 1)
        self.y_low, self.y_high = (
            Message(sides[0, side] | shifted(sides[-1, side], nx) | shifted(sides[1, side], -nx), 0) for side in (-1, 1)
        )
        self.corner_low, self.corner_high = (Message(sides[side, -1] | sides[side, 1], 1) for side in (-1, 1))

    def row(self, x, y, run=0, part=0, comp=0):
        return ((run * 6 + part * 3 + comp) * self.wide + x + STEPS) * self.ring + y % self.ring

    def rows(self, what, x, y, axis, count):
        _, _, comp, run, part = what
        start = self.row(x, y, run, part, comp)
        return pl.ds(start, count, stride=self.ring) if axis == 0 and count > 1 else pl.ds(start, count)


class State:
    def __init__(self, efield, hfield, coef):
        self.by_kind = {"E": efield, "H": hfield, "C": [coef]}

    def __call__(self, what):
        return self.by_kind[what[0]][what[1]]


def pack(plan, message, state, dx, dy, out):
    for what, x, y, count, at in message.runs:
        out[pl.ds(at, count), :] = state(what)[plan.rows(what, x + dx, y + dy, message.axis, count), :]


def pack_y_kernel(plan, fwd, adj, eps, e0, h0, e1, h1, coef, z_up, z_down, sems):
    nx, ny = plan.nx, plan.ny
    own = (pl.ds(STEPS, nx), pl.ds(0, ny), slice(None))
    copies = []
    for run, ref in enumerate((fwd, adj)):
        for kind, array in enumerate((e0, h0)):
            for i in range(6):
                copies.append(
                    pltpu.make_async_copy(ref.at[kind * 6 + i], array.at[(run * 6 + i, *own)], sems.at[len(copies)])
                )
    copies.append(pltpu.make_async_copy(eps, coef.at[own], sems.at[len(copies)]))
    for copy in copies:
        copy.start()
    for copy in copies:
        copy.wait()
    for x in range(nx):
        coef[STEPS + x, pl.ds(0, ny), :] = (0.5 * courant) / coef[STEPS + x, pl.ds(0, ny), :]
    e0, h0, e1, h1, coef = (array.reshape((-1, array.shape[-1])) for array in (e0, h0, e1, h1, coef))
    Sweeps(plan, [e0, e1], [h0, h1], coef, ny).both(1, range(nx), range(nx - 1))
    state = State([e0, e1], [h0, h1], coef)
    pack(plan, plan.y_low, state, 0, ny, z_up)
    pack(plan, plan.y_high, state, 0, -ny, z_down)


def pack_x_kernel(plan, e0, h0, e1, h1, coef, x_up, x_down):
    state = State([e0, e1], [h0, h1], coef)
    pack(plan, plan.x_low, state, plan.nx, 0, x_up)
    pack(plan, plan.x_high, state, -plan.nx, 0, x_down)


def turns_kernel(groups, table, index, tiles, turns):
    row = index[0]
    phi_x, phi_y = table[row, 0], table[row, 1]
    at_x, at_y = lax.axis_index("gx"), lax.axis_index("gy")
    none = jnp.float32(0.0)
    ax_low = jnp.where(at_x == 0, -phi_x, none)
    ax_high = jnp.where(at_x == lax.axis_size("gx") - 1, phi_x, none)
    ay_low = jnp.where(at_y == 0, -phi_y, none)
    ay_high = jnp.where(at_y == lax.axis_size("gy") - 1, phi_y, none)
    sub = lax.broadcasted_iota(jnp.int32, (SUB, turns.shape[1]), 0)
    angles = jnp.zeros(sub.shape, jnp.float32)
    for i, angle in enumerate((ax_low, ax_high, ay_low, ay_high, ax_low + ay_low, ax_low + ay_high,
                               ax_high + ay_low, ax_high + ay_high)):
        angles = jnp.where(sub == i, angle, angles)
    turns[pl.ds(0, SUB), :] = jnp.cos(angles)
    turns[pl.ds(SUB, SUB), :] = jnp.sin(angles)
    own_tile = at_x * lax.axis_size("gy") + at_y
    chosen = tiles[0] == own_tile
    for i in range(1, tiles.shape[0]):
        chosen = jnp.logical_or(chosen, tiles[i] == own_tile)
    weight = jnp.where(chosen, jnp.float32(1.0 / groups), none)
    turns[pl.ds(2 * SUB, SUB), :] = jnp.full(sub.shape, weight, jnp.float32)


def corner_kernel(plan, z_low, z_high, c_up, c_down):
    for message, dx, out in ((plan.corner_low, plan.nx, c_up), (plan.corner_high, -plan.nx, c_down)):
        for (what, x, y), row in message.at.items():
            ref, source = (z_low, plan.y_low) if y < 0 else (z_high, plan.y_high)
            out[pl.ds(row, 1), :] = ref[pl.ds(source.at[what, x + dx, y], 1), :]


def turned(real, imag, cosine, sine):
    return real * cosine - imag * sine, real * sine + imag * cosine


def unpack(plan, message, ref, which, turns, state, kinds, level, layers=None):
    axis = message.axis
    for (kind, at_level, comp, run, part), x, y, count, at in message.runs:
        if kind not in kinds or at_level != level or part == 1:
            continue
        pieces = [(x, y, count, at)]
        if layers is not None:
            pieces = [(x + i, y, 1, at + i) for i in range(count) if x + i in layers]
        for cell_x, cell_y, size, row in pieces:
            what = (kind, at_level, comp, run, 0)
            real = ref[pl.ds(row, size), :]
            if kind == "C":
                state(what)[plan.rows(what, cell_x, cell_y, axis, size), :] = real
                continue
            twin = (kind, at_level, comp, run, 1)
            imag = ref[pl.ds(message.at[twin, cell_x, cell_y], size), :]
            turn = which(y)
            cosine, sine = turns[pl.ds(turn, 1), :], turns[pl.ds(SUB + turn, 1), :]
            real, imag = turned(real, imag, cosine, sine if run == 0 else -sine)
            state(what)[plan.rows(what, cell_x, cell_y, axis, size), :] = real
            state(twin)[plan.rows(twin, cell_x, cell_y, axis, size), :] = imag


class Sweeps:
    def __init__(self, plan, efield, hfield, coef, height):
        self.plan, self.efield, self.hfield, self.coef, self.height = plan, efield, hfield, coef, height
        lane = lax.broadcasted_iota(jnp.int32, (height, coef.shape[1]), 1)
        self.first, self.last = lane == 0, lane == coef.shape[1] - 1

    def rows(self, group, comp, x):
        plan = self.plan
        start = (group * 3 + comp) * plan.wide * plan.ring + (x + STEPS) * plan.ring
        return pl.ds(start if isinstance(start, int) else pl.multiple_of(start, SUB), self.height)

    def next_z(self, value):
        return jnp.where(self.last, 0.0, pltpu.roll(value, value.shape[1] - 1, 1))

    def prev_z(self, value):
        return jnp.where(self.first, 0.0, pltpu.roll(value, 1, 1))

    def next_y(self, value):
        return pltpu.roll(value, self.height - 1, 0)

    def prev_y(self, value):
        return pltpu.roll(value, 1, 0)

    def update_h(self, step, group, x):
        efield, old, new = self.efield[step - 1], self.hfield[step - 1], self.hfield[step]
        ex, ey, ez = (efield[self.rows(group, comp, x), :] for comp in range(3))
        ey_x, ez_x = (efield[self.rows(group, comp, x + 1), :] for comp in (1, 2))
        hx, hy, hz = (old[self.rows(group, comp, x), :] for comp in range(3))
        if step == 1:
            hx, hy, hz = hx + hx, hy + hy, hz + hz
        new[self.rows(group, 0, x), :] = hx - ((self.next_y(ez) - ez) - (self.next_z(ey) - ey))
        new[self.rows(group, 1, x), :] = hy - ((self.next_z(ex) - ex) - (ez_x - ez))
        new[self.rows(group, 2, x), :] = hz - ((ey_x - ey) - (self.next_y(ex) - ex))

    def update_e(self, step, group, x):
        old, new, hfield = self.efield[step - 1], self.efield[step], self.hfield[step]
        ex, ey, ez = (old[self.rows(group, comp, x), :] for comp in range(3))
        hx, hy, hz = (hfield[self.rows(group, comp, x), :] for comp in range(3))
        hy_x, hz_x = (hfield[self.rows(group, comp, x - 1), :] for comp in (1, 2))
        scale = self.coef[self.rows(0, 0, x), :]
        new[self.rows(group, 0, x), :] = ex + scale * ((hz - self.prev_y(hz)) - (hy - self.prev_z(hy)))
        new[self.rows(group, 1, x), :] = ey + scale * ((hx - self.prev_z(hx)) - (hz - hz_x))
        new[self.rows(group, 2, x), :] = ez + scale * ((hy - hy_x) - (hx - self.prev_y(hx)))

    def both(self, step, h_layers, e_layers, after_h=None, after_e=None):
        for update, layers, after in ((self.update_h, h_layers, after_h), (self.update_e, e_layers, after_e)):

            @pl.loop(0, 2)
            def _(run):
                for part in (0, 1):
                    for x in layers:
                        update(step, run * 2 + part, x)

            if after is not None:
                after()


def middle_kernel(plan, e0_in, h0_in, e1_in, h1_in, coef_in, z_low, z_high, turns, *arrays):
    nx = plan.nx
    efield, hfield, coef = arrays[: STEPS + 1], arrays[STEPS + 1 : 2 * STEPS + 2], arrays[-1]
    state = State(efield, hfield, coef)

    def take(kinds, level):
        unpack(plan, plan.y_low, z_low, lambda y: 2, turns, state, kinds, level)
        unpack(plan, plan.y_high, z_high, lambda y: 3, turns, state, kinds, level)

    take("EHC", 0)
    sweeps = Sweeps(plan, efield, hfield, coef, plan.ring)
    for step in range(1, STEPS + 1):
        after = [lambda: take("H", 1), lambda: take("E", 1)] if step == 1 else []
        sweeps.both(step, range(step - 1, nx - step), range(step, nx - step), *after)


def edges_kernel(plan, groups, *refs):
    nx, ny = plan.nx, plan.ny
    count = 2 * STEPS + 3
    x_low, x_high, c_low, c_high, z_low, z_high, turns, spec_f, spec_a = refs[count : count + 9]
    arrays = refs[count + 9 : 2 * count + 9]
    out_f, out_a, parts = refs[2 * count + 9 :]
    efield, hfield, coef = arrays[: STEPS + 1], arrays[STEPS + 1 : 2 * STEPS + 2], arrays[-1]
    state = State(efield, hfield, coef)

    def take(kinds, level, layers=()):
        unpack(plan, plan.x_low, x_low, lambda y: 0, turns, state, kinds, level)
        unpack(plan, plan.x_high, x_high, lambda y: 1, turns, state, kinds, level)
        unpack(plan, plan.corner_low, c_low, lambda y: 4 + (y >= 0), turns, state, kinds, level)
        unpack(plan, plan.corner_high, c_high, lambda y: 6 + (y >= 0), turns, state, kinds, level)
        unpack(plan, plan.y_low, z_low, lambda y: 2, turns, state, kinds, level, layers)
        unpack(plan, plan.y_high, z_high, lambda y: 3, turns, state, kinds, level, layers)

    take("EHC", 0)
    sweeps = Sweeps(plan, efield, hfield, coef, plan.ring)
    for step in range(1, STEPS + 1):
        low, high = step - STEPS, nx - step
        h_layers = [*range(low - 1, step - 1), *range(high, nx + STEPS - step)]
        e_layers = [*range(low, step), *range(high, nx + STEPS - step)]
        after = []
        if step == 1:
            after = [functools.partial(take, "H", 1, h_layers), functools.partial(take, "E", 1, e_layers)]
        sweeps.both(step, h_layers, e_layers, *after)

    share = parts.shape[2]
    shift = lax.rem(groups - lax.axis_index("angle"), groups) * share
    weight = turns[pl.ds(2 * SUB, SUB), :]
    tiles = ny // SUB

    @pl.loop(0, nx * tiles)
    def _(i):
        x, tile = i // tiles, lax.rem(i, tiles)
        total = jnp.zeros(weight.shape, jnp.float32)
        for comp in range(3):
            ends = []
            for run, (spec, out) in enumerate(((spec_f, out_f), (spec_a, out_a))):
                at = [pl.ds(pl.multiple_of(((part * 3 + comp) * nx + x) * ny + tile * SUB, SUB), SUB) for part in (0, 1)]
                real, imag = spec[at[0], :], spec[at[1], :]
                for step in range(1, STEPS + 1):
                    theta = omega_step * step
                    ends_e = [
                        efield[step][pl.ds(pl.multiple_of(plan.row(x, 0, run, part, comp) + tile * SUB, SUB), SUB), :]
                        for part in (0, 1)
                    ]
                    more = turned(*ends_e, math.cos(theta), math.sin(theta))
                    real, imag = real + more[0], imag + more[1]
                out[at[0], :], out[at[1], :] = real, imag
                ends.append((real, imag))
            total = total + (ends[0][0] * ends[1][0] - ends[0][1] * ends[1][1])
        total = pltpu.roll(total * weight, shift, 1)
        for k in range(groups):
            parts[k, pl.ds(pl.multiple_of(i * SUB, SUB), SUB), :] = total[:, k * share : (k + 1) * share]


def write_kernel(tr_f, tr_a, out_f, out_a, sems):
    copies = []
    for source, target in ((tr_f, out_f), (tr_a, out_a)):
        for i in range(source.shape[0]):
            copies.append(pltpu.make_async_copy(source.at[i], target.at[i], sems.at[len(copies)]))
    for copy in copies:
        copy.start()
    for copy in copies:
        copy.wait()


def ring_pairs(axis, offset):
    size = lax.axis_size(axis)
    return [(i, (i + offset) % size) for i in range(size)]


def shards(
    forward_fields,
    adjoint_fields,
    forward_spectrum,
    adjoint_spectrum,
    permittivity,
    phase_table,
    angle_index,
    design_tiles,
):
    nx, ny, depth = permittivity.shape
    plan = Plan(nx, ny)
    groups = lax.axis_size("angle")
    wide, ring = plan.wide, plan.ring

    def array(*shape):
        return jax.ShapeDtypeStruct(shape, jnp.float32)

    def lines(count):
        return array(count, depth)

    def params(mib):
        return pltpu.CompilerParams(vmem_limit_bytes=mib * 2**20)

    def cost(size):
        return pl.CostEstimate(flops=size, bytes_accessed=size, transcendentals=0)

    with jax.named_scope("pack_y"):
        *first, coef, z_up, z_down = pl.pallas_call(
            functools.partial(pack_y_kernel, plan),
            out_shape=(
                *[array(12, wide, ring, depth)] * 4,
                array(wide, ring, depth),
                lines(plan.y_low.lines),
                lines(plan.y_high.lines),
            ),
            in_specs=[HBM] * 3,
            out_specs=[VMEM] * 7,
            scratch_shapes=[pltpu.SemaphoreType.DMA((25,))],
            compiler_params=params(8),
        )(*(pltpu.with_memory_space_constraint(array, pltpu.HBM) for array in (forward_fields[0], adjoint_fields[0], permittivity)))
    e0, h0, e1, h1, coef = (state.reshape((-1, depth)) for state in (*first, coef))
    with jax.named_scope("send_y"):
        z_low = lax.ppermute(z_up, "gy", ring_pairs("gy", 1))
        z_high = lax.ppermute(z_down, "gy", ring_pairs("gy", -1))
    with jax.named_scope("pack_x"):
        x_up, x_down = pl.pallas_call(
            functools.partial(pack_x_kernel, plan),
            out_shape=(lines(plan.x_low.lines), lines(plan.x_high.lines)),
            in_specs=[VMEM] * 5,
            out_specs=[VMEM] * 2,
            compiler_params=params(8),
            cost_estimate=cost(40 * 2**20),
        )(e0, h0, e1, h1, coef)
    with jax.named_scope("send_x"):
        x_low = lax.ppermute(x_up, "gx", ring_pairs("gx", 1))
        x_high = lax.ppermute(x_down, "gx", ring_pairs("gx", -1))
    with jax.named_scope("turns"):
        turns = pl.pallas_call(
            functools.partial(turns_kernel, groups),
            out_shape=lines(3 * SUB),
            in_specs=[SMEM] * 3,
            out_specs=VMEM,
            compiler_params=params(4),
        )(phase_table, angle_index, design_tiles)
    with jax.named_scope("relay_corners"):
        c_up, c_down = pl.pallas_call(
            functools.partial(corner_kernel, plan),
            out_shape=(lines(plan.corner_low.lines), lines(plan.corner_high.lines)),
            in_specs=[VMEM] * 2,
            out_specs=[VMEM] * 2,
            compiler_params=params(4),
        )(z_low, z_high)
        c_low = lax.ppermute(c_up, "gx", ring_pairs("gx", 1))
        c_high = lax.ppermute(c_down, "gx", ring_pairs("gx", -1))
    level = lines(12 * wide * ring)
    count = 2 * STEPS + 3
    levels = [level] * (count - 1) + [lines(wide * ring)]
    with jax.named_scope("middle"):
        state = pl.pallas_call(
            functools.partial(middle_kernel, plan),
            out_shape=levels,
            in_specs=[VMEM] * 8,
            out_specs=[VMEM] * count,
            input_output_aliases={0: 0, 1: STEPS + 1, 2: 1, 3: STEPS + 2, 4: count - 1},
            compiler_params=params(8),
            cost_estimate=cost(2**32),
        )(e0, h0, e1, h1, coef, z_low, z_high, turns)
    with jax.named_scope("edges"):
        spectra = [spectrum.reshape((-1, depth)) for spectrum in (forward_spectrum, adjoint_spectrum)]
        *_, tr_f, tr_a, parts = pl.pallas_call(
            functools.partial(edges_kernel, plan, groups),
            out_shape=[*levels, lines(6 * nx * ny), lines(6 * nx * ny), array(groups, nx * ny, depth // groups)],
            in_specs=[VMEM] * (count + 9),
            out_specs=[VMEM] * (count + 3),
            input_output_aliases={i: i for i in range(count)},
            compiler_params=params(8),
        )(*state, x_low, x_high, c_low, c_high, z_low, z_high, turns, *spectra)
    with jax.named_scope("sum_angles"):
        gradient = parts[0]
        for k in range(1, groups):
            gradient = gradient + lax.ppermute(parts[k], "angle", ring_pairs("angle", k))
    with jax.named_scope("write"):
        out_f, out_a = pl.pallas_call(
            write_kernel,
            out_shape=[array(6, nx, ny, depth)] * 2,
            in_specs=[VMEM] * 2,
            out_specs=[HBM] * 2,
            scratch_shapes=[pltpu.SemaphoreType.DMA((12,))],
            compiler_params=params(4),
        )(tr_f.reshape((6, nx, ny, depth)), tr_a.reshape((6, nx, ny, depth)))
    return (
        out_f.reshape(forward_spectrum.shape),
        out_a.reshape(adjoint_spectrum.shape),
        gradient.reshape((nx, ny, depth // groups)),
    )


def solution(mesh):
    in_specs = (
        P("angle", None, "gx", "gy", None),
        P("angle", None, "gx", "gy", None),
        P("angle", None, "gx", "gy", None),
        P("angle", None, "gx", "gy", None),
        P("gx", "gy", None),
        P(),
        P("angle"),
        P(),
    )
    out_specs = (
        P("angle", None, "gx", "gy", None),
        P("angle", None, "gx", "gy", None),
        P("gx", "gy", "angle"),
    )
    return jax.shard_map(shards, mesh=mesh, in_specs=in_specs, out_specs=out_specs, check_vma=False)
```

time: 33.5 us -> 30.4 us (0.907)
  waiting for transfers between devices: 12.3 us -> 9.67 us
  starting transfers between devices: 9.03 us -> 7.97 us
  Pallas kernels: 9.92 us -> 10.6 us
    ppermute x1, waiting for transfers between devices: 8.14 us -> 5.67 us  [shards(): z_high = lax.ppermute(z_down, 'gy', ring_pairs('gy', -1))]
    ppermute x1, starting transfers between devices: 1.73 us -> 0.73 us  [shards(): x_high = lax.ppermute(x_down, 'gx', ring_pairs('gx', -1))]
    ppermute x1, waiting for transfers between devices: 0.83 us -> 0.11 us  [shards(): c_high = lax.ppermute(c_down, 'gx', ring_pairs('gx', -1))]
    pallas_call x3, Pallas kernels: 1.89 us -> 2.48 us  [the longest x1 2.3 us: shards(): pl.pallas_call(functools.partial(pack_y_kernel, plan), out_shape=(*[array...]
    ppermute x1, waiting for transfers between devices: 1.54 us -> 2.08 us  [shards(): c_low = lax.ppermute(c_up, 'gx', ring_pairs('gx', 1))]
  transfers between devices with their start and end apart: 7 -> 7, of which waited for: 4 -> 4; matrix products, arithmetic and copies ran while one was open for 0% -> 0% of each run, Pallas kernels for 10% -> 12%
where the time goes in v4:
time: 30.4 us; the launch traced here: 30.2 us
  Pallas kernels  10.6 us (35%)
  waiting for transfers between devices  9.67 us (32%)
  starting transfers between devices  7.97 us (26%)
  between operations  1.35 us (4%)
  other arithmetic  0.64 us (2%)
    ppermute x1, waiting for transfers between devices, shards(): z_high = lax.ppermute(z_down, 'gy', ring_pairs('gy', -1))  5.67 us
    pallas_call x1, Pallas kernels, shards(): pl.pallas_call(functools.partial(edges_kernel, plan, groups), out_shape=[...  4.81 us
    ppermute x1, starting transfers between devices, shards(): z_low = lax.ppermute(z_up, 'gy', ring_pairs('gy', 1))  3.08 us
    pallas_call x1, Pallas kernels, shards(): pl.pallas_call(functools.partial(pack_y_kernel, plan), out_shape=(*[array...  2.3 us
    ppermute x1, starting transfers between devices, shards(): z_high = lax.ppermute(z_down, 'gy', ring_pairs('gy', -1))  2.09 us
    ppermute x1, waiting for transfers between devices, shards(): c_low = lax.ppermute(c_up, 'gx', ring_pairs('gx', 1))  2.08 us
    ppermute x1, waiting for transfers between devices, shards(): lax.ppermute(parts[k], 'angle', ring_pairs('angle', k))  1.8 us
    pallas_call x1, Pallas kernels, shards(): pl.pallas_call(functools.partial(middle_kernel, plan), out_shape=levels,...  1.74 us
  transfers between devices with their start and end apart: 7, of which 4 were waited for; matrix products, arithmetic and copies ran while one was open for 0% of the time, Pallas kernels for 12%

profile of v4, /device:TPU:0, one launch (start us, length us, event | category | flops | bytes accessed | tf_op | source)
XLA Modules:
  0.0 30.2 jit_solution(6029434872931873974)
XLA Ops:
  0.6 2.3 %pack_y.1 = (f32[12,14,24,128]{3,2,1,0:T(8,128)S(1)}, f32[12,14,24,128]{3,2,1,0:T(8,128)S(1)}, f32[12,14,24,128]{3,2,1,0:T(8,128)S(1)}, f32[12,14,24,128]{3,2,1,...) custom-call(f32[12,8,16,128]{3,2,1,0:T(8,128)} %bitcast.32, ...), custom_call_target="tpu_custom_call" | custom-call | tf_op jit(solution)/shard_map/pack_y/pallas_call | solution.py:391
  2.9 3.1 %collective-permute-start = (f32[400,128]{1,0:T(8,128)S(1)}, f32[400,128]{1,0:T(8,128)S(1)}, u32[]{:S(2)}, u32[]{:S(2)}) collective-permute-start(f32[400,128]{1,0:T(8,128)S(1)} %get-tuple-element.33), channel_id=1, source_target_pairs={{0,1},{1,2},{2,3},{3,0},{4,5},{5,6},{6,7},{7,4},{8,9},{9,10},{10,1... | collective-permute-start | bytes 614408 | tf_op jit(solution)/shard_map/send_y/ppermute | solution.py:406
  6.0 2.1 %collective-permute-start.1 = (f32[304,128]{1,0:T(8,128)S(1)}, f32[304,128]{1,0:T(8,128)S(1)}, u32[]{:S(2)}, u32[]{:S(2)}) collective-permute-start(f32[304,128]{1,0:T(8,128)S(1)} %get-tuple-element.34), channel_id=1, source_target_pairs={{0,3},{1,0},{2,1},{3,2},{4,7},{5,4},{6,5},{7,6},{8,11},{9,8},{10,9... | collective-permute-start | bytes 466952 | tf_op jit(solution)/shard_map/send_y/ppermute | solution.py:407
  8.1 0.0 copy-start.2
  8.1 0.0 copy-start.3
  8.1 0.1 pack_x.1
  8.2 0.7 %collective-permute-start.3 = (f32[568,128]{1,0:T(8,128)S(1)}, f32[568,128]{1,0:T(8,128)S(1)}, u32[]{:S(2)}, u32[]{:S(2)}) collective-permute-start(f32[568,128]{1,0:T(8,128)S(1)} %get-tuple-element.45), channel_id=1, source_target_pairs={{0,12},{4,0},{8,4},{12,8},{1,13},{5,1},{9,5},{13,9},{2,14},{6,2},{... | collective-permute-start | bytes 872456 | tf_op jit(solution)/shard_map/send_x/ppermute | solution.py:419
  8.9 0.0 collective-permute-start.2
  9.6 0.0 copy-done.2
  9.6 0.0 copy-done.3
  9.6 0.6 %turns.1.refs_15_ = f32[24,128]{1,0:T(8,128)S(1)} custom-call(f32[2,2]{1,0:T(2,128)S(1)} %copy-done.2, s32[1]{0:T(128)S(6)} %copy.39.index, s32[4]{0:T(128)S(1)} %copy-done.3), custom_call_target="tpu_custom_call" | custom-call | tf_op jit(solution)/shard_map/turns/pallas_call | solution.py:421
  10.2 5.7 %collective-permute-done.1.z_high.refs_14_ = f32[304,128]{1,0:T(8,128)S(1)} collective-permute-done((f32[304,128]{1,0:T(8,128)S(1)}, f32[304,128]{1,0:T(8,128)S(1)}, u32[]{:S(2)}, u32[]{:S(2)}) %collective-permute-start.1) | collective-permute-done | bytes 155680 | tf_op jit(solution)/shard_map/send_y/ppermute | solution.py:407
  15.9 0.0 collective-permute-done.z_low.refs_13_
  15.9 0.1 relay_corners.1
  16.0 0.6 %collective-permute-start.5 = (f32[112,128]{1,0:T(8,128)S(1)}, f32[112,128]{1,0:T(8,128)S(1)}, u32[]{:S(2)}, u32[]{:S(2)}) collective-permute-start(f32[112,128]{1,0:T(8,128)S(1)} %get-tuple-element.47), channel_id=1, source_target_pairs={{0,12},{4,0},{8,4},{12,8},{1,13},{5,1},{9,5},{13,9},{2,14},{6,2},{... | collective-permute-start | bytes 172040 | tf_op jit(solution)/shard_map/relay_corners/ppermute | solution.py:437
  16.6 0.0 copy-start
  16.6 0.0 copy-start.1
  16.6 0.0 collective-permute-start.4
  16.6 1.7 %middle.1 = (f32[4032,128]{1,0:T(8,128)S(1)}, f32[4032,128]{1,0:T(8,128)S(1)}, f32[4032,128]{1,0:T(8,128)S(1)}, f32[4032,128]{1,0:T(8,128)S(1)}, f32[4032,128]{1...) custom-call(f32[4032,128]{1,0:T(8,128)S(1)} %bitcast.19, ...), custom_call_target="tpu_custom_call", output_to_operand_aliasing={{0}: (0, {}), {4}: (1, {}), {1}: (2, {}), {5}: (3, {}), {8}... | custom-call | flops 4294967296 | bytes 4294967296 | tf_op jit(solution)/shard_map/middle/pallas_call | solution.py:442
  18.3 0.1 collective-permute-done.5.refs_12_
  18.4 2.1 %collective-permute-done.4.refs_11_ = f32[144,128]{1,0:T(8,128)S(1)} collective-permute-done((f32[144,128]{1,0:T(8,128)S(1)}, f32[144,128]{1,0:T(8,128)S(1)}, u32[]{:S(2)}, u32[]{:S(2)}) %collective-permute-start.4) | collective-permute-done | bytes 73760 | tf_op jit(solution)/shard_map/relay_corners/ppermute | solution.py:436
  20.5 0.0 collective-permute-done.3.refs_10_
  20.5 0.0 collective-permute-done.2.refs_9_
  20.5 0.0 copy-done
  20.5 0.0 copy-done.1
  20.5 4.8 %edges.1 = (f32[4032,128]{1,0:T(8,128)S(1)}, f32[4032,128]{1,0:T(8,128)S(1)}, f32[4032,128]{1,0:T(8,128)S(1)}, f32[4032,128]{1,0:T(8,128)S(1)}, f32[4032,128]{1,...) custom-call(f32[4032,128]{1,0:T(8,128)S(1)} %get-tuple-element.35.re, ...), custom_call_target="tpu_custom_call", output_to_operand_aliasing={{0}: (0, {}), {1}: (1, {}), {2}: (2, {}), {3}: (3, {}), {4}... | custom-call | tf_op jit(solution)/shard_map/edges/pallas_call | solution.py:453
  25.3 1.5 %collective-permute-start.6 = (f32[128,64]{1,0:T(8,128)S(1)}, f32[128,64]{1,0:T(8,128)S(1)}, u32[]{:S(2)}, u32[]{:S(2)}) collective-permute-start(f32[128,64]{1,0:T(8,128)S(1)} %slice_bitcast_fusion), channel_id=1, source_target_pairs={{0,16},{16,0},{1,17},{17,1},{2,18},{18,2},{3,19},{19,3},{4,20},{20... | collective-permute-start | bytes 98312 | tf_op jit(solution)/shard_map/sum_angles/ppermute | solution.py:464
  26.8 1.0 %write.1 = (f32[6,8,16,128]{3,2,1,0:T(8,128)}, f32[6,8,16,128]{3,2,1,0:T(8,128)}) custom-call(f32[6,8,16,128]{3,2,1,0:T(8,128)S(1)} %bitcast.28, f32[6,8,16,128]{3,2,1,0:T(8,128)S(1)} %bitcast.29), custom_call_target="tpu_custom_call" | custom-call | tf_op jit(solution)/shard_map/write/pallas_call | solution.py:466
  27.8 1.8 %collective-permute-done.6 = f32[128,64]{1,0:T(8,128)S(1)} collective-permute-done((f32[128,64]{1,0:T(8,128)S(1)}, f32[128,64]{1,0:T(8,128)S(1)}, u32[]{:S(2)}, u32[]{:S(2)}) %collective-permute-start.6) | collective-permute-done | bytes 32800 | tf_op jit(solution)/shard_map/sum_angles/ppermute | solution.py:464
  29.6 0.6 %bitcast_add_fusion = f32[128,64]{1,0:T(8,128)} fusion(f32[128,64]{1,0:T(8,128)S(1)} %collective-permute-done.6, f32[2,128,64]{2,1,0:T(8,128)S(1)} %get-tuple-element.52), kind=kLoop, calls=%fused_computation | loop fusion | flops 8192 | bytes 98304 | tf_op jit(solution)/shard_map/sum_angles/add | solution.py:464
  (1 shorter events, 0.0 us)
Async XLA Ops:
  2.9 13.0 %collective-permute-start = (f32[400,128]{1,0:T(8,128)S(1)}, f32[400,128]{1,0:T(8,128)S(1)}, u32[]{:S(2)}, u32[]{:S(2)}) collective-permute-start(f32[400,128]{1,0:T(8,128)S(1)} %get-tuple-element.33), channel_id=1, source_target_pairs={{0,1},{1,2},{2,3},{3,0},{4,5},{5,6},{6,7},{7,4},{8,9},{9,10},{10,1... | collective-permute-start | bytes 614408 | tf_op jit(solution)/shard_map/send_y/ppermute | solution.py:406
  6.0 9.9 %collective-permute-start.1 = (f32[304,128]{1,0:T(8,128)S(1)}, f32[304,128]{1,0:T(8,128)S(1)}, u32[]{:S(2)}, u32[]{:S(2)}) collective-permute-start(f32[304,128]{1,0:T(8,128)S(1)} %get-tuple-element.34), channel_id=1, source_target_pairs={{0,3},{1,0},{2,1},{3,2},{4,7},{5,4},{6,5},{7,6},{8,11},{9,8},{10,9... | collective-permute-start | bytes 466952 | tf_op jit(solution)/shard_map/send_y/ppermute | solution.py:407
  8.1 1.5 %copy-start.2 = (f32[2,2]{1,0:T(2,128)S(1)}, f32[2,2]{1,0:T(2,128)}, u32[]{:S(2)}) copy-start(f32[2,2]{1,0:T(2,128)} %table.1) | copy-start | bytes 52
  8.1 1.5 %copy-start.3 = (s32[4]{0:T(128)S(1)}, s32[4]{0:T(128)}, u32[]{:S(2)}) copy-start(s32[4]{0:T(128)} %tiles.1) | copy-start | bytes 52
  8.2 12.3 %collective-permute-start.3 = (f32[568,128]{1,0:T(8,128)S(1)}, f32[568,128]{1,0:T(8,128)S(1)}, u32[]{:S(2)}, u32[]{:S(2)}) collective-permute-start(f32[568,128]{1,0:T(8,128)S(1)} %get-tuple-element.45), channel_id=1, source_target_pairs={{0,12},{4,0},{8,4},{12,8},{1,13},{5,1},{9,5},{13,9},{2,14},{6,2},{... | collective-permute-start | bytes 872456 | tf_op jit(solution)/shard_map/send_x/ppermute | solution.py:419
  8.9 11.6 %collective-permute-start.2 = (f32[760,128]{1,0:T(8,128)S(1)}, f32[760,128]{1,0:T(8,128)S(1)}, u32[]{:S(2)}, u32[]{:S(2)}) collective-permute-start(f32[760,128]{1,0:T(8,128)S(1)} %get-tuple-element.44), channel_id=1, source_target_pairs={{0,4},{4,8},{8,12},{12,0},{1,5},{5,9},{9,13},{13,1},{2,6},{6,10},{... | collective-permute-start | bytes 1167368 | tf_op jit(solution)/shard_map/send_x/ppermute | solution.py:418
  16.0 2.4 %collective-permute-start.5 = (f32[112,128]{1,0:T(8,128)S(1)}, f32[112,128]{1,0:T(8,128)S(1)}, u32[]{:S(2)}, u32[]{:S(2)}) collective-permute-start(f32[112,128]{1,0:T(8,128)S(1)} %get-tuple-element.47), channel_id=1, source_target_pairs={{0,12},{4,0},{8,4},{12,8},{1,13},{5,1},{9,5},{13,9},{2,14},{6,2},{... | collective-permute-start | bytes 172040 | tf_op jit(solution)/shard_map/relay_corners/ppermute | solution.py:437
  16.6 4.0 %copy-start = (f32[1,6,8,16,128]{4,3,2,1,0:T(8,128)S(1)}, f32[1,6,8,16,128]{4,3,2,1,0:T(8,128)}, u32[]{:S(2)}) copy-start(f32[1,6,8,16,128]{4,3,2,1,0:T(8,128)} %param.10) | copy-start | bytes 1179652
  16.6 4.0 %copy-start.1 = (f32[1,6,8,16,128]{4,3,2,1,0:T(8,128)S(1)}, f32[1,6,8,16,128]{4,3,2,1,0:T(8,128)}, u32[]{:S(2)}) copy-start(f32[1,6,8,16,128]{4,3,2,1,0:T(8,128)} %param.11) | copy-start | bytes 1179652
  16.6 3.9 %collective-permute-start.4 = (f32[144,128]{1,0:T(8,128)S(1)}, f32[144,128]{1,0:T(8,128)S(1)}, u32[]{:S(2)}, u32[]{:S(2)}) collective-permute-start(f32[144,128]{1,0:T(8,128)S(1)} %get-tuple-element.46), channel_id=1, source_target_pairs={{0,4},{4,8},{8,12},{12,0},{1,5},{5,9},{9,13},{13,1},{2,6},{6,10},{... | collective-permute-start | bytes 221192 | tf_op jit(solution)/shard_map/relay_corners/ppermute | solution.py:436
  25.3 4.3 %collective-permute-start.6 = (f32[128,64]{1,0:T(8,128)S(1)}, f32[128,64]{1,0:T(8,128)S(1)}, u32[]{:S(2)}, u32[]{:S(2)}) collective-permute-start(f32[128,64]{1,0:T(8,128)S(1)} %slice_bitcast_fusion), channel_id=1, source_target_pairs={{0,16},{16,0},{1,17},{17,1},{2,18},{18,2},{3,19},{19,3},{4,20},{20... | collective-permute-start | bytes 98312 | tf_op jit(solution)/shard_map/sum_angles/ppermute | solution.py:464

commit v5 on v4

--- a/solution.py
+++ b/solution.py
@@ -128,22 +128,24 @@
 def pack_y_kernel(plan, fwd, adj, eps, e0, h0, e1, h1, coef, z_up, z_down, sems):
     nx, ny = plan.nx, plan.ny
     own = (pl.ds(STEPS, nx), pl.ds(0, ny), slice(None))
-    copies = []
+    copies = [pltpu.make_async_copy(eps, coef.at[own], sems.at[0])]
     for run, ref in enumerate((fwd, adj)):
         for kind, array in enumerate((e0, h0)):
             for i in range(6):
                 copies.append(
                     pltpu.make_async_copy(ref.at[kind * 6 + i], array.at[(run * 6 + i, *own)], sems.at[len(copies)])
                 )
-    copies.append(pltpu.make_async_copy(eps, coef.at[own], sems.at[len(copies)]))
     for copy in copies:
         copy.start()
-    for copy in copies:
-        copy.wait()
+    copies[0].wait()
     for x in range(nx):
         coef[STEPS + x, pl.ds(0, ny), :] = (0.5 * courant) / coef[STEPS + x, pl.ds(0, ny), :]
     e0, h0, e1, h1, coef = (array.reshape((-1, array.shape[-1])) for array in (e0, h0, e1, h1, coef))
-    Sweeps(plan, [e0, e1], [h0, h1], coef, ny).both(1, range(nx), range(nx - 1))
+    sweeps = Sweeps(plan, [e0, e1], [h0, h1], coef, ny)
+    for run in (0, 1):
+        for copy in copies[1 + 12 * run : 13 + 12 * run]:
+            copy.wait()
+        sweeps.both(1, range(nx), range(nx - 1), runs=(run,))
     state = State([e0, e1], [h0, h1], coef)
     pack(plan, plan.y_low, state, 0, ny, z_up)
     pack(plan, plan.y_high, state, 0, -ny, z_down)
@@ -216,19 +218,17 @@
 class Sweeps:
     def __init__(self, plan, efield, hfield, coef, height):
         self.plan, self.efield, self.hfield, self.coef, self.height = plan, efield, hfield, coef, height
-        lane = lax.broadcasted_iota(jnp.int32, (height, coef.shape[1]), 1)
-        self.first, self.last = lane == 0, lane == coef.shape[1] - 1
-
-    def rows(self, group, comp, x):
-        plan = self.plan
-        start = (group * 3 + comp) * plan.wide * plan.ring + (x + STEPS) * plan.ring
-        return pl.ds(start if isinstance(start, int) else pl.multiple_of(start, SUB), self.height)
+
+    def rows(self, run, part, comp, x, height=None):
+        return pl.ds(self.plan.row(x, 0, run, part, comp), height or self.height)
 
     def next_z(self, value):
-        return jnp.where(self.last, 0.0, pltpu.roll(value, value.shape[1] - 1, 1))
+        lane = lax.broadcasted_iota(jnp.int32, value.shape, 1)
+        return jnp.where(lane == value.shape[1] - 1, 0.0, pltpu.roll(value, value.shape[1] - 1, 1))
 
     def prev_z(self, value):
-        return jnp.where(self.first, 0.0, pltpu.roll(value, 1, 1))
+        lane = lax.broadcasted_iota(jnp.int32, value.shape, 1)
+        return jnp.where(lane == 0, 0.0, pltpu.roll(value, 1, 1))
 
     def next_y(self, value):
         return pltpu.roll(value, self.height - 1, 0)
@@ -236,36 +236,42 @@
     def prev_y(self, value):
         return pltpu.roll(value, 1, 0)
 
-    def update_h(self, step, group, x):
+    def update_h(self, step, run, part, x):
         efield, old, new = self.efield[step - 1], self.hfield[step - 1], self.hfield[step]
-        ex, ey, ez = (efield[self.rows(group, comp, x), :] for comp in range(3))
-        ey_x, ez_x = (efield[self.rows(group, comp, x + 1), :] for comp in (1, 2))
-        hx, hy, hz = (old[self.rows(group, comp, x), :] for comp in range(3))
+        ex, ey, ez = (efield[self.rows(run, part, comp, x), :] for comp in range(3))
+        ey_x, ez_x = (efield[self.rows(run, part, comp, x + 1), :] for comp in (1, 2))
+        hx, hy, hz = (old[self.rows(run, part, comp, x), :] for comp in range(3))
         if step == 1:
             hx, hy, hz = hx + hx, hy + hy, hz + hz
-        new[self.rows(group, 0, x), :] = hx - ((self.next_y(ez) - ez) - (self.next_z(ey) - ey))
-        new[self.rows(group, 1, x), :] = hy - ((self.next_z(ex) - ex) - (ez_x - ez))
-        new[self.rows(group, 2, x), :] = hz - ((ey_x - ey) - (self.next_y(ex) - ex))
-
-    def update_e(self, step, group, x):
+        new[self.rows(run, part, 0, x), :] = hx - ((self.next_y(ez) - ez) - (self.next_z(ey) - ey))
+        new[self.rows(run, part, 2, x), :] = hz - ((ey_x - ey) - (self.next_y(ex) - ex))
+        height = self.last_height(step)
+        ex, ez, ez_x, hy = (value[:height] for value in (ex, ez, ez_x, hy))
+        new[self.rows(run, part, 1, x, height), :] = hy - ((self.next_z(ex) - ex) - (ez_x - ez))
+
+    def update_e(self, step, run, part, x):
         old, new, hfield = self.efield[step - 1], self.efield[step], self.hfield[step]
-        ex, ey, ez = (old[self.rows(group, comp, x), :] for comp in range(3))
-        hx, hy, hz = (hfield[self.rows(group, comp, x), :] for comp in range(3))
-        hy_x, hz_x = (hfield[self.rows(group, comp, x - 1), :] for comp in (1, 2))
-        scale = self.coef[self.rows(0, 0, x), :]
-        new[self.rows(group, 0, x), :] = ex + scale * ((hz - self.prev_y(hz)) - (hy - self.prev_z(hy)))
-        new[self.rows(group, 1, x), :] = ey + scale * ((hx - self.prev_z(hx)) - (hz - hz_x))
-        new[self.rows(group, 2, x), :] = ez + scale * ((hy - hy_x) - (hx - self.prev_y(hx)))
-
-    def both(self, step, h_layers, e_layers, after_h=None, after_e=None):
+        height = self.last_height(step)
+        ex, ey, ez = (old[self.rows(run, part, comp, x, height), :] for comp in range(3))
+        hx, hz = (hfield[self.rows(run, part, comp, x), :] for comp in (0, 2))
+        hx_y, hz_y = self.prev_y(hx)[:height], self.prev_y(hz)[:height]
+        hx, hz = hx[:height], hz[:height]
+        hy = hfield[self.rows(run, part, 1, x, height), :]
+        hy_x, hz_x = (hfield[self.rows(run, part, comp, x - 1, height), :] for comp in (1, 2))
+        scale = self.coef[self.rows(0, 0, 0, x, height), :]
+        new[self.rows(run, part, 0, x, height), :] = ex + scale * ((hz - hz_y) - (hy - self.prev_z(hy)))
+        new[self.rows(run, part, 1, x, height), :] = ey + scale * ((hx - self.prev_z(hx)) - (hz - hz_x))
+        new[self.rows(run, part, 2, x, height), :] = ez + scale * ((hy - hy_x) - (hx - hx_y))
+
+    def last_height(self, step):
+        return self.plan.ny if step == STEPS else self.height
+
+    def both(self, step, h_layers, e_layers, after_h=None, after_e=None, runs=(0, 1)):
         for update, layers, after in ((self.update_h, h_layers, after_h), (self.update_e, e_layers, after_e)):
-
-            @pl.loop(0, 2)
-            def _(run):
-                for part in (0, 1):
-                    for x in layers:
-                        update(step, run * 2 + part, x)
-
+            for x in layers:
+                for run in runs:
+                    for part in (0, 1):
+                        update(step, run, part, x)
             if after is not None:
                 after()
 
@@ -319,19 +325,18 @@
     weight = turns[pl.ds(2 * SUB, SUB), :]
     tiles = ny // SUB
 
-    @pl.loop(0, nx * tiles)
-    def _(i):
-        x, tile = i // tiles, lax.rem(i, tiles)
+    for i in range(nx * tiles):
+        x, tile = i // tiles, i % tiles
         total = jnp.zeros(weight.shape, jnp.float32)
         for comp in range(3):
             ends = []
             for run, (spec, out) in enumerate(((spec_f, out_f), (spec_a, out_a))):
-                at = [pl.ds(pl.multiple_of(((part * 3 + comp) * nx + x) * ny + tile * SUB, SUB), SUB) for part in (0, 1)]
+                at = [pl.ds(((part * 3 + comp) * nx + x) * ny + tile * SUB, SUB) for part in (0, 1)]
                 real, imag = spec[at[0], :], spec[at[1], :]
                 for step in range(1, STEPS + 1):
                     theta = omega_step * step
                     ends_e = [
-                        efield[step][pl.ds(pl.multiple_of(plan.row(x, 0, run, part, comp) + tile * SUB, SUB), SUB), :]
+                        efield[step][pl.ds(plan.row(x, tile * SUB, run, part, comp), SUB), :]
                         for part in (0, 1)
                     ]
                     more = turned(*ends_e, math.cos(theta), math.sin(theta))
@@ -341,7 +346,7 @@
             total = total + (ends[0][0] * ends[1][0] - ends[0][1] * ends[1][1])
         total = pltpu.roll(total * weight, shift, 1)
         for k in range(groups):
-            parts[k, pl.ds(pl.multiple_of(i * SUB, SUB), SUB), :] = total[:, k * share : (k + 1) * share]
+            parts[k, pl.ds(i * SUB, SUB), :] = total[:, k * share : (k + 1) * share]
 
 
 def write_kernel(tr_f, tr_a, out_f, out_a, sems):

time: 30.4 us -> 27.7 us (0.911)
  Pallas kernels: 10.6 us -> 7.4 us
  waiting for transfers between devices: 9.67 us -> 10.1 us
    pallas_call x1, Pallas kernels: 4.81 us -> 2.34 us  [shards(): pl.pallas_call(functools.partial(edges_kernel, plan, groups), out_shape=[...]
    ppermute x1, waiting for transfers between devices: 0.11 us -> 0.54 us  [shards(): c_high = lax.ppermute(c_down, 'gx', ring_pairs('gx', -1))]
    pallas_call x1, Pallas kernels: 1.74 us -> 1.31 us  [shards(): pl.pallas_call(functools.partial(middle_kernel, plan), out_shape=levels,...]
  transfers between devices with their start and end apart: 7 -> 7, of which waited for: 4 -> 4; matrix products, arithmetic and copies ran while one was open for 0% -> 0% of each run, Pallas kernels for 12% -> 11%
where the time goes in v5:
time: 27.7 us; the launch traced here: 27.5 us
  waiting for transfers between devices  10.1 us (36%)
  starting transfers between devices  8 us (29%)
  Pallas kernels  7.4 us (27%)
  between operations  1.35 us (5%)
  other arithmetic  0.64 us (2%)
    ppermute x1, waiting for transfers between devices, shards(): z_high = lax.ppermute(z_down, 'gy', ring_pairs('gy', -1))  5.67 us
    ppermute x1, starting transfers between devices, shards(): z_low = lax.ppermute(z_up, 'gy', ring_pairs('gy', 1))  3.08 us
    pallas_call x1, Pallas kernels, shards(): pl.pallas_call(functools.partial(edges_kernel, plan, groups), out_shape=[...  2.34 us
    ppermute x1, starting transfers between devices, shards(): z_high = lax.ppermute(z_down, 'gy', ring_pairs('gy', -1))  2.09 us
    ppermute x1, waiting for transfers between devices, shards(): c_low = lax.ppermute(c_up, 'gx', ring_pairs('gx', 1))  2.08 us
    pallas_call x1, Pallas kernels, shards(): pl.pallas_call(functools.partial(pack_y_kernel, plan), out_shape=(*[array...  2 us
    ppermute x1, waiting for transfers between devices, shards(): lax.ppermute(parts[k], 'angle', ring_pairs('angle', k))  1.8 us
    ppermute x1, starting transfers between devices, shards(): lax.ppermute(parts[k], 'angle', ring_pairs('angle', k))  1.53 us
  transfers between devices with their start and end apart: 7, of which 4 were waited for; matrix products, arithmetic and copies ran while one was open for 0% of the time, Pallas kernels for 11%

profile of v5, /device:TPU:0, one launch (start us, length us, event | category | flops | bytes accessed | tf_op | source)
XLA Modules:
  0.0 27.5 jit_solution(8869384108488815711)
XLA Ops:
  0.6 2.0 %pack_y.1 = (f32[12,14,24,128]{3,2,1,0:T(8,128)S(1)}, f32[12,14,24,128]{3,2,1,0:T(8,128)S(1)}, f32[12,14,24,128]{3,2,1,0:T(8,128)S(1)}, f32[12,14,24,128]{3,2,1,...) custom-call(f32[12,8,16,128]{3,2,1,0:T(8,128)} %bitcast.32, ...), custom_call_target="tpu_custom_call" | custom-call | tf_op jit(solution)/shard_map/pack_y/pallas_call | solution.py:396
  2.6 3.1 %collective-permute-start = (f32[400,128]{1,0:T(8,128)S(1)}, f32[400,128]{1,0:T(8,128)S(1)}, u32[]{:S(2)}, u32[]{:S(2)}) collective-permute-start(f32[400,128]{1,0:T(8,128)S(1)} %get-tuple-element.33), channel_id=1, source_target_pairs={{0,1},{1,2},{2,3},{3,0},{4,5},{5,6},{6,7},{7,4},{8,9},{9,10},{10,1... | collective-permute-start | bytes 614408 | tf_op jit(solution)/shard_map/send_y/ppermute | solution.py:411
  5.7 2.1 %collective-permute-start.1 = (f32[304,128]{1,0:T(8,128)S(1)}, f32[304,128]{1,0:T(8,128)S(1)}, u32[]{:S(2)}, u32[]{:S(2)}) collective-permute-start(f32[304,128]{1,0:T(8,128)S(1)} %get-tuple-element.34), channel_id=1, source_target_pairs={{0,3},{1,0},{2,1},{3,2},{4,7},{5,4},{6,5},{7,6},{8,11},{9,8},{10,9... | collective-permute-start | bytes 466952 | tf_op jit(solution)/shard_map/send_y/ppermute | solution.py:412
  7.8 0.0 copy-start.2
  7.8 0.0 copy-start.3
  7.8 0.1 pack_x.1
  7.9 0.7 %collective-permute-start.3 = (f32[568,128]{1,0:T(8,128)S(1)}, f32[568,128]{1,0:T(8,128)S(1)}, u32[]{:S(2)}, u32[]{:S(2)}) collective-permute-start(f32[568,128]{1,0:T(8,128)S(1)} %get-tuple-element.45), channel_id=1, source_target_pairs={{0,12},{4,0},{8,4},{12,8},{1,13},{5,1},{9,5},{13,9},{2,14},{6,2},{... | collective-permute-start | bytes 872456 | tf_op jit(solution)/shard_map/send_x/ppermute | solution.py:424
  8.6 0.0 collective-permute-start.2
  9.3 0.0 copy-done.2
  9.3 0.0 copy-done.3
  9.3 0.6 %turns.1.refs_15_ = f32[24,128]{1,0:T(8,128)S(1)} custom-call(f32[2,2]{1,0:T(2,128)S(1)} %copy-done.2, s32[1]{0:T(128)S(6)} %copy.39.index, s32[4]{0:T(128)S(1)} %copy-done.3), custom_call_target="tpu_custom_call" | custom-call | tf_op jit(solution)/shard_map/turns/pallas_call | solution.py:426
  9.9 5.7 %collective-permute-done.1.z_high.refs_14_ = f32[304,128]{1,0:T(8,128)S(1)} collective-permute-done((f32[304,128]{1,0:T(8,128)S(1)}, f32[304,128]{1,0:T(8,128)S(1)}, u32[]{:S(2)}, u32[]{:S(2)}) %collective-permute-start.1) | collective-permute-done | bytes 155680 | tf_op jit(solution)/shard_map/send_y/ppermute | solution.py:412
  15.6 0.0 collective-permute-done.z_low.refs_13_
  15.6 0.1 relay_corners.1
  15.7 0.6 %collective-permute-start.5 = (f32[112,128]{1,0:T(8,128)S(1)}, f32[112,128]{1,0:T(8,128)S(1)}, u32[]{:S(2)}, u32[]{:S(2)}) collective-permute-start(f32[112,128]{1,0:T(8,128)S(1)} %get-tuple-element.47), channel_id=1, source_target_pairs={{0,12},{4,0},{8,4},{12,8},{1,13},{5,1},{9,5},{13,9},{2,14},{6,2},{... | collective-permute-start | bytes 172040 | tf_op jit(solution)/shard_map/relay_corners/ppermute | solution.py:442
  16.3 0.0 copy-start
  16.3 0.0 copy-start.1
  16.3 0.0 collective-permute-start.4
  16.3 1.3 %middle.1 = (f32[4032,128]{1,0:T(8,128)S(1)}, f32[4032,128]{1,0:T(8,128)S(1)}, f32[4032,128]{1,0:T(8,128)S(1)}, f32[4032,128]{1,0:T(8,128)S(1)}, f32[4032,128]{1...) custom-call(f32[4032,128]{1,0:T(8,128)S(1)} %bitcast.19, ...), custom_call_target="tpu_custom_call", output_to_operand_aliasing={{0}: (0, {}), {4}: (1, {}), {1}: (2, {}), {5}: (3, {}), {8}... | custom-call | flops 4294967296 | bytes 4294967296 | tf_op jit(solution)/shard_map/middle/pallas_call | solution.py:447
  17.6 0.5 %collective-permute-done.5.refs_12_ = f32[112,128]{1,0:T(8,128)S(1)} collective-permute-done((f32[112,128]{1,0:T(8,128)S(1)}, f32[112,128]{1,0:T(8,128)S(1)}, u32[]{:S(2)}, u32[]{:S(2)}) %collective-permute-start.5) | collective-permute-done | bytes 57376 | tf_op jit(solution)/shard_map/relay_corners/ppermute | solution.py:442
  18.1 2.1 %collective-permute-done.4.refs_11_ = f32[144,128]{1,0:T(8,128)S(1)} collective-permute-done((f32[144,128]{1,0:T(8,128)S(1)}, f32[144,128]{1,0:T(8,128)S(1)}, u32[]{:S(2)}, u32[]{:S(2)}) %collective-permute-start.4) | collective-permute-done | bytes 73760 | tf_op jit(solution)/shard_map/relay_corners/ppermute | solution.py:441
  20.2 0.0 collective-permute-done.3.refs_10_
  20.2 0.0 collective-permute-done.2.refs_9_
  20.2 0.0 copy-done
  20.2 0.0 copy-done.1
  20.2 2.3 %edges.1 = (f32[4032,128]{1,0:T(8,128)S(1)}, f32[4032,128]{1,0:T(8,128)S(1)}, f32[4032,128]{1,0:T(8,128)S(1)}, f32[4032,128]{1,0:T(8,128)S(1)}, f32[4032,128]{1,...) custom-call(f32[4032,128]{1,0:T(8,128)S(1)} %get-tuple-element.35.re, ...), custom_call_target="tpu_custom_call", output_to_operand_aliasing={{0}: (0, {}), {1}: (1, {}), {2}: (2, {}), {3}: (3, {}), {4}... | custom-call | tf_op jit(solution)/shard_map/edges/pallas_call | solution.py:458
  22.6 1.5 %collective-permute-start.6 = (f32[128,64]{1,0:T(8,128)S(1)}, f32[128,64]{1,0:T(8,128)S(1)}, u32[]{:S(2)}, u32[]{:S(2)}) collective-permute-start(f32[128,64]{1,0:T(8,128)S(1)} %slice_bitcast_fusion), channel_id=1, source_target_pairs={{0,16},{16,0},{1,17},{17,1},{2,18},{18,2},{3,19},{19,3},{4,20},{20... | collective-permute-start | bytes 98312 | tf_op jit(solution)/shard_map/sum_angles/ppermute | solution.py:469
  24.1 1.0 %write.1 = (f32[6,8,16,128]{3,2,1,0:T(8,128)}, f32[6,8,16,128]{3,2,1,0:T(8,128)}) custom-call(f32[6,8,16,128]{3,2,1,0:T(8,128)S(1)} %bitcast.28, f32[6,8,16,128]{3,2,1,0:T(8,128)S(1)} %bitcast.29), custom_call_target="tpu_custom_call" | custom-call | tf_op jit(solution)/shard_map/write/pallas_call | solution.py:471
  25.1 1.8 %collective-permute-done.6 = f32[128,64]{1,0:T(8,128)S(1)} collective-permute-done((f32[128,64]{1,0:T(8,128)S(1)}, f32[128,64]{1,0:T(8,128)S(1)}, u32[]{:S(2)}, u32[]{:S(2)}) %collective-permute-start.6) | collective-permute-done | bytes 32800 | tf_op jit(solution)/shard_map/sum_angles/ppermute | solution.py:469
  26.9 0.6 %bitcast_add_fusion = f32[128,64]{1,0:T(8,128)} fusion(f32[128,64]{1,0:T(8,128)S(1)} %collective-permute-done.6, f32[2,128,64]{2,1,0:T(8,128)S(1)} %get-tuple-element.52), kind=kLoop, calls=%fused_computation | loop fusion | flops 8192 | bytes 98304 | tf_op jit(solution)/shard_map/sum_angles/add | solution.py:469
  (1 shorter events, 0.0 us)
Async XLA Ops:
  2.6 13.0 %collective-permute-start = (f32[400,128]{1,0:T(8,128)S(1)}, f32[400,128]{1,0:T(8,128)S(1)}, u32[]{:S(2)}, u32[]{:S(2)}) collective-permute-start(f32[400,128]{1,0:T(8,128)S(1)} %get-tuple-element.33), channel_id=1, source_target_pairs={{0,1},{1,2},{2,3},{3,0},{4,5},{5,6},{6,7},{7,4},{8,9},{9,10},{10,1... | collective-permute-start | bytes 614408 | tf_op jit(solution)/shard_map/send_y/ppermute | solution.py:411
  5.7 9.9 %collective-permute-start.1 = (f32[304,128]{1,0:T(8,128)S(1)}, f32[304,128]{1,0:T(8,128)S(1)}, u32[]{:S(2)}, u32[]{:S(2)}) collective-permute-start(f32[304,128]{1,0:T(8,128)S(1)} %get-tuple-element.34), channel_id=1, source_target_pairs={{0,3},{1,0},{2,1},{3,2},{4,7},{5,4},{6,5},{7,6},{8,11},{9,8},{10,9... | collective-permute-start | bytes 466952 | tf_op jit(solution)/shard_map/send_y/ppermute | solution.py:412
  7.8 1.5 %copy-start.2 = (f32[2,2]{1,0:T(2,128)S(1)}, f32[2,2]{1,0:T(2,128)}, u32[]{:S(2)}) copy-start(f32[2,2]{1,0:T(2,128)} %table.1) | copy-start | bytes 52
  7.8 1.5 %copy-start.3 = (s32[4]{0:T(128)S(1)}, s32[4]{0:T(128)}, u32[]{:S(2)}) copy-start(s32[4]{0:T(128)} %tiles.1) | copy-start | bytes 52
  7.9 12.3 %collective-permute-start.3 = (f32[568,128]{1,0:T(8,128)S(1)}, f32[568,128]{1,0:T(8,128)S(1)}, u32[]{:S(2)}, u32[]{:S(2)}) collective-permute-start(f32[568,128]{1,0:T(8,128)S(1)} %get-tuple-element.45), channel_id=1, source_target_pairs={{0,12},{4,0},{8,4},{12,8},{1,13},{5,1},{9,5},{13,9},{2,14},{6,2},{... | collective-permute-start | bytes 872456 | tf_op jit(solution)/shard_map/send_x/ppermute | solution.py:424
  8.6 11.6 %collective-permute-start.2 = (f32[760,128]{1,0:T(8,128)S(1)}, f32[760,128]{1,0:T(8,128)S(1)}, u32[]{:S(2)}, u32[]{:S(2)}) collective-permute-start(f32[760,128]{1,0:T(8,128)S(1)} %get-tuple-element.44), channel_id=1, source_target_pairs={{0,4},{4,8},{8,12},{12,0},{1,5},{5,9},{9,13},{13,1},{2,6},{6,10},{... | collective-permute-start | bytes 1167368 | tf_op jit(solution)/shard_map/send_x/ppermute | solution.py:423
  15.7 2.4 %collective-permute-start.5 = (f32[112,128]{1,0:T(8,128)S(1)}, f32[112,128]{1,0:T(8,128)S(1)}, u32[]{:S(2)}, u32[]{:S(2)}) collective-permute-start(f32[112,128]{1,0:T(8,128)S(1)} %get-tuple-element.47), channel_id=1, source_target_pairs={{0,12},{4,0},{8,4},{12,8},{1,13},{5,1},{9,5},{13,9},{2,14},{6,2},{... | collective-permute-start | bytes 172040 | tf_op jit(solution)/shard_map/relay_corners/ppermute | solution.py:442
  16.3 4.0 %copy-start = (f32[1,6,8,16,128]{4,3,2,1,0:T(8,128)S(1)}, f32[1,6,8,16,128]{4,3,2,1,0:T(8,128)}, u32[]{:S(2)}) copy-start(f32[1,6,8,16,128]{4,3,2,1,0:T(8,128)} %param.10) | copy-start | bytes 1179652
  16.3 4.0 %copy-start.1 = (f32[1,6,8,16,128]{4,3,2,1,0:T(8,128)S(1)}, f32[1,6,8,16,128]{4,3,2,1,0:T(8,128)}, u32[]{:S(2)}) copy-start(f32[1,6,8,16,128]{4,3,2,1,0:T(8,128)} %param.11) | copy-start | bytes 1179652
  16.3 3.9 %collective-permute-start.4 = (f32[144,128]{1,0:T(8,128)S(1)}, f32[144,128]{1,0:T(8,128)S(1)}, u32[]{:S(2)}, u32[]{:S(2)}) collective-permute-start(f32[144,128]{1,0:T(8,128)S(1)} %get-tuple-element.46), channel_id=1, source_target_pairs={{0,4},{4,8},{8,12},{12,0},{1,5},{5,9},{9,13},{13,1},{2,6},{6,10},{... | collective-permute-start | bytes 221192 | tf_op jit(solution)/shard_map/relay_corners/ppermute | solution.py:441
  22.6 4.3 %collective-permute-start.6 = (f32[128,64]{1,0:T(8,128)S(1)}, f32[128,64]{1,0:T(8,128)S(1)}, u32[]{:S(2)}, u32[]{:S(2)}) collective-permute-start(f32[128,64]{1,0:T(8,128)S(1)} %slice_bitcast_fusion), channel_id=1, source_target_pairs={{0,16},{16,0},{1,17},{17,1},{2,18},{18,2},{3,19},{19,3},{4,20},{20... | collective-permute-start | bytes 98312 | tf_op jit(solution)/shard_map/sum_angles/ppermute | solution.py:469

commit v6 on v5

--- a/solution.py
+++ b/solution.py
@@ -97,11 +97,17 @@
         def shifted(found, dx):
             return {(*node[:3], node[3] + dx, node[4]) for node in found}
 
-        self.x_low, self.x_high = Message(sides[-1, 0], 1), Message(sides[1, 0], 1)
         self.y_low, self.y_high = (
             Message(sides[0, side] | shifted(sides[-1, side], nx) | shifted(sides[1, side], -nx), 0) for side in (-1, 1)
         )
-        self.corner_low, self.corner_high = (Message(sides[side, -1] | sides[side, 1], 1) for side in (-1, 1))
+        self.mate_side, self.far_side = (1, -1), (-1, 1)
+        self.x_mate, self.x_far = ([Message(sides[side, 0], 1) for side in order] for order in (self.mate_side, self.far_side))
+        self.x_lines = max(message.lines for message in self.x_mate)
+        self.mate = [Message(sides[side, -1] | sides[side, 1], 1) for side in self.mate_side]
+        self.far_low, self.far_high = ([Message(sides[side, end], 1) for side in self.far_side] for end in (-1, 1))
+        self.mate_lines, self.far_low_lines, self.far_high_lines = (
+            max(message.lines for message in messages) for messages in (self.mate, self.far_low, self.far_high)
+        )
 
     def row(self, x, y, run=0, part=0, comp=0):
         return ((run * 6 + part * 3 + comp) * self.wide + x + STEPS) * self.ring + y % self.ring
@@ -125,7 +131,13 @@
         out[pl.ds(at, count), :] = state(what)[plan.rows(what, x + dx, y + dy, message.axis, count), :]
 
 
-def pack_y_kernel(plan, fwd, adj, eps, e0, h0, e1, h1, coef, z_up, z_down, sems):
+def by_parity(offset, body):
+    parity = lax.rem(lax.axis_index("gx") + offset, 2)
+    for value in (0, 1):
+        pl.when(parity == value)(functools.partial(body, value))
+
+
+def pack_y_kernel(plan, fwd, adj, eps, e0, h0, e1, h1, coef, z_up, sems):
     nx, ny = plan.nx, plan.ny
     own = (pl.ds(STEPS, nx), pl.ds(0, ny), slice(None))
     copies = [pltpu.make_async_copy(eps, coef.at[own], sems.at[0])]
@@ -148,13 +160,29 @@
         sweeps.both(1, range(nx), range(nx - 1), runs=(run,))
     state = State([e0, e1], [h0, h1], coef)
     pack(plan, plan.y_low, state, 0, ny, z_up)
+
+
+def pack_x_kernel(plan, e0, h0, e1, h1, coef, to_far, to_mate):
+    state = State([e0, e1], [h0, h1], coef)
+
+    def faces(receiver):
+        pack(plan, plan.x_far[receiver], state, -plan.nx * plan.far_side[receiver], 0, to_far)
+        pack(plan, plan.x_mate[receiver], state, -plan.nx * plan.mate_side[receiver], 0, to_mate)
+
+    by_parity(1, faces)
+
+
+def pack_rest_kernel(plan, e0, h0, e1, h1, coef, after, z_down, far_up, far_down):
+    nx, ny = plan.nx, plan.ny
+    state = State([e0, e1], [h0, h1], coef)
     pack(plan, plan.y_high, state, 0, -ny, z_down)
 
-
-def pack_x_kernel(plan, e0, h0, e1, h1, coef, x_up, x_down):
-    state = State([e0, e1], [h0, h1], coef)
-    pack(plan, plan.x_low, state, plan.nx, 0, x_up)
-    pack(plan, plan.x_high, state, -plan.nx, 0, x_down)
+    def far(receiver):
+        dx = -nx * plan.far_side[receiver]
+        pack(plan, plan.far_low[receiver], state, dx, ny, far_up)
+        pack(plan, plan.far_high[receiver], state, dx, -ny, far_down)
+
+    by_parity(1, far)
 
 
 def turns_kernel(groups, table, index, tiles, turns):
@@ -181,11 +209,14 @@
     turns[pl.ds(2 * SUB, SUB), :] = jnp.full(sub.shape, weight, jnp.float32)
 
 
-def corner_kernel(plan, z_low, z_high, c_up, c_down):
-    for message, dx, out in ((plan.corner_low, plan.nx, c_up), (plan.corner_high, -plan.nx, c_down)):
-        for (what, x, y), row in message.at.items():
+def relay_kernel(plan, z_low, z_high, after, other_after, out):
+    def mate(receiver):
+        dx = -plan.nx * plan.mate_side[receiver]
+        for (what, x, y), row in plan.mate[receiver].at.items():
             ref, source = (z_low, plan.y_low) if y < 0 else (z_high, plan.y_high)
             out[pl.ds(row, 1), :] = ref[pl.ds(source.at[what, x + dx, y], 1), :]
+
+    by_parity(1, mate)
 
 
 def turned(real, imag, cosine, sine):
@@ -295,17 +326,27 @@
 def edges_kernel(plan, groups, *refs):
     nx, ny = plan.nx, plan.ny
     count = 2 * STEPS + 3
-    x_low, x_high, c_low, c_high, z_low, z_high, turns, spec_f, spec_a = refs[count : count + 9]
-    arrays = refs[count + 9 : 2 * count + 9]
-    out_f, out_a, parts = refs[2 * count + 9 :]
+    x_far, x_mate, far_low, far_high, mate, z_low, z_high, turns, spec_f, spec_a = refs[count : count + 10]
+    arrays = refs[count + 10 : 2 * count + 10]
+    out_f, out_a, parts = refs[2 * count + 10 :]
     efield, hfield, coef = arrays[: STEPS + 1], arrays[STEPS + 1 : 2 * STEPS + 2], arrays[-1]
     state = State(efield, hfield, coef)
 
     def take(kinds, level, layers=()):
-        unpack(plan, plan.x_low, x_low, lambda y: 0, turns, state, kinds, level)
-        unpack(plan, plan.x_high, x_high, lambda y: 1, turns, state, kinds, level)
-        unpack(plan, plan.corner_low, c_low, lambda y: 4 + (y >= 0), turns, state, kinds, level)
-        unpack(plan, plan.corner_high, c_high, lambda y: 6 + (y >= 0), turns, state, kinds, level)
+
+        def sides(receiver):
+            for messages, ref, side in ((plan.x_far, x_far, plan.far_side), (plan.x_mate, x_mate, plan.mate_side)):
+                first = 0 if side[receiver] < 0 else 1
+                unpack(plan, messages[receiver], ref, lambda y: first, turns, state, kinds, level)
+            for messages, ref, side in (
+                (plan.far_low, far_low, plan.far_side),
+                (plan.far_high, far_high, plan.far_side),
+                (plan.mate, mate, plan.mate_side),
+            ):
+                first = 4 if side[receiver] < 0 else 6
+                unpack(plan, messages[receiver], ref, lambda y: first + (y >= 0), turns, state, kinds, level)
+
+        by_parity(0, sides)
         unpack(plan, plan.y_low, z_low, lambda y: 2, turns, state, kinds, level, layers)
         unpack(plan, plan.y_high, z_high, lambda y: 3, turns, state, kinds, level, layers)
 
@@ -365,6 +406,19 @@
     return [(i, (i + offset) % size) for i in range(size)]
 
 
+def mate_pairs():
+    return [(i, i ^ 1) for i in range(lax.axis_size("gx"))]
+
+
+def far_pairs(offset):
+    size_x, size_y = lax.axis_size("gx"), lax.axis_size("gy")
+    return [
+        (x * size_y + y, (x + (1 if x % 2 else -1)) % size_x * size_y + (y + offset) % size_y)
+        for x in range(size_x)
+        for y in range(size_y)
+    ]
+
+
 def shards(
     forward_fields,
     adjoint_fields,
@@ -392,36 +446,44 @@
     def cost(size):
         return pl.CostEstimate(flops=size, bytes_accessed=size, transcendentals=0)
 
+    assert lax.axis_size("gx") % 2 == 0
     with jax.named_scope("pack_y"):
-        *first, coef, z_up, z_down = pl.pallas_call(
+        *first, coef, z_up = pl.pallas_call(
             functools.partial(pack_y_kernel, plan),
-            out_shape=(
-                *[array(12, wide, ring, depth)] * 4,
-                array(wide, ring, depth),
-                lines(plan.y_low.lines),
-                lines(plan.y_high.lines),
-            ),
+            out_shape=(*[array(12, wide, ring, depth)] * 4, array(wide, ring, depth), lines(plan.y_low.lines)),
             in_specs=[HBM] * 3,
-            out_specs=[VMEM] * 7,
+            out_specs=[VMEM] * 6,
             scratch_shapes=[pltpu.SemaphoreType.DMA((25,))],
             compiler_params=params(8),
         )(*(pltpu.with_memory_space_constraint(array, pltpu.HBM) for array in (forward_fields[0], adjoint_fields[0], permittivity)))
-    e0, h0, e1, h1, coef = (state.reshape((-1, depth)) for state in (*first, coef))
-    with jax.named_scope("send_y"):
+    first = [state.reshape((-1, depth)) for state in (*first, coef)]
+    with jax.named_scope("send_y_up"):
         z_low = lax.ppermute(z_up, "gy", ring_pairs("gy", 1))
-        z_high = lax.ppermute(z_down, "gy", ring_pairs("gy", -1))
     with jax.named_scope("pack_x"):
-        x_up, x_down = pl.pallas_call(
+        to_far, to_mate = pl.pallas_call(
             functools.partial(pack_x_kernel, plan),
-            out_shape=(lines(plan.x_low.lines), lines(plan.x_high.lines)),
+            out_shape=[lines(plan.x_lines)] * 2,
             in_specs=[VMEM] * 5,
             out_specs=[VMEM] * 2,
             compiler_params=params(8),
-            cost_estimate=cost(40 * 2**20),
-        )(e0, h0, e1, h1, coef)
+            cost_estimate=cost(2**10),
+        )(*first)
     with jax.named_scope("send_x"):
-        x_low = lax.ppermute(x_up, "gx", ring_pairs("gx", 1))
-        x_high = lax.ppermute(x_down, "gx", ring_pairs("gx", -1))
+        x_far = lax.ppermute(to_far, ("gx", "gy"), far_pairs(0))
+        x_mate = lax.ppermute(to_mate, "gx", mate_pairs())
+    with jax.named_scope("pack_rest"):
+        z_down, far_up, far_down = pl.pallas_call(
+            functools.partial(pack_rest_kernel, plan),
+            out_shape=(lines(plan.y_high.lines), lines(plan.far_low_lines), lines(plan.far_high_lines)),
+            in_specs=[VMEM] * 6,
+            out_specs=[VMEM] * 3,
+            compiler_params=params(8),
+            cost_estimate=cost(2**10),
+        )(*first, x_mate)
+    with jax.named_scope("send_rest"):
+        z_high = lax.ppermute(z_down, "gy", ring_pairs("gy", -1))
+        far_low = lax.ppermute(far_up, ("gx", "gy"), far_pairs(1))
+        far_high = lax.ppermute(far_down, ("gx", "gy"), far_pairs(-1))
     with jax.named_scope("turns"):
         turns = pl.pallas_call(
             functools.partial(turns_kernel, groups),
@@ -431,15 +493,14 @@
             compiler_params=params(4),
         )(phase_table, angle_index, design_tiles)
     with jax.named_scope("relay_corners"):
-        c_up, c_down = pl.pallas_call(
-            functools.partial(corner_kernel, plan),
-            out_shape=(lines(plan.corner_low.lines), lines(plan.corner_high.lines)),
-            in_specs=[VMEM] * 2,
-            out_specs=[VMEM] * 2,
+        relayed = pl.pallas_call(
+            functools.partial(relay_kernel, plan),
+            out_shape=lines(plan.mate_lines),
+            in_specs=[VMEM] * 4,
+            out_specs=VMEM,
             compiler_params=params(4),
-        )(z_low, z_high)
-        c_low = lax.ppermute(c_up, "gx", ring_pairs("gx", 1))
-        c_high = lax.ppermute(c_down, "gx", ring_pairs("gx", -1))
+        )(z_low, z_high, far_low, far_high)
+        mate = lax.ppermute(relayed, "gx", mate_pairs())
     level = lines(12 * wide * ring)
     count = 2 * STEPS + 3
     levels = [level] * (count - 1) + [lines(wide * ring)]
@@ -451,18 +512,18 @@
             out_specs=[VMEM] * count,
             input_output_aliases={0: 0, 1: STEPS + 1, 2: 1, 3: STEPS + 2, 4: count - 1},
             compiler_params=params(8),
-            cost_estimate=cost(2**32),
-        )(e0, h0, e1, h1, coef, z_low, z_high, turns)
+            cost_estimate=cost(2**31),
+        )(*first, z_low, z_high, turns)
     with jax.named_scope("edges"):
         spectra = [spectrum.reshape((-1, depth)) for spectrum in (forward_spectrum, adjoint_spectrum)]
         *_, tr_f, tr_a, parts = pl.pallas_call(
             functools.partial(edges_kernel, plan, groups),
             out_shape=[*levels, lines(6 * nx * ny), lines(6 * nx * ny), array(groups, nx * ny, depth // groups)],
-            in_specs=[VMEM] * (count + 9),
+            in_specs=[VMEM] * (count + 10),
             out_specs=[VMEM] * (count + 3),
             input_output_aliases={i: i for i in range(count)},
             compiler_params=params(8),
-        )(*state, x_low, x_high, c_low, c_high, z_low, z_high, turns, *spectra)
+        )(*state, x_far, x_mate, far_low, far_high, mate, z_low, z_high, turns, *spectra)
     with jax.named_scope("sum_angles"):
         gradient = parts[0]
         for k in range(1, groups):

time: 27.7 us -> 28.4 us (1.025)
  starting transfers between devices: 8 us -> 13 us
  waiting for transfers between devices: 10.1 us -> 6.03 us
  Pallas kernels: 7.4 us -> 7.07 us
    ppermute x1, waiting for transfers between devices: 5.67 us -> 0.01 us  [shards(): z_high = lax.ppermute(z_down, 'gy', ring_pairs('gy', -1))]
    ppermute x4 -> x5, starting transfers between devices: 1.31 us -> 6.42 us  [the longest x1 4.44 us: shards(): far_high = lax.ppermute(far_down, ('gx', 'gy'), far_pairs(-1))]
    ppermute x4 -> x5, waiting for transfers between devices: 2.62 us -> 4.06 us  [the longest x1 4.05 us: shards(): far_high = lax.ppermute(far_down, ('gx', 'gy'), far_pairs(-1))]
    ppermute x1, starting transfers between devices: 3.08 us -> 2.64 us  [shards(): z_low = lax.ppermute(z_up, 'gy', ring_pairs('gy', 1))]
    ppermute x1, starting transfers between devices: 2.09 us -> 2.43 us  [shards(): z_high = lax.ppermute(z_down, 'gy', ring_pairs('gy', -1))]
  transfers between devices with their start and end apart: 7 -> 8, of which waited for: 4 -> 2; matrix products, arithmetic and copies ran while one was open for 0% -> 0% of each run, Pallas kernels for 11% -> 10%
where the time goes in v6:
time: 28.4 us; the launch traced here: 28.2 us
  starting transfers between devices  13 us (46%)
  Pallas kernels  7.07 us (25%)
  waiting for transfers between devices  6.03 us (21%)
  between operations  1.41 us (5%)
  other arithmetic  0.64 us (2%)
    ppermute x1, starting transfers between devices, shards(): far_high = lax.ppermute(far_down, ('gx', 'gy'), far_pairs(-1))  4.44 us
    ppermute x1, waiting for transfers between devices, shards(): far_high = lax.ppermute(far_down, ('gx', 'gy'), far_pairs(-1))  4.05 us
    ppermute x1, starting transfers between devices, shards(): z_low = lax.ppermute(z_up, 'gy', ring_pairs('gy', 1))  2.64 us
    ppermute x1, starting transfers between devices, shards(): z_high = lax.ppermute(z_down, 'gy', ring_pairs('gy', -1))  2.43 us
    pallas_call x1, Pallas kernels, shards(): pl.pallas_call(functools.partial(edges_kernel, plan, groups), out_shape=[...  2.08 us
    ppermute x1, waiting for transfers between devices, shards(): lax.ppermute(parts[k], 'angle', ring_pairs('angle', k))  1.96 us
    pallas_call x1, Pallas kernels, shards(): pl.pallas_call(functools.partial(pack_y_kernel, plan), out_shape=(*[array...  1.94 us
    ppermute x1, starting transfers between devices, shards(): lax.ppermute(parts[k], 'angle', ring_pairs('angle', k))  1.53 us
  transfers between devices with their start and end apart: 8, of which 2 were waited for; matrix products, arithmetic and copies ran while one was open for 0% of the time, Pallas kernels for 10%

profile of v6, /device:TPU:0, one launch (start us, length us, event | category | flops | bytes accessed | tf_op | source)
XLA Modules:
  0.0 28.2 jit_solution(13313142410324002937)
XLA Ops:
  0.6 1.9 %pack_y.1 = (f32[12,14,24,128]{3,2,1,0:T(8,128)S(1)}, f32[12,14,24,128]{3,2,1,0:T(8,128)S(1)}, f32[12,14,24,128]{3,2,1,0:T(8,128)S(1)}, f32[12,14,24,128]{3,2,1,...) custom-call(f32[12,8,16,128]{3,2,1,0:T(8,128)} %bitcast.37, f32[12,8,16,128]{3,2,1,0:T(8,128)} %bitcast.38, ...), custom_call_target="tpu_custom_call" | custom-call | tf_op jit(solution)/shard_map/pack_y/pallas_call | solution.py:451
  2.6 0.1 pack_x.1
  2.7 0.5 %collective-permute-start.1 = (f32[760,128]{1,0:T(8,128)S(1)}, f32[760,128]{1,0:T(8,128)S(1)}, u32[]{:S(2)}, u32[]{:S(2)}) collective-permute-start(f32[760,128]{1,0:T(8,128)S(1)} %get-tuple-element.34), channel_id=1, source_target_pairs={{0,4},{4,0},{8,12},{12,8},{1,5},{5,1},{9,13},{13,9},{2,6},{6,2},{1... | collective-permute-start | bytes 1167368 | tf_op jit(solution)/shard_map/send_x/ppermute | solution.py:473
  3.2 2.6 %collective-permute-start = (f32[400,128]{1,0:T(8,128)S(1)}, f32[400,128]{1,0:T(8,128)S(1)}, u32[]{:S(2)}, u32[]{:S(2)}) collective-permute-start(f32[400,128]{1,0:T(8,128)S(1)} %get-tuple-element.33), channel_id=1, source_target_pairs={{0,1},{1,2},{2,3},{3,0},{4,5},{5,6},{6,7},{7,4},{8,9},{9,10},{10,1... | collective-permute-start | bytes 614408 | tf_op jit(solution)/shard_map/send_y_up/ppermute | solution.py:461
  5.8 0.0 copy-start.2
  5.8 1.3 %collective-permute-start.3 = (f32[760,128]{1,0:T(8,128)S(1)}, f32[760,128]{1,0:T(8,128)S(1)}, u32[]{:S(2)}, u32[]{:S(2)}) collective-permute-start(f32[760,128]{1,0:T(8,128)S(1)} %get-tuple-element.45), channel_id=1, source_target_pairs={{0,12},{1,13},{2,14},{3,15},{4,8},{5,9},{6,10},{7,11},{8,4},{9,5},... | collective-permute-start | bytes 1167368 | tf_op jit(solution)/shard_map/send_x/ppermute | solution.py:472
  7.1 0.0 collective-permute-done.1.after.refs_10_
  7.1 0.1 pack_rest.1
  7.2 2.4 %collective-permute-start.2 = (f32[304,128]{1,0:T(8,128)S(1)}, f32[304,128]{1,0:T(8,128)S(1)}, u32[]{:S(2)}, u32[]{:S(2)}) collective-permute-start(f32[304,128]{1,0:T(8,128)S(1)} %get-tuple-element.35), channel_id=1, source_target_pairs={{0,3},{1,0},{2,1},{3,2},{4,7},{5,4},{6,5},{7,6},{8,11},{9,8},{10,9... | collective-permute-start | bytes 466952 | tf_op jit(solution)/shard_map/send_rest/ppermute | solution.py:484
  9.7 0.0 collective-permute-start.4
  9.7 4.4 %collective-permute-start.5 = (f32[72,128]{1,0:T(8,128)S(1)}, f32[72,128]{1,0:T(8,128)S(1)}, u32[]{:S(2)}, u32[]{:S(2)}) collective-permute-start(f32[72,128]{1,0:T(8,128)S(1)} %get-tuple-element.47), channel_id=1, source_target_pairs={{0,15},{1,12},{2,13},{3,14},{4,11},{5,8},{6,9},{7,10},{8,7},{9,4},... | collective-permute-start | bytes 110600 | tf_op jit(solution)/shard_map/send_rest/ppermute | solution.py:486
  14.8 0.0 copy-done.2
  14.8 0.0 copy-done.3
  14.8 0.6 %turns.1.refs_16_ = f32[24,128]{1,0:T(8,128)S(1)} custom-call(f32[2,2]{1,0:T(2,128)S(1)} %copy-done.2, s32[1]{0:T(128)S(6)} %copy.39.index, s32[4]{0:T(128)S(1)} %copy-done.3), custom_call_target="tpu_custom_call" | custom-call | tf_op jit(solution)/shard_map/turns/pallas_call | solution.py:488
  15.4 0.0 collective-permute-done.z_low.refs_14_
  15.4 4.0 %collective-permute-done.5.other_after.refs_12_ = f32[72,128]{1,0:T(8,128)S(1)} collective-permute-done((f32[72,128]{1,0:T(8,128)S(1)}, f32[72,128]{1,0:T(8,128)S(1)}, u32[]{:S(2)}, u32[]{:S(2)}) %collective-permute-start.5) | collective-permute-done | bytes 36896 | tf_op jit(solution)/shard_map/send_rest/ppermute | solution.py:486
  19.5 0.0 collective-permute-done.4.after.refs_11_
  19.5 0.0 collective-permute-done.2.z_high.refs_15_
  19.5 0.1 relay_corners.1
  19.5 0.0 copy-start
  19.5 0.0 copy-start.1
  19.5 0.2 collective-permute-start.6
  19.7 1.2 %middle.1 = (f32[4032,128]{1,0:T(8,128)S(1)}, f32[4032,128]{1,0:T(8,128)S(1)}, f32[4032,128]{1,0:T(8,128)S(1)}, f32[4032,128]{1,0:T(8,128)S(1)}, f32[4032,128]{1...) custom-call(f32[4032,128]{1,0:T(8,128)S(1)} %bitcast.20, ...), custom_call_target="tpu_custom_call", output_to_operand_aliasing={{0}: (0, {}), {4}: (1, {}), {1}: (2, {}), {5}: (3, {}), {8}... | custom-call | flops 2147483648 | bytes 2147483648 | tf_op jit(solution)/shard_map/middle/pallas_call | solution.py:508
  21.0 0.0 collective-permute-done.3.refs_9_
  21.0 0.0 collective-permute-done.6.refs_13_
  21.0 0.0 copy-done
  21.0 0.0 copy-done.1
  21.0 2.1 %edges.1 = (f32[4032,128]{1,0:T(8,128)S(1)}, f32[4032,128]{1,0:T(8,128)S(1)}, f32[4032,128]{1,0:T(8,128)S(1)}, f32[4032,128]{1,0:T(8,128)S(1)}, f32[4032,128]{1,...) custom-call(f32[4032,128]{1,0:T(8,128)S(1)} %get-tuple-element.36.re, ...), custom_call_target="tpu_custom_call", output_to_operand_aliasing={{0}: (0, {}), {1}: (1, {}), {2}: (2, {}), {3}: (3, {}), {4}... | custom-call | tf_op jit(solution)/shard_map/edges/pallas_call | solution.py:519
  23.1 1.5 %collective-permute-start.7 = (f32[128,64]{1,0:T(8,128)S(1)}, f32[128,64]{1,0:T(8,128)S(1)}, u32[]{:S(2)}, u32[]{:S(2)}) collective-permute-start(f32[128,64]{1,0:T(8,128)S(1)} %slice_bitcast_fusion), channel_id=1, source_target_pairs={{0,16},{16,0},{1,17},{17,1},{2,18},{18,2},{3,19},{19,3},{4,20},{20... | collective-permute-start | bytes 98312 | tf_op jit(solution)/shard_map/sum_angles/ppermute | solution.py:530
  24.6 1.0 %write.1 = (f32[6,8,16,128]{3,2,1,0:T(8,128)}, f32[6,8,16,128]{3,2,1,0:T(8,128)}) custom-call(f32[6,8,16,128]{3,2,1,0:T(8,128)S(1)} %bitcast.33, f32[6,8,16,128]{3,2,1,0:T(8,128)S(1)} %bitcast.34), custom_call_target="tpu_custom_call" | custom-call | tf_op jit(solution)/shard_map/write/pallas_call | solution.py:532
  25.6 2.0 %collective-permute-done.7 = f32[128,64]{1,0:T(8,128)S(1)} collective-permute-done((f32[128,64]{1,0:T(8,128)S(1)}, f32[128,64]{1,0:T(8,128)S(1)}, u32[]{:S(2)}, u32[]{:S(2)}) %collective-permute-start.7) | collective-permute-done | bytes 32800 | tf_op jit(solution)/shard_map/sum_angles/ppermute | solution.py:530
  27.5 0.6 %bitcast_add_fusion = f32[128,64]{1,0:T(8,128)} fusion(f32[128,64]{1,0:T(8,128)S(1)} %collective-permute-done.7, f32[2,128,64]{2,1,0:T(8,128)S(1)} %get-tuple-element.52), kind=kLoop, calls=%fused_computation | loop fusion | flops 8192 | bytes 98304 | tf_op jit(solution)/shard_map/sum_angles/add | solution.py:530
  (2 shorter events, 0.0 us)
Async XLA Ops:
  2.7 4.5 %collective-permute-start.1 = (f32[760,128]{1,0:T(8,128)S(1)}, f32[760,128]{1,0:T(8,128)S(1)}, u32[]{:S(2)}, u32[]{:S(2)}) collective-permute-start(f32[760,128]{1,0:T(8,128)S(1)} %get-tuple-element.34), channel_id=1, source_target_pairs={{0,4},{4,0},{8,12},{12,8},{1,5},{5,1},{9,13},{13,9},{2,6},{6,2},{1... | collective-permute-start | bytes 1167368 | tf_op jit(solution)/shard_map/send_x/ppermute | solution.py:473
  3.2 12.2 %collective-permute-start = (f32[400,128]{1,0:T(8,128)S(1)}, f32[400,128]{1,0:T(8,128)S(1)}, u32[]{:S(2)}, u32[]{:S(2)}) collective-permute-start(f32[400,128]{1,0:T(8,128)S(1)} %get-tuple-element.33), channel_id=1, source_target_pairs={{0,1},{1,2},{2,3},{3,0},{4,5},{5,6},{6,7},{7,4},{8,9},{9,10},{10,1... | collective-permute-start | bytes 614408 | tf_op jit(solution)/shard_map/send_y_up/ppermute | solution.py:461
  5.8 8.9 %copy-start.2 = (f32[2,2]{1,0:T(2,128)S(1)}, f32[2,2]{1,0:T(2,128)}, u32[]{:S(2)}) copy-start(f32[2,2]{1,0:T(2,128)} %table.1) | copy-start | bytes 52
  5.8 8.9 %copy-start.3 = (s32[4]{0:T(128)S(1)}, s32[4]{0:T(128)}, u32[]{:S(2)}) copy-start(s32[4]{0:T(128)} %tiles.1) | copy-start | bytes 52
  5.8 15.1 %collective-permute-start.3 = (f32[760,128]{1,0:T(8,128)S(1)}, f32[760,128]{1,0:T(8,128)S(1)}, u32[]{:S(2)}, u32[]{:S(2)}) collective-permute-start(f32[760,128]{1,0:T(8,128)S(1)} %get-tuple-element.45), channel_id=1, source_target_pairs={{0,12},{1,13},{2,14},{3,15},{4,8},{5,9},{6,10},{7,11},{8,4},{9,5},... | collective-permute-start | bytes 1167368 | tf_op jit(solution)/shard_map/send_x/ppermute | solution.py:472
  7.2 12.2 %collective-permute-start.2 = (f32[304,128]{1,0:T(8,128)S(1)}, f32[304,128]{1,0:T(8,128)S(1)}, u32[]{:S(2)}, u32[]{:S(2)}) collective-permute-start(f32[304,128]{1,0:T(8,128)S(1)} %get-tuple-element.35), channel_id=1, source_target_pairs={{0,3},{1,0},{2,1},{3,2},{4,7},{5,4},{6,5},{7,6},{8,11},{9,8},{10,9... | collective-permute-start | bytes 466952 | tf_op jit(solution)/shard_map/send_rest/ppermute | solution.py:484
  9.7 9.8 %collective-permute-start.4 = (f32[80,128]{1,0:T(8,128)S(1)}, f32[80,128]{1,0:T(8,128)S(1)}, u32[]{:S(2)}, u32[]{:S(2)}) collective-permute-start(f32[80,128]{1,0:T(8,128)S(1)} %get-tuple-element.46), channel_id=1, source_target_pairs={{0,13},{1,14},{2,15},{3,12},{4,9},{5,10},{6,11},{7,8},{8,5},{9,6},... | collective-permute-start | bytes 122888 | tf_op jit(solution)/shard_map/send_rest/ppermute | solution.py:485
  9.7 9.8 %collective-permute-start.5 = (f32[72,128]{1,0:T(8,128)S(1)}, f32[72,128]{1,0:T(8,128)S(1)}, u32[]{:S(2)}, u32[]{:S(2)}) collective-permute-start(f32[72,128]{1,0:T(8,128)S(1)} %get-tuple-element.47), channel_id=1, source_target_pairs={{0,15},{1,12},{2,13},{3,14},{4,11},{5,8},{6,9},{7,10},{8,7},{9,4},... | collective-permute-start | bytes 110600 | tf_op jit(solution)/shard_map/send_rest/ppermute | solution.py:486
  19.5 1.5 %copy-start = (f32[1,6,8,16,128]{4,3,2,1,0:T(8,128)S(1)}, f32[1,6,8,16,128]{4,3,2,1,0:T(8,128)}, u32[]{:S(2)}) copy-start(f32[1,6,8,16,128]{4,3,2,1,0:T(8,128)} %param.10) | copy-start | bytes 1179652
  19.5 1.5 %copy-start.1 = (f32[1,6,8,16,128]{4,3,2,1,0:T(8,128)S(1)}, f32[1,6,8,16,128]{4,3,2,1,0:T(8,128)}, u32[]{:S(2)}) copy-start(f32[1,6,8,16,128]{4,3,2,1,0:T(8,128)} %param.11) | copy-start | bytes 1179652
  19.5 1.4 %collective-permute-start.6 = (f32[144,128]{1,0:T(8,128)S(1)}, f32[144,128]{1,0:T(8,128)S(1)}, u32[]{:S(2)}, u32[]{:S(2)}) collective-permute-start(f32[144,128]{1,0:T(8,128)S(1)} %relay_corners.1), channel_id=1, source_target_pairs={{0,4},{4,0},{8,12},{12,8},{1,5},{5,1},{9,13},{13,9},{2,6},{6,2},{1... | collective-permute-start | bytes 221192 | tf_op jit(solution)/shard_map/relay_corners/ppermute | solution.py:503
  23.1 4.5 %collective-permute-start.7 = (f32[128,64]{1,0:T(8,128)S(1)}, f32[128,64]{1,0:T(8,128)S(1)}, u32[]{:S(2)}, u32[]{:S(2)}) collective-permute-start(f32[128,64]{1,0:T(8,128)S(1)} %slice_bitcast_fusion), channel_id=1, source_target_pairs={{0,16},{16,0},{1,17},{17,1},{2,18},{18,2},{3,19},{19,3},{4,20},{20... | collective-permute-start | bytes 98312 | tf_op jit(solution)/shard_map/sum_angles/ppermute | solution.py:530

commit v7 on v6

--- a/solution.py
+++ b/solution.py
@@ -103,11 +103,8 @@
         self.mate_side, self.far_side = (1, -1), (-1, 1)
         self.x_mate, self.x_far = ([Message(sides[side, 0], 1) for side in order] for order in (self.mate_side, self.far_side))
         self.x_lines = max(message.lines for message in self.x_mate)
-        self.mate = [Message(sides[side, -1] | sides[side, 1], 1) for side in self.mate_side]
-        self.far_low, self.far_high = ([Message(sides[side, end], 1) for side in self.far_side] for end in (-1, 1))
-        self.mate_lines, self.far_low_lines, self.far_high_lines = (
-            max(message.lines for message in messages) for messages in (self.mate, self.far_low, self.far_high)
-        )
+        self.mate, self.far = ([Message(sides[side, -1] | sides[side, 1], 1) for side in order] for order in (self.mate_side, self.far_side))
+        self.corner_lines = max(message.lines for message in self.mate)
 
     def row(self, x, y, run=0, part=0, comp=0):
         return ((run * 6 + part * 3 + comp) * self.wide + x + STEPS) * self.ring + y % self.ring
@@ -172,17 +169,8 @@
     by_parity(1, faces)
 
 
-def pack_rest_kernel(plan, e0, h0, e1, h1, coef, after, z_down, far_up, far_down):
-    nx, ny = plan.nx, plan.ny
-    state = State([e0, e1], [h0, h1], coef)
-    pack(plan, plan.y_high, state, 0, -ny, z_down)
-
-    def far(receiver):
-        dx = -nx * plan.far_side[receiver]
-        pack(plan, plan.far_low[receiver], state, dx, ny, far_up)
-        pack(plan, plan.far_high[receiver], state, dx, -ny, far_down)
-
-    by_parity(1, far)
+def pack_down_kernel(plan, e0, h0, e1, h1, coef, after, z_down):
+    pack(plan, plan.y_high, State([e0, e1], [h0, h1], coef), 0, -plan.ny, z_down)
 
 
 def turns_kernel(groups, table, index, tiles, turns):
@@ -209,14 +197,15 @@
     turns[pl.ds(2 * SUB, SUB), :] = jnp.full(sub.shape, weight, jnp.float32)
 
 
-def relay_kernel(plan, z_low, z_high, after, other_after, out):
-    def mate(receiver):
-        dx = -plan.nx * plan.mate_side[receiver]
-        for (what, x, y), row in plan.mate[receiver].at.items():
-            ref, source = (z_low, plan.y_low) if y < 0 else (z_high, plan.y_high)
-            out[pl.ds(row, 1), :] = ref[pl.ds(source.at[what, x + dx, y], 1), :]
-
-    by_parity(1, mate)
+def relay_kernel(plan, z_low, z_high, to_far, to_mate):
+    def corners(receiver):
+        for messages, side, out in ((plan.far, plan.far_side, to_far), (plan.mate, plan.mate_side, to_mate)):
+            dx = -plan.nx * side[receiver]
+            for (what, x, y), row in messages[receiver].at.items():
+                ref, source = (z_low, plan.y_low) if y < 0 else (z_high, plan.y_high)
+                out[pl.ds(row, 1), :] = ref[pl.ds(source.at[what, x + dx, y], 1), :]
+
+    by_parity(1, corners)
 
 
 def turned(real, imag, cosine, sine):
@@ -326,9 +315,9 @@
 def edges_kernel(plan, groups, *refs):
     nx, ny = plan.nx, plan.ny
     count = 2 * STEPS + 3
-    x_far, x_mate, far_low, far_high, mate, z_low, z_high, turns, spec_f, spec_a = refs[count : count + 10]
-    arrays = refs[count + 10 : 2 * count + 10]
-    out_f, out_a, parts = refs[2 * count + 10 :]
+    x_far, x_mate, far, mate, z_low, z_high, turns, spec_f, spec_a = refs[count : count + 9]
+    arrays = refs[count + 9 : 2 * count + 9]
+    out_f, out_a, parts = refs[2 * count + 9 :]
     efield, hfield, coef = arrays[: STEPS + 1], arrays[STEPS + 1 : 2 * STEPS + 2], arrays[-1]
     state = State(efield, hfield, coef)
 
@@ -338,11 +327,7 @@
             for messages, ref, side in ((plan.x_far, x_far, plan.far_side), (plan.x_mate, x_mate, plan.mate_side)):
                 first = 0 if side[receiver] < 0 else 1
                 unpack(plan, messages[receiver], ref, lambda y: first, turns, state, kinds, level)
-            for messages, ref, side in (
-                (plan.far_low, far_low, plan.far_side),
-                (plan.far_high, far_high, plan.far_side),
-                (plan.mate, mate, plan.mate_side),
-            ):
+            for messages, ref, side in ((plan.far, far, plan.far_side), (plan.mate, mate, plan.mate_side)):
                 first = 4 if side[receiver] < 0 else 6
                 unpack(plan, messages[receiver], ref, lambda y: first + (y >= 0), turns, state, kinds, level)
 
@@ -410,13 +395,9 @@
     return [(i, i ^ 1) for i in range(lax.axis_size("gx"))]
 
 
-def far_pairs(offset):
-    size_x, size_y = lax.axis_size("gx"), lax.axis_size("gy")
-    return [
-        (x * size_y + y, (x + (1 if x % 2 else -1)) % size_x * size_y + (y + offset) % size_y)
-        for x in range(size_x)
-        for y in range(size_y)
-    ]
+def far_pairs():
+    size = lax.axis_size("gx")
+    return [(i, (i + (1 if i % 2 else -1)) % size) for i in range(size)]
 
 
 def shards(
@@ -466,24 +447,20 @@
             in_specs=[VMEM] * 5,
             out_specs=[VMEM] * 2,
             compiler_params=params(8),
-            cost_estimate=cost(2**10),
         )(*first)
     with jax.named_scope("send_x"):
-        x_far = lax.ppermute(to_far, ("gx", "gy"), far_pairs(0))
+        x_far = lax.ppermute(to_far, "gx", far_pairs())
         x_mate = lax.ppermute(to_mate, "gx", mate_pairs())
-    with jax.named_scope("pack_rest"):
-        z_down, far_up, far_down = pl.pallas_call(
-            functools.partial(pack_rest_kernel, plan),
-            out_shape=(lines(plan.y_high.lines), lines(plan.far_low_lines), lines(plan.far_high_lines)),
+    with jax.named_scope("pack_y_down"):
+        z_down = pl.pallas_call(
+            functools.partial(pack_down_kernel, plan),
+            out_shape=lines(plan.y_high.lines),
             in_specs=[VMEM] * 6,
-            out_specs=[VMEM] * 3,
+            out_specs=VMEM,
             compiler_params=params(8),
-            cost_estimate=cost(2**10),
         )(*first, x_mate)
-    with jax.named_scope("send_rest"):
+    with jax.named_scope("send_y_down"):
         z_high = lax.ppermute(z_down, "gy", ring_pairs("gy", -1))
-        far_low = lax.ppermute(far_up, ("gx", "gy"), far_pairs(1))
-        far_high = lax.ppermute(far_down, ("gx", "gy"), far_pairs(-1))
     with jax.named_scope("turns"):
         turns = pl.pallas_call(
             functools.partial(turns_kernel, groups),
@@ -493,14 +470,15 @@
             compiler_params=params(4),
         )(phase_table, angle_index, design_tiles)
     with jax.named_scope("relay_corners"):
-        relayed = pl.pallas_call(
+        to_far, to_mate = pl.pallas_call(
             functools.partial(relay_kernel, plan),
-            out_shape=lines(plan.mate_lines),
-            in_specs=[VMEM] * 4,
-            out_specs=VMEM,
+            out_shape=[lines(plan.corner_lines)] * 2,
+            in_specs=[VMEM] * 2,
+            out_specs=[VMEM] * 2,
             compiler_params=params(4),
-        )(z_low, z_high, far_low, far_high)
-        mate = lax.ppermute(relayed, "gx", mate_pairs())
+        )(z_low, z_high)
+        far = lax.ppermute(to_far, "gx", far_pairs())
+        mate = lax.ppermute(to_mate, "gx", mate_pairs())
     level = lines(12 * wide * ring)
     count = 2 * STEPS + 3
     levels = [level] * (count - 1) + [lines(wide * ring)]
@@ -519,11 +497,11 @@
         *_, tr_f, tr_a, parts = pl.pallas_call(
             functools.partial(edges_kernel, plan, groups),
             out_shape=[*levels, lines(6 * nx * ny), lines(6 * nx * ny), array(groups, nx * ny, depth // groups)],
-            in_specs=[VMEM] * (count + 10),
+            in_specs=[VMEM] * (count + 9),
             out_specs=[VMEM] * (count + 3),
             input_output_aliases={i: i for i in range(count)},
             compiler_params=params(8),
-        )(*state, x_far, x_mate, far_low, far_high, mate, z_low, z_high, turns, *spectra)
+        )(*state, x_far, x_mate, far, mate, z_low, z_high, turns, *spectra)
     with jax.named_scope("sum_angles"):
         gradient = parts[0]
         for k in range(1, groups):

time: 28.4 us -> 28.7 us (1.011)
  waiting for transfers between devices: 6.03 us -> 9.17 us
  starting transfers between devices: 13 us -> 10.1 us
    ppermute x1, waiting for transfers between devices: 0.01 us -> 3.04 us  [shards(): z_high = lax.ppermute(z_down, 'gy', ring_pairs('gy', -1))]
    ppermute x1, waiting for transfers between devices: 0.01 us -> 2.94 us  [shards(): z_low = lax.ppermute(z_up, 'gy', ring_pairs('gy', 1))]
    ppermute x4 -> x3, starting transfers between devices: 5.9 us -> 2.99 us  [the longest x1 1.29 us: shards(): x_far = lax.ppermute(to_far, 'gx', far_pairs())]
    ppermute x4 -> x3, waiting for transfers between devices: 4.06 us -> 1.39 us  [the longest x1 1.38 us: shards(): far = lax.ppermute(to_far, 'gx', far_pairs())]
  transfers between devices with their start and end apart: 8 -> 7, of which waited for: 2 -> 4; matrix products, arithmetic and copies ran while one was open for 0% -> 0% of each run, Pallas kernels for 10% -> 11%
where the time goes in v7:
time: 28.7 us; the launch traced here: 28.5 us
  starting transfers between devices  10.1 us (35%)
  waiting for transfers between devices  9.17 us (32%)
  Pallas kernels  7.21 us (25%)
  between operations  1.36 us (5%)
  other arithmetic  0.64 us (2%)
    ppermute x1, waiting for transfers between devices, shards(): z_high = lax.ppermute(z_down, 'gy', ring_pairs('gy', -1))  3.04 us
    ppermute x1, waiting for transfers between devices, shards(): z_low = lax.ppermute(z_up, 'gy', ring_pairs('gy', 1))  2.94 us
    ppermute x1, starting transfers between devices, shards(): z_low = lax.ppermute(z_up, 'gy', ring_pairs('gy', 1))  2.64 us
    ppermute x1, starting transfers between devices, shards(): z_high = lax.ppermute(z_down, 'gy', ring_pairs('gy', -1))  2.43 us
    pallas_call x1, Pallas kernels, shards(): pl.pallas_call(functools.partial(edges_kernel, plan, groups), out_shape=[...  2.15 us
    pallas_call x1, Pallas kernels, shards(): pl.pallas_call(functools.partial(pack_y_kernel, plan), out_shape=(*[array...  1.95 us
    ppermute x1, waiting for transfers between devices, shards(): lax.ppermute(parts[k], 'angle', ring_pairs('angle', k))  1.8 us
    ppermute x1, starting transfers between devices, shards(): lax.ppermute(parts[k], 'angle', ring_pairs('angle', k))  1.53 us
  transfers between devices with their start and end apart: 7, of which 4 were waited for; matrix products, arithmetic and copies ran while one was open for 0% of the time, Pallas kernels for 11%

profile of v7, /device:TPU:0, one launch (start us, length us, event | category | flops | bytes accessed | tf_op | source)
XLA Modules:
  0.0 28.5 jit_solution(16744077971976104994)
XLA Ops:
  0.6 1.9 %pack_y.1 = (f32[12,14,24,128]{3,2,1,0:T(8,128)S(1)}, f32[12,14,24,128]{3,2,1,0:T(8,128)S(1)}, f32[12,14,24,128]{3,2,1,0:T(8,128)S(1)}, f32[12,14,24,128]{3,2,1,...) custom-call(f32[12,8,16,128]{3,2,1,0:T(8,128)} %bitcast.37, f32[12,8,16,128]{3,2,1,0:T(8,128)} %bitcast.38, ...), custom_call_target="tpu_custom_call" | custom-call | tf_op jit(solution)/shard_map/pack_y/pallas_call | solution.py:432
  2.6 0.1 pack_x.1
  2.7 0.5 %collective-permute-start.1 = (f32[760,128]{1,0:T(8,128)S(1)}, f32[760,128]{1,0:T(8,128)S(1)}, u32[]{:S(2)}, u32[]{:S(2)}) collective-permute-start(f32[760,128]{1,0:T(8,128)S(1)} %get-tuple-element.33), channel_id=1, source_target_pairs={{0,4},{4,0},{8,12},{12,8},{1,5},{5,1},{9,13},{13,9},{2,6},{6,2},{1... | collective-permute-start | bytes 1167368 | tf_op jit(solution)/shard_map/send_x/ppermute | solution.py:453
  3.2 2.6 %collective-permute-start = (f32[400,128]{1,0:T(8,128)S(1)}, f32[400,128]{1,0:T(8,128)S(1)}, u32[]{:S(2)}, u32[]{:S(2)}) collective-permute-start(f32[400,128]{1,0:T(8,128)S(1)} %get-tuple-element.32), channel_id=1, source_target_pairs={{0,1},{1,2},{2,3},{3,0},{4,5},{5,6},{6,7},{7,4},{8,9},{9,10},{10,1... | collective-permute-start | bytes 614408 | tf_op jit(solution)/shard_map/send_y_up/ppermute | solution.py:442
  5.9 0.0 copy-start.2
  5.9 0.0 copy-start.3
  5.9 1.3 %collective-permute-start.3 = (f32[760,128]{1,0:T(8,128)S(1)}, f32[760,128]{1,0:T(8,128)S(1)}, u32[]{:S(2)}, u32[]{:S(2)}) collective-permute-start(f32[760,128]{1,0:T(8,128)S(1)} %get-tuple-element.43), channel_id=1, source_target_pairs={{0,12},{4,8},{8,4},{12,0},{1,13},{5,9},{9,5},{13,1},{2,14},{6,10},... | collective-permute-start | bytes 1167368 | tf_op jit(solution)/shard_map/send_x/ppermute | solution.py:452
  7.2 0.0 collective-permute-done.1.after.refs_10_
  7.2 2.4 %collective-permute-start.2 = (f32[304,128]{1,0:T(8,128)S(1)}, f32[304,128]{1,0:T(8,128)S(1)}, u32[]{:S(2)}, u32[]{:S(2)}) collective-permute-start(f32[304,128]{1,0:T(8,128)S(1)} %pack_y_down.1), channel_id=1, source_target_pairs={{0,3},{1,0},{2,1},{3,2},{4,7},{5,4},{6,5},{7,6},{8,11},{9,8},{10,9... | collective-permute-start | bytes 466952 | tf_op jit(solution)/shard_map/send_y_down/ppermute | solution.py:463
  10.3 0.0 copy-done.2
  10.3 0.0 copy-done.3
  10.3 0.6 %turns.1.refs_15_ = f32[24,128]{1,0:T(8,128)S(1)} custom-call(f32[2,2]{1,0:T(2,128)S(1)} %copy-done.2, s32[1]{0:T(128)S(6)} %copy.39.index, s32[4]{0:T(128)S(1)} %copy-done.3), custom_call_target="tpu_custom_call" | custom-call | tf_op jit(solution)/shard_map/turns/pallas_call | solution.py:465
  10.9 2.9 %collective-permute-done.z_low.refs_13_ = f32[400,128]{1,0:T(8,128)S(1)} collective-permute-done((f32[400,128]{1,0:T(8,128)S(1)}, f32[400,128]{1,0:T(8,128)S(1)}, u32[]{:S(2)}, u32[]{:S(2)}) %collective-permute-start) | collective-permute-done | bytes 204832 | tf_op jit(solution)/shard_map/send_y_up/ppermute | solution.py:442
  13.9 3.0 %collective-permute-done.2.z_high.refs_14_ = f32[304,128]{1,0:T(8,128)S(1)} collective-permute-done((f32[304,128]{1,0:T(8,128)S(1)}, f32[304,128]{1,0:T(8,128)S(1)}, u32[]{:S(2)}, u32[]{:S(2)}) %collective-permute-start.2) | collective-permute-done | bytes 155680 | tf_op jit(solution)/shard_map/send_y_down/ppermute | solution.py:463
  16.9 0.1 relay_corners.1
  17.0 1.2 %collective-permute-start.4 = (f32[144,128]{1,0:T(8,128)S(1)}, f32[144,128]{1,0:T(8,128)S(1)}, u32[]{:S(2)}, u32[]{:S(2)}) collective-permute-start(f32[144,128]{1,0:T(8,128)S(1)} %get-tuple-element.44), channel_id=1, source_target_pairs={{0,12},{4,8},{8,4},{12,0},{1,13},{5,9},{9,5},{13,1},{2,14},{6,10},... | collective-permute-start | bytes 221192 | tf_op jit(solution)/shard_map/relay_corners/ppermute | solution.py:480
  18.2 0.0 copy-start
  18.2 0.0 copy-start.1
  18.2 0.5 %collective-permute-start.5 = (f32[144,128]{1,0:T(8,128)S(1)}, f32[144,128]{1,0:T(8,128)S(1)}, u32[]{:S(2)}, u32[]{:S(2)}) collective-permute-start(f32[144,128]{1,0:T(8,128)S(1)} %get-tuple-element.45), channel_id=1, source_target_pairs={{0,4},{4,0},{8,12},{12,8},{1,5},{5,1},{9,13},{13,9},{2,6},{6,2},{1... | collective-permute-start | bytes 221192 | tf_op jit(solution)/shard_map/relay_corners/ppermute | solution.py:481
  18.7 1.3 %middle.1 = (f32[4032,128]{1,0:T(8,128)S(1)}, f32[4032,128]{1,0:T(8,128)S(1)}, f32[4032,128]{1,0:T(8,128)S(1)}, f32[4032,128]{1,0:T(8,128)S(1)}, f32[4032,128]{1...) custom-call(f32[4032,128]{1,0:T(8,128)S(1)} %bitcast.20, ...), custom_call_target="tpu_custom_call", output_to_operand_aliasing={{0}: (0, {}), {4}: (1, {}), {1}: (2, {}), {5}: (3, {}), {8}... | custom-call | flops 2147483648 | bytes 2147483648 | tf_op jit(solution)/shard_map/middle/pallas_call | solution.py:486
  20.0 0.0 collective-permute-done.3.refs_9_
  20.0 1.4 %collective-permute-done.4.refs_11_ = f32[144,128]{1,0:T(8,128)S(1)} collective-permute-done((f32[144,128]{1,0:T(8,128)S(1)}, f32[144,128]{1,0:T(8,128)S(1)}, u32[]{:S(2)}, u32[]{:S(2)}) %collective-permute-start.4) | collective-permute-done | bytes 73760 | tf_op jit(solution)/shard_map/relay_corners/ppermute | solution.py:480
  21.4 0.0 collective-permute-done.5.refs_12_
  21.4 0.0 copy-done
  21.4 0.0 copy-done.1
  21.4 2.1 %edges.1 = (f32[4032,128]{1,0:T(8,128)S(1)}, f32[4032,128]{1,0:T(8,128)S(1)}, f32[4032,128]{1,0:T(8,128)S(1)}, f32[4032,128]{1,0:T(8,128)S(1)}, f32[4032,128]{1,...) custom-call(f32[4032,128]{1,0:T(8,128)S(1)} %get-tuple-element.34.re, ...), custom_call_target="tpu_custom_call", output_to_operand_aliasing={{0}: (0, {}), {1}: (1, {}), {2}: (2, {}), {3}: (3, {}), {4}... | custom-call | tf_op jit(solution)/shard_map/edges/pallas_call | solution.py:497
  23.6 1.5 %collective-permute-start.6 = (f32[128,64]{1,0:T(8,128)S(1)}, f32[128,64]{1,0:T(8,128)S(1)}, u32[]{:S(2)}, u32[]{:S(2)}) collective-permute-start(f32[128,64]{1,0:T(8,128)S(1)} %slice_bitcast_fusion), channel_id=1, source_target_pairs={{0,16},{16,0},{1,17},{17,1},{2,18},{18,2},{3,19},{19,3},{4,20},{20... | collective-permute-start | bytes 98312 | tf_op jit(solution)/shard_map/sum_angles/ppermute | solution.py:508
  25.1 1.0 %write.1 = (f32[6,8,16,128]{3,2,1,0:T(8,128)}, f32[6,8,16,128]{3,2,1,0:T(8,128)}) custom-call(f32[6,8,16,128]{3,2,1,0:T(8,128)S(1)} %bitcast.33, f32[6,8,16,128]{3,2,1,0:T(8,128)S(1)} %bitcast.34), custom_call_target="tpu_custom_call" | custom-call | tf_op jit(solution)/shard_map/write/pallas_call | solution.py:510
  26.1 1.8 %collective-permute-done.6 = f32[128,64]{1,0:T(8,128)S(1)} collective-permute-done((f32[128,64]{1,0:T(8,128)S(1)}, f32[128,64]{1,0:T(8,128)S(1)}, u32[]{:S(2)}, u32[]{:S(2)}) %collective-permute-start.6) | collective-permute-done | bytes 32800 | tf_op jit(solution)/shard_map/sum_angles/ppermute | solution.py:508
  27.9 0.6 %bitcast_add_fusion = f32[128,64]{1,0:T(8,128)} fusion(f32[128,64]{1,0:T(8,128)S(1)} %collective-permute-done.6, f32[2,128,64]{2,1,0:T(8,128)S(1)} %get-tuple-element.50), kind=kLoop, calls=%fused_computation | loop fusion | flops 8192 | bytes 98304 | tf_op jit(solution)/shard_map/sum_angles/add | solution.py:508
  (2 shorter events, 0.1 us)
Async XLA Ops:
  2.7 4.5 %collective-permute-start.1 = (f32[760,128]{1,0:T(8,128)S(1)}, f32[760,128]{1,0:T(8,128)S(1)}, u32[]{:S(2)}, u32[]{:S(2)}) collective-permute-start(f32[760,128]{1,0:T(8,128)S(1)} %get-tuple-element.33), channel_id=1, source_target_pairs={{0,4},{4,0},{8,12},{12,8},{1,5},{5,1},{9,13},{13,9},{2,6},{6,2},{1... | collective-permute-start | bytes 1167368 | tf_op jit(solution)/shard_map/send_x/ppermute | solution.py:453
  3.2 10.6 %collective-permute-start = (f32[400,128]{1,0:T(8,128)S(1)}, f32[400,128]{1,0:T(8,128)S(1)}, u32[]{:S(2)}, u32[]{:S(2)}) collective-permute-start(f32[400,128]{1,0:T(8,128)S(1)} %get-tuple-element.32), channel_id=1, source_target_pairs={{0,1},{1,2},{2,3},{3,0},{4,5},{5,6},{6,7},{7,4},{8,9},{9,10},{10,1... | collective-permute-start | bytes 614408 | tf_op jit(solution)/shard_map/send_y_up/ppermute | solution.py:442
  5.9 4.4 %copy-start.2 = (f32[2,2]{1,0:T(2,128)S(1)}, f32[2,2]{1,0:T(2,128)}, u32[]{:S(2)}) copy-start(f32[2,2]{1,0:T(2,128)} %table.1) | copy-start | bytes 52
  5.9 4.4 %copy-start.3 = (s32[4]{0:T(128)S(1)}, s32[4]{0:T(128)}, u32[]{:S(2)}) copy-start(s32[4]{0:T(128)} %tiles.1) | copy-start | bytes 52
  5.9 14.1 %collective-permute-start.3 = (f32[760,128]{1,0:T(8,128)S(1)}, f32[760,128]{1,0:T(8,128)S(1)}, u32[]{:S(2)}, u32[]{:S(2)}) collective-permute-start(f32[760,128]{1,0:T(8,128)S(1)} %get-tuple-element.43), channel_id=1, source_target_pairs={{0,12},{4,8},{8,4},{12,0},{1,13},{5,9},{9,5},{13,1},{2,14},{6,10},... | collective-permute-start | bytes 1167368 | tf_op jit(solution)/shard_map/send_x/ppermute | solution.py:452
  7.2 9.7 %collective-permute-start.2 = (f32[304,128]{1,0:T(8,128)S(1)}, f32[304,128]{1,0:T(8,128)S(1)}, u32[]{:S(2)}, u32[]{:S(2)}) collective-permute-start(f32[304,128]{1,0:T(8,128)S(1)} %pack_y_down.1), channel_id=1, source_target_pairs={{0,3},{1,0},{2,1},{3,2},{4,7},{5,4},{6,5},{7,6},{8,11},{9,8},{10,9... | collective-permute-start | bytes 466952 | tf_op jit(solution)/shard_map/send_y_down/ppermute | solution.py:463
  17.0 4.4 %collective-permute-start.4 = (f32[144,128]{1,0:T(8,128)S(1)}, f32[144,128]{1,0:T(8,128)S(1)}, u32[]{:S(2)}, u32[]{:S(2)}) collective-permute-start(f32[144,128]{1,0:T(8,128)S(1)} %get-tuple-element.44), channel_id=1, source_target_pairs={{0,12},{4,8},{8,4},{12,0},{1,13},{5,9},{9,5},{13,1},{2,14},{6,10},... | collective-permute-start | bytes 221192 | tf_op jit(solution)/shard_map/relay_corners/ppermute | solution.py:480
  18.2 3.1 %copy-start = (f32[1,6,8,16,128]{4,3,2,1,0:T(8,128)S(1)}, f32[1,6,8,16,128]{4,3,2,1,0:T(8,128)}, u32[]{:S(2)}) copy-start(f32[1,6,8,16,128]{4,3,2,1,0:T(8,128)} %param.10) | copy-start | bytes 1179652
  18.2 3.1 %copy-start.1 = (f32[1,6,8,16,128]{4,3,2,1,0:T(8,128)S(1)}, f32[1,6,8,16,128]{4,3,2,1,0:T(8,128)}, u32[]{:S(2)}) copy-start(f32[1,6,8,16,128]{4,3,2,1,0:T(8,128)} %param.11) | copy-start | bytes 1179652
  18.2 3.1 %collective-permute-start.5 = (f32[144,128]{1,0:T(8,128)S(1)}, f32[144,128]{1,0:T(8,128)S(1)}, u32[]{:S(2)}, u32[]{:S(2)}) collective-permute-start(f32[144,128]{1,0:T(8,128)S(1)} %get-tuple-element.45), channel_id=1, source_target_pairs={{0,4},{4,0},{8,12},{12,8},{1,5},{5,1},{9,13},{13,9},{2,6},{6,2},{1... | collective-permute-start | bytes 221192 | tf_op jit(solution)/shard_map/relay_corners/ppermute | solution.py:481
  23.6 4.3 %collective-permute-start.6 = (f32[128,64]{1,0:T(8,128)S(1)}, f32[128,64]{1,0:T(8,128)S(1)}, u32[]{:S(2)}, u32[]{:S(2)}) collective-permute-start(f32[128,64]{1,0:T(8,128)S(1)} %slice_bitcast_fusion), channel_id=1, source_target_pairs={{0,16},{16,0},{1,17},{17,1},{2,18},{18,2},{3,19},{19,3},{4,20},{20... | collective-permute-start | bytes 98312 | tf_op jit(solution)/shard_map/sum_angles/ppermute | solution.py:508

commit v8 on v5

--- a/solution.py
+++ b/solution.py
@@ -97,11 +97,13 @@
         def shifted(found, dx):
             return {(*node[:3], node[3] + dx, node[4]) for node in found}
 
-        self.x_low, self.x_high = Message(sides[-1, 0], 1), Message(sides[1, 0], 1)
         self.y_low, self.y_high = (
             Message(sides[0, side] | shifted(sides[-1, side], nx) | shifted(sides[1, side], -nx), 0) for side in (-1, 1)
         )
-        self.corner_low, self.corner_high = (Message(sides[side, -1] | sides[side, 1], 1) for side in (-1, 1))
+        self.x_low, self.x_high = Message(sides[-1, 0], 1), Message(sides[1, 0], 1)
+        self.mate_side, self.far_side = (1, -1), (-1, 1)
+        self.mate, self.far = ([Message(sides[side, -1] | sides[side, 1], 1) for side in order] for order in (self.mate_side, self.far_side))
+        self.corner_lines = max(message.lines for message in self.mate)
 
     def row(self, x, y, run=0, part=0, comp=0):
         return ((run * 6 + part * 3 + comp) * self.wide + x + STEPS) * self.ring + y % self.ring
@@ -123,6 +125,12 @@
 def pack(plan, message, state, dx, dy, out):
     for what, x, y, count, at in message.runs:
         out[pl.ds(at, count), :] = state(what)[plan.rows(what, x + dx, y + dy, message.axis, count), :]
+
+
+def by_parity(offset, body):
+    parity = lax.rem(lax.axis_index("gx") + offset, 2)
+    for value in (0, 1):
+        pl.when(parity == value)(functools.partial(body, value))
 
 
 def pack_y_kernel(plan, fwd, adj, eps, e0, h0, e1, h1, coef, z_up, z_down, sems):
@@ -181,11 +189,15 @@
     turns[pl.ds(2 * SUB, SUB), :] = jnp.full(sub.shape, weight, jnp.float32)
 
 
-def corner_kernel(plan, z_low, z_high, c_up, c_down):
-    for message, dx, out in ((plan.corner_low, plan.nx, c_up), (plan.corner_high, -plan.nx, c_down)):
-        for (what, x, y), row in message.at.items():
-            ref, source = (z_low, plan.y_low) if y < 0 else (z_high, plan.y_high)
-            out[pl.ds(row, 1), :] = ref[pl.ds(source.at[what, x + dx, y], 1), :]
+def relay_kernel(plan, z_low, z_high, to_far, to_mate):
+    def corners(receiver):
+        for messages, side, out in ((plan.far, plan.far_side, to_far), (plan.mate, plan.mate_side, to_mate)):
+            dx = -plan.nx * side[receiver]
+            for (what, x, y), row in messages[receiver].at.items():
+                ref, source = (z_low, plan.y_low) if y < 0 else (z_high, plan.y_high)
+                out[pl.ds(row, 1), :] = ref[pl.ds(source.at[what, x + dx, y], 1), :]
+
+    by_parity(1, corners)
 
 
 def turned(real, imag, cosine, sine):
@@ -295,7 +307,7 @@
 def edges_kernel(plan, groups, *refs):
     nx, ny = plan.nx, plan.ny
     count = 2 * STEPS + 3
-    x_low, x_high, c_low, c_high, z_low, z_high, turns, spec_f, spec_a = refs[count : count + 9]
+    x_low, x_high, far, mate, z_low, z_high, turns, spec_f, spec_a = refs[count : count + 9]
     arrays = refs[count + 9 : 2 * count + 9]
     out_f, out_a, parts = refs[2 * count + 9 :]
     efield, hfield, coef = arrays[: STEPS + 1], arrays[STEPS + 1 : 2 * STEPS + 2], arrays[-1]
@@ -304,8 +316,13 @@
     def take(kinds, level, layers=()):
         unpack(plan, plan.x_low, x_low, lambda y: 0, turns, state, kinds, level)
         unpack(plan, plan.x_high, x_high, lambda y: 1, turns, state, kinds, level)
-        unpack(plan, plan.corner_low, c_low, lambda y: 4 + (y >= 0), turns, state, kinds, level)
-        unpack(plan, plan.corner_high, c_high, lambda y: 6 + (y >= 0), turns, state, kinds, level)
+
+        def corners(receiver):
+            for messages, ref, side in ((plan.far, far, plan.far_side), (plan.mate, mate, plan.mate_side)):
+                first = 4 if side[receiver] < 0 else 6
+                unpack(plan, messages[receiver], ref, lambda y: first + (y >= 0), turns, state, kinds, level)
+
+        by_parity(0, corners)
         unpack(plan, plan.y_low, z_low, lambda y: 2, turns, state, kinds, level, layers)
         unpack(plan, plan.y_high, z_high, lambda y: 3, turns, state, kinds, level, layers)
 
@@ -365,6 +382,15 @@
     return [(i, (i + offset) % size) for i in range(size)]
 
 
+def mate_pairs():
+    return [(i, i ^ 1) for i in range(lax.axis_size("gx"))]
+
+
+def far_pairs():
+    size = lax.axis_size("gx")
+    return [(i, (i + (1 if i % 2 else -1)) % size) for i in range(size)]
+
+
 def shards(
     forward_fields,
     adjoint_fields,
@@ -392,6 +418,7 @@
     def cost(size):
         return pl.CostEstimate(flops=size, bytes_accessed=size, transcendentals=0)
 
+    assert lax.axis_size("gx") % 2 == 0
     with jax.named_scope("pack_y"):
         *first, coef, z_up, z_down = pl.pallas_call(
             functools.partial(pack_y_kernel, plan),
@@ -431,15 +458,15 @@
             compiler_params=params(4),
         )(phase_table, angle_index, design_tiles)
     with jax.named_scope("relay_corners"):
-        c_up, c_down = pl.pallas_call(
-            functools.partial(corner_kernel, plan),
-            out_shape=(lines(plan.corner_low.lines), lines(plan.corner_high.lines)),
+        to_far, to_mate = pl.pallas_call(
+            functools.partial(relay_kernel, plan),
+            out_shape=[lines(plan.corner_lines)] * 2,
             in_specs=[VMEM] * 2,
             out_specs=[VMEM] * 2,
             compiler_params=params(4),
         )(z_low, z_high)
-        c_low = lax.ppermute(c_up, "gx", ring_pairs("gx", 1))
-        c_high = lax.ppermute(c_down, "gx", ring_pairs("gx", -1))
+        far = lax.ppermute(to_far, "gx", far_pairs())
+        mate = lax.ppermute(to_mate, "gx", mate_pairs())
     level = lines(12 * wide * ring)
     count = 2 * STEPS + 3
     levels = [level] * (count - 1) + [lines(wide * ring)]
@@ -462,7 +489,7 @@
             out_specs=[VMEM] * (count + 3),
             input_output_aliases={i: i for i in range(count)},
             compiler_params=params(8),
-        )(*state, x_low, x_high, c_low, c_high, z_low, z_high, turns, *spectra)
+        )(*state, x_low, x_high, far, mate, z_low, z_high, turns, *spectra)
     with jax.named_scope("sum_angles"):
         gradient = parts[0]
         for k in range(1, groups):

time: 27.7 us -> 27.6 us (level)
  starting transfers between devices: 8 us -> 9.13 us
  waiting for transfers between devices: 10.1 us -> 9.01 us
    ppermute x2, starting transfers between devices: 0.58 us -> 1.7 us  [the longest x1 1.11 us: shards(): mate = lax.ppermute(to_mate, 'gx', mate_pairs())]
    ppermute x2, waiting for transfers between devices: 2.62 us -> 1.54 us  [the longest x1 1.53 us: shards(): far = lax.ppermute(to_far, 'gx', far_pairs())]
  transfers between devices with their start and end apart: 7 -> 7, of which waited for: 4 -> 3; matrix products, arithmetic and copies ran while one was open for 0% -> 0% of each run, Pallas kernels for 11% -> 11%
where the time goes in v8:
time: 27.6 us; the launch traced here: 27.4 us
  starting transfers between devices  9.13 us (33%)
  waiting for transfers between devices  9.01 us (33%)
  Pallas kernels  7.25 us (26%)
  between operations  1.36 us (5%)
  other arithmetic  0.64 us (2%)
    ppermute x1, waiting for transfers between devices, shards(): z_high = lax.ppermute(z_down, 'gy', ring_pairs('gy', -1))  5.67 us
    ppermute x1, starting transfers between devices, shards(): z_low = lax.ppermute(z_up, 'gy', ring_pairs('gy', 1))  3.08 us
    pallas_call x1, Pallas kernels, shards(): pl.pallas_call(functools.partial(edges_kernel, plan, groups), out_shape=[...  2.18 us
    ppermute x1, starting transfers between devices, shards(): z_high = lax.ppermute(z_down, 'gy', ring_pairs('gy', -1))  2.09 us
    pallas_call x1, Pallas kernels, shards(): pl.pallas_call(functools.partial(pack_y_kernel, plan), out_shape=(*[array...  2 us
    ppermute x1, waiting for transfers between devices, shards(): lax.ppermute(parts[k], 'angle', ring_pairs('angle', k))  1.8 us
    ppermute x1, waiting for transfers between devices, shards(): far = lax.ppermute(to_far, 'gx', far_pairs())  1.53 us
    ppermute x1, starting transfers between devices, shards(): lax.ppermute(parts[k], 'angle', ring_pairs('angle', k))  1.53 us
  transfers between devices with their start and end apart: 7, of which 3 were waited for; matrix products, arithmetic and copies ran while one was open for 0% of the time, Pallas kernels for 11%

profile of v8, /device:TPU:0, one launch (start us, length us, event | category | flops | bytes accessed | tf_op | source)
XLA Modules:
  0.0 27.4 jit_solution(8083024738320133201)
XLA Ops:
  0.6 2.0 %pack_y.1 = (f32[12,14,24,128]{3,2,1,0:T(8,128)S(1)}, f32[12,14,24,128]{3,2,1,0:T(8,128)S(1)}, f32[12,14,24,128]{3,2,1,0:T(8,128)S(1)}, f32[12,14,24,128]{3,2,1,...) custom-call(f32[12,8,16,128]{3,2,1,0:T(8,128)} %bitcast.32, ...), custom_call_target="tpu_custom_call" | custom-call | tf_op jit(solution)/shard_map/pack_y/pallas_call | solution.py:423
  2.6 3.1 %collective-permute-start = (f32[400,128]{1,0:T(8,128)S(1)}, f32[400,128]{1,0:T(8,128)S(1)}, u32[]{:S(2)}, u32[]{:S(2)}) collective-permute-start(f32[400,128]{1,0:T(8,128)S(1)} %get-tuple-element.33), channel_id=1, source_target_pairs={{0,1},{1,2},{2,3},{3,0},{4,5},{5,6},{6,7},{7,4},{8,9},{9,10},{10,1... | collective-permute-start | bytes 614408 | tf_op jit(solution)/shard_map/send_y/ppermute | solution.py:438
  5.7 2.1 %collective-permute-start.1 = (f32[304,128]{1,0:T(8,128)S(1)}, f32[304,128]{1,0:T(8,128)S(1)}, u32[]{:S(2)}, u32[]{:S(2)}) collective-permute-start(f32[304,128]{1,0:T(8,128)S(1)} %get-tuple-element.34), channel_id=1, source_target_pairs={{0,3},{1,0},{2,1},{3,2},{4,7},{5,4},{6,5},{7,6},{8,11},{9,8},{10,9... | collective-permute-start | bytes 466952 | tf_op jit(solution)/shard_map/send_y/ppermute | solution.py:439
  7.8 0.0 copy-start.2
  7.8 0.0 copy-start.3
  7.8 0.1 pack_x.1
  7.9 0.7 %collective-permute-start.3 = (f32[568,128]{1,0:T(8,128)S(1)}, f32[568,128]{1,0:T(8,128)S(1)}, u32[]{:S(2)}, u32[]{:S(2)}) collective-permute-start(f32[568,128]{1,0:T(8,128)S(1)} %get-tuple-element.45), channel_id=1, source_target_pairs={{0,12},{4,0},{8,4},{12,8},{1,13},{5,1},{9,5},{13,9},{2,14},{6,2},{... | collective-permute-start | bytes 872456 | tf_op jit(solution)/shard_map/send_x/ppermute | solution.py:451
  8.6 0.0 collective-permute-start.2
  9.3 0.0 copy-done.2
  9.3 0.0 copy-done.3
  9.3 0.6 %turns.1.refs_15_ = f32[24,128]{1,0:T(8,128)S(1)} custom-call(f32[2,2]{1,0:T(2,128)S(1)} %copy-done.2, s32[1]{0:T(128)S(6)} %copy.39.index, s32[4]{0:T(128)S(1)} %copy-done.3), custom_call_target="tpu_custom_call" | custom-call | tf_op jit(solution)/shard_map/turns/pallas_call | solution.py:453
  9.9 5.7 %collective-permute-done.1.z_high.refs_14_ = f32[304,128]{1,0:T(8,128)S(1)} collective-permute-done((f32[304,128]{1,0:T(8,128)S(1)}, f32[304,128]{1,0:T(8,128)S(1)}, u32[]{:S(2)}, u32[]{:S(2)}) %collective-permute-start.1) | collective-permute-done | bytes 155680 | tf_op jit(solution)/shard_map/send_y/ppermute | solution.py:439
  15.6 0.0 collective-permute-done.z_low.refs_13_
  15.6 0.1 relay_corners.1
  15.7 0.6 %collective-permute-start.4 = (f32[144,128]{1,0:T(8,128)S(1)}, f32[144,128]{1,0:T(8,128)S(1)}, u32[]{:S(2)}, u32[]{:S(2)}) collective-permute-start(f32[144,128]{1,0:T(8,128)S(1)} %get-tuple-element.46), channel_id=1, source_target_pairs={{0,12},{4,8},{8,4},{12,0},{1,13},{5,9},{9,5},{13,1},{2,14},{6,10},... | collective-permute-start | bytes 221192 | tf_op jit(solution)/shard_map/relay_corners/ppermute | solution.py:468
  16.3 0.0 copy-start
  16.3 0.0 copy-start.1
  16.3 1.1 %collective-permute-start.5 = (f32[144,128]{1,0:T(8,128)S(1)}, f32[144,128]{1,0:T(8,128)S(1)}, u32[]{:S(2)}, u32[]{:S(2)}) collective-permute-start(f32[144,128]{1,0:T(8,128)S(1)} %get-tuple-element.47), channel_id=1, source_target_pairs={{0,4},{4,0},{8,12},{12,8},{1,5},{5,1},{9,13},{13,9},{2,6},{6,2},{1... | collective-permute-start | bytes 221192 | tf_op jit(solution)/shard_map/relay_corners/ppermute | solution.py:469
  17.4 1.3 %middle.1 = (f32[4032,128]{1,0:T(8,128)S(1)}, f32[4032,128]{1,0:T(8,128)S(1)}, f32[4032,128]{1,0:T(8,128)S(1)}, f32[4032,128]{1,0:T(8,128)S(1)}, f32[4032,128]{1...) custom-call(f32[4032,128]{1,0:T(8,128)S(1)} %bitcast.19, ...), custom_call_target="tpu_custom_call", output_to_operand_aliasing={{0}: (0, {}), {4}: (1, {}), {1}: (2, {}), {5}: (3, {}), {8}... | custom-call | flops 4294967296 | bytes 4294967296 | tf_op jit(solution)/shard_map/middle/pallas_call | solution.py:474
  18.7 1.5 %collective-permute-done.4.refs_11_ = f32[144,128]{1,0:T(8,128)S(1)} collective-permute-done((f32[144,128]{1,0:T(8,128)S(1)}, f32[144,128]{1,0:T(8,128)S(1)}, u32[]{:S(2)}, u32[]{:S(2)}) %collective-permute-start.4) | collective-permute-done | bytes 73760 | tf_op jit(solution)/shard_map/relay_corners/ppermute | solution.py:468
  20.2 0.0 collective-permute-done.5.refs_12_
  20.2 0.0 collective-permute-done.3.refs_10_
  20.2 0.0 collective-permute-done.2.refs_9_
  20.3 0.0 copy-done
  20.3 0.0 copy-done.1
  20.3 2.2 %edges.1 = (f32[4032,128]{1,0:T(8,128)S(1)}, f32[4032,128]{1,0:T(8,128)S(1)}, f32[4032,128]{1,0:T(8,128)S(1)}, f32[4032,128]{1,0:T(8,128)S(1)}, f32[4032,128]{1,...) custom-call(f32[4032,128]{1,0:T(8,128)S(1)} %get-tuple-element.35.re, ...), custom_call_target="tpu_custom_call", output_to_operand_aliasing={{0}: (0, {}), {1}: (1, {}), {2}: (2, {}), {3}: (3, {}), {4}... | custom-call | tf_op jit(solution)/shard_map/edges/pallas_call | solution.py:485
  22.5 1.5 %collective-permute-start.6 = (f32[128,64]{1,0:T(8,128)S(1)}, f32[128,64]{1,0:T(8,128)S(1)}, u32[]{:S(2)}, u32[]{:S(2)}) collective-permute-start(f32[128,64]{1,0:T(8,128)S(1)} %slice_bitcast_fusion), channel_id=1, source_target_pairs={{0,16},{16,0},{1,17},{17,1},{2,18},{18,2},{3,19},{19,3},{4,20},{20... | collective-permute-start | bytes 98312 | tf_op jit(solution)/shard_map/sum_angles/ppermute | solution.py:496
  24.0 1.0 %write.1 = (f32[6,8,16,128]{3,2,1,0:T(8,128)}, f32[6,8,16,128]{3,2,1,0:T(8,128)}) custom-call(f32[6,8,16,128]{3,2,1,0:T(8,128)S(1)} %bitcast.28, f32[6,8,16,128]{3,2,1,0:T(8,128)S(1)} %bitcast.29), custom_call_target="tpu_custom_call" | custom-call | tf_op jit(solution)/shard_map/write/pallas_call | solution.py:498
  25.0 1.8 %collective-permute-done.6 = f32[128,64]{1,0:T(8,128)S(1)} collective-permute-done((f32[128,64]{1,0:T(8,128)S(1)}, f32[128,64]{1,0:T(8,128)S(1)}, u32[]{:S(2)}, u32[]{:S(2)}) %collective-permute-start.6) | collective-permute-done | bytes 32800 | tf_op jit(solution)/shard_map/sum_angles/ppermute | solution.py:496
  26.8 0.6 %bitcast_add_fusion = f32[128,64]{1,0:T(8,128)} fusion(f32[128,64]{1,0:T(8,128)S(1)} %collective-permute-done.6, f32[2,128,64]{2,1,0:T(8,128)S(1)} %get-tuple-element.52), kind=kLoop, calls=%fused_computation | loop fusion | flops 8192 | bytes 98304 | tf_op jit(solution)/shard_map/sum_angles/add | solution.py:496
  (1 shorter events, 0.0 us)
Async XLA Ops:
  2.6 13.0 %collective-permute-start = (f32[400,128]{1,0:T(8,128)S(1)}, f32[400,128]{1,0:T(8,128)S(1)}, u32[]{:S(2)}, u32[]{:S(2)}) collective-permute-start(f32[400,128]{1,0:T(8,128)S(1)} %get-tuple-element.33), channel_id=1, source_target_pairs={{0,1},{1,2},{2,3},{3,0},{4,5},{5,6},{6,7},{7,4},{8,9},{9,10},{10,1... | collective-permute-start | bytes 614408 | tf_op jit(solution)/shard_map/send_y/ppermute | solution.py:438
  5.7 9.9 %collective-permute-start.1 = (f32[304,128]{1,0:T(8,128)S(1)}, f32[304,128]{1,0:T(8,128)S(1)}, u32[]{:S(2)}, u32[]{:S(2)}) collective-permute-start(f32[304,128]{1,0:T(8,128)S(1)} %get-tuple-element.34), channel_id=1, source_target_pairs={{0,3},{1,0},{2,1},{3,2},{4,7},{5,4},{6,5},{7,6},{8,11},{9,8},{10,9... | collective-permute-start | bytes 466952 | tf_op jit(solution)/shard_map/send_y/ppermute | solution.py:439
  7.8 1.5 %copy-start.2 = (f32[2,2]{1,0:T(2,128)S(1)}, f32[2,2]{1,0:T(2,128)}, u32[]{:S(2)}) copy-start(f32[2,2]{1,0:T(2,128)} %table.1) | copy-start | bytes 52
  7.8 1.5 %copy-start.3 = (s32[4]{0:T(128)S(1)}, s32[4]{0:T(128)}, u32[]{:S(2)}) copy-start(s32[4]{0:T(128)} %tiles.1) | copy-start | bytes 52
  7.9 12.3 %collective-permute-start.3 = (f32[568,128]{1,0:T(8,128)S(1)}, f32[568,128]{1,0:T(8,128)S(1)}, u32[]{:S(2)}, u32[]{:S(2)}) collective-permute-start(f32[568,128]{1,0:T(8,128)S(1)} %get-tuple-element.45), channel_id=1, source_target_pairs={{0,12},{4,0},{8,4},{12,8},{1,13},{5,1},{9,5},{13,9},{2,14},{6,2},{... | collective-permute-start | bytes 872456 | tf_op jit(solution)/shard_map/send_x/ppermute | solution.py:451
  8.6 11.6 %collective-permute-start.2 = (f32[760,128]{1,0:T(8,128)S(1)}, f32[760,128]{1,0:T(8,128)S(1)}, u32[]{:S(2)}, u32[]{:S(2)}) collective-permute-start(f32[760,128]{1,0:T(8,128)S(1)} %get-tuple-element.44), channel_id=1, source_target_pairs={{0,4},{4,8},{8,12},{12,0},{1,5},{5,9},{9,13},{13,1},{2,6},{6,10},{... | collective-permute-start | bytes 1167368 | tf_op jit(solution)/shard_map/send_x/ppermute | solution.py:450
  15.7 4.6 %collective-permute-start.4 = (f32[144,128]{1,0:T(8,128)S(1)}, f32[144,128]{1,0:T(8,128)S(1)}, u32[]{:S(2)}, u32[]{:S(2)}) collective-permute-start(f32[144,128]{1,0:T(8,128)S(1)} %get-tuple-element.46), channel_id=1, source_target_pairs={{0,12},{4,8},{8,4},{12,0},{1,13},{5,9},{9,5},{13,1},{2,14},{6,10},... | collective-permute-start | bytes 221192 | tf_op jit(solution)/shard_map/relay_corners/ppermute | solution.py:468
  16.3 4.0 %copy-start = (f32[1,6,8,16,128]{4,3,2,1,0:T(8,128)S(1)}, f32[1,6,8,16,128]{4,3,2,1,0:T(8,128)}, u32[]{:S(2)}) copy-start(f32[1,6,8,16,128]{4,3,2,1,0:T(8,128)} %param.10) | copy-start | bytes 1179652
  16.3 4.0 %copy-start.1 = (f32[1,6,8,16,128]{4,3,2,1,0:T(8,128)S(1)}, f32[1,6,8,16,128]{4,3,2,1,0:T(8,128)}, u32[]{:S(2)}) copy-start(f32[1,6,8,16,128]{4,3,2,1,0:T(8,128)} %param.11) | copy-start | bytes 1179652
  16.3 4.0 %collective-permute-start.5 = (f32[144,128]{1,0:T(8,128)S(1)}, f32[144,128]{1,0:T(8,128)S(1)}, u32[]{:S(2)}, u32[]{:S(2)}) collective-permute-start(f32[144,128]{1,0:T(8,128)S(1)} %get-tuple-element.47), channel_id=1, source_target_pairs={{0,4},{4,0},{8,12},{12,8},{1,5},{5,1},{9,13},{13,9},{2,6},{6,2},{1... | collective-permute-start | bytes 221192 | tf_op jit(solution)/shard_map/relay_corners/ppermute | solution.py:469
  22.5 4.3 %collective-permute-start.6 = (f32[128,64]{1,0:T(8,128)S(1)}, f32[128,64]{1,0:T(8,128)S(1)}, u32[]{:S(2)}, u32[]{:S(2)}) collective-permute-start(f32[128,64]{1,0:T(8,128)S(1)} %slice_bitcast_fusion), channel_id=1, source_target_pairs={{0,16},{16,0},{1,17},{17,1},{2,18},{18,2},{3,19},{19,3},{4,20},{20... | collective-permute-start | bytes 98312 | tf_op jit(solution)/shard_map/sum_angles/ppermute | solution.py:496

commit v9 on v8

--- a/solution.py
+++ b/solution.py
@@ -478,7 +478,7 @@
             out_specs=[VMEM] * count,
             input_output_aliases={0: 0, 1: STEPS + 1, 2: 1, 3: STEPS + 2, 4: count - 1},
             compiler_params=params(8),
-            cost_estimate=cost(2**32),
+            cost_estimate=cost(2**31),
         )(e0, h0, e1, h1, coef, z_low, z_high, turns)
     with jax.named_scope("edges"):
         spectra = [spectrum.reshape((-1, depth)) for spectrum in (forward_spectrum, adjoint_spectrum)]

time: 27.6 us -> 27.9 us (1.011)
  starting transfers between devices: 9.13 us -> 9.93 us
  waiting for transfers between devices: 9.01 us -> 8.49 us
    ppermute x1, starting transfers between devices: 0.59 us -> 1.33 us  [shards(): far = lax.ppermute(to_far, 'gx', far_pairs())]
    ppermute x1, starting transfers between devices: 1.11 us -> 0.43 us  [shards(): mate = lax.ppermute(to_mate, 'gx', mate_pairs())]
    ppermute x1, starting transfers between devices: 0.73 us -> 1.4 us  [shards(): x_high = lax.ppermute(x_down, 'gx', ring_pairs('gx', -1))]
where the time goes in v9:
time: 27.9 us; the launch traced here: 27.7 us
  starting transfers between devices  9.93 us (36%)
  waiting for transfers between devices  8.49 us (30%)
  Pallas kernels  7.24 us (26%)
  between operations  1.36 us (5%)
  other arithmetic  0.64 us (2%)
    ppermute x1, waiting for transfers between devices, shards(): z_high = lax.ppermute(z_down, 'gy', ring_pairs('gy', -1))  5.42 us
    ppermute x1, starting transfers between devices, shards(): z_low = lax.ppermute(z_up, 'gy', ring_pairs('gy', 1))  3.08 us
    pallas_call x1, Pallas kernels, shards(): pl.pallas_call(functools.partial(edges_kernel, plan, groups), out_shape=[...  2.18 us
    ppermute x1, starting transfers between devices, shards(): z_high = lax.ppermute(z_down, 'gy', ring_pairs('gy', -1))  2.12 us
    pallas_call x1, Pallas kernels, shards(): pl.pallas_call(functools.partial(pack_y_kernel, plan), out_shape=(*[array...  2 us
    ppermute x1, waiting for transfers between devices, shards(): lax.ppermute(parts[k], 'angle', ring_pairs('angle', k))  1.8 us
    ppermute x1, starting transfers between devices, shards(): lax.ppermute(parts[k], 'angle', ring_pairs('angle', k))  1.53 us
    ppermute x1, starting transfers between devices, shards(): x_high = lax.ppermute(x_down, 'gx', ring_pairs('gx', -1))  1.4 us
  transfers between devices with their start and end apart: 7, of which 3 were waited for; matrix products, arithmetic and copies ran while one was open for 0% of the time, Pallas kernels for 11%

profile of v9, /device:TPU:0, one launch (start us, length us, event | category | flops | bytes accessed | tf_op | source)
XLA Modules:
  0.0 27.7 jit_solution(5493223613362458144)
XLA Ops:
  0.6 2.0 %pack_y.1 = (f32[12,14,24,128]{3,2,1,0:T(8,128)S(1)}, f32[12,14,24,128]{3,2,1,0:T(8,128)S(1)}, f32[12,14,24,128]{3,2,1,0:T(8,128)S(1)}, f32[12,14,24,128]{3,2,1,...) custom-call(f32[12,8,16,128]{3,2,1,0:T(8,128)} %bitcast.32, ...), custom_call_target="tpu_custom_call" | custom-call | tf_op jit(solution)/shard_map/pack_y/pallas_call | solution.py:423
  2.6 3.1 %collective-permute-start = (f32[400,128]{1,0:T(8,128)S(1)}, f32[400,128]{1,0:T(8,128)S(1)}, u32[]{:S(2)}, u32[]{:S(2)}) collective-permute-start(f32[400,128]{1,0:T(8,128)S(1)} %get-tuple-element.33), channel_id=1, source_target_pairs={{0,1},{1,2},{2,3},{3,0},{4,5},{5,6},{6,7},{7,4},{8,9},{9,10},{10,1... | collective-permute-start | bytes 614408 | tf_op jit(solution)/shard_map/send_y/ppermute | solution.py:438
  5.7 0.0 copy-start.2
  5.7 0.0 copy-start.3
  5.7 0.1 pack_x.1
  5.8 0.1 collective-permute-start.2
  5.9 2.1 %collective-permute-start.1 = (f32[304,128]{1,0:T(8,128)S(1)}, f32[304,128]{1,0:T(8,128)S(1)}, u32[]{:S(2)}, u32[]{:S(2)}) collective-permute-start(f32[304,128]{1,0:T(8,128)S(1)} %get-tuple-element.34), channel_id=1, source_target_pairs={{0,3},{1,0},{2,1},{3,2},{4,7},{5,4},{6,5},{7,6},{8,11},{9,8},{10,9... | collective-permute-start | bytes 466952 | tf_op jit(solution)/shard_map/send_y/ppermute | solution.py:439
  8.0 1.4 %collective-permute-start.3 = (f32[568,128]{1,0:T(8,128)S(1)}, f32[568,128]{1,0:T(8,128)S(1)}, u32[]{:S(2)}, u32[]{:S(2)}) collective-permute-start(f32[568,128]{1,0:T(8,128)S(1)} %get-tuple-element.45), channel_id=1, source_target_pairs={{0,12},{4,0},{8,4},{12,8},{1,13},{5,1},{9,5},{13,9},{2,14},{6,2},{... | collective-permute-start | bytes 872456 | tf_op jit(solution)/shard_map/send_x/ppermute | solution.py:451
  10.0 0.0 copy-done.2
  10.1 0.0 copy-done.3
  10.1 0.6 %turns.1.refs_15_ = f32[24,128]{1,0:T(8,128)S(1)} custom-call(f32[2,2]{1,0:T(2,128)S(1)} %copy-done.2, s32[1]{0:T(128)S(6)} %copy.39.index, s32[4]{0:T(128)S(1)} %copy-done.3), custom_call_target="tpu_custom_call" | custom-call | tf_op jit(solution)/shard_map/turns/pallas_call | solution.py:453
  10.7 5.4 %collective-permute-done.1.z_high.refs_14_ = f32[304,128]{1,0:T(8,128)S(1)} collective-permute-done((f32[304,128]{1,0:T(8,128)S(1)}, f32[304,128]{1,0:T(8,128)S(1)}, u32[]{:S(2)}, u32[]{:S(2)}) %collective-permute-start.1) | collective-permute-done | bytes 155680 | tf_op jit(solution)/shard_map/send_y/ppermute | solution.py:439
  16.1 0.0 collective-permute-done.z_low.refs_13_
  16.1 0.1 relay_corners.1
  16.2 1.3 %collective-permute-start.4 = (f32[144,128]{1,0:T(8,128)S(1)}, f32[144,128]{1,0:T(8,128)S(1)}, u32[]{:S(2)}, u32[]{:S(2)}) collective-permute-start(f32[144,128]{1,0:T(8,128)S(1)} %get-tuple-element.46), channel_id=1, source_target_pairs={{0,12},{4,8},{8,4},{12,0},{1,13},{5,9},{9,5},{13,1},{2,14},{6,10},... | collective-permute-start | bytes 221192 | tf_op jit(solution)/shard_map/relay_corners/ppermute | solution.py:468
  17.5 0.0 copy-start
  17.5 0.0 copy-start.1
  17.5 0.4 %collective-permute-start.5 = (f32[144,128]{1,0:T(8,128)S(1)}, f32[144,128]{1,0:T(8,128)S(1)}, u32[]{:S(2)}, u32[]{:S(2)}) collective-permute-start(f32[144,128]{1,0:T(8,128)S(1)} %get-tuple-element.47), channel_id=1, source_target_pairs={{0,4},{4,0},{8,12},{12,8},{1,5},{5,1},{9,13},{13,9},{2,6},{6,2},{1... | collective-permute-start | bytes 221192 | tf_op jit(solution)/shard_map/relay_corners/ppermute | solution.py:469
  18.0 1.3 %middle.1 = (f32[4032,128]{1,0:T(8,128)S(1)}, f32[4032,128]{1,0:T(8,128)S(1)}, f32[4032,128]{1,0:T(8,128)S(1)}, f32[4032,128]{1,0:T(8,128)S(1)}, f32[4032,128]{1...) custom-call(f32[4032,128]{1,0:T(8,128)S(1)} %bitcast.19, ...), custom_call_target="tpu_custom_call", output_to_operand_aliasing={{0}: (0, {}), {4}: (1, {}), {1}: (2, {}), {5}: (3, {}), {8}... | custom-call | flops 2147483648 | bytes 2147483648 | tf_op jit(solution)/shard_map/middle/pallas_call | solution.py:474
  19.3 1.3 %collective-permute-done.4.refs_11_ = f32[144,128]{1,0:T(8,128)S(1)} collective-permute-done((f32[144,128]{1,0:T(8,128)S(1)}, f32[144,128]{1,0:T(8,128)S(1)}, u32[]{:S(2)}, u32[]{:S(2)}) %collective-permute-start.4) | collective-permute-done | bytes 73760 | tf_op jit(solution)/shard_map/relay_corners/ppermute | solution.py:468
  20.5 0.0 collective-permute-done.5.refs_12_
  20.5 0.0 collective-permute-done.3.refs_10_
  20.5 0.0 collective-permute-done.2.refs_9_
  20.5 0.0 copy-done
  20.5 0.0 copy-done.1
  20.6 2.2 %edges.1 = (f32[4032,128]{1,0:T(8,128)S(1)}, f32[4032,128]{1,0:T(8,128)S(1)}, f32[4032,128]{1,0:T(8,128)S(1)}, f32[4032,128]{1,0:T(8,128)S(1)}, f32[4032,128]{1,...) custom-call(f32[4032,128]{1,0:T(8,128)S(1)} %get-tuple-element.35.re, ...), custom_call_target="tpu_custom_call", output_to_operand_aliasing={{0}: (0, {}), {1}: (1, {}), {2}: (2, {}), {3}: (3, {}), {4}... | custom-call | tf_op jit(solution)/shard_map/edges/pallas_call | solution.py:485
  22.7 1.5 %collective-permute-start.6 = (f32[128,64]{1,0:T(8,128)S(1)}, f32[128,64]{1,0:T(8,128)S(1)}, u32[]{:S(2)}, u32[]{:S(2)}) collective-permute-start(f32[128,64]{1,0:T(8,128)S(1)} %slice_bitcast_fusion), channel_id=1, source_target_pairs={{0,16},{16,0},{1,17},{17,1},{2,18},{18,2},{3,19},{19,3},{4,20},{20... | collective-permute-start | bytes 98312 | tf_op jit(solution)/shard_map/sum_angles/ppermute | solution.py:496
  24.3 1.0 %write.1 = (f32[6,8,16,128]{3,2,1,0:T(8,128)}, f32[6,8,16,128]{3,2,1,0:T(8,128)}) custom-call(f32[6,8,16,128]{3,2,1,0:T(8,128)S(1)} %bitcast.28, f32[6,8,16,128]{3,2,1,0:T(8,128)S(1)} %bitcast.29), custom_call_target="tpu_custom_call" | custom-call | tf_op jit(solution)/shard_map/write/pallas_call | solution.py:498
  25.2 1.8 %collective-permute-done.6 = f32[128,64]{1,0:T(8,128)S(1)} collective-permute-done((f32[128,64]{1,0:T(8,128)S(1)}, f32[128,64]{1,0:T(8,128)S(1)}, u32[]{:S(2)}, u32[]{:S(2)}) %collective-permute-start.6) | collective-permute-done | bytes 32800 | tf_op jit(solution)/shard_map/sum_angles/ppermute | solution.py:496
  27.0 0.6 %bitcast_add_fusion = f32[128,64]{1,0:T(8,128)} fusion(f32[128,64]{1,0:T(8,128)S(1)} %collective-permute-done.6, f32[2,128,64]{2,1,0:T(8,128)S(1)} %get-tuple-element.52), kind=kLoop, calls=%fused_computation | loop fusion | flops 8192 | bytes 98304 | tf_op jit(solution)/shard_map/sum_angles/add | solution.py:496
  (1 shorter events, 0.0 us)
Async XLA Ops:
  2.6 13.5 %collective-permute-start = (f32[400,128]{1,0:T(8,128)S(1)}, f32[400,128]{1,0:T(8,128)S(1)}, u32[]{:S(2)}, u32[]{:S(2)}) collective-permute-start(f32[400,128]{1,0:T(8,128)S(1)} %get-tuple-element.33), channel_id=1, source_target_pairs={{0,1},{1,2},{2,3},{3,0},{4,5},{5,6},{6,7},{7,4},{8,9},{9,10},{10,1... | collective-permute-start | bytes 614408 | tf_op jit(solution)/shard_map/send_y/ppermute | solution.py:438
  5.7 4.3 %copy-start.2 = (f32[2,2]{1,0:T(2,128)S(1)}, f32[2,2]{1,0:T(2,128)}, u32[]{:S(2)}) copy-start(f32[2,2]{1,0:T(2,128)} %table.1) | copy-start | bytes 52
  5.7 4.3 %copy-start.3 = (s32[4]{0:T(128)S(1)}, s32[4]{0:T(128)}, u32[]{:S(2)}) copy-start(s32[4]{0:T(128)} %tiles.1) | copy-start | bytes 52
  5.8 14.7 %collective-permute-start.2 = (f32[760,128]{1,0:T(8,128)S(1)}, f32[760,128]{1,0:T(8,128)S(1)}, u32[]{:S(2)}, u32[]{:S(2)}) collective-permute-start(f32[760,128]{1,0:T(8,128)S(1)} %get-tuple-element.44), channel_id=1, source_target_pairs={{0,4},{4,8},{8,12},{12,0},{1,5},{5,9},{9,13},{13,1},{2,6},{6,10},{... | collective-permute-start | bytes 1167368 | tf_op jit(solution)/shard_map/send_x/ppermute | solution.py:450
  5.9 10.2 %collective-permute-start.1 = (f32[304,128]{1,0:T(8,128)S(1)}, f32[304,128]{1,0:T(8,128)S(1)}, u32[]{:S(2)}, u32[]{:S(2)}) collective-permute-start(f32[304,128]{1,0:T(8,128)S(1)} %get-tuple-element.34), channel_id=1, source_target_pairs={{0,3},{1,0},{2,1},{3,2},{4,7},{5,4},{6,5},{7,6},{8,11},{9,8},{10,9... | collective-permute-start | bytes 466952 | tf_op jit(solution)/shard_map/send_y/ppermute | solution.py:439
  8.0 12.5 %collective-permute-start.3 = (f32[568,128]{1,0:T(8,128)S(1)}, f32[568,128]{1,0:T(8,128)S(1)}, u32[]{:S(2)}, u32[]{:S(2)}) collective-permute-start(f32[568,128]{1,0:T(8,128)S(1)} %get-tuple-element.45), channel_id=1, source_target_pairs={{0,12},{4,0},{8,4},{12,8},{1,13},{5,1},{9,5},{13,9},{2,14},{6,2},{... | collective-permute-start | bytes 872456 | tf_op jit(solution)/shard_map/send_x/ppermute | solution.py:451
  16.2 4.3 %collective-permute-start.4 = (f32[144,128]{1,0:T(8,128)S(1)}, f32[144,128]{1,0:T(8,128)S(1)}, u32[]{:S(2)}, u32[]{:S(2)}) collective-permute-start(f32[144,128]{1,0:T(8,128)S(1)} %get-tuple-element.46), channel_id=1, source_target_pairs={{0,12},{4,8},{8,4},{12,0},{1,13},{5,9},{9,5},{13,1},{2,14},{6,10},... | collective-permute-start | bytes 221192 | tf_op jit(solution)/shard_map/relay_corners/ppermute | solution.py:468
  17.5 3.0 %copy-start = (f32[1,6,8,16,128]{4,3,2,1,0:T(8,128)S(1)}, f32[1,6,8,16,128]{4,3,2,1,0:T(8,128)}, u32[]{:S(2)}) copy-start(f32[1,6,8,16,128]{4,3,2,1,0:T(8,128)} %param.10) | copy-start | bytes 1179652
  17.5 3.0 %copy-start.1 = (f32[1,6,8,16,128]{4,3,2,1,0:T(8,128)S(1)}, f32[1,6,8,16,128]{4,3,2,1,0:T(8,128)}, u32[]{:S(2)}) copy-start(f32[1,6,8,16,128]{4,3,2,1,0:T(8,128)} %param.11) | copy-start | bytes 1179652
  17.5 3.0 %collective-permute-start.5 = (f32[144,128]{1,0:T(8,128)S(1)}, f32[144,128]{1,0:T(8,128)S(1)}, u32[]{:S(2)}, u32[]{:S(2)}) collective-permute-start(f32[144,128]{1,0:T(8,128)S(1)} %get-tuple-element.47), channel_id=1, source_target_pairs={{0,4},{4,0},{8,12},{12,8},{1,5},{5,1},{9,13},{13,9},{2,6},{6,2},{1... | collective-permute-start | bytes 221192 | tf_op jit(solution)/shard_map/relay_corners/ppermute | solution.py:469
  22.7 4.3 %collective-permute-start.6 = (f32[128,64]{1,0:T(8,128)S(1)}, f32[128,64]{1,0:T(8,128)S(1)}, u32[]{:S(2)}, u32[]{:S(2)}) collective-permute-start(f32[128,64]{1,0:T(8,128)S(1)} %slice_bitcast_fusion), channel_id=1, source_target_pairs={{0,16},{16,0},{1,17},{17,1},{2,18},{18,2},{3,19},{19,3},{4,20},{20... | collective-permute-start | bytes 98312 | tf_op jit(solution)/shard_map/sum_angles/ppermute | solution.py:496

commit v10 on v8

--- a/solution.py
+++ b/solution.py
@@ -47,7 +47,7 @@
             return True
         return node[1] == 1 and all(block(other) == block(node) and alone(other) for other in reads(node))
 
-    found, seen = set(), set()
+    found, made, seen = set(), set(), set()
     todo = [("E", STEPS, comp, x, y) for comp in range(3) for x in range(nx) for y in range(ny)]
     while todo:
         node = todo.pop()
@@ -57,8 +57,9 @@
         if block(node) != (0, 0) and alone(node):
             found.add(node)
         elif node[1]:
+            made.add(node)
             todo += reads(node)
-    return found
+    return found, made
 
 
 class Message:
@@ -86,10 +87,15 @@
 
 
 class Plan:
-    def __init__(self, nx, ny):
+    def __init__(self, nx, ny, depth):
+        self.depth = depth
         self.nx, self.ny = nx, ny
         self.wide, self.ring = nx + 2 * STEPS, ny + SUB
-        nodes = wanted(nx, ny)
+        nodes, made = wanted(nx, ny)
+        self.made = {}
+        for kind, level, comp, x, y in made:
+            heights = self.made.setdefault((kind, level, x), {})
+            heights[comp] = max(heights.get(comp, 0), ny if 0 <= y < ny else self.ring)
         sides = {}
         for node in nodes:
             sides.setdefault((node[3] // nx, node[4] // ny), set()).add(node)
@@ -231,8 +237,16 @@
     def __init__(self, plan, efield, hfield, coef, height):
         self.plan, self.efield, self.hfield, self.coef, self.height = plan, efield, hfield, coef, height
 
-    def rows(self, run, part, comp, x, height=None):
-        return pl.ds(self.plan.row(x, 0, run, part, comp), height or self.height)
+    def rows(self, run, part, comp, x, height):
+        return pl.ds(self.plan.row(x, 0, run, part, comp), height)
+
+    def get(self, array, run, part, comp, x):
+        return array[self.rows(run, part, comp, x, self.height), :]
+
+    def heights(self, kind, step, x):
+        if self.height == self.plan.ring:
+            return self.plan.made.get((kind, step, x), {})
+        return dict.fromkeys(range(3), self.height)
 
     def next_z(self, value):
         lane = lax.broadcasted_iota(jnp.int32, value.shape, 1)
@@ -250,33 +264,36 @@
 
     def update_h(self, step, run, part, x):
         efield, old, new = self.efield[step - 1], self.hfield[step - 1], self.hfield[step]
-        ex, ey, ez = (efield[self.rows(run, part, comp, x), :] for comp in range(3))
-        ey_x, ez_x = (efield[self.rows(run, part, comp, x + 1), :] for comp in (1, 2))
-        hx, hy, hz = (old[self.rows(run, part, comp, x), :] for comp in range(3))
-        if step == 1:
-            hx, hy, hz = hx + hx, hy + hy, hz + hz
-        new[self.rows(run, part, 0, x), :] = hx - ((self.next_y(ez) - ez) - (self.next_z(ey) - ey))
-        new[self.rows(run, part, 2, x), :] = hz - ((ey_x - ey) - (self.next_y(ex) - ex))
-        height = self.last_height(step)
-        ex, ez, ez_x, hy = (value[:height] for value in (ex, ez, ez_x, hy))
-        new[self.rows(run, part, 1, x, height), :] = hy - ((self.next_z(ex) - ex) - (ez_x - ez))
+        ex, ey, ez = (self.get(efield, run, part, comp, x) for comp in range(3))
+        for comp, height in self.heights("H", step, x).items():
+            if comp == 0:
+                curl = (self.next_y(ez) - ez)[:height] - (self.next_z(ey[:height]) - ey[:height])
+            elif comp == 1:
+                ez_x = self.get(efield, run, part, 2, x + 1)
+                curl = (self.next_z(ex[:height]) - ex[:height]) - (ez_x - ez)[:height]
+            else:
+                ey_x = self.get(efield, run, part, 1, x + 1)
+                curl = (ey_x - ey)[:height] - (self.next_y(ex) - ex)[:height]
+            before = self.get(old, run, part, comp, x)[:height]
+            if step == 1:
+                before = before + before
+            new[self.rows(run, part, comp, x, height), :] = before - curl
 
     def update_e(self, step, run, part, x):
         old, new, hfield = self.efield[step - 1], self.efield[step], self.hfield[step]
-        height = self.last_height(step)
-        ex, ey, ez = (old[self.rows(run, part, comp, x, height), :] for comp in range(3))
-        hx, hz = (hfield[self.rows(run, part, comp, x), :] for comp in (0, 2))
-        hx_y, hz_y = self.prev_y(hx)[:height], self.prev_y(hz)[:height]
-        hx, hz = hx[:height], hz[:height]
-        hy = hfield[self.rows(run, part, 1, x, height), :]
-        hy_x, hz_x = (hfield[self.rows(run, part, comp, x - 1, height), :] for comp in (1, 2))
-        scale = self.coef[self.rows(0, 0, 0, x, height), :]
-        new[self.rows(run, part, 0, x, height), :] = ex + scale * ((hz - hz_y) - (hy - self.prev_z(hy)))
-        new[self.rows(run, part, 1, x, height), :] = ey + scale * ((hx - self.prev_z(hx)) - (hz - hz_x))
-        new[self.rows(run, part, 2, x, height), :] = ez + scale * ((hy - hy_x) - (hx - hx_y))
-
-    def last_height(self, step):
-        return self.plan.ny if step == STEPS else self.height
+        hx, hy, hz = (self.get(hfield, run, part, comp, x) for comp in range(3))
+        scale = self.get(self.coef, 0, 0, 0, x)
+        for comp, height in self.heights("E", step, x).items():
+            if comp == 0:
+                curl = (hz - self.prev_y(hz))[:height] - (hy[:height] - self.prev_z(hy[:height]))
+            elif comp == 1:
+                hz_x = self.get(hfield, run, part, 2, x - 1)
+                curl = (hx[:height] - self.prev_z(hx[:height])) - (hz - hz_x)[:height]
+            else:
+                hy_x = self.get(hfield, run, part, 1, x - 1)
+                curl = (hy - hy_x)[:height] - (hx - self.prev_y(hx))[:height]
+            before = self.get(old, run, part, comp, x)[:height]
+            new[self.rows(run, part, comp, x, height), :] = before + scale[:height] * curl
 
     def both(self, step, h_layers, e_layers, after_h=None, after_e=None, runs=(0, 1)):
         for update, layers, after in ((self.update_h, h_layers, after_h), (self.update_e, e_layers, after_e)):
@@ -304,18 +321,54 @@
         sweeps.both(step, range(step - 1, nx - step), range(step, nx - step), *after)
 
 
+def add_known(plan, efield, levels, transform, out):
+    nx, ny = plan.nx, plan.ny
+    for x in range(nx):
+        for tile in range(ny // SUB):
+            for comp in range(3):
+                ends = []
+                for run in (0, 1):
+                    at = [pl.ds(((part * 3 + comp) * nx + x) * ny + tile * SUB, SUB) for part in (0, 1)]
+                    real, imag = transform[run][at[0], :], transform[run][at[1], :]
+                    for level in levels(x):
+                        theta = omega_step * level
+                        here = [efield[level][pl.ds(plan.row(x, tile * SUB, run, part, comp), SUB), :] for part in (0, 1)]
+                        more = turned(*here, math.cos(theta), math.sin(theta))
+                        real, imag = real + more[0], imag + more[1]
+                    out[run][at[0], :], out[run][at[1], :] = real, imag
+                    ends.append((real, imag))
+                yield x, tile, comp, ends
+
+
+def known(plan, x):
+    return [level for level in range(1, STEPS + 1) if level <= x < plan.nx - level]
+
+
+def faces_kernel(plan, *refs):
+    efield, hfield, coef = refs[: STEPS + 1], refs[STEPS + 1], refs[STEPS + 2]
+    x_low, x_high, turns, spec_f, spec_a = refs[STEPS + 3 : STEPS + 8]
+    *_, out_f, out_a = refs
+    e0, h0, coef = refs[STEPS + 8 : STEPS + 11]
+    state = State([e0], [h0], coef)
+    unpack(plan, plan.x_low, x_low, lambda y: 0, turns, state, "EHC", 0)
+    unpack(plan, plan.x_high, x_high, lambda y: 1, turns, state, "EHC", 0)
+    for _ in add_known(plan, efield, functools.partial(known, plan), (spec_f, spec_a), (out_f, out_a)):
+        pass
+
+
 def edges_kernel(plan, groups, *refs):
     nx, ny = plan.nx, plan.ny
     count = 2 * STEPS + 3
-    x_low, x_high, far, mate, z_low, z_high, turns, spec_f, spec_a = refs[count : count + 9]
+    x_low, x_high, far, mate, z_low, z_high, turns, part_f, part_a = refs[count : count + 9]
     arrays = refs[count + 9 : 2 * count + 9]
-    out_f, out_a, parts = refs[2 * count + 9 :]
+    out_f, out_a, *parts = refs[2 * count + 9 :]
     efield, hfield, coef = arrays[: STEPS + 1], arrays[STEPS + 1 : 2 * STEPS + 2], arrays[-1]
     state = State(efield, hfield, coef)
 
     def take(kinds, level, layers=()):
-        unpack(plan, plan.x_low, x_low, lambda y: 0, turns, state, kinds, level)
-        unpack(plan, plan.x_high, x_high, lambda y: 1, turns, state, kinds, level)
+        if level:
+            unpack(plan, plan.x_low, x_low, lambda y: 0, turns, state, kinds, level)
+            unpack(plan, plan.x_high, x_high, lambda y: 1, turns, state, kinds, level)
 
         def corners(receiver):
             for messages, ref, side in ((plan.far, far, plan.far_side), (plan.mate, mate, plan.mate_side)):
@@ -337,33 +390,38 @@
             after = [functools.partial(take, "H", 1, h_layers), functools.partial(take, "E", 1, e_layers)]
         sweeps.both(step, h_layers, e_layers, *after)
 
-    share = parts.shape[2]
+    share = plan.depth // groups
     shift = lax.rem(groups - lax.axis_index("angle"), groups) * share
     weight = turns[pl.ds(2 * SUB, SUB), :]
-    tiles = ny // SUB
-
-    for i in range(nx * tiles):
-        x, tile = i // tiles, i % tiles
-        total = jnp.zeros(weight.shape, jnp.float32)
-        for comp in range(3):
-            ends = []
-            for run, (spec, out) in enumerate(((spec_f, out_f), (spec_a, out_a))):
-                at = [pl.ds(((part * 3 + comp) * nx + x) * ny + tile * SUB, SUB) for part in (0, 1)]
-                real, imag = spec[at[0], :], spec[at[1], :]
-                for step in range(1, STEPS + 1):
-                    theta = omega_step * step
-                    ends_e = [
-                        efield[step][pl.ds(plan.row(x, tile * SUB, run, part, comp), SUB), :]
-                        for part in (0, 1)
-                    ]
-                    more = turned(*ends_e, math.cos(theta), math.sin(theta))
-                    real, imag = real + more[0], imag + more[1]
-                out[at[0], :], out[at[1], :] = real, imag
-                ends.append((real, imag))
-            total = total + (ends[0][0] * ends[1][0] - ends[0][1] * ends[1][1])
-        total = pltpu.roll(total * weight, shift, 1)
-        for k in range(groups):
-            parts[k, pl.ds(i * SUB, SUB), :] = total[:, k * share : (k + 1) * share]
+
+    def rest(x):
+        return [level for level in range(1, STEPS + 1) if level not in known(plan, x)]
+
+    totals = {}
+    for x, tile, _, ends in add_known(plan, efield, rest, (part_f, part_a), (out_f, out_a)):
+        term = ends[0][0] * ends[1][0] - ends[0][1] * ends[1][1]
+        totals[x, tile] = totals[x, tile] + term if (x, tile) in totals else term
+    block = lax.broadcasted_iota(jnp.int32, weight.shape, 1) // share
+    tiles = [pltpu.roll(total * weight, shift, 1) for total in totals.values()]
+    for k, part in enumerate(parts):
+        for i in range(len(tiles) // groups):
+            packed = jnp.zeros(weight.shape, jnp.float32)
+            for t in range(groups):
+                lanes = (t - k) % groups * share
+                value = tiles[i * groups + t]
+                packed = jnp.where(block == t, pltpu.roll(value, lanes, 1) if lanes else value, packed)
+            part[pl.ds(i * SUB, SUB), :] = packed
+
+
+def sum_kernel(groups, *refs):
+    *parts, out = refs
+    share = out.shape[1]
+    for i in range(parts[0].shape[0] // SUB):
+        total = parts[0][pl.ds(i * SUB, SUB), :]
+        for part in parts[1:]:
+            total = total + part[pl.ds(i * SUB, SUB), :]
+        for t in range(groups):
+            out[pl.ds((i * groups + t) * SUB, SUB), :] = total[:, t * share : (t + 1) * share]
 
 
 def write_kernel(tr_f, tr_a, out_f, out_a, sems):
@@ -402,7 +460,7 @@
     design_tiles,
 ):
     nx, ny, depth = permittivity.shape
-    plan = Plan(nx, ny)
+    plan = Plan(nx, ny, depth)
     groups = lax.axis_size("angle")
     wide, ring = plan.wide, plan.ring
 
@@ -418,7 +476,7 @@
     def cost(size):
         return pl.CostEstimate(flops=size, bytes_accessed=size, transcendentals=0)
 
-    assert lax.axis_size("gx") % 2 == 0
+    assert lax.axis_size("gx") % 2 == 0 and nx * ny % (groups * SUB) == 0
     with jax.named_scope("pack_y"):
         *first, coef, z_up, z_down = pl.pallas_call(
             functools.partial(pack_y_kernel, plan),
@@ -480,20 +538,38 @@
             compiler_params=params(8),
             cost_estimate=cost(2**32),
         )(e0, h0, e1, h1, coef, z_low, z_high, turns)
+    transforms = [lines(6 * nx * ny)] * 2
+    with jax.named_scope("faces"):
+        spectra = [spectrum.reshape((-1, depth)) for spectrum in (forward_spectrum, adjoint_spectrum)]
+        e0, h0, coef, *sums = pl.pallas_call(
+            functools.partial(faces_kernel, plan),
+            out_shape=[level, level, levels[-1], *transforms],
+            in_specs=[VMEM] * (STEPS + 8),
+            out_specs=[VMEM] * 5,
+            input_output_aliases={0: 0, STEPS + 1: 1, STEPS + 2: 2},
+            compiler_params=params(8),
+            cost_estimate=cost(2**10),
+        )(*state[: STEPS + 2], state[-1], x_low, x_high, turns, *spectra)
+        state = [e0, *state[1 : STEPS + 1], h0, *state[STEPS + 2 : -1], coef]
     with jax.named_scope("edges"):
-        spectra = [spectrum.reshape((-1, depth)) for spectrum in (forward_spectrum, adjoint_spectrum)]
-        *_, tr_f, tr_a, parts = pl.pallas_call(
+        results = pl.pallas_call(
             functools.partial(edges_kernel, plan, groups),
-            out_shape=[*levels, lines(6 * nx * ny), lines(6 * nx * ny), array(groups, nx * ny, depth // groups)],
+            out_shape=[*levels, *transforms, *[lines(nx * ny // groups)] * groups],
             in_specs=[VMEM] * (count + 9),
-            out_specs=[VMEM] * (count + 3),
-            input_output_aliases={i: i for i in range(count)},
+            out_specs=[VMEM] * (count + 2 + groups),
+            input_output_aliases={i: i for i in range(count)} | {count + 7: count, count + 8: count + 1},
             compiler_params=params(8),
-        )(*state, x_low, x_high, far, mate, z_low, z_high, turns, *spectra)
+        )(*state, x_low, x_high, far, mate, z_low, z_high, turns, *sums)
+        tr_f, tr_a, own, *others = results[count:]
     with jax.named_scope("sum_angles"):
-        gradient = parts[0]
-        for k in range(1, groups):
-            gradient = gradient + lax.ppermute(parts[k], "angle", ring_pairs("angle", k))
+        others = [lax.ppermute(part, "angle", ring_pairs("angle", k + 1)) for k, part in enumerate(others)]
+        gradient = pl.pallas_call(
+            functools.partial(sum_kernel, groups),
+            out_shape=array(nx * ny, depth // groups),
+            in_specs=[VMEM] * groups,
+            out_specs=VMEM,
+            compiler_params=params(4),
+        )(own, *others)
     with jax.named_scope("write"):
         out_f, out_a = pl.pallas_call(
             write_kernel,

time: 27.6 us -> 27 us (0.978)
  other arithmetic: 0.64 us -> 0 us
  Pallas kernels: 7.25 us -> 7.84 us
  waiting for transfers between devices: 9.01 us -> 8.45 us
    pallas_call x0 -> x2, Pallas kernels: none -> 0.96 us  [the longest x1 0.71 us: shards(): pl.pallas_call(functools.partial(sum_kernel, groups), out_shape=array(nx...]
    add x1 -> x0, other arithmetic: 0.64 us -> none  [shards(): gradient + lax.ppermute(parts[k], 'angle', ring_pairs('angle', k))]
    ppermute x1, waiting for transfers between devices: 1.8 us -> 1.45 us  [shards(): lax.ppermute(part, 'angle', ring_pairs('angle', k + 1))]
  transfers between devices with their start and end apart: 7 -> 7, of which waited for: 3 -> 3; matrix products, arithmetic and copies ran while one was open for 0% -> 0% of each run, Pallas kernels for 11% -> 12%
where the time goes in v10:
time: 27 us; the launch traced here: 26.8 us
  starting transfers between devices  9.11 us (34%)
  waiting for transfers between devices  8.45 us (31%)
  Pallas kernels  7.84 us (29%)
  between operations  1.38 us (5%)
    ppermute x1, waiting for transfers between devices, shards(): z_high = lax.ppermute(z_down, 'gy', ring_pairs('gy', -1))  5.67 us
    ppermute x1, starting transfers between devices, shards(): z_low = lax.ppermute(z_up, 'gy', ring_pairs('gy', 1))  3.08 us
    ppermute x1, starting transfers between devices, shards(): z_high = lax.ppermute(z_down, 'gy', ring_pairs('gy', -1))  2.09 us
    pallas_call x1, Pallas kernels, shards(): pl.pallas_call(functools.partial(pack_y_kernel, plan), out_shape=(*[array...  1.99 us
    pallas_call x1, Pallas kernels, shards(): pl.pallas_call(functools.partial(edges_kernel, plan, groups), out_shape=[...  1.91 us
    ppermute x1, starting transfers between devices, shards(): lax.ppermute(part, 'angle', ring_pairs('angle', k + 1))  1.51 us
    ppermute x1, waiting for transfers between devices, shards(): lax.ppermute(part, 'angle', ring_pairs('angle', k + 1))  1.45 us
    ppermute x1, waiting for transfers between devices, shards(): far = lax.ppermute(to_far, 'gx', far_pairs())  1.32 us
  transfers between devices with their start and end apart: 7, of which 3 were waited for; matrix products, arithmetic and copies ran while one was open for 0% of the time, Pallas kernels for 12%

profile of v10, /device:TPU:0, one launch (start us, length us, event | category | flops | bytes accessed | tf_op | source)
XLA Modules:
  0.0 26.8 jit_solution(4045782980504105960)
XLA Ops:
  0.6 2.0 %pack_y.1 = (f32[12,14,24,128]{3,2,1,0:T(8,128)S(1)}, f32[12,14,24,128]{3,2,1,0:T(8,128)S(1)}, f32[12,14,24,128]{3,2,1,0:T(8,128)S(1)}, f32[12,14,24,128]{3,2,1,...) custom-call(f32[12,8,16,128]{3,2,1,0:T(8,128)} %bitcast.28, ...), custom_call_target="tpu_custom_call" | custom-call | tf_op jit(solution)/shard_map/pack_y/pallas_call | solution.py:481
  2.6 3.1 %collective-permute-start = (f32[400,128]{1,0:T(8,128)S(1)}, f32[400,128]{1,0:T(8,128)S(1)}, u32[]{:S(2)}, u32[]{:S(2)}) collective-permute-start(f32[400,128]{1,0:T(8,128)S(1)} %get-tuple-element.39), channel_id=1, source_target_pairs={{0,1},{1,2},{2,3},{3,0},{4,5},{5,6},{6,7},{7,4},{8,9},{9,10},{10,1... | collective-permute-start | bytes 614408 | tf_op jit(solution)/shard_map/send_y/ppermute | solution.py:496
  5.7 2.1 %collective-permute-start.1 = (f32[304,128]{1,0:T(8,128)S(1)}, f32[304,128]{1,0:T(8,128)S(1)}, u32[]{:S(2)}, u32[]{:S(2)}) collective-permute-start(f32[304,128]{1,0:T(8,128)S(1)} %get-tuple-element.40), channel_id=1, source_target_pairs={{0,3},{1,0},{2,1},{3,2},{4,7},{5,4},{6,5},{7,6},{8,11},{9,8},{10,9... | collective-permute-start | bytes 466952 | tf_op jit(solution)/shard_map/send_y/ppermute | solution.py:497
  7.8 0.0 copy-start.2
  7.8 0.0 copy-start.3
  7.8 0.1 pack_x.1
  7.9 0.7 %collective-permute-start.3 = (f32[568,128]{1,0:T(8,128)S(1)}, f32[568,128]{1,0:T(8,128)S(1)}, u32[]{:S(2)}, u32[]{:S(2)}) collective-permute-start(f32[568,128]{1,0:T(8,128)S(1)} %get-tuple-element.48), channel_id=1, source_target_pairs={{0,12},{4,0},{8,4},{12,8},{1,13},{5,1},{9,5},{13,9},{2,14},{6,2},{... | collective-permute-start | bytes 872456 | tf_op jit(solution)/shard_map/send_x/ppermute | solution.py:509
  8.6 0.0 collective-permute-start.2
  9.3 0.0 copy-done.2
  9.3 0.0 copy-done.3
  9.3 0.6 %turns.1.refs_8_.refs_15_ = f32[24,128]{1,0:T(8,128)S(1)} custom-call(f32[2,2]{1,0:T(2,128)S(1)} %copy-done.2, s32[1]{0:T(128)S(6)} %copy.49.index, s32[4]{0:T(128)S(1)} %copy-done.3), custom_call_target="tpu_custom_call" | custom-call | tf_op jit(solution)/shard_map/turns/pallas_call | solution.py:511
  9.9 5.7 %collective-permute-done.1.z_high.refs_14_ = f32[304,128]{1,0:T(8,128)S(1)} collective-permute-done((f32[304,128]{1,0:T(8,128)S(1)}, f32[304,128]{1,0:T(8,128)S(1)}, u32[]{:S(2)}, u32[]{:S(2)}) %collective-permute-start.1) | collective-permute-done | bytes 155680 | tf_op jit(solution)/shard_map/send_y/ppermute | solution.py:497
  15.6 0.0 collective-permute-done.z_low.refs_13_
  15.6 0.1 relay_corners.1
  15.7 0.6 %collective-permute-start.4 = (f32[144,128]{1,0:T(8,128)S(1)}, f32[144,128]{1,0:T(8,128)S(1)}, u32[]{:S(2)}, u32[]{:S(2)}) collective-permute-start(f32[144,128]{1,0:T(8,128)S(1)} %get-tuple-element.55), channel_id=1, source_target_pairs={{0,12},{4,8},{8,4},{12,0},{1,13},{5,9},{9,5},{13,1},{2,14},{6,10},... | collective-permute-start | bytes 221192 | tf_op jit(solution)/shard_map/relay_corners/ppermute | solution.py:526
  16.3 0.0 copy-start
  16.3 0.0 copy-start.1
  16.3 1.1 %collective-permute-start.5 = (f32[144,128]{1,0:T(8,128)S(1)}, f32[144,128]{1,0:T(8,128)S(1)}, u32[]{:S(2)}, u32[]{:S(2)}) collective-permute-start(f32[144,128]{1,0:T(8,128)S(1)} %get-tuple-element.56), channel_id=1, source_target_pairs={{0,4},{4,0},{8,12},{12,8},{1,5},{5,1},{9,13},{13,9},{2,6},{6,2},{1... | collective-permute-start | bytes 221192 | tf_op jit(solution)/shard_map/relay_corners/ppermute | solution.py:527
  17.4 1.2 %middle.1 = (f32[4032,128]{1,0:T(8,128)S(1)}, f32[4032,128]{1,0:T(8,128)S(1)}, f32[4032,128]{1,0:T(8,128)S(1)}, f32[4032,128]{1,0:T(8,128)S(1)}, f32[4032,128]{1...) custom-call(f32[4032,128]{1,0:T(8,128)S(1)} %bitcast.15, ...), custom_call_target="tpu_custom_call", output_to_operand_aliasing={{0}: (0, {}), {4}: (1, {}), {1}: (2, {}), {5}: (3, {}), {8}... | custom-call | flops 4294967296 | bytes 4294967296 | tf_op jit(solution)/shard_map/middle/pallas_call | solution.py:532
  18.6 0.0 collective-permute-done.3.refs_7_.refs_10_
  18.6 0.0 collective-permute-done.2.refs_6_.refs_9_
  18.6 0.0 copy-done
  18.7 0.0 copy-done.1
  18.7 0.3 faces.1
  18.9 1.3 %collective-permute-done.4.refs_11_ = f32[144,128]{1,0:T(8,128)S(1)} collective-permute-done((f32[144,128]{1,0:T(8,128)S(1)}, f32[144,128]{1,0:T(8,128)S(1)}, u32[]{:S(2)}, u32[]{:S(2)}) %collective-permute-start.4) | collective-permute-done | bytes 73760 | tf_op jit(solution)/shard_map/relay_corners/ppermute | solution.py:526
  20.2 0.0 collective-permute-done.5.refs_12_
  20.2 1.9 %edges.1 = (f32[4032,128]{1,0:T(8,128)S(1)}, f32[4032,128]{1,0:T(8,128)S(1)}, f32[4032,128]{1,0:T(8,128)S(1)}, f32[4032,128]{1,0:T(8,128)S(1)}, f32[4032,128]{1,...) custom-call(f32[4032,128]{1,0:T(8,128)S(1)} %get-tuple-element.49.re, ...), custom_call_target="tpu_custom_call", output_to_operand_aliasing={{0}: (0, {}), {1}: (1, {}), {2}: (2, {}), {3}: (3, {}), {4}... | custom-call | tf_op jit(solution)/shard_map/edges/pallas_call | solution.py:555
  22.1 1.5 %collective-permute-start.6 = (f32[64,128]{1,0:T(8,128)S(1)}, f32[64,128]{1,0:T(8,128)S(1)}, u32[]{:S(2)}, u32[]{:S(2)}) collective-permute-start(f32[64,128]{1,0:T(8,128)S(1)} %get-tuple-element.64), channel_id=1, source_target_pairs={{0,16},{16,0},{1,17},{17,1},{2,18},{18,2},{3,19},{19,3},{4,20},{20... | collective-permute-start | bytes 98312 | tf_op jit(solution)/shard_map/sum_angles/ppermute | solution.py:565
  23.7 1.0 %write.1 = (f32[6,8,16,128]{3,2,1,0:T(8,128)}, f32[6,8,16,128]{3,2,1,0:T(8,128)}) custom-call(f32[6,8,16,128]{3,2,1,0:T(8,128)S(1)} %bitcast.22, f32[6,8,16,128]{3,2,1,0:T(8,128)S(1)} %bitcast.23), custom_call_target="tpu_custom_call" | custom-call | tf_op jit(solution)/shard_map/write/pallas_call | solution.py:574
  24.6 1.4 %collective-permute-done.6.refs_1_ = f32[64,128]{1,0:T(8,128)S(1)} collective-permute-done((f32[64,128]{1,0:T(8,128)S(1)}, f32[64,128]{1,0:T(8,128)S(1)}, u32[]{:S(2)}, u32[]{:S(2)}) %collective-permute-start.6) | collective-permute-done | bytes 32800 | tf_op jit(solution)/shard_map/sum_angles/ppermute | solution.py:565
  26.1 0.7 %sum_angles.1 = f32[128,64]{1,0:T(8,128)} custom-call(f32[64,128]{1,0:T(8,128)S(1)} %get-tuple-element.63.refs_0_, f32[64,128]{1,0:T(8,128)S(1)} %collective-permute-done.6.refs_1_), custom_call_target="tpu_custom_call" | custom-call | tf_op jit(solution)/shard_map/sum_angles/pallas_call | solution.py:566
Async XLA Ops:
  2.6 13.0 %collective-permute-start = (f32[400,128]{1,0:T(8,128)S(1)}, f32[400,128]{1,0:T(8,128)S(1)}, u32[]{:S(2)}, u32[]{:S(2)}) collective-permute-start(f32[400,128]{1,0:T(8,128)S(1)} %get-tuple-element.39), channel_id=1, source_target_pairs={{0,1},{1,2},{2,3},{3,0},{4,5},{5,6},{6,7},{7,4},{8,9},{9,10},{10,1... | collective-permute-start | bytes 614408 | tf_op jit(solution)/shard_map/send_y/ppermute | solution.py:496
  5.7 9.9 %collective-permute-start.1 = (f32[304,128]{1,0:T(8,128)S(1)}, f32[304,128]{1,0:T(8,128)S(1)}, u32[]{:S(2)}, u32[]{:S(2)}) collective-permute-start(f32[304,128]{1,0:T(8,128)S(1)} %get-tuple-element.40), channel_id=1, source_target_pairs={{0,3},{1,0},{2,1},{3,2},{4,7},{5,4},{6,5},{7,6},{8,11},{9,8},{10,9... | collective-permute-start | bytes 466952 | tf_op jit(solution)/shard_map/send_y/ppermute | solution.py:497
  7.8 1.5 %copy-start.2 = (f32[2,2]{1,0:T(2,128)S(1)}, f32[2,2]{1,0:T(2,128)}, u32[]{:S(2)}) copy-start(f32[2,2]{1,0:T(2,128)} %table.1) | copy-start | bytes 52
  7.8 1.5 %copy-start.3 = (s32[4]{0:T(128)S(1)}, s32[4]{0:T(128)}, u32[]{:S(2)}) copy-start(s32[4]{0:T(128)} %tiles.1) | copy-start | bytes 52
  7.9 10.7 %collective-permute-start.3 = (f32[568,128]{1,0:T(8,128)S(1)}, f32[568,128]{1,0:T(8,128)S(1)}, u32[]{:S(2)}, u32[]{:S(2)}) collective-permute-start(f32[568,128]{1,0:T(8,128)S(1)} %get-tuple-element.48), channel_id=1, source_target_pairs={{0,12},{4,0},{8,4},{12,8},{1,13},{5,1},{9,5},{13,9},{2,14},{6,2},{... | collective-permute-start | bytes 872456 | tf_op jit(solution)/shard_map/send_x/ppermute | solution.py:509
  8.6 10.0 %collective-permute-start.2 = (f32[760,128]{1,0:T(8,128)S(1)}, f32[760,128]{1,0:T(8,128)S(1)}, u32[]{:S(2)}, u32[]{:S(2)}) collective-permute-start(f32[760,128]{1,0:T(8,128)S(1)} %get-tuple-element.47), channel_id=1, source_target_pairs={{0,4},{4,8},{8,12},{12,0},{1,5},{5,9},{9,13},{13,1},{2,6},{6,10},{... | collective-permute-start | bytes 1167368 | tf_op jit(solution)/shard_map/send_x/ppermute | solution.py:508
  15.7 4.6 %collective-permute-start.4 = (f32[144,128]{1,0:T(8,128)S(1)}, f32[144,128]{1,0:T(8,128)S(1)}, u32[]{:S(2)}, u32[]{:S(2)}) collective-permute-start(f32[144,128]{1,0:T(8,128)S(1)} %get-tuple-element.55), channel_id=1, source_target_pairs={{0,12},{4,8},{8,4},{12,0},{1,13},{5,9},{9,5},{13,1},{2,14},{6,10},... | collective-permute-start | bytes 221192 | tf_op jit(solution)/shard_map/relay_corners/ppermute | solution.py:526
  16.3 2.4 %copy-start = (f32[1,6,8,16,128]{4,3,2,1,0:T(8,128)S(1)}, f32[1,6,8,16,128]{4,3,2,1,0:T(8,128)}, u32[]{:S(2)}) copy-start(f32[1,6,8,16,128]{4,3,2,1,0:T(8,128)} %param.10) | copy-start | bytes 1179652
  16.3 2.4 %copy-start.1 = (f32[1,6,8,16,128]{4,3,2,1,0:T(8,128)S(1)}, f32[1,6,8,16,128]{4,3,2,1,0:T(8,128)}, u32[]{:S(2)}) copy-start(f32[1,6,8,16,128]{4,3,2,1,0:T(8,128)} %param.11) | copy-start | bytes 1179652
  16.3 4.0 %collective-permute-start.5 = (f32[144,128]{1,0:T(8,128)S(1)}, f32[144,128]{1,0:T(8,128)S(1)}, u32[]{:S(2)}, u32[]{:S(2)}) collective-permute-start(f32[144,128]{1,0:T(8,128)S(1)} %get-tuple-element.56), channel_id=1, source_target_pairs={{0,4},{4,0},{8,12},{12,8},{1,5},{5,1},{9,13},{13,9},{2,6},{6,2},{1... | collective-permute-start | bytes 221192 | tf_op jit(solution)/shard_map/relay_corners/ppermute | solution.py:527
  22.1 3.9 %collective-permute-start.6 = (f32[64,128]{1,0:T(8,128)S(1)}, f32[64,128]{1,0:T(8,128)S(1)}, u32[]{:S(2)}, u32[]{:S(2)}) collective-permute-start(f32[64,128]{1,0:T(8,128)S(1)} %get-tuple-element.64), channel_id=1, source_target_pairs={{0,16},{16,0},{1,17},{17,1},{2,18},{18,2},{3,19},{19,3},{4,20},{20... | collective-permute-start | bytes 98312 | tf_op jit(solution)/shard_map/sum_angles/ppermute | solution.py:565

commit v11 on v10

--- a/solution.py
+++ b/solution.py
@@ -92,10 +92,24 @@
         self.nx, self.ny = nx, ny
         self.wide, self.ring = nx + 2 * STEPS, ny + SUB
         nodes, made = wanted(nx, ny)
-        self.made = {}
-        for kind, level, comp, x, y in made:
-            heights = self.made.setdefault((kind, level, x), {})
-            heights[comp] = max(heights.get(comp, 0), ny if 0 <= y < ny else self.ring)
+        self.made, self.free, self.rest = {}, {}, {}
+        tiles, ready = {}, set()
+        for node in made:
+            tiles.setdefault((node[1], "HE".index(node[0]), *node[2:4], node[4] % self.ring // SUB), []).append(node)
+
+        def early(node):
+            if node in made:
+                return node in ready
+            return node not in nodes or 0 <= node[3] < nx or 0 <= node[4] < ny
+
+        for (level, order, comp, x, tile), members in sorted(tiles.items()):
+            key = ("HE"[order], level, x)
+            middle = level - 1 + order <= x < nx - level
+            free = middle or all(early(other) for node in members for other in reads(node))
+            if free:
+                ready.update(members)
+            for into in (self.made, self.free if free else self.rest):
+                into.setdefault(key, {}).setdefault(comp, set()).add(tile)
         sides = {}
         for node in nodes:
             sides.setdefault((node[3] // nx, node[4] // ny), set()).add(node)
@@ -234,19 +248,27 @@
 
 
 class Sweeps:
-    def __init__(self, plan, efield, hfield, coef, height):
+    def __init__(self, plan, efield, hfield, coef, height, todo=None):
         self.plan, self.efield, self.hfield, self.coef, self.height = plan, efield, hfield, coef, height
-
-    def rows(self, run, part, comp, x, height):
-        return pl.ds(self.plan.row(x, 0, run, part, comp), height)
+        self.todo = todo
+
+    def rows(self, run, part, comp, x, start, stop):
+        return pl.ds(self.plan.row(x, 0, run, part, comp) + start, stop - start)
 
     def get(self, array, run, part, comp, x):
-        return array[self.rows(run, part, comp, x, self.height), :]
-
-    def heights(self, kind, step, x):
-        if self.height == self.plan.ring:
-            return self.plan.made.get((kind, step, x), {})
-        return dict.fromkeys(range(3), self.height)
+        return array[self.rows(run, part, comp, x, 0, self.height), :]
+
+    def pieces(self, kind, step, x):
+        if self.todo is None:
+            return [(comp, 0, self.height) for comp in range(3)]
+        found = []
+        for comp, tiles in sorted(self.todo.get((kind, step, x), {}).items()):
+            for tile in sorted(tiles):
+                if found and found[-1][0] == comp and found[-1][2] == tile * SUB:
+                    found[-1] = (comp, found[-1][1], (tile + 1) * SUB)
+                else:
+                    found.append((comp, tile * SUB, (tile + 1) * SUB))
+        return found
 
     def next_z(self, value):
         lane = lax.broadcasted_iota(jnp.int32, value.shape, 1)
@@ -265,35 +287,37 @@
     def update_h(self, step, run, part, x):
         efield, old, new = self.efield[step - 1], self.hfield[step - 1], self.hfield[step]
         ex, ey, ez = (self.get(efield, run, part, comp, x) for comp in range(3))
-        for comp, height in self.heights("H", step, x).items():
+        for comp, start, stop in self.pieces("H", step, x):
+            here = slice(start, stop)
             if comp == 0:
-                curl = (self.next_y(ez) - ez)[:height] - (self.next_z(ey[:height]) - ey[:height])
+                curl = (self.next_y(ez) - ez)[here] - (self.next_z(ey[here]) - ey[here])
             elif comp == 1:
                 ez_x = self.get(efield, run, part, 2, x + 1)
-                curl = (self.next_z(ex[:height]) - ex[:height]) - (ez_x - ez)[:height]
+                curl = (self.next_z(ex[here]) - ex[here]) - (ez_x - ez)[here]
             else:
                 ey_x = self.get(efield, run, part, 1, x + 1)
-                curl = (ey_x - ey)[:height] - (self.next_y(ex) - ex)[:height]
-            before = self.get(old, run, part, comp, x)[:height]
+                curl = (ey_x - ey)[here] - (self.next_y(ex) - ex)[here]
+            before = self.get(old, run, part, comp, x)[here]
             if step == 1:
                 before = before + before
-            new[self.rows(run, part, comp, x, height), :] = before - curl
+            new[self.rows(run, part, comp, x, start, stop), :] = before - curl
 
     def update_e(self, step, run, part, x):
         old, new, hfield = self.efield[step - 1], self.efield[step], self.hfield[step]
         hx, hy, hz = (self.get(hfield, run, part, comp, x) for comp in range(3))
         scale = self.get(self.coef, 0, 0, 0, x)
-        for comp, height in self.heights("E", step, x).items():
+        for comp, start, stop in self.pieces("E", step, x):
+            here = slice(start, stop)
             if comp == 0:
-                curl = (hz - self.prev_y(hz))[:height] - (hy[:height] - self.prev_z(hy[:height]))
+                curl = (hz - self.prev_y(hz))[here] - (hy[here] - self.prev_z(hy[here]))
             elif comp == 1:
                 hz_x = self.get(hfield, run, part, 2, x - 1)
-                curl = (hx[:height] - self.prev_z(hx[:height])) - (hz - hz_x)[:height]
+                curl = (hx[here] - self.prev_z(hx[here])) - (hz - hz_x)[here]
             else:
                 hy_x = self.get(hfield, run, part, 1, x - 1)
-                curl = (hy - hy_x)[:height] - (hx - self.prev_y(hx))[:height]
-            before = self.get(old, run, part, comp, x)[:height]
-            new[self.rows(run, part, comp, x, height), :] = before + scale[:height] * curl
+                curl = (hy - hy_x)[here] - (hx - self.prev_y(hx))[here]
+            before = self.get(old, run, part, comp, x)[here]
+            new[self.rows(run, part, comp, x, start, stop), :] = before + scale[here] * curl
 
     def both(self, step, h_layers, e_layers, after_h=None, after_e=None, runs=(0, 1)):
         for update, layers, after in ((self.update_h, h_layers, after_h), (self.update_e, e_layers, after_e)):
@@ -315,7 +339,7 @@
         unpack(plan, plan.y_high, z_high, lambda y: 3, turns, state, kinds, level)
 
     take("EHC", 0)
-    sweeps = Sweeps(plan, efield, hfield, coef, plan.ring)
+    sweeps = Sweeps(plan, efield, hfield, coef, plan.ring, plan.made)
     for step in range(1, STEPS + 1):
         after = [lambda: take("H", 1), lambda: take("E", 1)] if step == 1 else []
         sweeps.both(step, range(step - 1, nx - step), range(step, nx - step), *after)
@@ -330,34 +354,53 @@
                 for run in (0, 1):
                     at = [pl.ds(((part * 3 + comp) * nx + x) * ny + tile * SUB, SUB) for part in (0, 1)]
                     real, imag = transform[run][at[0], :], transform[run][at[1], :]
-                    for level in levels(x):
+                    for level in levels(x, tile, comp):
                         theta = omega_step * level
                         here = [efield[level][pl.ds(plan.row(x, tile * SUB, run, part, comp), SUB), :] for part in (0, 1)]
                         more = turned(*here, math.cos(theta), math.sin(theta))
                         real, imag = real + more[0], imag + more[1]
                     out[run][at[0], :], out[run][at[1], :] = real, imag
                     ends.append((real, imag))
-                yield x, tile, comp, ends
-
-
-def known(plan, x):
-    return [level for level in range(1, STEPS + 1) if level <= x < plan.nx - level]
+                yield x, tile, ends
+
+
+def known(plan, x, tile, comp):
+    def ready(level):
+        return level <= x < plan.nx - level or tile in plan.free.get(("E", level, x), {}).get(comp, ())
+
+    return [level for level in range(1, STEPS + 1) if ready(level)]
+
+
+def do_valleys(plan, sweeps, take):
+    for step in range(1, STEPS + 1):
+        low, high = step - STEPS, plan.nx - step
+        h_layers = [*range(low - 1, step - 1), *range(high, plan.nx + STEPS - step)]
+        e_layers = [*range(low, step), *range(high, plan.nx + STEPS - step)]
+        after = [functools.partial(take, "H", 1, h_layers), functools.partial(take, "E", 1, e_layers)] if step == 1 else []
+        sweeps.both(step, h_layers, e_layers, *after)
 
 
 def faces_kernel(plan, *refs):
-    efield, hfield, coef = refs[: STEPS + 1], refs[STEPS + 1], refs[STEPS + 2]
-    x_low, x_high, turns, spec_f, spec_a = refs[STEPS + 3 : STEPS + 8]
-    *_, out_f, out_a = refs
-    e0, h0, coef = refs[STEPS + 8 : STEPS + 11]
-    state = State([e0], [h0], coef)
-    unpack(plan, plan.x_low, x_low, lambda y: 0, turns, state, "EHC", 0)
-    unpack(plan, plan.x_high, x_high, lambda y: 1, turns, state, "EHC", 0)
+    count = 2 * STEPS + 3
+    x_low, x_high, z_low, z_high, turns, spec_f, spec_a = refs[count : count + 7]
+    arrays = refs[count + 7 : 2 * count + 7]
+    out_f, out_a = refs[2 * count + 7 :]
+    efield, hfield, coef = arrays[: STEPS + 1], arrays[STEPS + 1 : 2 * STEPS + 2], arrays[-1]
+    state = State(efield, hfield, coef)
+
+    def take(kinds, level, layers):
+        unpack(plan, plan.x_low, x_low, lambda y: 0, turns, state, kinds, level)
+        unpack(plan, plan.x_high, x_high, lambda y: 1, turns, state, kinds, level)
+        unpack(plan, plan.y_low, z_low, lambda y: 2, turns, state, kinds, level, layers)
+        unpack(plan, plan.y_high, z_high, lambda y: 3, turns, state, kinds, level, layers)
+
+    take("EHC", 0, ())
+    do_valleys(plan, Sweeps(plan, efield, hfield, coef, plan.ring, plan.free), take)
     for _ in add_known(plan, efield, functools.partial(known, plan), (spec_f, spec_a), (out_f, out_a)):
         pass
 
 
 def edges_kernel(plan, groups, *refs):
-    nx, ny = plan.nx, plan.ny
     count = 2 * STEPS + 3
     x_low, x_high, far, mate, z_low, z_high, turns, part_f, part_a = refs[count : count + 9]
     arrays = refs[count + 9 : 2 * count + 9]
@@ -365,7 +408,7 @@
     efield, hfield, coef = arrays[: STEPS + 1], arrays[STEPS + 1 : 2 * STEPS + 2], arrays[-1]
     state = State(efield, hfield, coef)
 
-    def take(kinds, level, layers=()):
+    def take(kinds, level, layers):
         if level:
             unpack(plan, plan.x_low, x_low, lambda y: 0, turns, state, kinds, level)
             unpack(plan, plan.x_high, x_high, lambda y: 1, turns, state, kinds, level)
@@ -379,26 +422,18 @@
         unpack(plan, plan.y_low, z_low, lambda y: 2, turns, state, kinds, level, layers)
         unpack(plan, plan.y_high, z_high, lambda y: 3, turns, state, kinds, level, layers)
 
-    take("EHC", 0)
-    sweeps = Sweeps(plan, efield, hfield, coef, plan.ring)
-    for step in range(1, STEPS + 1):
-        low, high = step - STEPS, nx - step
-        h_layers = [*range(low - 1, step - 1), *range(high, nx + STEPS - step)]
-        e_layers = [*range(low, step), *range(high, nx + STEPS - step)]
-        after = []
-        if step == 1:
-            after = [functools.partial(take, "H", 1, h_layers), functools.partial(take, "E", 1, e_layers)]
-        sweeps.both(step, h_layers, e_layers, *after)
+    take("EHC", 0, ())
+    do_valleys(plan, Sweeps(plan, efield, hfield, coef, plan.ring, plan.rest), take)
 
     share = plan.depth // groups
     shift = lax.rem(groups - lax.axis_index("angle"), groups) * share
     weight = turns[pl.ds(2 * SUB, SUB), :]
 
-    def rest(x):
-        return [level for level in range(1, STEPS + 1) if level not in known(plan, x)]
+    def rest(x, tile, comp):
+        return [level for level in range(1, STEPS + 1) if level not in known(plan, x, tile, comp)]
 
     totals = {}
-    for x, tile, _, ends in add_known(plan, efield, rest, (part_f, part_a), (out_f, out_a)):
+    for x, tile, ends in add_known(plan, efield, rest, (part_f, part_a), (out_f, out_a)):
         term = ends[0][0] * ends[1][0] - ends[0][1] * ends[1][1]
         totals[x, tile] = totals[x, tile] + term if (x, tile) in totals else term
     block = lax.broadcasted_iota(jnp.int32, weight.shape, 1) // share
@@ -541,16 +576,15 @@
     transforms = [lines(6 * nx * ny)] * 2
     with jax.named_scope("faces"):
         spectra = [spectrum.reshape((-1, depth)) for spectrum in (forward_spectrum, adjoint_spectrum)]
-        e0, h0, coef, *sums = pl.pallas_call(
+        results = pl.pallas_call(
             functools.partial(faces_kernel, plan),
-            out_shape=[level, level, levels[-1], *transforms],
-            in_specs=[VMEM] * (STEPS + 8),
-            out_specs=[VMEM] * 5,
-            input_output_aliases={0: 0, STEPS + 1: 1, STEPS + 2: 2},
+            out_shape=[*levels, *transforms],
+            in_specs=[VMEM] * (count + 7),
+            out_specs=[VMEM] * (count + 2),
+            input_output_aliases={i: i for i in range(count)},
             compiler_params=params(8),
-            cost_estimate=cost(2**10),
-        )(*state[: STEPS + 2], state[-1], x_low, x_high, turns, *spectra)
-        state = [e0, *state[1 : STEPS + 1], h0, *state[STEPS + 2 : -1], coef]
+        )(*state, x_low, x_high, z_low, z_high, turns, *spectra)
+        state, sums = results[:count], results[count:]
     with jax.named_scope("edges"):
         results = pl.pallas_call(
             functools.partial(edges_kernel, plan, groups),

time: 27 us -> 26.6 us (0.985)
  waiting for transfers between devices: 8.45 us -> 7.88 us
    ppermute x1, waiting for transfers between devices: 1.32 us -> 0.75 us  [shards(): far = lax.ppermute(to_far, 'gx', far_pairs())]
    pallas_call x1, Pallas kernels: 0.25 us -> 0.78 us  [shards(): pl.pallas_call(functools.partial(faces_kernel, plan), out_shape=[*levels,...]
    pallas_call x1, Pallas kernels: 1.91 us -> 1.5 us  [shards(): pl.pallas_call(functools.partial(edges_kernel, plan, groups), out_shape=[...]
  transfers between devices with their start and end apart: 7 -> 7, of which waited for: 3 -> 3; matrix products, arithmetic and copies ran while one was open for 0% -> 0% of each run, Pallas kernels for 12% -> 14%
where the time goes in v11:
time: 26.6 us; the launch traced here: 26.4 us
  starting transfers between devices  9.12 us (34%)
  Pallas kernels  8 us (30%)
  waiting for transfers between devices  7.88 us (30%)
  between operations  1.37 us (5%)
    ppermute x1, waiting for transfers between devices, shards(): z_high = lax.ppermute(z_down, 'gy', ring_pairs('gy', -1))  5.67 us
    ppermute x1, starting transfers between devices, shards(): z_low = lax.ppermute(z_up, 'gy', ring_pairs('gy', 1))  3.08 us
    ppermute x1, starting transfers between devices, shards(): z_high = lax.ppermute(z_down, 'gy', ring_pairs('gy', -1))  2.09 us
    pallas_call x1, Pallas kernels, shards(): pl.pallas_call(functools.partial(pack_y_kernel, plan), out_shape=(*[array...  1.99 us
    ppermute x1, starting transfers between devices, shards(): lax.ppermute(part, 'angle', ring_pairs('angle', k + 1))  1.52 us
    pallas_call x1, Pallas kernels, shards(): pl.pallas_call(functools.partial(edges_kernel, plan, groups), out_shape=[...  1.5 us
    ppermute x1, waiting for transfers between devices, shards(): lax.ppermute(part, 'angle', ring_pairs('angle', k + 1))  1.45 us
    pallas_call x1, Pallas kernels, shards(): pl.pallas_call(functools.partial(middle_kernel, plan), out_shape=levels,...  1.27 us
  transfers between devices with their start and end apart: 7, of which 3 were waited for; matrix products, arithmetic and copies ran while one was open for 0% of the time, Pallas kernels for 14%

profile of v11, /device:TPU:0, one launch (start us, length us, event | category | flops | bytes accessed | tf_op | source)
XLA Modules:
  0.0 26.4 jit_solution(9251825097127470448)
XLA Ops:
  0.6 2.0 %pack_y.1 = (f32[12,14,24,128]{3,2,1,0:T(8,128)S(1)}, f32[12,14,24,128]{3,2,1,0:T(8,128)S(1)}, f32[12,14,24,128]{3,2,1,0:T(8,128)S(1)}, f32[12,14,24,128]{3,2,1,...) custom-call(f32[12,8,16,128]{3,2,1,0:T(8,128)} %bitcast.28, ...), custom_call_target="tpu_custom_call" | custom-call | tf_op jit(solution)/shard_map/pack_y/pallas_call | solution.py:516
  2.6 3.1 %collective-permute-start = (f32[400,128]{1,0:T(8,128)S(1)}, f32[400,128]{1,0:T(8,128)S(1)}, u32[]{:S(2)}, u32[]{:S(2)}) collective-permute-start(f32[400,128]{1,0:T(8,128)S(1)} %get-tuple-element.45), channel_id=1, source_target_pairs={{0,1},{1,2},{2,3},{3,0},{4,5},{5,6},{6,7},{7,4},{8,9},{9,10},{10,1... | collective-permute-start | bytes 614408 | tf_op jit(solution)/shard_map/send_y/ppermute | solution.py:531
  5.7 2.1 %collective-permute-start.1 = (f32[304,128]{1,0:T(8,128)S(1)}, f32[304,128]{1,0:T(8,128)S(1)}, u32[]{:S(2)}, u32[]{:S(2)}) collective-permute-start(f32[304,128]{1,0:T(8,128)S(1)} %get-tuple-element.46), channel_id=1, source_target_pairs={{0,3},{1,0},{2,1},{3,2},{4,7},{5,4},{6,5},{7,6},{8,11},{9,8},{10,9... | collective-permute-start | bytes 466952 | tf_op jit(solution)/shard_map/send_y/ppermute | solution.py:532
  7.8 0.0 copy-start.2
  7.8 0.0 copy-start.3
  7.8 0.1 pack_x.1
  7.9 0.7 %collective-permute-start.3 = (f32[568,128]{1,0:T(8,128)S(1)}, f32[568,128]{1,0:T(8,128)S(1)}, u32[]{:S(2)}, u32[]{:S(2)}) collective-permute-start(f32[568,128]{1,0:T(8,128)S(1)} %get-tuple-element.57), channel_id=1, source_target_pairs={{0,12},{4,0},{8,4},{12,8},{1,13},{5,1},{9,5},{13,9},{2,14},{6,2},{... | collective-permute-start | bytes 872456 | tf_op jit(solution)/shard_map/send_x/ppermute | solution.py:544
  8.6 0.0 collective-permute-start.2
  9.3 0.0 copy-done.2
  9.3 0.0 copy-done.3
  9.3 0.6 %turns.1.refs_13_.refs_15_ = f32[24,128]{1,0:T(8,128)S(1)} custom-call(f32[2,2]{1,0:T(2,128)S(1)} %copy-done.2, s32[1]{0:T(128)S(6)} %copy.61.index, s32[4]{0:T(128)S(1)} %copy-done.3), custom_call_target="tpu_custom_call" | custom-call | tf_op jit(solution)/shard_map/turns/pallas_call | solution.py:546
  9.9 5.7 %collective-permute-done.1.z_high.refs_12_.refs_14_ = f32[304,128]{1,0:T(8,128)S(1)} collective-permute-done((f32[304,128]{1,0:T(8,128)S(1)}, f32[304,128]{1,0:T(8,128)S(1)}, u32[]{:S(2)}, u32[]{:S(2)}) %collective-permute-start.1) | collective-permute-done | bytes 155680 | tf_op jit(solution)/shard_map/send_y/ppermute | solution.py:532
  15.6 0.0 collective-permute-done.z_low.refs_11_.refs_13_
  15.6 0.1 relay_corners.1
  15.7 0.6 %collective-permute-start.4 = (f32[144,128]{1,0:T(8,128)S(1)}, f32[144,128]{1,0:T(8,128)S(1)}, u32[]{:S(2)}, u32[]{:S(2)}) collective-permute-start(f32[144,128]{1,0:T(8,128)S(1)} %get-tuple-element.67), channel_id=1, source_target_pairs={{0,12},{4,8},{8,4},{12,0},{1,13},{5,9},{9,5},{13,1},{2,14},{6,10},... | collective-permute-start | bytes 221192 | tf_op jit(solution)/shard_map/relay_corners/ppermute | solution.py:561
  16.3 0.0 copy-start
  16.3 0.0 copy-start.1
  16.3 1.1 %collective-permute-start.5 = (f32[144,128]{1,0:T(8,128)S(1)}, f32[144,128]{1,0:T(8,128)S(1)}, u32[]{:S(2)}, u32[]{:S(2)}) collective-permute-start(f32[144,128]{1,0:T(8,128)S(1)} %get-tuple-element.68), channel_id=1, source_target_pairs={{0,4},{4,0},{8,12},{12,8},{1,5},{5,1},{9,13},{13,9},{2,6},{6,2},{1... | collective-permute-start | bytes 221192 | tf_op jit(solution)/shard_map/relay_corners/ppermute | solution.py:562
  17.4 1.3 %middle.1 = (f32[4032,128]{1,0:T(8,128)S(1)}, f32[4032,128]{1,0:T(8,128)S(1)}, f32[4032,128]{1,0:T(8,128)S(1)}, f32[4032,128]{1,0:T(8,128)S(1)}, f32[4032,128]{1...) custom-call(f32[4032,128]{1,0:T(8,128)S(1)} %bitcast.15, ...), custom_call_target="tpu_custom_call", output_to_operand_aliasing={{0}: (0, {}), {4}: (1, {}), {1}: (2, {}), {5}: (3, {}), {8}... | custom-call | flops 4294967296 | bytes 4294967296 | tf_op jit(solution)/shard_map/middle/pallas_call | solution.py:567
  18.7 0.0 collective-permute-done.3.refs_10_
  18.7 0.0 collective-permute-done.2.refs_9_
  18.7 0.0 copy-done
  18.7 0.0 copy-done.1
  18.7 0.8 %faces.1 = (f32[4032,128]{1,0:T(8,128)S(1)}, f32[4032,128]{1,0:T(8,128)S(1)}, f32[4032,128]{1,0:T(8,128)S(1)}, f32[4032,128]{1,0:T(8,128)S(1)}, f32[4032,128]{1,...) custom-call(f32[4032,128]{1,0:T(8,128)S(1)} %get-tuple-element.47.re, ...), custom_call_target="tpu_custom_call", output_to_operand_aliasing={{0}: (0, {}), {1}: (1, {}), {2}: (2, {}), {3}: (3, {}), {4}... | custom-call | tf_op jit(solution)/shard_map/faces/pallas_call | solution.py:579
  19.5 0.8 %collective-permute-done.4.refs_11_ = f32[144,128]{1,0:T(8,128)S(1)} collective-permute-done((f32[144,128]{1,0:T(8,128)S(1)}, f32[144,128]{1,0:T(8,128)S(1)}, u32[]{:S(2)}, u32[]{:S(2)}) %collective-permute-start.4) | collective-permute-done | bytes 73760 | tf_op jit(solution)/shard_map/relay_corners/ppermute | solution.py:561
  20.2 0.0 collective-permute-done.5.refs_12_
  20.2 1.5 %edges.1 = (f32[4032,128]{1,0:T(8,128)S(1)}, f32[4032,128]{1,0:T(8,128)S(1)}, f32[4032,128]{1,0:T(8,128)S(1)}, f32[4032,128]{1,0:T(8,128)S(1)}, f32[4032,128]{1,...) custom-call(f32[4032,128]{1,0:T(8,128)S(1)} %get-tuple-element.58.re, ...), custom_call_target="tpu_custom_call", output_to_operand_aliasing={{0}: (0, {}), {1}: (1, {}), {2}: (2, {}), {3}: (3, {}), {4}... | custom-call | tf_op jit(solution)/shard_map/edges/pallas_call | solution.py:589
  21.7 1.5 %collective-permute-start.6 = (f32[64,128]{1,0:T(8,128)S(1)}, f32[64,128]{1,0:T(8,128)S(1)}, u32[]{:S(2)}, u32[]{:S(2)}) collective-permute-start(f32[64,128]{1,0:T(8,128)S(1)} %get-tuple-element.76), channel_id=1, source_target_pairs={{0,16},{16,0},{1,17},{17,1},{2,18},{18,2},{3,19},{19,3},{4,20},{20... | collective-permute-start | bytes 98312 | tf_op jit(solution)/shard_map/sum_angles/ppermute | solution.py:599
  23.3 1.0 %write.1 = (f32[6,8,16,128]{3,2,1,0:T(8,128)}, f32[6,8,16,128]{3,2,1,0:T(8,128)}) custom-call(f32[6,8,16,128]{3,2,1,0:T(8,128)S(1)} %bitcast.22, f32[6,8,16,128]{3,2,1,0:T(8,128)S(1)} %bitcast.23), custom_call_target="tpu_custom_call" | custom-call | tf_op jit(solution)/shard_map/write/pallas_call | solution.py:608
  24.2 1.4 %collective-permute-done.6.refs_1_ = f32[64,128]{1,0:T(8,128)S(1)} collective-permute-done((f32[64,128]{1,0:T(8,128)S(1)}, f32[64,128]{1,0:T(8,128)S(1)}, u32[]{:S(2)}, u32[]{:S(2)}) %collective-permute-start.6) | collective-permute-done | bytes 32800 | tf_op jit(solution)/shard_map/sum_angles/ppermute | solution.py:599
  25.7 0.7 %sum_angles.1 = f32[128,64]{1,0:T(8,128)} custom-call(f32[64,128]{1,0:T(8,128)S(1)} %get-tuple-element.75.refs_0_, f32[64,128]{1,0:T(8,128)S(1)} %collective-permute-done.6.refs_1_), custom_call_target="tpu_custom_call" | custom-call | tf_op jit(solution)/shard_map/sum_angles/pallas_call | solution.py:600
Async XLA Ops:
  2.6 13.0 %collective-permute-start = (f32[400,128]{1,0:T(8,128)S(1)}, f32[400,128]{1,0:T(8,128)S(1)}, u32[]{:S(2)}, u32[]{:S(2)}) collective-permute-start(f32[400,128]{1,0:T(8,128)S(1)} %get-tuple-element.45), channel_id=1, source_target_pairs={{0,1},{1,2},{2,3},{3,0},{4,5},{5,6},{6,7},{7,4},{8,9},{9,10},{10,1... | collective-permute-start | bytes 614408 | tf_op jit(solution)/shard_map/send_y/ppermute | solution.py:531
  5.7 9.9 %collective-permute-start.1 = (f32[304,128]{1,0:T(8,128)S(1)}, f32[304,128]{1,0:T(8,128)S(1)}, u32[]{:S(2)}, u32[]{:S(2)}) collective-permute-start(f32[304,128]{1,0:T(8,128)S(1)} %get-tuple-element.46), channel_id=1, source_target_pairs={{0,3},{1,0},{2,1},{3,2},{4,7},{5,4},{6,5},{7,6},{8,11},{9,8},{10,9... | collective-permute-start | bytes 466952 | tf_op jit(solution)/shard_map/send_y/ppermute | solution.py:532
  7.8 1.5 %copy-start.2 = (f32[2,2]{1,0:T(2,128)S(1)}, f32[2,2]{1,0:T(2,128)}, u32[]{:S(2)}) copy-start(f32[2,2]{1,0:T(2,128)} %table.1) | copy-start | bytes 52
  7.8 1.5 %copy-start.3 = (s32[4]{0:T(128)S(1)}, s32[4]{0:T(128)}, u32[]{:S(2)}) copy-start(s32[4]{0:T(128)} %tiles.1) | copy-start | bytes 52
  7.9 10.8 %collective-permute-start.3 = (f32[568,128]{1,0:T(8,128)S(1)}, f32[568,128]{1,0:T(8,128)S(1)}, u32[]{:S(2)}, u32[]{:S(2)}) collective-permute-start(f32[568,128]{1,0:T(8,128)S(1)} %get-tuple-element.57), channel_id=1, source_target_pairs={{0,12},{4,0},{8,4},{12,8},{1,13},{5,1},{9,5},{13,9},{2,14},{6,2},{... | collective-permute-start | bytes 872456 | tf_op jit(solution)/shard_map/send_x/ppermute | solution.py:544
  8.6 10.0 %collective-permute-start.2 = (f32[760,128]{1,0:T(8,128)S(1)}, f32[760,128]{1,0:T(8,128)S(1)}, u32[]{:S(2)}, u32[]{:S(2)}) collective-permute-start(f32[760,128]{1,0:T(8,128)S(1)} %get-tuple-element.56), channel_id=1, source_target_pairs={{0,4},{4,8},{8,12},{12,0},{1,5},{5,9},{9,13},{13,1},{2,6},{6,10},{... | collective-permute-start | bytes 1167368 | tf_op jit(solution)/shard_map/send_x/ppermute | solution.py:543
  15.7 4.6 %collective-permute-start.4 = (f32[144,128]{1,0:T(8,128)S(1)}, f32[144,128]{1,0:T(8,128)S(1)}, u32[]{:S(2)}, u32[]{:S(2)}) collective-permute-start(f32[144,128]{1,0:T(8,128)S(1)} %get-tuple-element.67), channel_id=1, source_target_pairs={{0,12},{4,8},{8,4},{12,0},{1,13},{5,9},{9,5},{13,1},{2,14},{6,10},... | collective-permute-start | bytes 221192 | tf_op jit(solution)/shard_map/relay_corners/ppermute | solution.py:561
  16.3 2.4 %copy-start = (f32[1,6,8,16,128]{4,3,2,1,0:T(8,128)S(1)}, f32[1,6,8,16,128]{4,3,2,1,0:T(8,128)}, u32[]{:S(2)}) copy-start(f32[1,6,8,16,128]{4,3,2,1,0:T(8,128)} %param.10) | copy-start | bytes 1179652
  16.3 2.4 %copy-start.1 = (f32[1,6,8,16,128]{4,3,2,1,0:T(8,128)S(1)}, f32[1,6,8,16,128]{4,3,2,1,0:T(8,128)}, u32[]{:S(2)}) copy-start(f32[1,6,8,16,128]{4,3,2,1,0:T(8,128)} %param.11) | copy-start | bytes 1179652
  16.3 4.0 %collective-permute-start.5 = (f32[144,128]{1,0:T(8,128)S(1)}, f32[144,128]{1,0:T(8,128)S(1)}, u32[]{:S(2)}, u32[]{:S(2)}) collective-permute-start(f32[144,128]{1,0:T(8,128)S(1)} %get-tuple-element.68), channel_id=1, source_target_pairs={{0,4},{4,0},{8,12},{12,8},{1,5},{5,1},{9,13},{13,9},{2,6},{6,2},{1... | collective-permute-start | bytes 221192 | tf_op jit(solution)/shard_map/relay_corners/ppermute | solution.py:562
  21.7 3.9 %collective-permute-start.6 = (f32[64,128]{1,0:T(8,128)S(1)}, f32[64,128]{1,0:T(8,128)S(1)}, u32[]{:S(2)}, u32[]{:S(2)}) collective-permute-start(f32[64,128]{1,0:T(8,128)S(1)} %get-tuple-element.76), channel_id=1, source_target_pairs={{0,16},{16,0},{1,17},{17,1},{2,18},{18,2},{3,19},{19,3},{4,20},{20... | collective-permute-start | bytes 98312 | tf_op jit(solution)/shard_map/sum_angles/ppermute | solution.py:599

commit v12 on v11

--- a/solution.py
+++ b/solution.py
@@ -63,8 +63,11 @@
 
 
 class Message:
-    def __init__(self, nodes, axis):
+    def __init__(self, nodes, axis, folded=()):
         self.axis, self.runs, self.at, self.size = axis, [], {}, 0
+        assert nodes.issuperset(folded)
+        self.zeros = Message(set(folded), axis).runs if folded else []
+        nodes = nodes - set(folded)
         stretches = []
         for node in sorted(nodes):
             before = list(node)
@@ -117,10 +120,13 @@
         def shifted(found, dx):
             return {(*node[:3], node[3] + dx, node[4]) for node in found}
 
-        self.y_low, self.y_high = (
-            Message(sides[0, side] | shifted(sides[-1, side], nx) | shifted(sides[1, side], -nx), 0) for side in (-1, 1)
-        )
-        self.x_low, self.x_high = Message(sides[-1, 0], 1), Message(sides[1, 0], 1)
+        y_low, y_high = (sides[0, side] | shifted(sides[-1, side], nx) | shifted(sides[1, side], -nx) for side in (-1, 1))
+        self.x_folds = (1, ny - 2), (2, ny - 2)
+        self.y_folds = (2, nx - 2), (3, nx - 2)
+        x_folded = [("E", 1, comp, -2, y) for comp in range(3) for y in range(*self.x_folds[comp == 0])]
+        y_folded = [("E", 1, comp, x, -2) for comp in range(3) for x in range(*self.y_folds[comp == 1])]
+        self.y_low, self.y_high = Message(y_low, 0, y_folded), Message(y_high, 0)
+        self.x_low, self.x_high = Message(sides[-1, 0], 1, x_folded), Message(sides[1, 0], 1)
         self.mate_side, self.far_side = (1, -1), (-1, 1)
         self.mate, self.far = ([Message(sides[side, -1] | sides[side, 1], 1) for side in order] for order in (self.mate_side, self.far_side))
         self.corner_lines = max(message.lines for message in self.mate)
@@ -142,9 +148,59 @@
         return self.by_kind[what[0]][what[1]]
 
 
-def pack(plan, message, state, dx, dy, out):
+def pack(plan, message, state, dx, dy, out, changed=None):
     for what, x, y, count, at in message.runs:
-        out[pl.ds(at, count), :] = state(what)[plan.rows(what, x + dx, y + dy, message.axis, count), :]
+        layer, first = (y, x) if message.axis == 0 else (x, y)
+        if changed and (what, layer) in changed:
+            ref, row = changed[what, layer]
+            value = ref[pl.ds(row + first, count), :]
+        else:
+            value = state(what)[plan.rows(what, x + dx, y + dy, message.axis, count), :]
+        out[pl.ds(at, count), :] = value
+
+
+def fold(plan, state, axis, scratch):
+    nx, ny = plan.nx, plan.ny
+    size, normal = (nx, 1) if axis == 0 else (ny, 0)
+    before, after = ((0, 2) if axis == 0 else (1, 2))
+    cell = lax.broadcasted_iota(jnp.int32, (size, scratch.shape[1]), 0)
+    lane = lax.broadcasted_iota(jnp.int32, cell.shape, 1)
+    folds = plan.y_folds if axis == 0 else plan.x_folds
+    changed = {}
+
+    def lines(what, layer):
+        place = (0, ny + layer) if axis == 0 else (nx + layer, 0)
+        return state(what)[plan.rows(what, *place, axis, size), :]
+
+    def inside(value, fold):
+        return jnp.where((cell >= fold[0]) & (cell < fold[1]), value, 0.0)
+
+    for run in (0, 1):
+        for part in (0, 1):
+
+            def get(kind, level, comp, layer):
+                return lines((kind, level, comp, run, part), layer)
+
+            def put(kind, level, comp, layer, value):
+                row = len(changed) * size
+                scratch[pl.ds(row, size), :] = value
+                changed[(kind, level, comp, run, part), layer] = scratch, row
+
+            low, high = (inside(get("E", 1, comp, -2), folds[0]) for comp in (before, after))
+            along = inside(get("E", 1, normal, -2), folds[1])
+            along_z = jnp.where(lane == lane.shape[1] - 1, 0.0, pltpu.roll(along, lane.shape[1] - 1, 1)) - along
+            along_next = pltpu.roll(along, size - 1, 0) - along
+            sign = 1.0 if axis == 0 else -1.0
+            d_before = sign * (high + along_z)
+            d_after = -sign * (low + along_next)
+            scale = lines(("C", 0, 0, 0, 0), -1)
+            put("H", 1, before, -2, get("H", 1, before, -2) + d_before)
+            put("H", 1, after, -2, get("H", 1, after, -2) + d_after)
+            put("E", 0, before, -1, get("E", 0, before, -1) + sign * scale * d_after)
+            put("E", 0, after, -1, get("E", 0, after, -1) - sign * scale * d_before)
+            put("H", 0, before, -1, get("H", 0, before, -1) + 0.5 * scale * d_before)
+            put("H", 0, after, -1, get("H", 0, after, -1) + 0.5 * scale * d_after)
+    return changed
 
 
 def by_parity(offset, body):
@@ -153,7 +209,7 @@
         pl.when(parity == value)(functools.partial(body, value))
 
 
-def pack_y_kernel(plan, fwd, adj, eps, e0, h0, e1, h1, coef, z_up, z_down, sems):
+def pack_y_kernel(plan, fwd, adj, eps, e0, h0, e1, h1, coef, z_up, z_down, sems, scratch):
     nx, ny = plan.nx, plan.ny
     own = (pl.ds(STEPS, nx), pl.ds(0, ny), slice(None))
     copies = [pltpu.make_async_copy(eps, coef.at[own], sems.at[0])]
@@ -175,13 +231,13 @@
             copy.wait()
         sweeps.both(1, range(nx), range(nx - 1), runs=(run,))
     state = State([e0, e1], [h0, h1], coef)
-    pack(plan, plan.y_low, state, 0, ny, z_up)
+    pack(plan, plan.y_low, state, 0, ny, z_up, fold(plan, state, 0, scratch))
     pack(plan, plan.y_high, state, 0, -ny, z_down)
 
 
-def pack_x_kernel(plan, e0, h0, e1, h1, coef, x_up, x_down):
+def pack_x_kernel(plan, e0, h0, e1, h1, coef, x_up, x_down, scratch):
     state = State([e0, e1], [h0, h1], coef)
-    pack(plan, plan.x_low, state, plan.nx, 0, x_up)
+    pack(plan, plan.x_low, state, plan.nx, 0, x_up, fold(plan, state, 1, scratch))
     pack(plan, plan.x_high, state, -plan.nx, 0, x_down)
 
 
@@ -245,6 +301,9 @@
             real, imag = turned(real, imag, cosine, sine if run == 0 else -sine)
             state(what)[plan.rows(what, cell_x, cell_y, axis, size), :] = real
             state(twin)[plan.rows(twin, cell_x, cell_y, axis, size), :] = imag
+    for what, x, y, count, _ in message.zeros:
+        if what[0] in kinds and what[1] == level and layers is None:
+            state(what)[plan.rows(what, x, y, axis, count), :] = jnp.zeros((count, ref.shape[1]), jnp.float32)
 
 
 class Sweeps:
@@ -523,7 +582,7 @@
             ),
             in_specs=[HBM] * 3,
             out_specs=[VMEM] * 7,
-            scratch_shapes=[pltpu.SemaphoreType.DMA((25,))],
+            scratch_shapes=[pltpu.SemaphoreType.DMA((25,)), pltpu.VMEM((24 * nx, depth), jnp.float32)],
             compiler_params=params(8),
         )(*(pltpu.with_memory_space_constraint(array, pltpu.HBM) for array in (forward_fields[0], adjoint_fields[0], permittivity)))
     e0, h0, e1, h1, coef = (state.reshape((-1, depth)) for state in (*first, coef))
@@ -536,6 +595,7 @@
             out_shape=(lines(plan.x_low.lines), lines(plan.x_high.lines)),
             in_specs=[VMEM] * 5,
             out_specs=[VMEM] * 2,
+            scratch_shapes=[pltpu.VMEM((24 * ny, depth), jnp.float32)],
             compiler_params=params(8),
             cost_estimate=cost(40 * 2**20),
         )(e0, h0, e1, h1, coef)

time: 26.6 us -> 26.2 us (0.985)
  waiting for transfers between devices: 7.88 us -> 7.48 us
    ppermute x1, waiting for transfers between devices: 5.67 us -> 5.21 us  [shards(): z_high = lax.ppermute(z_down, 'gy', ring_pairs('gy', -1))]
where the time goes in v12:
time: 26.2 us; the launch traced here: 26 us
  starting transfers between devices  9.12 us (35%)
  Pallas kernels  7.98 us (30%)
  waiting for transfers between devices  7.48 us (29%)
  between operations  1.37 us (5%)
    ppermute x1, waiting for transfers between devices, shards(): z_high = lax.ppermute(z_down, 'gy', ring_pairs('gy', -1))  5.21 us
    ppermute x1, starting transfers between devices, shards(): z_low = lax.ppermute(z_up, 'gy', ring_pairs('gy', 1))  3.08 us
    ppermute x1, starting transfers between devices, shards(): z_high = lax.ppermute(z_down, 'gy', ring_pairs('gy', -1))  2.09 us
    pallas_call x1, Pallas kernels, shards(): pl.pallas_call(functools.partial(pack_y_kernel, plan), out_shape=(*[array...  2.02 us
    ppermute x1, starting transfers between devices, shards(): lax.ppermute(part, 'angle', ring_pairs('angle', k + 1))  1.51 us
    pallas_call x1, Pallas kernels, shards(): pl.pallas_call(functools.partial(edges_kernel, plan, groups), out_shape=[...  1.49 us
    ppermute x1, waiting for transfers between devices, shards(): lax.ppermute(part, 'angle', ring_pairs('angle', k + 1))  1.45 us
    pallas_call x1, Pallas kernels, shards(): pl.pallas_call(functools.partial(middle_kernel, plan), out_shape=levels,...  1.23 us
  transfers between devices with their start and end apart: 7, of which 3 were waited for; matrix products, arithmetic and copies ran while one was open for 0% of the time, Pallas kernels for 14%

profile of v12, /device:TPU:0, one launch (start us, length us, event | category | flops | bytes accessed | tf_op | source)
XLA Modules:
  0.0 26.0 jit_solution(335125406013787444)
XLA Ops:
  0.6 2.0 %pack_y.1 = (f32[12,14,24,128]{3,2,1,0:T(8,128)S(1)}, f32[12,14,24,128]{3,2,1,0:T(8,128)S(1)}, f32[12,14,24,128]{3,2,1,0:T(8,128)S(1)}, f32[12,14,24,128]{3,2,1,...) custom-call(f32[12,8,16,128]{3,2,1,0:T(8,128)} %bitcast.28, ...), custom_call_target="tpu_custom_call" | custom-call | tf_op jit(solution)/shard_map/pack_y/pallas_call | solution.py:575
  2.7 3.1 %collective-permute-start = (f32[360,128]{1,0:T(8,128)S(1)}, f32[360,128]{1,0:T(8,128)S(1)}, u32[]{:S(2)}, u32[]{:S(2)}) collective-permute-start(f32[360,128]{1,0:T(8,128)S(1)} %get-tuple-element.45), channel_id=1, source_target_pairs={{0,1},{1,2},{2,3},{3,0},{4,5},{5,6},{6,7},{7,4},{8,9},{9,10},{10,1... | collective-permute-start | bytes 552968 | tf_op jit(solution)/shard_map/send_y/ppermute | solution.py:590
  5.7 2.1 %collective-permute-start.1 = (f32[304,128]{1,0:T(8,128)S(1)}, f32[304,128]{1,0:T(8,128)S(1)}, u32[]{:S(2)}, u32[]{:S(2)}) collective-permute-start(f32[304,128]{1,0:T(8,128)S(1)} %get-tuple-element.46), channel_id=1, source_target_pairs={{0,3},{1,0},{2,1},{3,2},{4,7},{5,4},{6,5},{7,6},{8,11},{9,8},{10,9... | collective-permute-start | bytes 466952 | tf_op jit(solution)/shard_map/send_y/ppermute | solution.py:591
  7.8 0.0 copy-start.2
  7.8 0.0 copy-start.3
  7.8 0.1 pack_x.1
  8.0 0.7 %collective-permute-start.3 = (f32[568,128]{1,0:T(8,128)S(1)}, f32[568,128]{1,0:T(8,128)S(1)}, u32[]{:S(2)}, u32[]{:S(2)}) collective-permute-start(f32[568,128]{1,0:T(8,128)S(1)} %get-tuple-element.57), channel_id=1, source_target_pairs={{0,12},{4,0},{8,4},{12,8},{1,13},{5,1},{9,5},{13,9},{2,14},{6,2},{... | collective-permute-start | bytes 872456 | tf_op jit(solution)/shard_map/send_x/ppermute | solution.py:604
  8.7 0.0 collective-permute-start.2
  9.3 0.0 copy-done.2
  9.3 0.0 copy-done.3
  9.4 0.6 %turns.1.refs_13_.refs_15_ = f32[24,128]{1,0:T(8,128)S(1)} custom-call(f32[2,2]{1,0:T(2,128)S(1)} %copy-done.2, s32[1]{0:T(128)S(6)} %copy.61.index, s32[4]{0:T(128)S(1)} %copy-done.3), custom_call_target="tpu_custom_call" | custom-call | tf_op jit(solution)/shard_map/turns/pallas_call | solution.py:606
  10.0 5.2 %collective-permute-done.1.z_high.refs_12_.refs_14_ = f32[304,128]{1,0:T(8,128)S(1)} collective-permute-done((f32[304,128]{1,0:T(8,128)S(1)}, f32[304,128]{1,0:T(8,128)S(1)}, u32[]{:S(2)}, u32[]{:S(2)}) %collective-permute-start.1) | collective-permute-done | bytes 155680 | tf_op jit(solution)/shard_map/send_y/ppermute | solution.py:591
  15.2 0.0 collective-permute-done.z_low.refs_11_.refs_13_
  15.2 0.1 relay_corners.1
  15.3 0.6 %collective-permute-start.4 = (f32[144,128]{1,0:T(8,128)S(1)}, f32[144,128]{1,0:T(8,128)S(1)}, u32[]{:S(2)}, u32[]{:S(2)}) collective-permute-start(f32[144,128]{1,0:T(8,128)S(1)} %get-tuple-element.67), channel_id=1, source_target_pairs={{0,12},{4,8},{8,4},{12,0},{1,13},{5,9},{9,5},{13,1},{2,14},{6,10},... | collective-permute-start | bytes 221192 | tf_op jit(solution)/shard_map/relay_corners/ppermute | solution.py:621
  15.9 0.0 copy-start
  15.9 0.0 copy-start.1
  15.9 1.1 %collective-permute-start.5 = (f32[144,128]{1,0:T(8,128)S(1)}, f32[144,128]{1,0:T(8,128)S(1)}, u32[]{:S(2)}, u32[]{:S(2)}) collective-permute-start(f32[144,128]{1,0:T(8,128)S(1)} %get-tuple-element.68), channel_id=1, source_target_pairs={{0,4},{4,0},{8,12},{12,8},{1,5},{5,1},{9,13},{13,9},{2,6},{6,2},{1... | collective-permute-start | bytes 221192 | tf_op jit(solution)/shard_map/relay_corners/ppermute | solution.py:622
  17.0 1.2 %middle.1 = (f32[4032,128]{1,0:T(8,128)S(1)}, f32[4032,128]{1,0:T(8,128)S(1)}, f32[4032,128]{1,0:T(8,128)S(1)}, f32[4032,128]{1,0:T(8,128)S(1)}, f32[4032,128]{1...) custom-call(f32[4032,128]{1,0:T(8,128)S(1)} %bitcast.15, ...), custom_call_target="tpu_custom_call", output_to_operand_aliasing={{0}: (0, {}), {4}: (1, {}), {1}: (2, {}), {5}: (3, {}), {8}... | custom-call | flops 4294967296 | bytes 4294967296 | tf_op jit(solution)/shard_map/middle/pallas_call | solution.py:627
  18.2 0.0 collective-permute-done.3.refs_10_
  18.2 0.0 collective-permute-done.2.refs_9_
  18.2 0.0 copy-done
  18.2 0.0 copy-done.1
  18.3 0.8 %faces.1 = (f32[4032,128]{1,0:T(8,128)S(1)}, f32[4032,128]{1,0:T(8,128)S(1)}, f32[4032,128]{1,0:T(8,128)S(1)}, f32[4032,128]{1,0:T(8,128)S(1)}, f32[4032,128]{1,...) custom-call(f32[4032,128]{1,0:T(8,128)S(1)} %get-tuple-element.47.re, ...), custom_call_target="tpu_custom_call", output_to_operand_aliasing={{0}: (0, {}), {1}: (1, {}), {2}: (2, {}), {3}: (3, {}), {4}... | custom-call | tf_op jit(solution)/shard_map/faces/pallas_call | solution.py:639
  19.0 0.8 %collective-permute-done.4.refs_11_ = f32[144,128]{1,0:T(8,128)S(1)} collective-permute-done((f32[144,128]{1,0:T(8,128)S(1)}, f32[144,128]{1,0:T(8,128)S(1)}, u32[]{:S(2)}, u32[]{:S(2)}) %collective-permute-start.4) | collective-permute-done | bytes 73760 | tf_op jit(solution)/shard_map/relay_corners/ppermute | solution.py:621
  19.8 0.0 collective-permute-done.5.refs_12_
  19.8 1.5 %edges.1 = (f32[4032,128]{1,0:T(8,128)S(1)}, f32[4032,128]{1,0:T(8,128)S(1)}, f32[4032,128]{1,0:T(8,128)S(1)}, f32[4032,128]{1,0:T(8,128)S(1)}, f32[4032,128]{1,...) custom-call(f32[4032,128]{1,0:T(8,128)S(1)} %get-tuple-element.58.re, ...), custom_call_target="tpu_custom_call", output_to_operand_aliasing={{0}: (0, {}), {1}: (1, {}), {2}: (2, {}), {3}: (3, {}), {4}... | custom-call | tf_op jit(solution)/shard_map/edges/pallas_call | solution.py:649
  21.3 1.5 %collective-permute-start.6 = (f32[64,128]{1,0:T(8,128)S(1)}, f32[64,128]{1,0:T(8,128)S(1)}, u32[]{:S(2)}, u32[]{:S(2)}) collective-permute-start(f32[64,128]{1,0:T(8,128)S(1)} %get-tuple-element.76), channel_id=1, source_target_pairs={{0,16},{16,0},{1,17},{17,1},{2,18},{18,2},{3,19},{19,3},{4,20},{20... | collective-permute-start | bytes 98312 | tf_op jit(solution)/shard_map/sum_angles/ppermute | solution.py:659
  22.8 1.0 %write.1 = (f32[6,8,16,128]{3,2,1,0:T(8,128)}, f32[6,8,16,128]{3,2,1,0:T(8,128)}) custom-call(f32[6,8,16,128]{3,2,1,0:T(8,128)S(1)} %bitcast.22, f32[6,8,16,128]{3,2,1,0:T(8,128)S(1)} %bitcast.23), custom_call_target="tpu_custom_call" | custom-call | tf_op jit(solution)/shard_map/write/pallas_call | solution.py:668
  23.8 1.4 %collective-permute-done.6.refs_1_ = f32[64,128]{1,0:T(8,128)S(1)} collective-permute-done((f32[64,128]{1,0:T(8,128)S(1)}, f32[64,128]{1,0:T(8,128)S(1)}, u32[]{:S(2)}, u32[]{:S(2)}) %collective-permute-start.6) | collective-permute-done | bytes 32800 | tf_op jit(solution)/shard_map/sum_angles/ppermute | solution.py:659
  25.3 0.7 %sum_angles.1 = f32[128,64]{1,0:T(8,128)} custom-call(f32[64,128]{1,0:T(8,128)S(1)} %get-tuple-element.75.refs_0_, f32[64,128]{1,0:T(8,128)S(1)} %collective-permute-done.6.refs_1_), custom_call_target="tpu_custom_call" | custom-call | tf_op jit(solution)/shard_map/sum_angles/pallas_call | solution.py:660
Async XLA Ops:
  2.7 12.5 %collective-permute-start = (f32[360,128]{1,0:T(8,128)S(1)}, f32[360,128]{1,0:T(8,128)S(1)}, u32[]{:S(2)}, u32[]{:S(2)}) collective-permute-start(f32[360,128]{1,0:T(8,128)S(1)} %get-tuple-element.45), channel_id=1, source_target_pairs={{0,1},{1,2},{2,3},{3,0},{4,5},{5,6},{6,7},{7,4},{8,9},{9,10},{10,1... | collective-permute-start | bytes 552968 | tf_op jit(solution)/shard_map/send_y/ppermute | solution.py:590
  5.7 9.4 %collective-permute-start.1 = (f32[304,128]{1,0:T(8,128)S(1)}, f32[304,128]{1,0:T(8,128)S(1)}, u32[]{:S(2)}, u32[]{:S(2)}) collective-permute-start(f32[304,128]{1,0:T(8,128)S(1)} %get-tuple-element.46), channel_id=1, source_target_pairs={{0,3},{1,0},{2,1},{3,2},{4,7},{5,4},{6,5},{7,6},{8,11},{9,8},{10,9... | collective-permute-start | bytes 466952 | tf_op jit(solution)/shard_map/send_y/ppermute | solution.py:591
  7.8 1.5 %copy-start.2 = (f32[2,2]{1,0:T(2,128)S(1)}, f32[2,2]{1,0:T(2,128)}, u32[]{:S(2)}) copy-start(f32[2,2]{1,0:T(2,128)} %table.1) | copy-start | bytes 52
  7.8 1.5 %copy-start.3 = (s32[4]{0:T(128)S(1)}, s32[4]{0:T(128)}, u32[]{:S(2)}) copy-start(s32[4]{0:T(128)} %tiles.1) | copy-start | bytes 52
  8.0 10.3 %collective-permute-start.3 = (f32[568,128]{1,0:T(8,128)S(1)}, f32[568,128]{1,0:T(8,128)S(1)}, u32[]{:S(2)}, u32[]{:S(2)}) collective-permute-start(f32[568,128]{1,0:T(8,128)S(1)} %get-tuple-element.57), channel_id=1, source_target_pairs={{0,12},{4,0},{8,4},{12,8},{1,13},{5,1},{9,5},{13,9},{2,14},{6,2},{... | collective-permute-start | bytes 872456 | tf_op jit(solution)/shard_map/send_x/ppermute | solution.py:604
  8.7 9.5 %collective-permute-start.2 = (f32[608,128]{1,0:T(8,128)S(1)}, f32[608,128]{1,0:T(8,128)S(1)}, u32[]{:S(2)}, u32[]{:S(2)}) collective-permute-start(f32[608,128]{1,0:T(8,128)S(1)} %get-tuple-element.56), channel_id=1, source_target_pairs={{0,4},{4,8},{8,12},{12,0},{1,5},{5,9},{9,13},{13,1},{2,6},{6,10},{... | collective-permute-start | bytes 933896 | tf_op jit(solution)/shard_map/send_x/ppermute | solution.py:603
  15.3 4.6 %collective-permute-start.4 = (f32[144,128]{1,0:T(8,128)S(1)}, f32[144,128]{1,0:T(8,128)S(1)}, u32[]{:S(2)}, u32[]{:S(2)}) collective-permute-start(f32[144,128]{1,0:T(8,128)S(1)} %get-tuple-element.67), channel_id=1, source_target_pairs={{0,12},{4,8},{8,4},{12,0},{1,13},{5,9},{9,5},{13,1},{2,14},{6,10},... | collective-permute-start | bytes 221192 | tf_op jit(solution)/shard_map/relay_corners/ppermute | solution.py:621
  15.9 2.4 %copy-start = (f32[1,6,8,16,128]{4,3,2,1,0:T(8,128)S(1)}, f32[1,6,8,16,128]{4,3,2,1,0:T(8,128)}, u32[]{:S(2)}) copy-start(f32[1,6,8,16,128]{4,3,2,1,0:T(8,128)} %param.10) | copy-start | bytes 1179652
  15.9 2.4 %copy-start.1 = (f32[1,6,8,16,128]{4,3,2,1,0:T(8,128)S(1)}, f32[1,6,8,16,128]{4,3,2,1,0:T(8,128)}, u32[]{:S(2)}) copy-start(f32[1,6,8,16,128]{4,3,2,1,0:T(8,128)} %param.11) | copy-start | bytes 1179652
  15.9 4.0 %collective-permute-start.5 = (f32[144,128]{1,0:T(8,128)S(1)}, f32[144,128]{1,0:T(8,128)S(1)}, u32[]{:S(2)}, u32[]{:S(2)}) collective-permute-start(f32[144,128]{1,0:T(8,128)S(1)} %get-tuple-element.68), channel_id=1, source_target_pairs={{0,4},{4,0},{8,12},{12,8},{1,5},{5,1},{9,13},{13,9},{2,6},{6,2},{1... | collective-permute-start | bytes 221192 | tf_op jit(solution)/shard_map/relay_corners/ppermute | solution.py:622
  21.3 3.9 %collective-permute-start.6 = (f32[64,128]{1,0:T(8,128)S(1)}, f32[64,128]{1,0:T(8,128)S(1)}, u32[]{:S(2)}, u32[]{:S(2)}) collective-permute-start(f32[64,128]{1,0:T(8,128)S(1)} %get-tuple-element.76), channel_id=1, source_target_pairs={{0,16},{16,0},{1,17},{17,1},{2,18},{18,2},{3,19},{19,3},{4,20},{20... | collective-permute-start | bytes 98312 | tf_op jit(solution)/shard_map/sum_angles/ppermute | solution.py:659

commit v13 on v12

--- a/solution.py
+++ b/solution.py
@@ -128,8 +128,8 @@
         self.y_low, self.y_high = Message(y_low, 0, y_folded), Message(y_high, 0)
         self.x_low, self.x_high = Message(sides[-1, 0], 1, x_folded), Message(sides[1, 0], 1)
         self.mate_side, self.far_side = (1, -1), (-1, 1)
-        self.mate, self.far = ([Message(sides[side, -1] | sides[side, 1], 1) for side in order] for order in (self.mate_side, self.far_side))
-        self.corner_lines = max(message.lines for message in self.mate)
+        self.mate = [Message(sides[side, -1] | sides[side, 1], 1) for side in self.mate_side]
+        self.far_low, self.far_high = ([Message(sides[side, end], 1) for side in self.far_side] for end in (-1, 1))
 
     def row(self, x, y, run=0, part=0, comp=0):
         return ((run * 6 + part * 3 + comp) * self.wide + x + STEPS) * self.ring + y % self.ring
@@ -265,12 +265,14 @@
     turns[pl.ds(2 * SUB, SUB), :] = jnp.full(sub.shape, weight, jnp.float32)
 
 
-def relay_kernel(plan, z_low, z_high, to_far, to_mate):
+def relay_kernel(plan, jobs, *refs):
+    faces, outs = refs[: len(refs) - len(jobs)], refs[len(refs) - len(jobs) :]
+
     def corners(receiver):
-        for messages, side, out in ((plan.far, plan.far_side, to_far), (plan.mate, plan.mate_side, to_mate)):
+        for (messages, side), out in zip(jobs, outs, strict=True):
             dx = -plan.nx * side[receiver]
             for (what, x, y), row in messages[receiver].at.items():
-                ref, source = (z_low, plan.y_low) if y < 0 else (z_high, plan.y_high)
+                ref, source = (faces[0], plan.y_low) if y < 0 else (faces[1], plan.y_high)
                 out[pl.ds(row, 1), :] = ref[pl.ds(source.at[what, x + dx, y], 1), :]
 
     by_parity(1, corners)
@@ -461,9 +463,9 @@
 
 def edges_kernel(plan, groups, *refs):
     count = 2 * STEPS + 3
-    x_low, x_high, far, mate, z_low, z_high, turns, part_f, part_a = refs[count : count + 9]
-    arrays = refs[count + 9 : 2 * count + 9]
-    out_f, out_a, *parts = refs[2 * count + 9 :]
+    x_low, x_high, far_low, far_high, mate, z_low, z_high, turns, part_f, part_a = refs[count : count + 10]
+    arrays = refs[count + 10 : 2 * count + 10]
+    out_f, out_a, *parts = refs[2 * count + 10 :]
     efield, hfield, coef = arrays[: STEPS + 1], arrays[STEPS + 1 : 2 * STEPS + 2], arrays[-1]
     state = State(efield, hfield, coef)
 
@@ -473,7 +475,11 @@
             unpack(plan, plan.x_high, x_high, lambda y: 1, turns, state, kinds, level)
 
         def corners(receiver):
-            for messages, ref, side in ((plan.far, far, plan.far_side), (plan.mate, mate, plan.mate_side)):
+            for messages, ref, side in (
+                (plan.far_low, far_low, plan.far_side),
+                (plan.far_high, far_high, plan.far_side),
+                (plan.mate, mate, plan.mate_side),
+            ):
                 first = 4 if side[receiver] < 0 else 6
                 unpack(plan, messages[receiver], ref, lambda y: first + (y >= 0), turns, state, kinds, level)
 
@@ -610,15 +616,22 @@
             out_specs=VMEM,
             compiler_params=params(4),
         )(phase_table, angle_index, design_tiles)
+    def relay(jobs, *faces):
+        return pl.pallas_call(
+            functools.partial(relay_kernel, plan, jobs),
+            out_shape=[lines(max(message.lines for message in messages)) for messages, _ in jobs],
+            in_specs=[VMEM] * len(faces),
+            out_specs=[VMEM] * len(jobs),
+            compiler_params=params(4),
+            cost_estimate=cost(2**10),
+        )(*faces)
+
+    with jax.named_scope("relay_low_corners"):
+        (to_far,) = relay([(plan.far_low, plan.far_side)], z_low)
+        far_low = lax.ppermute(to_far, "gx", far_pairs())
     with jax.named_scope("relay_corners"):
-        to_far, to_mate = pl.pallas_call(
-            functools.partial(relay_kernel, plan),
-            out_shape=[lines(plan.corner_lines)] * 2,
-            in_specs=[VMEM] * 2,
-            out_specs=[VMEM] * 2,
-            compiler_params=params(4),
-        )(z_low, z_high)
-        far = lax.ppermute(to_far, "gx", far_pairs())
+        to_far, to_mate = relay([(plan.far_high, plan.far_side), (plan.mate, plan.mate_side)], z_low, z_high)
+        far_high = lax.ppermute(to_far, "gx", far_pairs())
         mate = lax.ppermute(to_mate, "gx", mate_pairs())
     level = lines(12 * wide * ring)
     count = 2 * STEPS + 3
@@ -649,11 +662,11 @@
         results = pl.pallas_call(
             functools.partial(edges_kernel, plan, groups),
             out_shape=[*levels, *transforms, *[lines(nx * ny // groups)] * groups],
-            in_specs=[VMEM] * (count + 9),
+            in_specs=[VMEM] * (count + 10),
             out_specs=[VMEM] * (count + 2 + groups),
-            input_output_aliases={i: i for i in range(count)} | {count + 7: count, count + 8: count + 1},
+            input_output_aliases={i: i for i in range(count)} | {count + 8: count, count + 9: count + 1},
             compiler_params=params(8),
-        )(*state, x_low, x_high, far, mate, z_low, z_high, turns, *sums)
+        )(*state, x_low, x_high, far_low, far_high, mate, z_low, z_high, turns, *sums)
         tr_f, tr_a, own, *others = results[count:]
     with jax.named_scope("sum_angles"):
         others = [lax.ppermute(part, "angle", ring_pairs("angle", k + 1)) for k, part in enumerate(others)]

time: 26.2 us -> 25.6 us (0.977)
  waiting for transfers between devices: 7.48 us -> 6.84 us
    ppermute x1, waiting for transfers between devices: 5.21 us -> 1.79 us  [shards(): z_high = lax.ppermute(z_down, 'gy', ring_pairs('gy', -1))]
    ppermute x1, waiting for transfers between devices: 0.01 us -> 3.31 us  [shards(): z_low = lax.ppermute(z_up, 'gy', ring_pairs('gy', 1))]
    ppermute x1 -> x2, waiting for transfers between devices: 0.82 us -> 0.29 us  [the longest x1 0.28 us: shards(): far_high = lax.ppermute(to_far, 'gx', far_pairs())]
    ppermute x1 -> x2, starting transfers between devices: 0.59 us -> 0.66 us  [the longest x1 0.59 us: shards(): far_high = lax.ppermute(to_far, 'gx', far_pairs())]
  transfers between devices with their start and end apart: 7 -> 8, of which waited for: 3 -> 4; matrix products, arithmetic and copies ran while one was open for 0% -> 0% of each run, Pallas kernels for 14% -> 15%
where the time goes in v13:
time: 25.6 us; the launch traced here: 25.4 us
  starting transfers between devices  9.19 us (36%)
  Pallas kernels  7.97 us (31%)
  waiting for transfers between devices  6.84 us (27%)
  between operations  1.38 us (5%)
    ppermute x1, waiting for transfers between devices, shards(): z_low = lax.ppermute(z_up, 'gy', ring_pairs('gy', 1))  3.31 us
    ppermute x1, starting transfers between devices, shards(): z_low = lax.ppermute(z_up, 'gy', ring_pairs('gy', 1))  3.08 us
    ppermute x1, starting transfers between devices, shards(): z_high = lax.ppermute(z_down, 'gy', ring_pairs('gy', -1))  2.09 us
    pallas_call x1, Pallas kernels, shards(): pl.pallas_call(functools.partial(pack_y_kernel, plan), out_shape=(*[array...  2.02 us
    ppermute x1, waiting for transfers between devices, shards(): z_high = lax.ppermute(z_down, 'gy', ring_pairs('gy', -1))  1.79 us
    ppermute x1, starting transfers between devices, shards(): lax.ppermute(part, 'angle', ring_pairs('angle', k + 1))  1.52 us
    pallas_call x1, Pallas kernels, shards(): pl.pallas_call(functools.partial(edges_kernel, plan, groups), out_shape=[...  1.48 us
    ppermute x1, waiting for transfers between devices, shards(): lax.ppermute(part, 'angle', ring_pairs('angle', k + 1))  1.45 us
  transfers between devices with their start and end apart: 8, of which 4 were waited for; matrix products, arithmetic and copies ran while one was open for 0% of the time, Pallas kernels for 15%

profile of v13, /device:TPU:0, one launch (start us, length us, event | category | flops | bytes accessed | tf_op | source)
XLA Modules:
  0.0 25.4 jit_solution(14562718805572543411)
XLA Ops:
  0.6 2.0 %pack_y.1 = (f32[12,14,24,128]{3,2,1,0:T(8,128)S(1)}, f32[12,14,24,128]{3,2,1,0:T(8,128)S(1)}, f32[12,14,24,128]{3,2,1,0:T(8,128)S(1)}, f32[12,14,24,128]{3,2,1,...) custom-call(f32[12,8,16,128]{3,2,1,0:T(8,128)} %bitcast.28, ...), custom_call_target="tpu_custom_call" | custom-call | tf_op jit(solution)/shard_map/pack_y/pallas_call | solution.py:581
  2.7 3.1 %collective-permute-start = (f32[360,128]{1,0:T(8,128)S(1)}, f32[360,128]{1,0:T(8,128)S(1)}, u32[]{:S(2)}, u32[]{:S(2)}) collective-permute-start(f32[360,128]{1,0:T(8,128)S(1)} %get-tuple-element.45), channel_id=1, source_target_pairs={{0,1},{1,2},{2,3},{3,0},{4,5},{5,6},{6,7},{7,4},{8,9},{9,10},{10,1... | collective-permute-start | bytes 552968 | tf_op jit(solution)/shard_map/send_y/ppermute | solution.py:596
  5.7 2.1 %collective-permute-start.1 = (f32[304,128]{1,0:T(8,128)S(1)}, f32[304,128]{1,0:T(8,128)S(1)}, u32[]{:S(2)}, u32[]{:S(2)}) collective-permute-start(f32[304,128]{1,0:T(8,128)S(1)} %get-tuple-element.46), channel_id=1, source_target_pairs={{0,3},{1,0},{2,1},{3,2},{4,7},{5,4},{6,5},{7,6},{8,11},{9,8},{10,9... | collective-permute-start | bytes 466952 | tf_op jit(solution)/shard_map/send_y/ppermute | solution.py:597
  7.8 0.0 copy-start.2
  7.8 0.0 copy-start.3
  7.8 0.1 pack_x.1
  8.0 0.7 %collective-permute-start.3 = (f32[568,128]{1,0:T(8,128)S(1)}, f32[568,128]{1,0:T(8,128)S(1)}, u32[]{:S(2)}, u32[]{:S(2)}) collective-permute-start(f32[568,128]{1,0:T(8,128)S(1)} %get-tuple-element.57), channel_id=1, source_target_pairs={{0,12},{4,0},{8,4},{12,8},{1,13},{5,1},{9,5},{13,9},{2,14},{6,2},{... | collective-permute-start | bytes 872456 | tf_op jit(solution)/shard_map/send_x/ppermute | solution.py:610
  8.7 0.0 collective-permute-start.2
  9.3 0.0 copy-done.2
  9.3 0.0 copy-done.3
  9.4 0.6 %turns.1.refs_13_.refs_16_ = f32[24,128]{1,0:T(8,128)S(1)} custom-call(f32[2,2]{1,0:T(2,128)S(1)} %copy-done.2, s32[1]{0:T(128)S(6)} %copy.61.index, s32[4]{0:T(128)S(1)} %copy-done.3), custom_call_target="tpu_custom_call" | custom-call | tf_op jit(solution)/shard_map/turns/pallas_call | solution.py:612
  10.0 3.3 %collective-permute-done.z_low.refs_11_.refs_0_.refs_14_ = f32[360,128]{1,0:T(8,128)S(1)} collective-permute-done((f32[360,128]{1,0:T(8,128)S(1)}, f32[360,128]{1,0:T(8,128)S(1)}, u32[]{:S(2)}, u32[]{:S(2)}) %collective-permute-start) | collective-permute-done | bytes 184352 | tf_op jit(solution)/shard_map/send_y/ppermute | solution.py:596
  13.3 0.1 collective-permute-start.4
  13.4 1.8 %collective-permute-done.1.z_high.refs_12_.refs_1_.refs_15_ = f32[304,128]{1,0:T(8,128)S(1)} collective-permute-done((f32[304,128]{1,0:T(8,128)S(1)}, f32[304,128]{1,0:T(8,128)S(1)}, u32[]{:S(2)}, u32[]{:S(2)}) %collective-permute-start.1) | collective-permute-done | bytes 155680 | tf_op jit(solution)/shard_map/send_y/ppermute | solution.py:597
  15.2 0.1 relay_corners.1
  15.2 0.6 %collective-permute-start.5 = (f32[72,128]{1,0:T(8,128)S(1)}, f32[72,128]{1,0:T(8,128)S(1)}, u32[]{:S(2)}, u32[]{:S(2)}) collective-permute-start(f32[72,128]{1,0:T(8,128)S(1)} %get-tuple-element.67), channel_id=1, source_target_pairs={{0,12},{4,8},{8,4},{12,0},{1,13},{5,9},{9,5},{13,1},{2,14},{6,10},... | collective-permute-start | bytes 110600 | tf_op jit(solution)/shard_map/relay_corners/ppermute | solution.py:634
  15.8 0.0 copy-start
  15.8 1.1 %collective-permute-start.6 = (f32[144,128]{1,0:T(8,128)S(1)}, f32[144,128]{1,0:T(8,128)S(1)}, u32[]{:S(2)}, u32[]{:S(2)}) collective-permute-start(f32[144,128]{1,0:T(8,128)S(1)} %get-tuple-element.68), channel_id=1, source_target_pairs={{0,4},{4,0},{8,12},{12,8},{1,5},{5,1},{9,13},{13,9},{2,6},{6,2},{1... | collective-permute-start | bytes 221192 | tf_op jit(solution)/shard_map/relay_corners/ppermute | solution.py:635
  16.9 1.2 %middle.1 = (f32[4032,128]{1,0:T(8,128)S(1)}, f32[4032,128]{1,0:T(8,128)S(1)}, f32[4032,128]{1,0:T(8,128)S(1)}, f32[4032,128]{1,0:T(8,128)S(1)}, f32[4032,128]{1...) custom-call(f32[4032,128]{1,0:T(8,128)S(1)} %bitcast.15, ...), custom_call_target="tpu_custom_call", output_to_operand_aliasing={{0}: (0, {}), {4}: (1, {}), {1}: (2, {}), {5}: (3, {}), {8}... | custom-call | flops 4294967296 | bytes 4294967296 | tf_op jit(solution)/shard_map/middle/pallas_call | solution.py:640
  18.2 0.0 collective-permute-done.3.refs_10_
  18.2 0.0 collective-permute-done.2.refs_9_
  18.2 0.0 copy-done
  18.2 0.0 copy-done.1
  18.2 0.8 %faces.1 = (f32[4032,128]{1,0:T(8,128)S(1)}, f32[4032,128]{1,0:T(8,128)S(1)}, f32[4032,128]{1,0:T(8,128)S(1)}, f32[4032,128]{1,0:T(8,128)S(1)}, f32[4032,128]{1,...) custom-call(f32[4032,128]{1,0:T(8,128)S(1)} %get-tuple-element.47.re, ...), custom_call_target="tpu_custom_call", output_to_operand_aliasing={{0}: (0, {}), {1}: (1, {}), {2}: (2, {}), {3}: (3, {}), {4}... | custom-call | tf_op jit(solution)/shard_map/faces/pallas_call | solution.py:652
  19.0 0.3 %collective-permute-done.5.refs_12_ = f32[72,128]{1,0:T(8,128)S(1)} collective-permute-done((f32[72,128]{1,0:T(8,128)S(1)}, f32[72,128]{1,0:T(8,128)S(1)}, u32[]{:S(2)}, u32[]{:S(2)}) %collective-permute-start.5) | collective-permute-done | bytes 36896 | tf_op jit(solution)/shard_map/relay_corners/ppermute | solution.py:634
  19.3 0.0 collective-permute-done.4.refs_11_
  19.3 0.0 collective-permute-done.6.refs_13_
  19.3 1.5 %edges.1 = (f32[4032,128]{1,0:T(8,128)S(1)}, f32[4032,128]{1,0:T(8,128)S(1)}, f32[4032,128]{1,0:T(8,128)S(1)}, f32[4032,128]{1,0:T(8,128)S(1)}, f32[4032,128]{1,...) custom-call(f32[4032,128]{1,0:T(8,128)S(1)} %get-tuple-element.58.re, ...), custom_call_target="tpu_custom_call", output_to_operand_aliasing={{0}: (0, {}), {1}: (1, {}), {2}: (2, {}), {3}: (3, {}), {4}... | custom-call | tf_op jit(solution)/shard_map/edges/pallas_call | solution.py:662
  20.8 1.5 %collective-permute-start.7 = (f32[64,128]{1,0:T(8,128)S(1)}, f32[64,128]{1,0:T(8,128)S(1)}, u32[]{:S(2)}, u32[]{:S(2)}) collective-permute-start(f32[64,128]{1,0:T(8,128)S(1)} %get-tuple-element.76), channel_id=1, source_target_pairs={{0,16},{16,0},{1,17},{17,1},{2,18},{18,2},{3,19},{19,3},{4,20},{20... | collective-permute-start | bytes 98312 | tf_op jit(solution)/shard_map/sum_angles/ppermute | solution.py:672
  22.3 1.0 %write.1 = (f32[6,8,16,128]{3,2,1,0:T(8,128)}, f32[6,8,16,128]{3,2,1,0:T(8,128)}) custom-call(f32[6,8,16,128]{3,2,1,0:T(8,128)S(1)} %bitcast.22, f32[6,8,16,128]{3,2,1,0:T(8,128)S(1)} %bitcast.23), custom_call_target="tpu_custom_call" | custom-call | tf_op jit(solution)/shard_map/write/pallas_call | solution.py:681
  23.2 1.4 %collective-permute-done.7.refs_1_ = f32[64,128]{1,0:T(8,128)S(1)} collective-permute-done((f32[64,128]{1,0:T(8,128)S(1)}, f32[64,128]{1,0:T(8,128)S(1)}, u32[]{:S(2)}, u32[]{:S(2)}) %collective-permute-start.7) | collective-permute-done | bytes 32800 | tf_op jit(solution)/shard_map/sum_angles/ppermute | solution.py:672
  24.7 0.7 %sum_angles.1 = f32[128,64]{1,0:T(8,128)} custom-call(f32[64,128]{1,0:T(8,128)S(1)} %get-tuple-element.75.refs_0_, f32[64,128]{1,0:T(8,128)S(1)} %collective-permute-done.7.refs_1_), custom_call_target="tpu_custom_call" | custom-call | tf_op jit(solution)/shard_map/sum_angles/pallas_call | solution.py:673
  (2 shorter events, 0.0 us)
Async XLA Ops:
  2.7 10.6 %collective-permute-start = (f32[360,128]{1,0:T(8,128)S(1)}, f32[360,128]{1,0:T(8,128)S(1)}, u32[]{:S(2)}, u32[]{:S(2)}) collective-permute-start(f32[360,128]{1,0:T(8,128)S(1)} %get-tuple-element.45), channel_id=1, source_target_pairs={{0,1},{1,2},{2,3},{3,0},{4,5},{5,6},{6,7},{7,4},{8,9},{9,10},{10,1... | collective-permute-start | bytes 552968 | tf_op jit(solution)/shard_map/send_y/ppermute | solution.py:596
  5.7 9.4 %collective-permute-start.1 = (f32[304,128]{1,0:T(8,128)S(1)}, f32[304,128]{1,0:T(8,128)S(1)}, u32[]{:S(2)}, u32[]{:S(2)}) collective-permute-start(f32[304,128]{1,0:T(8,128)S(1)} %get-tuple-element.46), channel_id=1, source_target_pairs={{0,3},{1,0},{2,1},{3,2},{4,7},{5,4},{6,5},{7,6},{8,11},{9,8},{10,9... | collective-permute-start | bytes 466952 | tf_op jit(solution)/shard_map/send_y/ppermute | solution.py:597
  7.8 1.5 %copy-start.2 = (f32[2,2]{1,0:T(2,128)S(1)}, f32[2,2]{1,0:T(2,128)}, u32[]{:S(2)}) copy-start(f32[2,2]{1,0:T(2,128)} %table.1) | copy-start | bytes 52
  7.8 1.5 %copy-start.3 = (s32[4]{0:T(128)S(1)}, s32[4]{0:T(128)}, u32[]{:S(2)}) copy-start(s32[4]{0:T(128)} %tiles.1) | copy-start | bytes 52
  8.0 10.2 %collective-permute-start.3 = (f32[568,128]{1,0:T(8,128)S(1)}, f32[568,128]{1,0:T(8,128)S(1)}, u32[]{:S(2)}, u32[]{:S(2)}) collective-permute-start(f32[568,128]{1,0:T(8,128)S(1)} %get-tuple-element.57), channel_id=1, source_target_pairs={{0,12},{4,0},{8,4},{12,8},{1,13},{5,1},{9,5},{13,9},{2,14},{6,2},{... | collective-permute-start | bytes 872456 | tf_op jit(solution)/shard_map/send_x/ppermute | solution.py:610
  8.7 9.5 %collective-permute-start.2 = (f32[608,128]{1,0:T(8,128)S(1)}, f32[608,128]{1,0:T(8,128)S(1)}, u32[]{:S(2)}, u32[]{:S(2)}) collective-permute-start(f32[608,128]{1,0:T(8,128)S(1)} %get-tuple-element.56), channel_id=1, source_target_pairs={{0,4},{4,8},{8,12},{12,0},{1,5},{5,9},{9,13},{13,1},{2,6},{6,10},{... | collective-permute-start | bytes 933896 | tf_op jit(solution)/shard_map/send_x/ppermute | solution.py:609
  13.3 6.0 %collective-permute-start.4 = (f32[80,128]{1,0:T(8,128)S(1)}, f32[80,128]{1,0:T(8,128)S(1)}, u32[]{:S(2)}, u32[]{:S(2)}) collective-permute-start(f32[80,128]{1,0:T(8,128)S(1)} %relay_low_corners.1), channel_id=1, source_target_pairs={{0,12},{4,8},{8,4},{12,0},{1,13},{5,9},{9,5},{13,1},{2,14},{6,10},... | collective-permute-start | bytes 122888 | tf_op jit(solution)/shard_map/relay_low_corners/ppermute | solution.py:631
  15.2 4.0 %collective-permute-start.5 = (f32[72,128]{1,0:T(8,128)S(1)}, f32[72,128]{1,0:T(8,128)S(1)}, u32[]{:S(2)}, u32[]{:S(2)}) collective-permute-start(f32[72,128]{1,0:T(8,128)S(1)} %get-tuple-element.67), channel_id=1, source_target_pairs={{0,12},{4,8},{8,4},{12,0},{1,13},{5,9},{9,5},{13,1},{2,14},{6,10},... | collective-permute-start | bytes 110600 | tf_op jit(solution)/shard_map/relay_corners/ppermute | solution.py:634
  15.8 2.4 %copy-start = (f32[1,6,8,16,128]{4,3,2,1,0:T(8,128)S(1)}, f32[1,6,8,16,128]{4,3,2,1,0:T(8,128)}, u32[]{:S(2)}) copy-start(f32[1,6,8,16,128]{4,3,2,1,0:T(8,128)} %param.10) | copy-start | bytes 1179652
  15.8 2.4 %copy-start.1 = (f32[1,6,8,16,128]{4,3,2,1,0:T(8,128)S(1)}, f32[1,6,8,16,128]{4,3,2,1,0:T(8,128)}, u32[]{:S(2)}) copy-start(f32[1,6,8,16,128]{4,3,2,1,0:T(8,128)} %param.11) | copy-start | bytes 1179652
  15.8 3.4 %collective-permute-start.6 = (f32[144,128]{1,0:T(8,128)S(1)}, f32[144,128]{1,0:T(8,128)S(1)}, u32[]{:S(2)}, u32[]{:S(2)}) collective-permute-start(f32[144,128]{1,0:T(8,128)S(1)} %get-tuple-element.68), channel_id=1, source_target_pairs={{0,4},{4,0},{8,12},{12,8},{1,5},{5,1},{9,13},{13,9},{2,6},{6,2},{1... | collective-permute-start | bytes 221192 | tf_op jit(solution)/shard_map/relay_corners/ppermute | solution.py:635
  20.8 3.9 %collective-permute-start.7 = (f32[64,128]{1,0:T(8,128)S(1)}, f32[64,128]{1,0:T(8,128)S(1)}, u32[]{:S(2)}, u32[]{:S(2)}) collective-permute-start(f32[64,128]{1,0:T(8,128)S(1)} %get-tuple-element.76), channel_id=1, source_target_pairs={{0,16},{16,0},{1,17},{17,1},{2,18},{18,2},{3,19},{19,3},{4,20},{20... | collective-permute-start | bytes 98312 | tf_op jit(solution)/shard_map/sum_angles/ppermute | solution.py:672

commit v14 on v13

--- a/solution.py
+++ b/solution.py
@@ -241,6 +241,15 @@
     pack(plan, plan.x_high, state, -plan.nx, 0, x_down)
 
 
+def pack_diagonal_kernel(plan, e0, h0, e1, h1, coef, after, diagonal):
+    state = State([e0, e1], [h0, h1], coef)
+
+    def corners(receiver):
+        pack(plan, plan.far_high[receiver], state, -plan.nx * plan.far_side[receiver], -plan.ny, diagonal)
+
+    by_parity(1, corners)
+
+
 def turns_kernel(groups, table, index, tiles, turns):
     row = index[0]
     phi_x, phi_y = table[row, 0], table[row, 1]
@@ -549,6 +558,11 @@
     return [(i, (i + (1 if i % 2 else -1)) % size) for i in range(size)]
 
 
+def diagonal_pairs():
+    size = lax.axis_size("gy")
+    return [(x * size + y, far * size + (y - 1) % size) for x, far in far_pairs() for y in range(size)]
+
+
 def shards(
     forward_fields,
     adjoint_fields,
@@ -598,7 +612,7 @@
     with jax.named_scope("pack_x"):
         x_up, x_down = pl.pallas_call(
             functools.partial(pack_x_kernel, plan),
-            out_shape=(lines(plan.x_low.lines), lines(plan.x_high.lines)),
+            out_shape=[lines(plan.x_low.lines), lines(plan.x_high.lines)],
             in_specs=[VMEM] * 5,
             out_specs=[VMEM] * 2,
             scratch_shapes=[pltpu.VMEM((24 * ny, depth), jnp.float32)],
@@ -616,6 +630,16 @@
             out_specs=VMEM,
             compiler_params=params(4),
         )(phase_table, angle_index, design_tiles)
+    with jax.named_scope("diagonal_corners"):
+        to_diagonal = pl.pallas_call(
+            functools.partial(pack_diagonal_kernel, plan),
+            out_shape=lines(max(message.lines for message in plan.far_high)),
+            in_specs=[VMEM] * 6,
+            out_specs=VMEM,
+            compiler_params=params(4),
+        )(e0, h0, e1, h1, coef, x_up)
+        far_high = lax.ppermute(to_diagonal, ("gx", "gy"), diagonal_pairs())
+
     def relay(jobs, *faces):
         return pl.pallas_call(
             functools.partial(relay_kernel, plan, jobs),
@@ -630,8 +654,7 @@
         (to_far,) = relay([(plan.far_low, plan.far_side)], z_low)
         far_low = lax.ppermute(to_far, "gx", far_pairs())
     with jax.named_scope("relay_corners"):
-        to_far, to_mate = relay([(plan.far_high, plan.far_side), (plan.mate, plan.mate_side)], z_low, z_high)
-        far_high = lax.ppermute(to_far, "gx", far_pairs())
+        (to_mate,) = relay([(plan.mate, plan.mate_side)], z_low, z_high)
         mate = lax.ppermute(to_mate, "gx", mate_pairs())
     level = lines(12 * wide * ring)
     count = 2 * STEPS + 3
@@ -644,7 +667,7 @@
             out_specs=[VMEM] * count,
             input_output_aliases={0: 0, 1: STEPS + 1, 2: 1, 3: STEPS + 2, 4: count - 1},
             compiler_params=params(8),
-            cost_estimate=cost(2**32),
+            cost_estimate=cost(5 * 2**29),
         )(e0, h0, e1, h1, coef, z_low, z_high, turns)
     transforms = [lines(6 * nx * ny)] * 2
     with jax.named_scope("faces"):

time: 25.6 us -> 25 us (0.977)
  waiting for transfers between devices: 6.84 us -> 4.3 us
  starting transfers between devices: 9.19 us -> 11.1 us
    ppermute x1, waiting for transfers between devices: 3.31 us -> 0.76 us  [shards(): z_low = lax.ppermute(z_up, 'gy', ring_pairs('gy', 1))]
    ppermute x1, starting transfers between devices: 1.11 us -> 0.07 us  [shards(): mate = lax.ppermute(to_mate, 'gx', mate_pairs())]
    ppermute x1, starting transfers between devices: 0.07 us -> 1.07 us  [shards(): far_low = lax.ppermute(to_far, 'gx', far_pairs())]
    ppermute x1, starting transfers between devices: 0.73 us -> 1.71 us  [shards(): x_high = lax.ppermute(x_down, 'gx', ring_pairs('gx', -1))]
    ppermute x1, starting transfers between devices: 0.59 us -> 1.46 us  [shards(): far_high = lax.ppermute(to_diagonal, ('gx', 'gy'), diagonal_pairs())]
    ppermute x1, waiting for transfers between devices: 0.01 us -> 0.87 us  [shards(): x_high = lax.ppermute(x_down, 'gx', ring_pairs('gx', -1))]
    ppermute x1, waiting for transfers between devices: 1.79 us -> 1.19 us  [shards(): z_high = lax.ppermute(z_down, 'gy', ring_pairs('gy', -1))]
    ppermute x1, waiting for transfers between devices: 0.28 us -> 0.01 us  [shards(): far_high = lax.ppermute(to_diagonal, ('gx', 'gy'), diagonal_pairs())]
where the time goes in v14:
time: 25 us; the launch traced here: 24.8 us
  starting transfers between devices  11.1 us (44%)
  Pallas kernels  7.94 us (32%)
  waiting for transfers between devices  4.3 us (17%)
  between operations  1.42 us (6%)
    ppermute x1, starting transfers between devices, shards(): z_low = lax.ppermute(z_up, 'gy', ring_pairs('gy', 1))  3.08 us
    ppermute x1, starting transfers between devices, shards(): z_high = lax.ppermute(z_down, 'gy', ring_pairs('gy', -1))  2.09 us
    pallas_call x1, Pallas kernels, shards(): pl.pallas_call(functools.partial(pack_y_kernel, plan), out_shape=(*[array...  2.01 us
    ppermute x1, starting transfers between devices, shards(): x_high = lax.ppermute(x_down, 'gx', ring_pairs('gx', -1))  1.71 us
    ppermute x1, starting transfers between devices, shards(): lax.ppermute(part, 'angle', ring_pairs('angle', k + 1))  1.58 us
    pallas_call x1, Pallas kernels, shards(): pl.pallas_call(functools.partial(edges_kernel, plan, groups), out_shape=[...  1.52 us
    ppermute x1, waiting for transfers between devices, shards(): lax.ppermute(part, 'angle', ring_pairs('angle', k + 1))  1.47 us
    ppermute x1, starting transfers between devices, shards(): far_high = lax.ppermute(to_diagonal, ('gx', 'gy'), diagonal_pairs())  1.46 us
  transfers between devices with their start and end apart: 8, of which 4 were waited for; matrix products, arithmetic and copies ran while one was open for 0% of the time, Pallas kernels for 15%

profile of v14, /device:TPU:0, one launch (start us, length us, event | category | flops | bytes accessed | tf_op | source)
XLA Modules:
  0.0 24.8 jit_solution(12208760255301952081)
XLA Ops:
  0.6 2.0 %pack_y.1 = (f32[12,14,24,128]{3,2,1,0:T(8,128)S(1)}, f32[12,14,24,128]{3,2,1,0:T(8,128)S(1)}, f32[12,14,24,128]{3,2,1,0:T(8,128)S(1)}, f32[12,14,24,128]{3,2,1,...) custom-call(f32[12,8,16,128]{3,2,1,0:T(8,128)} %bitcast.33, ...), custom_call_target="tpu_custom_call" | custom-call | tf_op jit(solution)/shard_map/pack_y/pallas_call | solution.py:595
  2.6 3.1 %collective-permute-start = (f32[360,128]{1,0:T(8,128)S(1)}, f32[360,128]{1,0:T(8,128)S(1)}, u32[]{:S(2)}, u32[]{:S(2)}) collective-permute-start(f32[360,128]{1,0:T(8,128)S(1)} %get-tuple-element.43), channel_id=1, source_target_pairs={{0,1},{1,2},{2,3},{3,0},{4,5},{5,6},{6,7},{7,4},{8,9},{9,10},{10,1... | collective-permute-start | bytes 552968 | tf_op jit(solution)/shard_map/send_y/ppermute | solution.py:610
  5.7 2.1 %collective-permute-start.1 = (f32[304,128]{1,0:T(8,128)S(1)}, f32[304,128]{1,0:T(8,128)S(1)}, u32[]{:S(2)}, u32[]{:S(2)}) collective-permute-start(f32[304,128]{1,0:T(8,128)S(1)} %get-tuple-element.44), channel_id=1, source_target_pairs={{0,3},{1,0},{2,1},{3,2},{4,7},{5,4},{6,5},{7,6},{8,11},{9,8},{10,9... | collective-permute-start | bytes 466952 | tf_op jit(solution)/shard_map/send_y/ppermute | solution.py:611
  7.8 0.1 pack_x.1
  7.9 0.1 collective-permute-start.2
  8.0 0.0 copy-start.2
  8.0 0.0 copy-start.3
  8.0 1.7 %collective-permute-start.3 = (f32[568,128]{1,0:T(8,128)S(1)}, f32[568,128]{1,0:T(8,128)S(1)}, u32[]{:S(2)}, u32[]{:S(2)}) collective-permute-start(f32[568,128]{1,0:T(8,128)S(1)} %get-tuple-element.55), channel_id=1, source_target_pairs={{0,12},{4,0},{8,4},{12,8},{1,13},{5,1},{9,5},{13,9},{2,14},{6,2},{... | collective-permute-start | bytes 872456 | tf_op jit(solution)/shard_map/send_x/ppermute | solution.py:624
  9.8 1.5 %collective-permute-start.5 = (f32[72,128]{1,0:T(8,128)S(1)}, f32[72,128]{1,0:T(8,128)S(1)}, u32[]{:S(2)}, u32[]{:S(2)}) collective-permute-start(f32[72,128]{1,0:T(8,128)S(1)} %diagonal_corners.1), channel_id=1, source_target_pairs={{0,15},{1,12},{2,13},{3,14},{4,11},{5,8},{6,9},{7,10},{8,7},{9,4},... | collective-permute-start | bytes 110600 | tf_op jit(solution)/shard_map/diagonal_corners/ppermute | solution.py:641
  11.9 0.0 copy-done.2
  11.9 0.0 copy-done.3
  11.9 0.6 %turns.1.refs_13_.refs_16_ = f32[24,128]{1,0:T(8,128)S(1)} custom-call(f32[2,2]{1,0:T(2,128)S(1)} %copy-done.2, s32[1]{0:T(128)S(6)} %copy.61.index, s32[4]{0:T(128)S(1)} %copy-done.3), custom_call_target="tpu_custom_call" | custom-call | tf_op jit(solution)/shard_map/turns/pallas_call | solution.py:626
  12.5 0.8 %collective-permute-done.z_low.refs_11_.refs_0_.refs_14_ = f32[360,128]{1,0:T(8,128)S(1)} collective-permute-done((f32[360,128]{1,0:T(8,128)S(1)}, f32[360,128]{1,0:T(8,128)S(1)}, u32[]{:S(2)}, u32[]{:S(2)}) %collective-permute-start) | collective-permute-done | bytes 184352 | tf_op jit(solution)/shard_map/send_y/ppermute | solution.py:610
  13.3 1.1 %collective-permute-start.4 = (f32[80,128]{1,0:T(8,128)S(1)}, f32[80,128]{1,0:T(8,128)S(1)}, u32[]{:S(2)}, u32[]{:S(2)}) collective-permute-start(f32[80,128]{1,0:T(8,128)S(1)} %relay_low_corners.1), channel_id=1, source_target_pairs={{0,12},{4,8},{8,4},{12,0},{1,13},{5,9},{9,5},{13,1},{2,14},{6,10},... | collective-permute-start | bytes 122888 | tf_op jit(solution)/shard_map/relay_low_corners/ppermute | solution.py:655
  14.4 1.2 %collective-permute-done.1.z_high.refs_12_.refs_1_.refs_15_ = f32[304,128]{1,0:T(8,128)S(1)} collective-permute-done((f32[304,128]{1,0:T(8,128)S(1)}, f32[304,128]{1,0:T(8,128)S(1)}, u32[]{:S(2)}, u32[]{:S(2)}) %collective-permute-start.1) | collective-permute-done | bytes 155680 | tf_op jit(solution)/shard_map/send_y/ppermute | solution.py:611
  15.6 0.1 relay_corners.1
  15.6 0.0 copy-start
  15.6 0.0 copy-start.1
  15.6 0.1 collective-permute-start.6
  15.7 1.2 %middle.1 = (f32[4032,128]{1,0:T(8,128)S(1)}, f32[4032,128]{1,0:T(8,128)S(1)}, f32[4032,128]{1,0:T(8,128)S(1)}, f32[4032,128]{1,0:T(8,128)S(1)}, f32[4032,128]{1...) custom-call(f32[4032,128]{1,0:T(8,128)S(1)} %bitcast.16, ...), custom_call_target="tpu_custom_call", output_to_operand_aliasing={{0}: (0, {}), {4}: (1, {}), {1}: (2, {}), {5}: (3, {}), {8}... | custom-call | flops 2684354560 | bytes 2684354560 | tf_op jit(solution)/shard_map/middle/pallas_call | solution.py:663
  16.9 0.9 %collective-permute-done.3.refs_10_ = f32[568,128]{1,0:T(8,128)S(1)} collective-permute-done((f32[568,128]{1,0:T(8,128)S(1)}, f32[568,128]{1,0:T(8,128)S(1)}, u32[]{:S(2)}, u32[]{:S(2)}) %collective-permute-start.3) | collective-permute-done | bytes 290848 | tf_op jit(solution)/shard_map/send_x/ppermute | solution.py:624
  17.8 0.0 collective-permute-done.2.refs_9_
  17.8 0.0 copy-done
  17.8 0.7 %faces.1 = (f32[4032,128]{1,0:T(8,128)S(1)}, f32[4032,128]{1,0:T(8,128)S(1)}, f32[4032,128]{1,0:T(8,128)S(1)}, f32[4032,128]{1,0:T(8,128)S(1)}, f32[4032,128]{1,...) custom-call(f32[4032,128]{1,0:T(8,128)S(1)} %get-tuple-element.45.re, ...), custom_call_target="tpu_custom_call", output_to_operand_aliasing={{0}: (0, {}), {1}: (1, {}), {2}: (2, {}), {3}: (3, {}), {4}... | custom-call | tf_op jit(solution)/shard_map/faces/pallas_call | solution.py:675
  18.5 0.0 collective-permute-done.5.refs_12_
  18.5 0.0 collective-permute-done.4.refs_11_
  18.5 0.0 collective-permute-done.6.refs_13_
  18.6 1.5 %edges.1 = (f32[4032,128]{1,0:T(8,128)S(1)}, f32[4032,128]{1,0:T(8,128)S(1)}, f32[4032,128]{1,0:T(8,128)S(1)}, f32[4032,128]{1,0:T(8,128)S(1)}, f32[4032,128]{1,...) custom-call(f32[4032,128]{1,0:T(8,128)S(1)} %get-tuple-element.56.re, ...), custom_call_target="tpu_custom_call", output_to_operand_aliasing={{0}: (0, {}), {1}: (1, {}), {2}: (2, {}), {3}: (3, {}), {4}... | custom-call | tf_op jit(solution)/shard_map/edges/pallas_call | solution.py:685
  20.1 1.6 %collective-permute-start.7 = (f32[64,128]{1,0:T(8,128)S(1)}, f32[64,128]{1,0:T(8,128)S(1)}, u32[]{:S(2)}, u32[]{:S(2)}) collective-permute-start(f32[64,128]{1,0:T(8,128)S(1)} %get-tuple-element.72), channel_id=1, source_target_pairs={{0,16},{16,0},{1,17},{17,1},{2,18},{18,2},{3,19},{19,3},{4,20},{20... | collective-permute-start | bytes 98312 | tf_op jit(solution)/shard_map/sum_angles/ppermute | solution.py:695
  21.7 1.0 %write.1 = (f32[6,8,16,128]{3,2,1,0:T(8,128)}, f32[6,8,16,128]{3,2,1,0:T(8,128)}) custom-call(f32[6,8,16,128]{3,2,1,0:T(8,128)S(1)} %bitcast.29, f32[6,8,16,128]{3,2,1,0:T(8,128)S(1)} %bitcast.30), custom_call_target="tpu_custom_call" | custom-call | tf_op jit(solution)/shard_map/write/pallas_call | solution.py:704
  22.6 1.5 %collective-permute-done.7.refs_1_ = f32[64,128]{1,0:T(8,128)S(1)} collective-permute-done((f32[64,128]{1,0:T(8,128)S(1)}, f32[64,128]{1,0:T(8,128)S(1)}, u32[]{:S(2)}, u32[]{:S(2)}) %collective-permute-start.7) | collective-permute-done | bytes 32800 | tf_op jit(solution)/shard_map/sum_angles/ppermute | solution.py:695
  24.1 0.7 %sum_angles.1 = f32[128,64]{1,0:T(8,128)} custom-call(f32[64,128]{1,0:T(8,128)S(1)} %get-tuple-element.71.refs_0_, f32[64,128]{1,0:T(8,128)S(1)} %collective-permute-done.7.refs_1_), custom_call_target="tpu_custom_call" | custom-call | tf_op jit(solution)/shard_map/sum_angles/pallas_call | solution.py:696
  (3 shorter events, 0.0 us)
Async XLA Ops:
  2.6 10.6 %collective-permute-start = (f32[360,128]{1,0:T(8,128)S(1)}, f32[360,128]{1,0:T(8,128)S(1)}, u32[]{:S(2)}, u32[]{:S(2)}) collective-permute-start(f32[360,128]{1,0:T(8,128)S(1)} %get-tuple-element.43), channel_id=1, source_target_pairs={{0,1},{1,2},{2,3},{3,0},{4,5},{5,6},{6,7},{7,4},{8,9},{9,10},{10,1... | collective-permute-start | bytes 552968 | tf_op jit(solution)/shard_map/send_y/ppermute | solution.py:610
  5.7 9.8 %collective-permute-start.1 = (f32[304,128]{1,0:T(8,128)S(1)}, f32[304,128]{1,0:T(8,128)S(1)}, u32[]{:S(2)}, u32[]{:S(2)}) collective-permute-start(f32[304,128]{1,0:T(8,128)S(1)} %get-tuple-element.44), channel_id=1, source_target_pairs={{0,3},{1,0},{2,1},{3,2},{4,7},{5,4},{6,5},{7,6},{8,11},{9,8},{10,9... | collective-permute-start | bytes 466952 | tf_op jit(solution)/shard_map/send_y/ppermute | solution.py:611
  7.9 9.9 %collective-permute-start.2 = (f32[608,128]{1,0:T(8,128)S(1)}, f32[608,128]{1,0:T(8,128)S(1)}, u32[]{:S(2)}, u32[]{:S(2)}) collective-permute-start(f32[608,128]{1,0:T(8,128)S(1)} %get-tuple-element.54.after), channel_id=1, source_target_pairs={{0,4},{4,8},{8,12},{12,0},{1,5},{5,9},{9,13},{13,1},{2,6},{6,10},{... | collective-permute-start | bytes 933896 | tf_op jit(solution)/shard_map/send_x/ppermute | solution.py:623
  8.0 3.9 %copy-start.2 = (f32[2,2]{1,0:T(2,128)S(1)}, f32[2,2]{1,0:T(2,128)}, u32[]{:S(2)}) copy-start(f32[2,2]{1,0:T(2,128)} %table.1) | copy-start | bytes 52
  8.0 3.9 %copy-start.3 = (s32[4]{0:T(128)S(1)}, s32[4]{0:T(128)}, u32[]{:S(2)}) copy-start(s32[4]{0:T(128)} %tiles.1) | copy-start | bytes 52
  8.0 9.8 %collective-permute-start.3 = (f32[568,128]{1,0:T(8,128)S(1)}, f32[568,128]{1,0:T(8,128)S(1)}, u32[]{:S(2)}, u32[]{:S(2)}) collective-permute-start(f32[568,128]{1,0:T(8,128)S(1)} %get-tuple-element.55), channel_id=1, source_target_pairs={{0,12},{4,0},{8,4},{12,8},{1,13},{5,1},{9,5},{13,9},{2,14},{6,2},{... | collective-permute-start | bytes 872456 | tf_op jit(solution)/shard_map/send_x/ppermute | solution.py:624
  9.8 8.8 %collective-permute-start.5 = (f32[72,128]{1,0:T(8,128)S(1)}, f32[72,128]{1,0:T(8,128)S(1)}, u32[]{:S(2)}, u32[]{:S(2)}) collective-permute-start(f32[72,128]{1,0:T(8,128)S(1)} %diagonal_corners.1), channel_id=1, source_target_pairs={{0,15},{1,12},{2,13},{3,14},{4,11},{5,8},{6,9},{7,10},{8,7},{9,4},... | collective-permute-start | bytes 110600 | tf_op jit(solution)/shard_map/diagonal_corners/ppermute | solution.py:641
  13.3 5.3 %collective-permute-start.4 = (f32[80,128]{1,0:T(8,128)S(1)}, f32[80,128]{1,0:T(8,128)S(1)}, u32[]{:S(2)}, u32[]{:S(2)}) collective-permute-start(f32[80,128]{1,0:T(8,128)S(1)} %relay_low_corners.1), channel_id=1, source_target_pairs={{0,12},{4,8},{8,4},{12,0},{1,13},{5,9},{9,5},{13,1},{2,14},{6,10},... | collective-permute-start | bytes 122888 | tf_op jit(solution)/shard_map/relay_low_corners/ppermute | solution.py:655
  15.6 2.2 %copy-start = (f32[1,6,8,16,128]{4,3,2,1,0:T(8,128)S(1)}, f32[1,6,8,16,128]{4,3,2,1,0:T(8,128)}, u32[]{:S(2)}) copy-start(f32[1,6,8,16,128]{4,3,2,1,0:T(8,128)} %param.10) | copy-start | bytes 1179652
  15.6 2.2 %copy-start.1 = (f32[1,6,8,16,128]{4,3,2,1,0:T(8,128)S(1)}, f32[1,6,8,16,128]{4,3,2,1,0:T(8,128)}, u32[]{:S(2)}) copy-start(f32[1,6,8,16,128]{4,3,2,1,0:T(8,128)} %param.11) | copy-start | bytes 1179652
  15.6 2.9 %collective-permute-start.6 = (f32[144,128]{1,0:T(8,128)S(1)}, f32[144,128]{1,0:T(8,128)S(1)}, u32[]{:S(2)}, u32[]{:S(2)}) collective-permute-start(f32[144,128]{1,0:T(8,128)S(1)} %relay_corners.1), channel_id=1, source_target_pairs={{0,4},{4,0},{8,12},{12,8},{1,5},{5,1},{9,13},{13,9},{2,6},{6,2},{1... | collective-permute-start | bytes 221192 | tf_op jit(solution)/shard_map/relay_corners/ppermute | solution.py:658
  20.1 4.0 %collective-permute-start.7 = (f32[64,128]{1,0:T(8,128)S(1)}, f32[64,128]{1,0:T(8,128)S(1)}, u32[]{:S(2)}, u32[]{:S(2)}) collective-permute-start(f32[64,128]{1,0:T(8,128)S(1)} %get-tuple-element.72), channel_id=1, source_target_pairs={{0,16},{16,0},{1,17},{17,1},{2,18},{18,2},{3,19},{19,3},{4,20},{20... | collective-permute-start | bytes 98312 | tf_op jit(solution)/shard_map/sum_angles/ppermute | solution.py:695

commit v15 on v14

--- a/solution.py
+++ b/solution.py
@@ -667,7 +667,7 @@
             out_specs=[VMEM] * count,
             input_output_aliases={0: 0, 1: STEPS + 1, 2: 1, 3: STEPS + 2, 4: count - 1},
             compiler_params=params(8),
-            cost_estimate=cost(5 * 2**29),
+            cost_estimate=cost(3 * 2**29),
         )(e0, h0, e1, h1, coef, z_low, z_high, turns)
     transforms = [lines(6 * nx * ny)] * 2
     with jax.named_scope("faces"):

time: 25 us -> 24.4 us (0.976)
  waiting for transfers between devices: 4.3 us -> 3.2 us
  starting transfers between devices: 11.1 us -> 11.6 us
    ppermute x1, waiting for transfers between devices: 0.87 us -> 0.01 us  [shards(): x_high = lax.ppermute(x_down, 'gx', ring_pairs('gx', -1))]
    ppermute x1, waiting for transfers between devices: 0.76 us -> 0.14 us  [shards(): z_low = lax.ppermute(z_up, 'gy', ring_pairs('gy', 1))]
    ppermute x1, waiting for transfers between devices: 1.19 us -> 1.59 us  [shards(): z_high = lax.ppermute(z_down, 'gy', ring_pairs('gy', -1))]
    ppermute x1, starting transfers between devices: 1.07 us -> 1.46 us  [shards(): far_low = lax.ppermute(to_far, 'gx', far_pairs())]
    ppermute x1, starting transfers between devices: 1.71 us -> 1.4 us  [shards(): x_high = lax.ppermute(x_down, 'gx', ring_pairs('gx', -1))]
    ppermute x1, starting transfers between devices: 1.46 us -> 1.74 us  [shards(): far_high = lax.ppermute(to_diagonal, ('gx', 'gy'), diagonal_pairs())]
  transfers between devices with their start and end apart: 8 -> 8, of which waited for: 4 -> 3; matrix products, arithmetic and copies ran while one was open for 0% -> 0% of each run, Pallas kernels for 15% -> 15%
where the time goes in v15:
time: 24.4 us; the launch traced here: 24.2 us
  starting transfers between devices  11.6 us (48%)
  Pallas kernels  7.93 us (32%)
  waiting for transfers between devices  3.2 us (13%)
  between operations  1.43 us (6%)
    ppermute x1, starting transfers between devices, shards(): z_low = lax.ppermute(z_up, 'gy', ring_pairs('gy', 1))  3.08 us
    ppermute x1, starting transfers between devices, shards(): z_high = lax.ppermute(z_down, 'gy', ring_pairs('gy', -1))  2.09 us
    pallas_call x1, Pallas kernels, shards(): pl.pallas_call(functools.partial(pack_y_kernel, plan), out_shape=(*[array...  2.01 us
    ppermute x1, starting transfers between devices, shards(): far_high = lax.ppermute(to_diagonal, ('gx', 'gy'), diagonal_pairs())  1.74 us
    ppermute x1, waiting for transfers between devices, shards(): z_high = lax.ppermute(z_down, 'gy', ring_pairs('gy', -1))  1.59 us
    ppermute x1, starting transfers between devices, shards(): lax.ppermute(part, 'angle', ring_pairs('angle', k + 1))  1.52 us
    pallas_call x1, Pallas kernels, shards(): pl.pallas_call(functools.partial(edges_kernel, plan, groups), out_shape=[...  1.51 us
    ppermute x1, starting transfers between devices, shards(): far_low = lax.ppermute(to_far, 'gx', far_pairs())  1.46 us
  transfers between devices with their start and end apart: 8, of which 3 were waited for; matrix products, arithmetic and copies ran while one was open for 0% of the time, Pallas kernels for 15%

profile of v15, /device:TPU:0, one launch (start us, length us, event | category | flops | bytes accessed | tf_op | source)
XLA Modules:
  0.0 24.2 jit_solution(5782935946381325592)
XLA Ops:
  0.6 2.0 %pack_y.1 = (f32[12,14,24,128]{3,2,1,0:T(8,128)S(1)}, f32[12,14,24,128]{3,2,1,0:T(8,128)S(1)}, f32[12,14,24,128]{3,2,1,0:T(8,128)S(1)}, f32[12,14,24,128]{3,2,1,...) custom-call(f32[12,8,16,128]{3,2,1,0:T(8,128)} %bitcast.33, ...), custom_call_target="tpu_custom_call" | custom-call | tf_op jit(solution)/shard_map/pack_y/pallas_call | solution.py:595
  2.6 3.1 %collective-permute-start = (f32[360,128]{1,0:T(8,128)S(1)}, f32[360,128]{1,0:T(8,128)S(1)}, u32[]{:S(2)}, u32[]{:S(2)}) collective-permute-start(f32[360,128]{1,0:T(8,128)S(1)} %get-tuple-element.43), channel_id=1, source_target_pairs={{0,1},{1,2},{2,3},{3,0},{4,5},{5,6},{6,7},{7,4},{8,9},{9,10},{10,1... | collective-permute-start | bytes 552968 | tf_op jit(solution)/shard_map/send_y/ppermute | solution.py:610
  5.7 0.1 pack_x.1
  5.8 0.1 collective-permute-start.2
  5.9 2.1 %collective-permute-start.1 = (f32[304,128]{1,0:T(8,128)S(1)}, f32[304,128]{1,0:T(8,128)S(1)}, u32[]{:S(2)}, u32[]{:S(2)}) collective-permute-start(f32[304,128]{1,0:T(8,128)S(1)} %get-tuple-element.44), channel_id=1, source_target_pairs={{0,3},{1,0},{2,1},{3,2},{4,7},{5,4},{6,5},{7,6},{8,11},{9,8},{10,9... | collective-permute-start | bytes 466952 | tf_op jit(solution)/shard_map/send_y/ppermute | solution.py:611
  8.0 0.0 copy-start.2
  8.0 1.4 %collective-permute-start.3 = (f32[568,128]{1,0:T(8,128)S(1)}, f32[568,128]{1,0:T(8,128)S(1)}, u32[]{:S(2)}, u32[]{:S(2)}) collective-permute-start(f32[568,128]{1,0:T(8,128)S(1)} %get-tuple-element.55), channel_id=1, source_target_pairs={{0,12},{4,0},{8,4},{12,8},{1,13},{5,1},{9,5},{13,9},{2,14},{6,2},{... | collective-permute-start | bytes 872456 | tf_op jit(solution)/shard_map/send_x/ppermute | solution.py:624
  9.4 1.7 %collective-permute-start.5 = (f32[72,128]{1,0:T(8,128)S(1)}, f32[72,128]{1,0:T(8,128)S(1)}, u32[]{:S(2)}, u32[]{:S(2)}) collective-permute-start(f32[72,128]{1,0:T(8,128)S(1)} %diagonal_corners.1), channel_id=1, source_target_pairs={{0,15},{1,12},{2,13},{3,14},{4,11},{5,8},{6,9},{7,10},{8,7},{9,4},... | collective-permute-start | bytes 110600 | tf_op jit(solution)/shard_map/diagonal_corners/ppermute | solution.py:641
  11.8 0.0 copy-done.2
  11.8 0.0 copy-done.3
  11.8 0.6 %turns.1.refs_13_.refs_16_ = f32[24,128]{1,0:T(8,128)S(1)} custom-call(f32[2,2]{1,0:T(2,128)S(1)} %copy-done.2, s32[1]{0:T(128)S(6)} %copy.61.index, s32[4]{0:T(128)S(1)} %copy-done.3), custom_call_target="tpu_custom_call" | custom-call | tf_op jit(solution)/shard_map/turns/pallas_call | solution.py:626
  12.4 0.1 collective-permute-done.z_low.refs_11_.refs_0_.refs_14_
  12.6 1.5 %collective-permute-start.4 = (f32[80,128]{1,0:T(8,128)S(1)}, f32[80,128]{1,0:T(8,128)S(1)}, u32[]{:S(2)}, u32[]{:S(2)}) collective-permute-start(f32[80,128]{1,0:T(8,128)S(1)} %relay_low_corners.1), channel_id=1, source_target_pairs={{0,12},{4,8},{8,4},{12,0},{1,13},{5,9},{9,5},{13,1},{2,14},{6,10},... | collective-permute-start | bytes 122888 | tf_op jit(solution)/shard_map/relay_low_corners/ppermute | solution.py:655
  14.1 1.6 %collective-permute-done.1.z_high.refs_12_.refs_1_.refs_15_ = f32[304,128]{1,0:T(8,128)S(1)} collective-permute-done((f32[304,128]{1,0:T(8,128)S(1)}, f32[304,128]{1,0:T(8,128)S(1)}, u32[]{:S(2)}, u32[]{:S(2)}) %collective-permute-start.1) | collective-permute-done | bytes 155680 | tf_op jit(solution)/shard_map/send_y/ppermute | solution.py:611
  15.7 0.1 relay_corners.1
  15.7 0.0 copy-start
  15.7 0.0 copy-start.1
  15.7 0.3 %collective-permute-start.6 = (f32[144,128]{1,0:T(8,128)S(1)}, f32[144,128]{1,0:T(8,128)S(1)}, u32[]{:S(2)}, u32[]{:S(2)}) collective-permute-start(f32[144,128]{1,0:T(8,128)S(1)} %relay_corners.1), channel_id=1, source_target_pairs={{0,4},{4,0},{8,12},{12,8},{1,5},{5,1},{9,13},{13,9},{2,6},{6,2},{1... | collective-permute-start | bytes 221192 | tf_op jit(solution)/shard_map/relay_corners/ppermute | solution.py:658
  16.0 1.2 %middle.1 = (f32[4032,128]{1,0:T(8,128)S(1)}, f32[4032,128]{1,0:T(8,128)S(1)}, f32[4032,128]{1,0:T(8,128)S(1)}, f32[4032,128]{1,0:T(8,128)S(1)}, f32[4032,128]{1...) custom-call(f32[4032,128]{1,0:T(8,128)S(1)} %bitcast.16, ...), custom_call_target="tpu_custom_call", output_to_operand_aliasing={{0}: (0, {}), {4}: (1, {}), {1}: (2, {}), {5}: (3, {}), {8}... | custom-call | flops 1610612736 | bytes 1610612736 | tf_op jit(solution)/shard_map/middle/pallas_call | solution.py:663
  17.2 0.0 collective-permute-done.3.refs_10_
  17.2 0.0 collective-permute-done.2.refs_9_
  17.3 0.0 copy-done
  17.3 0.0 copy-done.1
  17.3 0.7 %faces.1 = (f32[4032,128]{1,0:T(8,128)S(1)}, f32[4032,128]{1,0:T(8,128)S(1)}, f32[4032,128]{1,0:T(8,128)S(1)}, f32[4032,128]{1,0:T(8,128)S(1)}, f32[4032,128]{1,...) custom-call(f32[4032,128]{1,0:T(8,128)S(1)} %get-tuple-element.45.re, ...), custom_call_target="tpu_custom_call", output_to_operand_aliasing={{0}: (0, {}), {1}: (1, {}), {2}: (2, {}), {3}: (3, {}), {4}... | custom-call | tf_op jit(solution)/shard_map/faces/pallas_call | solution.py:675
  18.0 0.0 collective-permute-done.5.refs_12_
  18.0 0.0 collective-permute-done.4.refs_11_
  18.0 0.0 collective-permute-done.6.refs_13_
  18.0 1.5 %edges.1 = (f32[4032,128]{1,0:T(8,128)S(1)}, f32[4032,128]{1,0:T(8,128)S(1)}, f32[4032,128]{1,0:T(8,128)S(1)}, f32[4032,128]{1,0:T(8,128)S(1)}, f32[4032,128]{1,...) custom-call(f32[4032,128]{1,0:T(8,128)S(1)} %get-tuple-element.56.re, ...), custom_call_target="tpu_custom_call", output_to_operand_aliasing={{0}: (0, {}), {1}: (1, {}), {2}: (2, {}), {3}: (3, {}), {4}... | custom-call | tf_op jit(solution)/shard_map/edges/pallas_call | solution.py:685
  19.5 1.5 %collective-permute-start.7 = (f32[64,128]{1,0:T(8,128)S(1)}, f32[64,128]{1,0:T(8,128)S(1)}, u32[]{:S(2)}, u32[]{:S(2)}) collective-permute-start(f32[64,128]{1,0:T(8,128)S(1)} %get-tuple-element.72), channel_id=1, source_target_pairs={{0,16},{16,0},{1,17},{17,1},{2,18},{18,2},{3,19},{19,3},{4,20},{20... | collective-permute-start | bytes 98312 | tf_op jit(solution)/shard_map/sum_angles/ppermute | solution.py:695
  21.1 1.0 %write.1 = (f32[6,8,16,128]{3,2,1,0:T(8,128)}, f32[6,8,16,128]{3,2,1,0:T(8,128)}) custom-call(f32[6,8,16,128]{3,2,1,0:T(8,128)S(1)} %bitcast.29, f32[6,8,16,128]{3,2,1,0:T(8,128)S(1)} %bitcast.30), custom_call_target="tpu_custom_call" | custom-call | tf_op jit(solution)/shard_map/write/pallas_call | solution.py:704
  22.0 1.4 %collective-permute-done.7.refs_1_ = f32[64,128]{1,0:T(8,128)S(1)} collective-permute-done((f32[64,128]{1,0:T(8,128)S(1)}, f32[64,128]{1,0:T(8,128)S(1)}, u32[]{:S(2)}, u32[]{:S(2)}) %collective-permute-start.7) | collective-permute-done | bytes 32800 | tf_op jit(solution)/shard_map/sum_angles/ppermute | solution.py:695
  23.5 0.7 %sum_angles.1 = f32[128,64]{1,0:T(8,128)} custom-call(f32[64,128]{1,0:T(8,128)S(1)} %get-tuple-element.71.refs_0_, f32[64,128]{1,0:T(8,128)S(1)} %collective-permute-done.7.refs_1_), custom_call_target="tpu_custom_call" | custom-call | tf_op jit(solution)/shard_map/sum_angles/pallas_call | solution.py:696
  (3 shorter events, 0.0 us)
Async XLA Ops:
  2.6 9.9 %collective-permute-start = (f32[360,128]{1,0:T(8,128)S(1)}, f32[360,128]{1,0:T(8,128)S(1)}, u32[]{:S(2)}, u32[]{:S(2)}) collective-permute-start(f32[360,128]{1,0:T(8,128)S(1)} %get-tuple-element.43), channel_id=1, source_target_pairs={{0,1},{1,2},{2,3},{3,0},{4,5},{5,6},{6,7},{7,4},{8,9},{9,10},{10,1... | collective-permute-start | bytes 552968 | tf_op jit(solution)/shard_map/send_y/ppermute | solution.py:610
  5.8 11.4 %collective-permute-start.2 = (f32[608,128]{1,0:T(8,128)S(1)}, f32[608,128]{1,0:T(8,128)S(1)}, u32[]{:S(2)}, u32[]{:S(2)}) collective-permute-start(f32[608,128]{1,0:T(8,128)S(1)} %get-tuple-element.54.after), channel_id=1, source_target_pairs={{0,4},{4,8},{8,12},{12,0},{1,5},{5,9},{9,13},{13,1},{2,6},{6,10},{... | collective-permute-start | bytes 933896 | tf_op jit(solution)/shard_map/send_x/ppermute | solution.py:623
  5.9 9.8 %collective-permute-start.1 = (f32[304,128]{1,0:T(8,128)S(1)}, f32[304,128]{1,0:T(8,128)S(1)}, u32[]{:S(2)}, u32[]{:S(2)}) collective-permute-start(f32[304,128]{1,0:T(8,128)S(1)} %get-tuple-element.44), channel_id=1, source_target_pairs={{0,3},{1,0},{2,1},{3,2},{4,7},{5,4},{6,5},{7,6},{8,11},{9,8},{10,9... | collective-permute-start | bytes 466952 | tf_op jit(solution)/shard_map/send_y/ppermute | solution.py:611
  8.0 3.8 %copy-start.2 = (f32[2,2]{1,0:T(2,128)S(1)}, f32[2,2]{1,0:T(2,128)}, u32[]{:S(2)}) copy-start(f32[2,2]{1,0:T(2,128)} %table.1) | copy-start | bytes 52
  8.0 3.8 %copy-start.3 = (s32[4]{0:T(128)S(1)}, s32[4]{0:T(128)}, u32[]{:S(2)}) copy-start(s32[4]{0:T(128)} %tiles.1) | copy-start | bytes 52
  8.0 9.2 %collective-permute-start.3 = (f32[568,128]{1,0:T(8,128)S(1)}, f32[568,128]{1,0:T(8,128)S(1)}, u32[]{:S(2)}, u32[]{:S(2)}) collective-permute-start(f32[568,128]{1,0:T(8,128)S(1)} %get-tuple-element.55), channel_id=1, source_target_pairs={{0,12},{4,0},{8,4},{12,8},{1,13},{5,1},{9,5},{13,9},{2,14},{6,2},{... | collective-permute-start | bytes 872456 | tf_op jit(solution)/shard_map/send_x/ppermute | solution.py:624
  9.4 8.6 %collective-permute-start.5 = (f32[72,128]{1,0:T(8,128)S(1)}, f32[72,128]{1,0:T(8,128)S(1)}, u32[]{:S(2)}, u32[]{:S(2)}) collective-permute-start(f32[72,128]{1,0:T(8,128)S(1)} %diagonal_corners.1), channel_id=1, source_target_pairs={{0,15},{1,12},{2,13},{3,14},{4,11},{5,8},{6,9},{7,10},{8,7},{9,4},... | collective-permute-start | bytes 110600 | tf_op jit(solution)/shard_map/diagonal_corners/ppermute | solution.py:641
  12.6 5.4 %collective-permute-start.4 = (f32[80,128]{1,0:T(8,128)S(1)}, f32[80,128]{1,0:T(8,128)S(1)}, u32[]{:S(2)}, u32[]{:S(2)}) collective-permute-start(f32[80,128]{1,0:T(8,128)S(1)} %relay_low_corners.1), channel_id=1, source_target_pairs={{0,12},{4,8},{8,4},{12,0},{1,13},{5,9},{9,5},{13,1},{2,14},{6,10},... | collective-permute-start | bytes 122888 | tf_op jit(solution)/shard_map/relay_low_corners/ppermute | solution.py:655
  15.7 1.5 %copy-start = (f32[1,6,8,16,128]{4,3,2,1,0:T(8,128)S(1)}, f32[1,6,8,16,128]{4,3,2,1,0:T(8,128)}, u32[]{:S(2)}) copy-start(f32[1,6,8,16,128]{4,3,2,1,0:T(8,128)} %param.10) | copy-start | bytes 1179652
  15.7 1.5 %copy-start.1 = (f32[1,6,8,16,128]{4,3,2,1,0:T(8,128)S(1)}, f32[1,6,8,16,128]{4,3,2,1,0:T(8,128)}, u32[]{:S(2)}) copy-start(f32[1,6,8,16,128]{4,3,2,1,0:T(8,128)} %param.11) | copy-start | bytes 1179652
  15.7 2.3 %collective-permute-start.6 = (f32[144,128]{1,0:T(8,128)S(1)}, f32[144,128]{1,0:T(8,128)S(1)}, u32[]{:S(2)}, u32[]{:S(2)}) collective-permute-start(f32[144,128]{1,0:T(8,128)S(1)} %relay_corners.1), channel_id=1, source_target_pairs={{0,4},{4,0},{8,12},{12,8},{1,5},{5,1},{9,13},{13,9},{2,6},{6,2},{1... | collective-permute-start | bytes 221192 | tf_op jit(solution)/shard_map/relay_corners/ppermute | solution.py:658
  19.5 3.9 %collective-permute-start.7 = (f32[64,128]{1,0:T(8,128)S(1)}, f32[64,128]{1,0:T(8,128)S(1)}, u32[]{:S(2)}, u32[]{:S(2)}) collective-permute-start(f32[64,128]{1,0:T(8,128)S(1)} %get-tuple-element.72), channel_id=1, source_target_pairs={{0,16},{16,0},{1,17},{17,1},{2,18},{18,2},{3,19},{19,3},{4,20},{20... | collective-permute-start | bytes 98312 | tf_op jit(solution)/shard_map/sum_angles/ppermute | solution.py:695

commit v16 on v15

--- a/solution.py
+++ b/solution.py
@@ -113,6 +113,10 @@
                 ready.update(members)
             for into in (self.made, self.free if free else self.rest):
                 into.setdefault(key, {}).setdefault(comp, set()).add(tile)
+        self.late = {
+            key: {comp: {tile for tile in found if (tile + 1) * SUB + STEPS > ny} for comp, found in comps.items()}
+            for key, comps in self.made.items()
+        }
         sides = {}
         for node in nodes:
             sides.setdefault((node[3] // nx, node[4] // ny), set()).add(node)
@@ -399,20 +403,37 @@
                 after()
 
 
-def middle_kernel(plan, e0_in, h0_in, e1_in, h1_in, coef_in, z_low, z_high, turns, *arrays):
+def do_middle(plan, arrays, todo, take):
     nx = plan.nx
-    efield, hfield, coef = arrays[: STEPS + 1], arrays[STEPS + 1 : 2 * STEPS + 2], arrays[-1]
-    state = State(efield, hfield, coef)
+    sweeps = Sweeps(plan, arrays[: STEPS + 1], arrays[STEPS + 1 : 2 * STEPS + 2], arrays[-1], plan.ring, todo)
+    for step in range(1, STEPS + 1):
+        after = [functools.partial(take, "H", 1), functools.partial(take, "E", 1)] if step == 1 else []
+        sweeps.both(step, range(step - 1, nx - step), range(step, nx - step), *after)
+
+
+def early_kernel(plan, e0_in, h0_in, e1_in, h1_in, coef_in, z_low, turns, *arrays):
+    state = State(arrays[: STEPS + 1], arrays[STEPS + 1 : 2 * STEPS + 2], arrays[-1])
 
     def take(kinds, level):
         unpack(plan, plan.y_low, z_low, lambda y: 2, turns, state, kinds, level)
+
+    take("EHC", 0)
+    do_middle(plan, arrays, plan.made, take)
+
+
+def middle_kernel(plan, *refs):
+    count = 2 * STEPS + 3
+    z_low, z_high, turns = refs[count : count + 3]
+    arrays = refs[count + 3 :]
+    state = State(arrays[: STEPS + 1], arrays[STEPS + 1 : 2 * STEPS + 2], arrays[-1])
+
+    def take(kinds, level):
+        if level:
+            unpack(plan, plan.y_low, z_low, lambda y: 2, turns, state, kinds, level)
         unpack(plan, plan.y_high, z_high, lambda y: 3, turns, state, kinds, level)
 
     take("EHC", 0)
-    sweeps = Sweeps(plan, efield, hfield, coef, plan.ring, plan.made)
-    for step in range(1, STEPS + 1):
-        after = [lambda: take("H", 1), lambda: take("E", 1)] if step == 1 else []
-        sweeps.both(step, range(step - 1, nx - step), range(step, nx - step), *after)
+    do_middle(plan, arrays, plan.late, take)
 
 
 def add_known(plan, efield, levels, transform, out):
@@ -653,22 +674,32 @@
     with jax.named_scope("relay_low_corners"):
         (to_far,) = relay([(plan.far_low, plan.far_side)], z_low)
         far_low = lax.ppermute(to_far, "gx", far_pairs())
-    with jax.named_scope("relay_corners"):
-        (to_mate,) = relay([(plan.mate, plan.mate_side)], z_low, z_high)
-        mate = lax.ppermute(to_mate, "gx", mate_pairs())
     level = lines(12 * wide * ring)
     count = 2 * STEPS + 3
     levels = [level] * (count - 1) + [lines(wide * ring)]
+    with jax.named_scope("early"):
+        state = pl.pallas_call(
+            functools.partial(early_kernel, plan),
+            out_shape=levels,
+            in_specs=[VMEM] * 7,
+            out_specs=[VMEM] * count,
+            input_output_aliases={0: 0, 1: STEPS + 1, 2: 1, 3: STEPS + 2, 4: count - 1},
+            compiler_params=params(8),
+            cost_estimate=cost(2**10),
+        )(e0, h0, e1, h1, coef, z_low, turns)
+    with jax.named_scope("relay_corners"):
+        (to_mate,) = relay([(plan.mate, plan.mate_side)], z_low, z_high, state[-1])
+        mate = lax.ppermute(to_mate, "gx", mate_pairs())
     with jax.named_scope("middle"):
         state = pl.pallas_call(
             functools.partial(middle_kernel, plan),
             out_shape=levels,
-            in_specs=[VMEM] * 8,
+            in_specs=[VMEM] * (count + 3),
             out_specs=[VMEM] * count,
-            input_output_aliases={0: 0, 1: STEPS + 1, 2: 1, 3: STEPS + 2, 4: count - 1},
+            input_output_aliases={i: i for i in range(count)},
             compiler_params=params(8),
             cost_estimate=cost(3 * 2**29),
-        )(e0, h0, e1, h1, coef, z_low, z_high, turns)
+        )(*state, z_low, z_high, turns)
     transforms = [lines(6 * nx * ny)] * 2
     with jax.named_scope("faces"):
         spectra = [spectrum.reshape((-1, depth)) for spectrum in (forward_spectrum, adjoint_spectrum)]

time: 24.4 us -> 24.8 us (1.016)
  waiting for transfers between devices: 3.2 us -> 2.05 us
  Pallas kernels: 7.93 us -> 8.78 us
  starting transfers between devices: 11.6 us -> 12.1 us
    ppermute x1, waiting for transfers between devices: 1.59 us -> 0.44 us  [shards(): z_high = lax.ppermute(z_down, 'gy', ring_pairs('gy', -1))]
    pallas_call x0 -> x1, Pallas kernels: none -> 1.14 us  [shards(): pl.pallas_call(functools.partial(early_kernel, plan), out_shape=levels, i...]
    ppermute x1, starting transfers between devices: 0.28 us -> 0.76 us  [shards(): mate = lax.ppermute(to_mate, 'gx', mate_pairs())]
    pallas_call x1, Pallas kernels: 1.2 us -> 0.84 us  [shards(): pl.pallas_call(functools.partial(middle_kernel, plan), out_shape=levels,...]
  transfers between devices with their start and end apart: 8 -> 8, of which waited for: 3 -> 3; matrix products, arithmetic and copies ran while one was open for 0% -> 0% of each run, Pallas kernels for 15% -> 18%
where the time goes in v16:
time: 24.8 us; the launch traced here: 24.6 us
  starting transfers between devices  12.1 us (49%)
  Pallas kernels  8.78 us (35%)
  waiting for transfers between devices  2.05 us (8%)
  between operations  1.4 us (6%)
  local copies, waits for them, and re-layouts  0.26 us (1%)
    ppermute x1, starting transfers between devices, shards(): z_low = lax.ppermute(z_up, 'gy', ring_pairs('gy', 1))  3.08 us
    ppermute x1, starting transfers between devices, shards(): z_high = lax.ppermute(z_down, 'gy', ring_pairs('gy', -1))  2.09 us
    pallas_call x1, Pallas kernels, shards(): pl.pallas_call(functools.partial(pack_y_kernel, plan), out_shape=(*[array...  2.01 us
    ppermute x1, starting transfers between devices, shards(): far_high = lax.ppermute(to_diagonal, ('gx', 'gy'), diagonal_pairs())  1.74 us
    pallas_call x1, Pallas kernels, shards(): pl.pallas_call(functools.partial(edges_kernel, plan, groups), out_shape=[...  1.56 us
    ppermute x1, starting transfers between devices, shards(): lax.ppermute(part, 'angle', ring_pairs('angle', k + 1))  1.51 us
    ppermute x1, starting transfers between devices, shards(): far_low = lax.ppermute(to_far, 'gx', far_pairs())  1.46 us
    ppermute x1, waiting for transfers between devices, shards(): lax.ppermute(part, 'angle', ring_pairs('angle', k + 1))  1.45 us
  transfers between devices with their start and end apart: 8, of which 3 were waited for; matrix products, arithmetic and copies ran while one was open for 0% of the time, Pallas kernels for 18%

profile of v16, /device:TPU:0, one launch (start us, length us, event | category | flops | bytes accessed | tf_op | source)
XLA Modules:
  0.0 24.6 jit_solution(9821929584554017813)
XLA Ops:
  0.6 2.0 %pack_y.1 = (f32[12,14,24,128]{3,2,1,0:T(8,128)S(1)}, f32[12,14,24,128]{3,2,1,0:T(8,128)S(1)}, f32[12,14,24,128]{3,2,1,0:T(8,128)S(1)}, f32[12,14,24,128]{3,2,1,...) custom-call(f32[12,8,16,128]{3,2,1,0:T(8,128)} %bitcast.33, ...), custom_call_target="tpu_custom_call" | custom-call | tf_op jit(solution)/shard_map/pack_y/pallas_call | solution.py:616
  2.6 3.1 %collective-permute-start = (f32[360,128]{1,0:T(8,128)S(1)}, f32[360,128]{1,0:T(8,128)S(1)}, u32[]{:S(2)}, u32[]{:S(2)}) collective-permute-start(f32[360,128]{1,0:T(8,128)S(1)} %get-tuple-element.52), channel_id=1, source_target_pairs={{0,1},{1,2},{2,3},{3,0},{4,5},{5,6},{6,7},{7,4},{8,9},{9,10},{10,1... | collective-permute-start | bytes 552968 | tf_op jit(solution)/shard_map/send_y/ppermute | solution.py:631
  5.7 0.1 pack_x.1
  5.8 0.1 collective-permute-start.2
  5.9 2.1 %collective-permute-start.1 = (f32[304,128]{1,0:T(8,128)S(1)}, f32[304,128]{1,0:T(8,128)S(1)}, u32[]{:S(2)}, u32[]{:S(2)}) collective-permute-start(f32[304,128]{1,0:T(8,128)S(1)} %get-tuple-element.62), channel_id=1, source_target_pairs={{0,3},{1,0},{2,1},{3,2},{4,7},{5,4},{6,5},{7,6},{8,11},{9,8},{10,9... | collective-permute-start | bytes 466952 | tf_op jit(solution)/shard_map/send_y/ppermute | solution.py:632
  8.0 0.0 copy-start.2
  8.0 1.4 %collective-permute-start.3 = (f32[568,128]{1,0:T(8,128)S(1)}, f32[568,128]{1,0:T(8,128)S(1)}, u32[]{:S(2)}, u32[]{:S(2)}) collective-permute-start(f32[568,128]{1,0:T(8,128)S(1)} %get-tuple-element.73), channel_id=1, source_target_pairs={{0,12},{4,0},{8,4},{12,8},{1,13},{5,1},{9,5},{13,9},{2,14},{6,2},{... | collective-permute-start | bytes 872456 | tf_op jit(solution)/shard_map/send_x/ppermute | solution.py:645
  9.4 1.7 %collective-permute-start.5 = (f32[72,128]{1,0:T(8,128)S(1)}, f32[72,128]{1,0:T(8,128)S(1)}, u32[]{:S(2)}, u32[]{:S(2)}) collective-permute-start(f32[72,128]{1,0:T(8,128)S(1)} %diagonal_corners.1), channel_id=1, source_target_pairs={{0,15},{1,12},{2,13},{3,14},{4,11},{5,8},{6,9},{7,10},{8,7},{9,4},... | collective-permute-start | bytes 110600 | tf_op jit(solution)/shard_map/diagonal_corners/ppermute | solution.py:662
  11.8 0.0 copy-done.2
  11.8 0.0 copy-done.3
  11.8 0.6 %turns.1.refs_11_.refs_13_.refs_16_ = f32[24,128]{1,0:T(8,128)S(1)} custom-call(f32[2,2]{1,0:T(2,128)S(1)} %copy-done.2, s32[1]{0:T(128)S(6)} %copy.79.index, s32[4]{0:T(128)S(1)} %copy-done.3), custom_call_target="tpu_custom_call" | custom-call | tf_op jit(solution)/shard_map/turns/pallas_call | solution.py:647
  12.4 0.1 collective-permute-done.z_low.refs_9_.refs_11_.refs_0_.refs_14_
  12.6 1.5 %collective-permute-start.4 = (f32[80,128]{1,0:T(8,128)S(1)}, f32[80,128]{1,0:T(8,128)S(1)}, u32[]{:S(2)}, u32[]{:S(2)}) collective-permute-start(f32[80,128]{1,0:T(8,128)S(1)} %relay_low_corners.1), channel_id=1, source_target_pairs={{0,12},{4,8},{8,4},{12,0},{1,13},{5,9},{9,5},{13,1},{2,14},{6,10},... | collective-permute-start | bytes 122888 | tf_op jit(solution)/shard_map/relay_low_corners/ppermute | solution.py:676
  14.1 1.1 %early.1 = (f32[4032,128]{1,0:T(8,128)S(1)}, f32[4032,128]{1,0:T(8,128)S(1)}, f32[4032,128]{1,0:T(8,128)S(1)}, f32[4032,128]{1,0:T(8,128)S(1)}, f32[4032,128]{1,...) custom-call(f32[4032,128]{1,0:T(8,128)S(1)} %bitcast.16, ...), custom_call_target="tpu_custom_call", output_to_operand_aliasing={{0}: (0, {}), {4}: (1, {}), {1}: (2, {}), {5}: (3, {}), {8}... | custom-call | flops 1024 | bytes 1024 | tf_op jit(solution)/shard_map/early/pallas_call | solution.py:681
  15.2 0.4 %collective-permute-done.1.refs_10_.refs_12_.refs_1_.refs_15_ = f32[304,128]{1,0:T(8,128)S(1)} collective-permute-done((f32[304,128]{1,0:T(8,128)S(1)}, f32[304,128]{1,0:T(8,128)S(1)}, u32[]{:S(2)}, u32[]{:S(2)}) %collective-permute-start.1) | collective-permute-done | bytes 155680 | tf_op jit(solution)/shard_map/send_y/ppermute | solution.py:632
  15.7 0.1 relay_corners.1
  15.7 0.8 %collective-permute-start.6 = (f32[144,128]{1,0:T(8,128)S(1)}, f32[144,128]{1,0:T(8,128)S(1)}, u32[]{:S(2)}, u32[]{:S(2)}) collective-permute-start(f32[144,128]{1,0:T(8,128)S(1)} %relay_corners.1), channel_id=1, source_target_pairs={{0,4},{4,0},{8,12},{12,8},{1,5},{5,1},{9,13},{13,9},{2,6},{6,2},{1... | collective-permute-start | bytes 221192 | tf_op jit(solution)/shard_map/relay_corners/ppermute | solution.py:692
  16.5 0.0 copy-start.1
  16.5 0.8 %middle.1 = (f32[4032,128]{1,0:T(8,128)S(1)}, f32[4032,128]{1,0:T(8,128)S(1)}, f32[4032,128]{1,0:T(8,128)S(1)}, f32[4032,128]{1,0:T(8,128)S(1)}, f32[4032,128]{1...) custom-call(f32[4032,128]{1,0:T(8,128)S(1)} %get-tuple-element.53.re, ...), custom_call_target="tpu_custom_call", output_to_operand_aliasing={{0}: (0, {}), {1}: (1, {}), {2}: (2, {}), {3}: (3, {}), {4}... | custom-call | flops 1610612736 | bytes 1610612736 | tf_op jit(solution)/shard_map/middle/pallas_call | solution.py:694
  17.3 0.0 collective-permute-done.3.refs_10_
  17.3 0.0 collective-permute-done.2.refs_9_
  17.4 0.1 copy-done
  17.5 0.1 copy-done.1
  17.6 0.7 %faces.1 = (f32[4032,128]{1,0:T(8,128)S(1)}, f32[4032,128]{1,0:T(8,128)S(1)}, f32[4032,128]{1,0:T(8,128)S(1)}, f32[4032,128]{1,0:T(8,128)S(1)}, f32[4032,128]{1,...) custom-call(f32[4032,128]{1,0:T(8,128)S(1)} %get-tuple-element.63.re, ...), custom_call_target="tpu_custom_call", output_to_operand_aliasing={{0}: (0, {}), {1}: (1, {}), {2}: (2, {}), {3}: (3, {}), {4}... | custom-call | tf_op jit(solution)/shard_map/faces/pallas_call | solution.py:706
  18.3 0.0 collective-permute-done.5.refs_12_
  18.4 0.0 collective-permute-done.4.refs_11_
  18.4 0.0 collective-permute-done.6.refs_13_
  18.4 1.6 %edges.1 = (f32[4032,128]{1,0:T(8,128)S(1)}, f32[4032,128]{1,0:T(8,128)S(1)}, f32[4032,128]{1,0:T(8,128)S(1)}, f32[4032,128]{1,0:T(8,128)S(1)}, f32[4032,128]{1,...) custom-call(f32[4032,128]{1,0:T(8,128)S(1)} %get-tuple-element.74.re, ...), custom_call_target="tpu_custom_call", output_to_operand_aliasing={{0}: (0, {}), {1}: (1, {}), {2}: (2, {}), {3}: (3, {}), {4}... | custom-call | tf_op jit(solution)/shard_map/edges/pallas_call | solution.py:716
  19.9 1.5 %collective-permute-start.7 = (f32[64,128]{1,0:T(8,128)S(1)}, f32[64,128]{1,0:T(8,128)S(1)}, u32[]{:S(2)}, u32[]{:S(2)}) collective-permute-start(f32[64,128]{1,0:T(8,128)S(1)} %get-tuple-element.90), channel_id=1, source_target_pairs={{0,16},{16,0},{1,17},{17,1},{2,18},{18,2},{3,19},{19,3},{4,20},{20... | collective-permute-start | bytes 98312 | tf_op jit(solution)/shard_map/sum_angles/ppermute | solution.py:726
  21.5 1.0 %write.1 = (f32[6,8,16,128]{3,2,1,0:T(8,128)}, f32[6,8,16,128]{3,2,1,0:T(8,128)}) custom-call(f32[6,8,16,128]{3,2,1,0:T(8,128)S(1)} %bitcast.29, f32[6,8,16,128]{3,2,1,0:T(8,128)S(1)} %bitcast.30), custom_call_target="tpu_custom_call" | custom-call | tf_op jit(solution)/shard_map/write/pallas_call | solution.py:735
  22.4 1.4 %collective-permute-done.7.refs_1_ = f32[64,128]{1,0:T(8,128)S(1)} collective-permute-done((f32[64,128]{1,0:T(8,128)S(1)}, f32[64,128]{1,0:T(8,128)S(1)}, u32[]{:S(2)}, u32[]{:S(2)}) %collective-permute-start.7) | collective-permute-done | bytes 32800 | tf_op jit(solution)/shard_map/sum_angles/ppermute | solution.py:726
  23.9 0.7 %sum_angles.1 = f32[128,64]{1,0:T(8,128)} custom-call(f32[64,128]{1,0:T(8,128)S(1)} %get-tuple-element.89.refs_0_, f32[64,128]{1,0:T(8,128)S(1)} %collective-permute-done.7.refs_1_), custom_call_target="tpu_custom_call" | custom-call | tf_op jit(solution)/shard_map/sum_angles/pallas_call | solution.py:727
  (4 shorter events, 0.0 us)
Async XLA Ops:
  2.6 9.9 %collective-permute-start = (f32[360,128]{1,0:T(8,128)S(1)}, f32[360,128]{1,0:T(8,128)S(1)}, u32[]{:S(2)}, u32[]{:S(2)}) collective-permute-start(f32[360,128]{1,0:T(8,128)S(1)} %get-tuple-element.52), channel_id=1, source_target_pairs={{0,1},{1,2},{2,3},{3,0},{4,5},{5,6},{6,7},{7,4},{8,9},{9,10},{10,1... | collective-permute-start | bytes 552968 | tf_op jit(solution)/shard_map/send_y/ppermute | solution.py:631
  5.8 11.5 %collective-permute-start.2 = (f32[608,128]{1,0:T(8,128)S(1)}, f32[608,128]{1,0:T(8,128)S(1)}, u32[]{:S(2)}, u32[]{:S(2)}) collective-permute-start(f32[608,128]{1,0:T(8,128)S(1)} %get-tuple-element.72.after), channel_id=1, source_target_pairs={{0,4},{4,8},{8,12},{12,0},{1,5},{5,9},{9,13},{13,1},{2,6},{6,10},{... | collective-permute-start | bytes 933896 | tf_op jit(solution)/shard_map/send_x/ppermute | solution.py:644
  5.9 9.8 %collective-permute-start.1 = (f32[304,128]{1,0:T(8,128)S(1)}, f32[304,128]{1,0:T(8,128)S(1)}, u32[]{:S(2)}, u32[]{:S(2)}) collective-permute-start(f32[304,128]{1,0:T(8,128)S(1)} %get-tuple-element.62), channel_id=1, source_target_pairs={{0,3},{1,0},{2,1},{3,2},{4,7},{5,4},{6,5},{7,6},{8,11},{9,8},{10,9... | collective-permute-start | bytes 466952 | tf_op jit(solution)/shard_map/send_y/ppermute | solution.py:632
  8.0 3.8 %copy-start.2 = (f32[2,2]{1,0:T(2,128)S(1)}, f32[2,2]{1,0:T(2,128)}, u32[]{:S(2)}) copy-start(f32[2,2]{1,0:T(2,128)} %table.1) | copy-start | bytes 52
  8.0 3.8 %copy-start.3 = (s32[4]{0:T(128)S(1)}, s32[4]{0:T(128)}, u32[]{:S(2)}) copy-start(s32[4]{0:T(128)} %tiles.1) | copy-start | bytes 52
  8.0 9.3 %collective-permute-start.3 = (f32[568,128]{1,0:T(8,128)S(1)}, f32[568,128]{1,0:T(8,128)S(1)}, u32[]{:S(2)}, u32[]{:S(2)}) collective-permute-start(f32[568,128]{1,0:T(8,128)S(1)} %get-tuple-element.73), channel_id=1, source_target_pairs={{0,12},{4,0},{8,4},{12,8},{1,13},{5,1},{9,5},{13,9},{2,14},{6,2},{... | collective-permute-start | bytes 872456 | tf_op jit(solution)/shard_map/send_x/ppermute | solution.py:645
  9.4 8.9 %collective-permute-start.5 = (f32[72,128]{1,0:T(8,128)S(1)}, f32[72,128]{1,0:T(8,128)S(1)}, u32[]{:S(2)}, u32[]{:S(2)}) collective-permute-start(f32[72,128]{1,0:T(8,128)S(1)} %diagonal_corners.1), channel_id=1, source_target_pairs={{0,15},{1,12},{2,13},{3,14},{4,11},{5,8},{6,9},{7,10},{8,7},{9,4},... | collective-permute-start | bytes 110600 | tf_op jit(solution)/shard_map/diagonal_corners/ppermute | solution.py:662
  12.6 5.7 %collective-permute-start.4 = (f32[80,128]{1,0:T(8,128)S(1)}, f32[80,128]{1,0:T(8,128)S(1)}, u32[]{:S(2)}, u32[]{:S(2)}) collective-permute-start(f32[80,128]{1,0:T(8,128)S(1)} %relay_low_corners.1), channel_id=1, source_target_pairs={{0,12},{4,8},{8,4},{12,0},{1,13},{5,9},{9,5},{13,1},{2,14},{6,10},... | collective-permute-start | bytes 122888 | tf_op jit(solution)/shard_map/relay_low_corners/ppermute | solution.py:676
  15.7 2.6 %collective-permute-start.6 = (f32[144,128]{1,0:T(8,128)S(1)}, f32[144,128]{1,0:T(8,128)S(1)}, u32[]{:S(2)}, u32[]{:S(2)}) collective-permute-start(f32[144,128]{1,0:T(8,128)S(1)} %relay_corners.1), channel_id=1, source_target_pairs={{0,4},{4,0},{8,12},{12,8},{1,5},{5,1},{9,13},{13,9},{2,6},{6,2},{1... | collective-permute-start | bytes 221192 | tf_op jit(solution)/shard_map/relay_corners/ppermute | solution.py:692
  16.5 1.0 %copy-start = (f32[1,6,8,16,128]{4,3,2,1,0:T(8,128)S(1)}, f32[1,6,8,16,128]{4,3,2,1,0:T(8,128)}, u32[]{:S(2)}) copy-start(f32[1,6,8,16,128]{4,3,2,1,0:T(8,128)} %param.10) | copy-start | bytes 1179652
  16.5 1.1 %copy-start.1 = (f32[1,6,8,16,128]{4,3,2,1,0:T(8,128)S(1)}, f32[1,6,8,16,128]{4,3,2,1,0:T(8,128)}, u32[]{:S(2)}) copy-start(f32[1,6,8,16,128]{4,3,2,1,0:T(8,128)} %param.11) | copy-start | bytes 1179652
  19.9 3.9 %collective-permute-start.7 = (f32[64,128]{1,0:T(8,128)S(1)}, f32[64,128]{1,0:T(8,128)S(1)}, u32[]{:S(2)}, u32[]{:S(2)}) collective-permute-start(f32[64,128]{1,0:T(8,128)S(1)} %get-tuple-element.90), channel_id=1, source_target_pairs={{0,16},{16,0},{1,17},{17,1},{2,18},{18,2},{3,19},{19,3},{4,20},{20... | collective-permute-start | bytes 98312 | tf_op jit(solution)/shard_map/sum_angles/ppermute | solution.py:726

commit v17 on v15

--- a/solution.py
+++ b/solution.py
@@ -95,24 +95,9 @@
         self.nx, self.ny = nx, ny
         self.wide, self.ring = nx + 2 * STEPS, ny + SUB
         nodes, made = wanted(nx, ny)
-        self.made, self.free, self.rest = {}, {}, {}
-        tiles, ready = {}, set()
-        for node in made:
-            tiles.setdefault((node[1], "HE".index(node[0]), *node[2:4], node[4] % self.ring // SUB), []).append(node)
-
-        def early(node):
-            if node in made:
-                return node in ready
-            return node not in nodes or 0 <= node[3] < nx or 0 <= node[4] < ny
-
-        for (level, order, comp, x, tile), members in sorted(tiles.items()):
-            key = ("HE"[order], level, x)
-            middle = level - 1 + order <= x < nx - level
-            free = middle or all(early(other) for node in members for other in reads(node))
-            if free:
-                ready.update(members)
-            for into in (self.made, self.free if free else self.rest):
-                into.setdefault(key, {}).setdefault(comp, set()).add(tile)
+        self.made = {}
+        for kind, level, comp, x, y in made:
+            self.made.setdefault((kind, level, x), {}).setdefault(comp, set()).add(y % self.ring // SUB)
         sides = {}
         for node in nodes:
             sides.setdefault((node[3] // nx, node[4] // ny), set()).add(node)
@@ -415,7 +400,7 @@
         sweeps.both(step, range(step - 1, nx - step), range(step, nx - step), *after)
 
 
-def add_known(plan, efield, levels, transform, out):
+def add_up(plan, efield, transform, out):
     nx, ny = plan.nx, plan.ny
     for x in range(nx):
         for tile in range(ny // SUB):
@@ -424,7 +409,7 @@
                 for run in (0, 1):
                     at = [pl.ds(((part * 3 + comp) * nx + x) * ny + tile * SUB, SUB) for part in (0, 1)]
                     real, imag = transform[run][at[0], :], transform[run][at[1], :]
-                    for level in levels(x, tile, comp):
+                    for level in range(1, STEPS + 1):
                         theta = omega_step * level
                         here = [efield[level][pl.ds(plan.row(x, tile * SUB, run, part, comp), SUB), :] for part in (0, 1)]
                         more = turned(*here, math.cos(theta), math.sin(theta))
@@ -434,13 +419,6 @@
                 yield x, tile, ends
 
 
-def known(plan, x, tile, comp):
-    def ready(level):
-        return level <= x < plan.nx - level or tile in plan.free.get(("E", level, x), {}).get(comp, ())
-
-    return [level for level in range(1, STEPS + 1) if ready(level)]
-
-
 def do_valleys(plan, sweeps, take):
     for step in range(1, STEPS + 1):
         low, high = step - STEPS, plan.nx - step
@@ -450,38 +428,17 @@
         sweeps.both(step, h_layers, e_layers, *after)
 
 
-def faces_kernel(plan, *refs):
-    count = 2 * STEPS + 3
-    x_low, x_high, z_low, z_high, turns, spec_f, spec_a = refs[count : count + 7]
-    arrays = refs[count + 7 : 2 * count + 7]
-    out_f, out_a = refs[2 * count + 7 :]
-    efield, hfield, coef = arrays[: STEPS + 1], arrays[STEPS + 1 : 2 * STEPS + 2], arrays[-1]
-    state = State(efield, hfield, coef)
-
-    def take(kinds, level, layers):
-        unpack(plan, plan.x_low, x_low, lambda y: 0, turns, state, kinds, level)
-        unpack(plan, plan.x_high, x_high, lambda y: 1, turns, state, kinds, level)
-        unpack(plan, plan.y_low, z_low, lambda y: 2, turns, state, kinds, level, layers)
-        unpack(plan, plan.y_high, z_high, lambda y: 3, turns, state, kinds, level, layers)
-
-    take("EHC", 0, ())
-    do_valleys(plan, Sweeps(plan, efield, hfield, coef, plan.ring, plan.free), take)
-    for _ in add_known(plan, efield, functools.partial(known, plan), (spec_f, spec_a), (out_f, out_a)):
-        pass
-
-
 def edges_kernel(plan, groups, *refs):
     count = 2 * STEPS + 3
-    x_low, x_high, far_low, far_high, mate, z_low, z_high, turns, part_f, part_a = refs[count : count + 10]
+    x_low, x_high, far_low, far_high, mate, z_low, z_high, turns, spec_f, spec_a = refs[count : count + 10]
     arrays = refs[count + 10 : 2 * count + 10]
     out_f, out_a, *parts = refs[2 * count + 10 :]
     efield, hfield, coef = arrays[: STEPS + 1], arrays[STEPS + 1 : 2 * STEPS + 2], arrays[-1]
     state = State(efield, hfield, coef)
 
     def take(kinds, level, layers):
-        if level:
-            unpack(plan, plan.x_low, x_low, lambda y: 0, turns, state, kinds, level)
-            unpack(plan, plan.x_high, x_high, lambda y: 1, turns, state, kinds, level)
+        unpack(plan, plan.x_low, x_low, lambda y: 0, turns, state, kinds, level)
+        unpack(plan, plan.x_high, x_high, lambda y: 1, turns, state, kinds, level)
 
         def corners(receiver):
             for messages, ref, side in (
@@ -497,17 +454,14 @@
         unpack(plan, plan.y_high, z_high, lambda y: 3, turns, state, kinds, level, layers)
 
     take("EHC", 0, ())
-    do_valleys(plan, Sweeps(plan, efield, hfield, coef, plan.ring, plan.rest), take)
+    do_valleys(plan, Sweeps(plan, efield, hfield, coef, plan.ring, plan.made), take)
 
     share = plan.depth // groups
     shift = lax.rem(groups - lax.axis_index("angle"), groups) * share
     weight = turns[pl.ds(2 * SUB, SUB), :]
 
-    def rest(x, tile, comp):
-        return [level for level in range(1, STEPS + 1) if level not in known(plan, x, tile, comp)]
-
     totals = {}
-    for x, tile, ends in add_known(plan, efield, rest, (part_f, part_a), (out_f, out_a)):
+    for x, tile, ends in add_up(plan, efield, (spec_f, spec_a), (out_f, out_a)):
         term = ends[0][0] * ends[1][0] - ends[0][1] * ends[1][1]
         totals[x, tile] = totals[x, tile] + term if (x, tile) in totals else term
     block = lax.broadcasted_iota(jnp.int32, weight.shape, 1) // share
@@ -670,26 +624,16 @@
             cost_estimate=cost(3 * 2**29),
         )(e0, h0, e1, h1, coef, z_low, z_high, turns)
     transforms = [lines(6 * nx * ny)] * 2
-    with jax.named_scope("faces"):
+    with jax.named_scope("edges"):
         spectra = [spectrum.reshape((-1, depth)) for spectrum in (forward_spectrum, adjoint_spectrum)]
-        results = pl.pallas_call(
-            functools.partial(faces_kernel, plan),
-            out_shape=[*levels, *transforms],
-            in_specs=[VMEM] * (count + 7),
-            out_specs=[VMEM] * (count + 2),
-            input_output_aliases={i: i for i in range(count)},
-            compiler_params=params(8),
-        )(*state, x_low, x_high, z_low, z_high, turns, *spectra)
-        state, sums = results[:count], results[count:]
-    with jax.named_scope("edges"):
         results = pl.pallas_call(
             functools.partial(edges_kernel, plan, groups),
             out_shape=[*levels, *transforms, *[lines(nx * ny // groups)] * groups],
             in_specs=[VMEM] * (count + 10),
             out_specs=[VMEM] * (count + 2 + groups),
-            input_output_aliases={i: i for i in range(count)} | {count + 8: count, count + 9: count + 1},
+            input_output_aliases={i: i for i in range(count)},
             compiler_params=params(8),
-        )(*state, x_low, x_high, far_low, far_high, mate, z_low, z_high, turns, *sums)
+        )(*state, x_low, x_high, far_low, far_high, mate, z_low, z_high, turns, *spectra)
         tr_f, tr_a, own, *others = results[count:]
     with jax.named_scope("sum_angles"):
         others = [lax.ppermute(part, "angle", ring_pairs("angle", k + 1)) for k, part in enumerate(others)]

time: 24.4 us -> 24.1 us (0.988)
  Pallas kernels: 7.93 us -> 7.38 us
  waiting for transfers between devices: 3.2 us -> 3.49 us
    pallas_call x1 -> x0, Pallas kernels: 0.72 us -> none  [shards(): pl.pallas_call(functools.partial(faces_kernel, plan), out_shape=[*levels,...]
    ppermute x1, waiting for transfers between devices: 0.01 us -> 0.3 us  [shards(): far_high = lax.ppermute(to_diagonal, ('gx', 'gy'), diagonal_pairs())]
    pallas_call x1, Pallas kernels: 1.51 us -> 1.78 us  [shards(): pl.pallas_call(functools.partial(edges_kernel, plan, groups), out_shape=[...]
  transfers between devices with their start and end apart: 8 -> 8, of which waited for: 3 -> 4; matrix products, arithmetic and copies ran while one was open for 0% -> 0% of each run, Pallas kernels for 15% -> 12%
where the time goes in v17:
time: 24.1 us; the launch traced here: 23.9 us
  starting transfers between devices  11.6 us (48%)
  Pallas kernels  7.38 us (31%)
  waiting for transfers between devices  3.49 us (14%)
  between operations  1.4 us (6%)
    ppermute x1, starting transfers between devices, shards(): z_low = lax.ppermute(z_up, 'gy', ring_pairs('gy', 1))  3.08 us
    ppermute x1, starting transfers between devices, shards(): z_high = lax.ppermute(z_down, 'gy', ring_pairs('gy', -1))  2.09 us
    pallas_call x1, Pallas kernels, shards(): pl.pallas_call(functools.partial(pack_y_kernel, plan), out_shape=(*[array...  1.99 us
    pallas_call x1, Pallas kernels, shards(): pl.pallas_call(functools.partial(edges_kernel, plan, groups), out_shape=[...  1.78 us
    ppermute x1, starting transfers between devices, shards(): far_high = lax.ppermute(to_diagonal, ('gx', 'gy'), diagonal_pairs())  1.74 us
    ppermute x1, waiting for transfers between devices, shards(): z_high = lax.ppermute(z_down, 'gy', ring_pairs('gy', -1))  1.59 us
    ppermute x1, starting transfers between devices, shards(): lax.ppermute(part, 'angle', ring_pairs('angle', k + 1))  1.51 us
    ppermute x1, starting transfers between devices, shards(): far_low = lax.ppermute(to_far, 'gx', far_pairs())  1.46 us
  transfers between devices with their start and end apart: 8, of which 4 were waited for; matrix products, arithmetic and copies ran while one was open for 0% of the time, Pallas kernels for 12%

profile of v17, /device:TPU:0, one launch (start us, length us, event | category | flops | bytes accessed | tf_op | source)
XLA Modules:
  0.0 23.9 jit_solution(8460871599769955866)
XLA Ops:
  0.6 2.0 %pack_y.1 = (f32[12,14,24,128]{3,2,1,0:T(8,128)S(1)}, f32[12,14,24,128]{3,2,1,0:T(8,128)S(1)}, f32[12,14,24,128]{3,2,1,0:T(8,128)S(1)}, f32[12,14,24,128]{3,2,1,...) custom-call(f32[12,8,16,128]{3,2,1,0:T(8,128)} %bitcast.33, ...), custom_call_target="tpu_custom_call" | custom-call | tf_op jit(solution)/shard_map/pack_y/pallas_call | solution.py:549
  2.6 3.1 %collective-permute-start = (f32[360,128]{1,0:T(8,128)S(1)}, f32[360,128]{1,0:T(8,128)S(1)}, u32[]{:S(2)}, u32[]{:S(2)}) collective-permute-start(f32[360,128]{1,0:T(8,128)S(1)} %get-tuple-element.32), channel_id=1, source_target_pairs={{0,1},{1,2},{2,3},{3,0},{4,5},{5,6},{6,7},{7,4},{8,9},{9,10},{10,1... | collective-permute-start | bytes 552968 | tf_op jit(solution)/shard_map/send_y/ppermute | solution.py:564
  5.7 0.1 pack_x.1
  5.8 0.1 collective-permute-start.2
  5.9 2.1 %collective-permute-start.1 = (f32[304,128]{1,0:T(8,128)S(1)}, f32[304,128]{1,0:T(8,128)S(1)}, u32[]{:S(2)}, u32[]{:S(2)}) collective-permute-start(f32[304,128]{1,0:T(8,128)S(1)} %get-tuple-element.33), channel_id=1, source_target_pairs={{0,3},{1,0},{2,1},{3,2},{4,7},{5,4},{6,5},{7,6},{8,11},{9,8},{10,9... | collective-permute-start | bytes 466952 | tf_op jit(solution)/shard_map/send_y/ppermute | solution.py:565
  8.0 0.0 copy-start.2
  8.0 0.0 copy-start.3
  8.0 1.4 %collective-permute-start.3 = (f32[568,128]{1,0:T(8,128)S(1)}, f32[568,128]{1,0:T(8,128)S(1)}, u32[]{:S(2)}, u32[]{:S(2)}) collective-permute-start(f32[568,128]{1,0:T(8,128)S(1)} %get-tuple-element.44), channel_id=1, source_target_pairs={{0,12},{4,0},{8,4},{12,8},{1,13},{5,1},{9,5},{13,9},{2,14},{6,2},{... | collective-permute-start | bytes 872456 | tf_op jit(solution)/shard_map/send_x/ppermute | solution.py:578
  9.4 1.7 %collective-permute-start.5 = (f32[72,128]{1,0:T(8,128)S(1)}, f32[72,128]{1,0:T(8,128)S(1)}, u32[]{:S(2)}, u32[]{:S(2)}) collective-permute-start(f32[72,128]{1,0:T(8,128)S(1)} %diagonal_corners.1), channel_id=1, source_target_pairs={{0,15},{1,12},{2,13},{3,14},{4,11},{5,8},{6,9},{7,10},{8,7},{9,4},... | collective-permute-start | bytes 110600 | tf_op jit(solution)/shard_map/diagonal_corners/ppermute | solution.py:595
  11.8 0.0 copy-done.2
  11.8 0.0 copy-done.3
  11.8 0.6 %turns.1.refs_16_ = f32[24,128]{1,0:T(8,128)S(1)} custom-call(f32[2,2]{1,0:T(2,128)S(1)} %copy-done.2, s32[1]{0:T(128)S(6)} %copy.39.index, s32[4]{0:T(128)S(1)} %copy-done.3), custom_call_target="tpu_custom_call" | custom-call | tf_op jit(solution)/shard_map/turns/pallas_call | solution.py:580
  12.4 0.1 collective-permute-done.z_low.refs_0_.refs_14_
  12.6 1.5 %collective-permute-start.4 = (f32[80,128]{1,0:T(8,128)S(1)}, f32[80,128]{1,0:T(8,128)S(1)}, u32[]{:S(2)}, u32[]{:S(2)}) collective-permute-start(f32[80,128]{1,0:T(8,128)S(1)} %relay_low_corners.1), channel_id=1, source_target_pairs={{0,12},{4,8},{8,4},{12,0},{1,13},{5,9},{9,5},{13,1},{2,14},{6,10},... | collective-permute-start | bytes 122888 | tf_op jit(solution)/shard_map/relay_low_corners/ppermute | solution.py:609
  14.1 1.6 %collective-permute-done.1.z_high.refs_1_.refs_15_ = f32[304,128]{1,0:T(8,128)S(1)} collective-permute-done((f32[304,128]{1,0:T(8,128)S(1)}, f32[304,128]{1,0:T(8,128)S(1)}, u32[]{:S(2)}, u32[]{:S(2)}) %collective-permute-start.1) | collective-permute-done | bytes 155680 | tf_op jit(solution)/shard_map/send_y/ppermute | solution.py:565
  15.7 0.1 relay_corners.1
  15.7 0.0 copy-start
  15.7 0.0 copy-start.1
  15.7 0.3 %collective-permute-start.6 = (f32[144,128]{1,0:T(8,128)S(1)}, f32[144,128]{1,0:T(8,128)S(1)}, u32[]{:S(2)}, u32[]{:S(2)}) collective-permute-start(f32[144,128]{1,0:T(8,128)S(1)} %relay_corners.1), channel_id=1, source_target_pairs={{0,4},{4,0},{8,12},{12,8},{1,5},{5,1},{9,13},{13,9},{2,6},{6,2},{1... | collective-permute-start | bytes 221192 | tf_op jit(solution)/shard_map/relay_corners/ppermute | solution.py:612
  16.0 1.1 %middle.1 = (f32[4032,128]{1,0:T(8,128)S(1)}, f32[4032,128]{1,0:T(8,128)S(1)}, f32[4032,128]{1,0:T(8,128)S(1)}, f32[4032,128]{1,0:T(8,128)S(1)}, f32[4032,128]{1...) custom-call(f32[4032,128]{1,0:T(8,128)S(1)} %bitcast.16, ...), custom_call_target="tpu_custom_call", output_to_operand_aliasing={{0}: (0, {}), {4}: (1, {}), {1}: (2, {}), {5}: (3, {}), {8}... | custom-call | flops 1610612736 | bytes 1610612736 | tf_op jit(solution)/shard_map/middle/pallas_call | solution.py:617
  17.1 0.3 %collective-permute-done.5.refs_12_ = f32[72,128]{1,0:T(8,128)S(1)} collective-permute-done((f32[72,128]{1,0:T(8,128)S(1)}, f32[72,128]{1,0:T(8,128)S(1)}, u32[]{:S(2)}, u32[]{:S(2)}) %collective-permute-start.5) | collective-permute-done | bytes 36896 | tf_op jit(solution)/shard_map/diagonal_corners/ppermute | solution.py:595
  17.4 0.0 collective-permute-done.4.refs_11_
  17.4 0.0 collective-permute-done.6.refs_13_
  17.4 0.0 collective-permute-done.3.refs_10_
  17.5 0.0 collective-permute-done.2.refs_9_
  17.5 0.0 copy-done
  17.5 0.0 copy-done.1
  17.5 1.8 %edges.1 = (f32[4032,128]{1,0:T(8,128)S(1)}, f32[4032,128]{1,0:T(8,128)S(1)}, f32[4032,128]{1,0:T(8,128)S(1)}, f32[4032,128]{1,0:T(8,128)S(1)}, f32[4032,128]{1,...) custom-call(f32[4032,128]{1,0:T(8,128)S(1)} %get-tuple-element.34.re, ...), custom_call_target="tpu_custom_call", output_to_operand_aliasing={{0}: (0, {}), {1}: (1, {}), {2}: (2, {}), {3}: (3, {}), {4}... | custom-call | tf_op jit(solution)/shard_map/edges/pallas_call | solution.py:629
  19.3 1.5 %collective-permute-start.7 = (f32[64,128]{1,0:T(8,128)S(1)}, f32[64,128]{1,0:T(8,128)S(1)}, u32[]{:S(2)}, u32[]{:S(2)}) collective-permute-start(f32[64,128]{1,0:T(8,128)S(1)} %get-tuple-element.50), channel_id=1, source_target_pairs={{0,16},{16,0},{1,17},{17,1},{2,18},{18,2},{3,19},{19,3},{4,20},{20... | collective-permute-start | bytes 98312 | tf_op jit(solution)/shard_map/sum_angles/ppermute | solution.py:639
  20.8 1.0 %write.1 = (f32[6,8,16,128]{3,2,1,0:T(8,128)}, f32[6,8,16,128]{3,2,1,0:T(8,128)}) custom-call(f32[6,8,16,128]{3,2,1,0:T(8,128)S(1)} %bitcast.29, f32[6,8,16,128]{3,2,1,0:T(8,128)S(1)} %bitcast.30), custom_call_target="tpu_custom_call" | custom-call | tf_op jit(solution)/shard_map/write/pallas_call | solution.py:648
  21.8 1.4 %collective-permute-done.7.refs_1_ = f32[64,128]{1,0:T(8,128)S(1)} collective-permute-done((f32[64,128]{1,0:T(8,128)S(1)}, f32[64,128]{1,0:T(8,128)S(1)}, u32[]{:S(2)}, u32[]{:S(2)}) %collective-permute-start.7) | collective-permute-done | bytes 32800 | tf_op jit(solution)/shard_map/sum_angles/ppermute | solution.py:639
  23.2 0.7 %sum_angles.1 = f32[128,64]{1,0:T(8,128)} custom-call(f32[64,128]{1,0:T(8,128)S(1)} %get-tuple-element.49.refs_0_, f32[64,128]{1,0:T(8,128)S(1)} %collective-permute-done.7.refs_1_), custom_call_target="tpu_custom_call" | custom-call | tf_op jit(solution)/shard_map/sum_angles/pallas_call | solution.py:640
  (2 shorter events, 0.0 us)
Async XLA Ops:
  2.6 9.9 %collective-permute-start = (f32[360,128]{1,0:T(8,128)S(1)}, f32[360,128]{1,0:T(8,128)S(1)}, u32[]{:S(2)}, u32[]{:S(2)}) collective-permute-start(f32[360,128]{1,0:T(8,128)S(1)} %get-tuple-element.32), channel_id=1, source_target_pairs={{0,1},{1,2},{2,3},{3,0},{4,5},{5,6},{6,7},{7,4},{8,9},{9,10},{10,1... | collective-permute-start | bytes 552968 | tf_op jit(solution)/shard_map/send_y/ppermute | solution.py:564
  5.8 11.6 %collective-permute-start.2 = (f32[608,128]{1,0:T(8,128)S(1)}, f32[608,128]{1,0:T(8,128)S(1)}, u32[]{:S(2)}, u32[]{:S(2)}) collective-permute-start(f32[608,128]{1,0:T(8,128)S(1)} %get-tuple-element.43.after), channel_id=1, source_target_pairs={{0,4},{4,8},{8,12},{12,0},{1,5},{5,9},{9,13},{13,1},{2,6},{6,10},{... | collective-permute-start | bytes 933896 | tf_op jit(solution)/shard_map/send_x/ppermute | solution.py:577
  5.9 9.8 %collective-permute-start.1 = (f32[304,128]{1,0:T(8,128)S(1)}, f32[304,128]{1,0:T(8,128)S(1)}, u32[]{:S(2)}, u32[]{:S(2)}) collective-permute-start(f32[304,128]{1,0:T(8,128)S(1)} %get-tuple-element.33), channel_id=1, source_target_pairs={{0,3},{1,0},{2,1},{3,2},{4,7},{5,4},{6,5},{7,6},{8,11},{9,8},{10,9... | collective-permute-start | bytes 466952 | tf_op jit(solution)/shard_map/send_y/ppermute | solution.py:565
  8.0 3.8 %copy-start.2 = (f32[2,2]{1,0:T(2,128)S(1)}, f32[2,2]{1,0:T(2,128)}, u32[]{:S(2)}) copy-start(f32[2,2]{1,0:T(2,128)} %table.1) | copy-start | bytes 52
  8.0 3.8 %copy-start.3 = (s32[4]{0:T(128)S(1)}, s32[4]{0:T(128)}, u32[]{:S(2)}) copy-start(s32[4]{0:T(128)} %tiles.1) | copy-start | bytes 52
  8.0 9.5 %collective-permute-start.3 = (f32[568,128]{1,0:T(8,128)S(1)}, f32[568,128]{1,0:T(8,128)S(1)}, u32[]{:S(2)}, u32[]{:S(2)}) collective-permute-start(f32[568,128]{1,0:T(8,128)S(1)} %get-tuple-element.44), channel_id=1, source_target_pairs={{0,12},{4,0},{8,4},{12,8},{1,13},{5,1},{9,5},{13,9},{2,14},{6,2},{... | collective-permute-start | bytes 872456 | tf_op jit(solution)/shard_map/send_x/ppermute | solution.py:578
  9.4 8.0 %collective-permute-start.5 = (f32[72,128]{1,0:T(8,128)S(1)}, f32[72,128]{1,0:T(8,128)S(1)}, u32[]{:S(2)}, u32[]{:S(2)}) collective-permute-start(f32[72,128]{1,0:T(8,128)S(1)} %diagonal_corners.1), channel_id=1, source_target_pairs={{0,15},{1,12},{2,13},{3,14},{4,11},{5,8},{6,9},{7,10},{8,7},{9,4},... | collective-permute-start | bytes 110600 | tf_op jit(solution)/shard_map/diagonal_corners/ppermute | solution.py:595
  12.6 4.8 %collective-permute-start.4 = (f32[80,128]{1,0:T(8,128)S(1)}, f32[80,128]{1,0:T(8,128)S(1)}, u32[]{:S(2)}, u32[]{:S(2)}) collective-permute-start(f32[80,128]{1,0:T(8,128)S(1)} %relay_low_corners.1), channel_id=1, source_target_pairs={{0,12},{4,8},{8,4},{12,0},{1,13},{5,9},{9,5},{13,1},{2,14},{6,10},... | collective-permute-start | bytes 122888 | tf_op jit(solution)/shard_map/relay_low_corners/ppermute | solution.py:609
  15.7 1.8 %copy-start = (f32[1,6,8,16,128]{4,3,2,1,0:T(8,128)S(1)}, f32[1,6,8,16,128]{4,3,2,1,0:T(8,128)}, u32[]{:S(2)}) copy-start(f32[1,6,8,16,128]{4,3,2,1,0:T(8,128)} %param.10) | copy-start | bytes 1179652
  15.7 1.8 %copy-start.1 = (f32[1,6,8,16,128]{4,3,2,1,0:T(8,128)S(1)}, f32[1,6,8,16,128]{4,3,2,1,0:T(8,128)}, u32[]{:S(2)}) copy-start(f32[1,6,8,16,128]{4,3,2,1,0:T(8,128)} %param.11) | copy-start | bytes 1179652
  15.7 1.7 %collective-permute-start.6 = (f32[144,128]{1,0:T(8,128)S(1)}, f32[144,128]{1,0:T(8,128)S(1)}, u32[]{:S(2)}, u32[]{:S(2)}) collective-permute-start(f32[144,128]{1,0:T(8,128)S(1)} %relay_corners.1), channel_id=1, source_target_pairs={{0,4},{4,0},{8,12},{12,8},{1,5},{5,1},{9,13},{13,9},{2,6},{6,2},{1... | collective-permute-start | bytes 221192 | tf_op jit(solution)/shard_map/relay_corners/ppermute | solution.py:612
  19.3 3.9 %collective-permute-start.7 = (f32[64,128]{1,0:T(8,128)S(1)}, f32[64,128]{1,0:T(8,128)S(1)}, u32[]{:S(2)}, u32[]{:S(2)}) collective-permute-start(f32[64,128]{1,0:T(8,128)S(1)} %get-tuple-element.50), channel_id=1, source_target_pairs={{0,16},{16,0},{1,17},{17,1},{2,18},{18,2},{3,19},{19,3},{4,20},{20... | collective-permute-start | bytes 98312 | tf_op jit(solution)/shard_map/sum_angles/ppermute | solution.py:639

commit v18 on v17

--- a/solution.py
+++ b/solution.py
@@ -384,7 +384,8 @@
                 after()
 
 
-def middle_kernel(plan, e0_in, h0_in, e1_in, h1_in, coef_in, z_low, z_high, turns, *arrays):
+def middle_kernel(plan, e0_in, h0_in, e1_in, h1_in, coef_in, z_low, z_high, turns, spec_f, spec_a, *refs):
+    *arrays, out_f, out_a = refs
     nx = plan.nx
     efield, hfield, coef = arrays[: STEPS + 1], arrays[STEPS + 1 : 2 * STEPS + 2], arrays[-1]
     state = State(efield, hfield, coef)
@@ -398,9 +399,11 @@
     for step in range(1, STEPS + 1):
         after = [lambda: take("H", 1), lambda: take("E", 1)] if step == 1 else []
         sweeps.both(step, range(step - 1, nx - step), range(step, nx - step), *after)
-
-
-def add_up(plan, efield, transform, out):
+    for _ in add_up(plan, efield, functools.partial(in_middle, plan), (spec_f, spec_a), (out_f, out_a)):
+        pass
+
+
+def add_up(plan, efield, levels, transform, out):
     nx, ny = plan.nx, plan.ny
     for x in range(nx):
         for tile in range(ny // SUB):
@@ -409,7 +412,7 @@
                 for run in (0, 1):
                     at = [pl.ds(((part * 3 + comp) * nx + x) * ny + tile * SUB, SUB) for part in (0, 1)]
                     real, imag = transform[run][at[0], :], transform[run][at[1], :]
-                    for level in range(1, STEPS + 1):
+                    for level in levels(x):
                         theta = omega_step * level
                         here = [efield[level][pl.ds(plan.row(x, tile * SUB, run, part, comp), SUB), :] for part in (0, 1)]
                         more = turned(*here, math.cos(theta), math.sin(theta))
@@ -419,6 +422,10 @@
                 yield x, tile, ends
 
 
+def in_middle(plan, x):
+    return [level for level in range(1, STEPS + 1) if level <= x < plan.nx - level]
+
+
 def do_valleys(plan, sweeps, take):
     for step in range(1, STEPS + 1):
         low, high = step - STEPS, plan.nx - step
@@ -430,7 +437,7 @@
 
 def edges_kernel(plan, groups, *refs):
     count = 2 * STEPS + 3
-    x_low, x_high, far_low, far_high, mate, z_low, z_high, turns, spec_f, spec_a = refs[count : count + 10]
+    x_low, x_high, far_low, far_high, mate, z_low, z_high, turns, part_f, part_a = refs[count : count + 10]
     arrays = refs[count + 10 : 2 * count + 10]
     out_f, out_a, *parts = refs[2 * count + 10 :]
     efield, hfield, coef = arrays[: STEPS + 1], arrays[STEPS + 1 : 2 * STEPS + 2], arrays[-1]
@@ -460,8 +467,11 @@
     shift = lax.rem(groups - lax.axis_index("angle"), groups) * share
     weight = turns[pl.ds(2 * SUB, SUB), :]
 
+    def rest(x):
+        return [level for level in range(1, STEPS + 1) if level not in in_middle(plan, x)]
+
     totals = {}
-    for x, tile, ends in add_up(plan, efield, (spec_f, spec_a), (out_f, out_a)):
+    for x, tile, ends in add_up(plan, efield, rest, (part_f, part_a), (out_f, out_a)):
         term = ends[0][0] * ends[1][0] - ends[0][1] * ends[1][1]
         totals[x, tile] = totals[x, tile] + term if (x, tile) in totals else term
     block = lax.broadcasted_iota(jnp.int32, weight.shape, 1) // share
@@ -613,27 +623,28 @@
     level = lines(12 * wide * ring)
     count = 2 * STEPS + 3
     levels = [level] * (count - 1) + [lines(wide * ring)]
+    transforms = [lines(6 * nx * ny)] * 2
     with jax.named_scope("middle"):
-        state = pl.pallas_call(
+        spectra = [spectrum.reshape((-1, depth)) for spectrum in (forward_spectrum, adjoint_spectrum)]
+        results = pl.pallas_call(
             functools.partial(middle_kernel, plan),
-            out_shape=levels,
-            in_specs=[VMEM] * 8,
-            out_specs=[VMEM] * count,
+            out_shape=[*levels, *transforms],
+            in_specs=[VMEM] * 10,
+            out_specs=[VMEM] * (count + 2),
             input_output_aliases={0: 0, 1: STEPS + 1, 2: 1, 3: STEPS + 2, 4: count - 1},
             compiler_params=params(8),
             cost_estimate=cost(3 * 2**29),
-        )(e0, h0, e1, h1, coef, z_low, z_high, turns)
-    transforms = [lines(6 * nx * ny)] * 2
+        )(e0, h0, e1, h1, coef, z_low, z_high, turns, *spectra)
+        state, sums = results[:count], results[count:]
     with jax.named_scope("edges"):
-        spectra = [spectrum.reshape((-1, depth)) for spectrum in (forward_spectrum, adjoint_spectrum)]
         results = pl.pallas_call(
             functools.partial(edges_kernel, plan, groups),
             out_shape=[*levels, *transforms, *[lines(nx * ny // groups)] * groups],
             in_specs=[VMEM] * (count + 10),
             out_specs=[VMEM] * (count + 2 + groups),
-            input_output_aliases={i: i for i in range(count)},
+            input_output_aliases={i: i for i in range(count)} | {count + 8: count, count + 9: count + 1},
             compiler_params=params(8),
-        )(*state, x_low, x_high, far_low, far_high, mate, z_low, z_high, turns, *spectra)
+        )(*state, x_low, x_high, far_low, far_high, mate, z_low, z_high, turns, *sums)
         tr_f, tr_a, own, *others = results[count:]
     with jax.named_scope("sum_angles"):
         others = [lax.ppermute(part, "angle", ring_pairs("angle", k + 1)) for k, part in enumerate(others)]

time: 24.1 us -> 24 us (level)
  waiting for transfers between devices: 3.49 us -> 3.19 us
  transfers between devices with their start and end apart: 8 -> 8, of which waited for: 4 -> 4; matrix products, arithmetic and copies ran while one was open for 0% -> 0% of each run, Pallas kernels for 12% -> 13%
where the time goes in v18:
time: 24 us; the launch traced here: 23.8 us
  starting transfers between devices  11.7 us (49%)
  Pallas kernels  7.54 us (31%)
  waiting for transfers between devices  3.19 us (13%)
  between operations  1.37 us (6%)
    ppermute x1, starting transfers between devices, shards(): z_low = lax.ppermute(z_up, 'gy', ring_pairs('gy', 1))  3.08 us
    ppermute x1, starting transfers between devices, shards(): z_high = lax.ppermute(z_down, 'gy', ring_pairs('gy', -1))  2.09 us
    pallas_call x1, Pallas kernels, shards(): pl.pallas_call(functools.partial(pack_y_kernel, plan), out_shape=(*[array...  1.99 us
    ppermute x1, starting transfers between devices, shards(): far_high = lax.ppermute(to_diagonal, ('gx', 'gy'), diagonal_pairs())  1.74 us
    pallas_call x1, Pallas kernels, shards(): pl.pallas_call(functools.partial(edges_kernel, plan, groups), out_shape=[...  1.74 us
    ppermute x1, waiting for transfers between devices, shards(): z_high = lax.ppermute(z_down, 'gy', ring_pairs('gy', -1))  1.53 us
    ppermute x1, starting transfers between devices, shards(): far_low = lax.ppermute(to_far, 'gx', far_pairs())  1.52 us
    ppermute x1, starting transfers between devices, shards(): lax.ppermute(part, 'angle', ring_pairs('angle', k + 1))  1.51 us
  transfers between devices with their start and end apart: 8, of which 4 were waited for; matrix products, arithmetic and copies ran while one was open for 0% of the time, Pallas kernels for 13%

profile of v18, /device:TPU:0, one launch (start us, length us, event | category | flops | bytes accessed | tf_op | source)
XLA Modules:
  0.0 23.8 jit_solution(3047719200678176624)
XLA Ops:
  0.6 2.0 %pack_y.1 = (f32[12,14,24,128]{3,2,1,0:T(8,128)S(1)}, f32[12,14,24,128]{3,2,1,0:T(8,128)S(1)}, f32[12,14,24,128]{3,2,1,0:T(8,128)S(1)}, f32[12,14,24,128]{3,2,1,...) custom-call(f32[12,8,16,128]{3,2,1,0:T(8,128)} %bitcast.33, ...), custom_call_target="tpu_custom_call" | custom-call | tf_op jit(solution)/shard_map/pack_y/pallas_call | solution.py:559
  2.6 3.1 %collective-permute-start = (f32[360,128]{1,0:T(8,128)S(1)}, f32[360,128]{1,0:T(8,128)S(1)}, u32[]{:S(2)}, u32[]{:S(2)}) collective-permute-start(f32[360,128]{1,0:T(8,128)S(1)} %get-tuple-element.34), channel_id=1, source_target_pairs={{0,1},{1,2},{2,3},{3,0},{4,5},{5,6},{6,7},{7,4},{8,9},{9,10},{10,1... | collective-permute-start | bytes 552968 | tf_op jit(solution)/shard_map/send_y/ppermute | solution.py:574
  5.7 0.1 pack_x.1
  5.8 0.1 collective-permute-start.2
  5.9 2.1 %collective-permute-start.1 = (f32[304,128]{1,0:T(8,128)S(1)}, f32[304,128]{1,0:T(8,128)S(1)}, u32[]{:S(2)}, u32[]{:S(2)}) collective-permute-start(f32[304,128]{1,0:T(8,128)S(1)} %get-tuple-element.35), channel_id=1, source_target_pairs={{0,3},{1,0},{2,1},{3,2},{4,7},{5,4},{6,5},{7,6},{8,11},{9,8},{10,9... | collective-permute-start | bytes 466952 | tf_op jit(solution)/shard_map/send_y/ppermute | solution.py:575
  8.0 0.0 copy-start.2
  8.0 0.0 copy-start.3
  8.0 0.0 copy-start
  8.0 0.0 copy-start.1
  8.0 1.5 %collective-permute-start.3 = (f32[568,128]{1,0:T(8,128)S(1)}, f32[568,128]{1,0:T(8,128)S(1)}, u32[]{:S(2)}, u32[]{:S(2)}) collective-permute-start(f32[568,128]{1,0:T(8,128)S(1)} %get-tuple-element.46), channel_id=1, source_target_pairs={{0,12},{4,0},{8,4},{12,8},{1,13},{5,1},{9,5},{13,9},{2,14},{6,2},{... | collective-permute-start | bytes 872456 | tf_op jit(solution)/shard_map/send_x/ppermute | solution.py:588
  9.5 1.7 %collective-permute-start.5 = (f32[72,128]{1,0:T(8,128)S(1)}, f32[72,128]{1,0:T(8,128)S(1)}, u32[]{:S(2)}, u32[]{:S(2)}) collective-permute-start(f32[72,128]{1,0:T(8,128)S(1)} %diagonal_corners.1), channel_id=1, source_target_pairs={{0,15},{1,12},{2,13},{3,14},{4,11},{5,8},{6,9},{7,10},{8,7},{9,4},... | collective-permute-start | bytes 110600 | tf_op jit(solution)/shard_map/diagonal_corners/ppermute | solution.py:605
  11.9 0.0 copy-done.2
  11.9 0.0 copy-done.3
  11.9 0.6 %turns.1.refs_16_ = f32[24,128]{1,0:T(8,128)S(1)} custom-call(f32[2,2]{1,0:T(2,128)S(1)} %copy-done.2, s32[1]{0:T(128)S(6)} %copy.43.index, s32[4]{0:T(128)S(1)} %copy-done.3), custom_call_target="tpu_custom_call" | custom-call | tf_op jit(solution)/shard_map/turns/pallas_call | solution.py:590
  12.5 0.1 collective-permute-done.z_low.refs_0_.refs_14_
  12.6 1.5 %collective-permute-start.4 = (f32[80,128]{1,0:T(8,128)S(1)}, f32[80,128]{1,0:T(8,128)S(1)}, u32[]{:S(2)}, u32[]{:S(2)}) collective-permute-start(f32[80,128]{1,0:T(8,128)S(1)} %relay_low_corners.1), channel_id=1, source_target_pairs={{0,12},{4,8},{8,4},{12,0},{1,13},{5,9},{9,5},{13,1},{2,14},{6,10},... | collective-permute-start | bytes 122888 | tf_op jit(solution)/shard_map/relay_low_corners/ppermute | solution.py:619
  14.1 1.5 %collective-permute-done.1.z_high.refs_1_.refs_15_ = f32[304,128]{1,0:T(8,128)S(1)} collective-permute-done((f32[304,128]{1,0:T(8,128)S(1)}, f32[304,128]{1,0:T(8,128)S(1)}, u32[]{:S(2)}, u32[]{:S(2)}) %collective-permute-start.1) | collective-permute-done | bytes 155680 | tf_op jit(solution)/shard_map/send_y/ppermute | solution.py:575
  15.7 0.1 relay_corners.1
  15.7 0.3 %collective-permute-start.6 = (f32[144,128]{1,0:T(8,128)S(1)}, f32[144,128]{1,0:T(8,128)S(1)}, u32[]{:S(2)}, u32[]{:S(2)}) collective-permute-start(f32[144,128]{1,0:T(8,128)S(1)} %relay_corners.1), channel_id=1, source_target_pairs={{0,4},{4,0},{8,12},{12,8},{1,5},{5,1},{9,13},{13,9},{2,6},{6,2},{1... | collective-permute-start | bytes 221192 | tf_op jit(solution)/shard_map/relay_corners/ppermute | solution.py:622
  16.0 0.0 copy-done
  16.0 0.0 copy-done.1
  16.0 1.3 %middle.1 = (f32[4032,128]{1,0:T(8,128)S(1)}, f32[4032,128]{1,0:T(8,128)S(1)}, f32[4032,128]{1,0:T(8,128)S(1)}, f32[4032,128]{1,0:T(8,128)S(1)}, f32[4032,128]{1...) custom-call(f32[4032,128]{1,0:T(8,128)S(1)} %bitcast.16, ...), custom_call_target="tpu_custom_call", output_to_operand_aliasing={{0}: (0, {}), {4}: (1, {}), {1}: (2, {}), {5}: (3, {}), {8}... | custom-call | flops 1610612736 | bytes 1610612736 | tf_op jit(solution)/shard_map/middle/pallas_call | solution.py:629
  17.3 0.1 collective-permute-done.5.refs_12_
  17.4 0.0 collective-permute-done.4.refs_11_
  17.4 0.0 collective-permute-done.6.refs_13_
  17.4 0.0 collective-permute-done.3.refs_10_
  17.4 0.0 collective-permute-done.2.refs_9_
  17.5 1.7 %edges.1 = (f32[4032,128]{1,0:T(8,128)S(1)}, f32[4032,128]{1,0:T(8,128)S(1)}, f32[4032,128]{1,0:T(8,128)S(1)}, f32[4032,128]{1,0:T(8,128)S(1)}, f32[4032,128]{1,...) custom-call(f32[4032,128]{1,0:T(8,128)S(1)} %get-tuple-element.36.re, ...), custom_call_target="tpu_custom_call", output_to_operand_aliasing={{0}: (0, {}), {1}: (1, {}), {2}: (2, {}), {3}: (3, {}), {4}... | custom-call | tf_op jit(solution)/shard_map/edges/pallas_call | solution.py:640
  19.2 1.5 %collective-permute-start.7 = (f32[64,128]{1,0:T(8,128)S(1)}, f32[64,128]{1,0:T(8,128)S(1)}, u32[]{:S(2)}, u32[]{:S(2)}) collective-permute-start(f32[64,128]{1,0:T(8,128)S(1)} %get-tuple-element.54), channel_id=1, source_target_pairs={{0,16},{16,0},{1,17},{17,1},{2,18},{18,2},{3,19},{19,3},{4,20},{20... | collective-permute-start | bytes 98312 | tf_op jit(solution)/shard_map/sum_angles/ppermute | solution.py:650
  20.7 1.0 %write.1 = (f32[6,8,16,128]{3,2,1,0:T(8,128)}, f32[6,8,16,128]{3,2,1,0:T(8,128)}) custom-call(f32[6,8,16,128]{3,2,1,0:T(8,128)S(1)} %bitcast.29, f32[6,8,16,128]{3,2,1,0:T(8,128)S(1)} %bitcast.30), custom_call_target="tpu_custom_call" | custom-call | tf_op jit(solution)/shard_map/write/pallas_call | solution.py:659
  21.7 1.4 %collective-permute-done.7.refs_1_ = f32[64,128]{1,0:T(8,128)S(1)} collective-permute-done((f32[64,128]{1,0:T(8,128)S(1)}, f32[64,128]{1,0:T(8,128)S(1)}, u32[]{:S(2)}, u32[]{:S(2)}) %collective-permute-start.7) | collective-permute-done | bytes 32800 | tf_op jit(solution)/shard_map/sum_angles/ppermute | solution.py:650
  23.1 0.7 %sum_angles.1 = f32[128,64]{1,0:T(8,128)} custom-call(f32[64,128]{1,0:T(8,128)S(1)} %get-tuple-element.53.refs_0_, f32[64,128]{1,0:T(8,128)S(1)} %collective-permute-done.7.refs_1_), custom_call_target="tpu_custom_call" | custom-call | tf_op jit(solution)/shard_map/sum_angles/pallas_call | solution.py:651
  (2 shorter events, 0.0 us)
Async XLA Ops:
  2.6 9.9 %collective-permute-start = (f32[360,128]{1,0:T(8,128)S(1)}, f32[360,128]{1,0:T(8,128)S(1)}, u32[]{:S(2)}, u32[]{:S(2)}) collective-permute-start(f32[360,128]{1,0:T(8,128)S(1)} %get-tuple-element.34), channel_id=1, source_target_pairs={{0,1},{1,2},{2,3},{3,0},{4,5},{5,6},{6,7},{7,4},{8,9},{9,10},{10,1... | collective-permute-start | bytes 552968 | tf_op jit(solution)/shard_map/send_y/ppermute | solution.py:574
  5.8 11.6 %collective-permute-start.2 = (f32[608,128]{1,0:T(8,128)S(1)}, f32[608,128]{1,0:T(8,128)S(1)}, u32[]{:S(2)}, u32[]{:S(2)}) collective-permute-start(f32[608,128]{1,0:T(8,128)S(1)} %get-tuple-element.45.after), channel_id=1, source_target_pairs={{0,4},{4,8},{8,12},{12,0},{1,5},{5,9},{9,13},{13,1},{2,6},{6,10},{... | collective-permute-start | bytes 933896 | tf_op jit(solution)/shard_map/send_x/ppermute | solution.py:587
  5.9 9.8 %collective-permute-start.1 = (f32[304,128]{1,0:T(8,128)S(1)}, f32[304,128]{1,0:T(8,128)S(1)}, u32[]{:S(2)}, u32[]{:S(2)}) collective-permute-start(f32[304,128]{1,0:T(8,128)S(1)} %get-tuple-element.35), channel_id=1, source_target_pairs={{0,3},{1,0},{2,1},{3,2},{4,7},{5,4},{6,5},{7,6},{8,11},{9,8},{10,9... | collective-permute-start | bytes 466952 | tf_op jit(solution)/shard_map/send_y/ppermute | solution.py:575
  8.0 3.9 %copy-start.2 = (f32[2,2]{1,0:T(2,128)S(1)}, f32[2,2]{1,0:T(2,128)}, u32[]{:S(2)}) copy-start(f32[2,2]{1,0:T(2,128)} %table.1) | copy-start | bytes 52
  8.0 3.9 %copy-start.3 = (s32[4]{0:T(128)S(1)}, s32[4]{0:T(128)}, u32[]{:S(2)}) copy-start(s32[4]{0:T(128)} %tiles.1) | copy-start | bytes 52
  8.0 8.0 %copy-start = (f32[1,6,8,16,128]{4,3,2,1,0:T(8,128)S(1)}, f32[1,6,8,16,128]{4,3,2,1,0:T(8,128)}, u32[]{:S(2)}) copy-start(f32[1,6,8,16,128]{4,3,2,1,0:T(8,128)} %param.10) | copy-start | bytes 1179652
  8.0 8.0 %copy-start.1 = (f32[1,6,8,16,128]{4,3,2,1,0:T(8,128)S(1)}, f32[1,6,8,16,128]{4,3,2,1,0:T(8,128)}, u32[]{:S(2)}) copy-start(f32[1,6,8,16,128]{4,3,2,1,0:T(8,128)} %param.11) | copy-start | bytes 1179652
  8.0 9.4 %collective-permute-start.3 = (f32[568,128]{1,0:T(8,128)S(1)}, f32[568,128]{1,0:T(8,128)S(1)}, u32[]{:S(2)}, u32[]{:S(2)}) collective-permute-start(f32[568,128]{1,0:T(8,128)S(1)} %get-tuple-element.46), channel_id=1, source_target_pairs={{0,12},{4,0},{8,4},{12,8},{1,13},{5,1},{9,5},{13,9},{2,14},{6,2},{... | collective-permute-start | bytes 872456 | tf_op jit(solution)/shard_map/send_x/ppermute | solution.py:588
  9.5 8.0 %collective-permute-start.5 = (f32[72,128]{1,0:T(8,128)S(1)}, f32[72,128]{1,0:T(8,128)S(1)}, u32[]{:S(2)}, u32[]{:S(2)}) collective-permute-start(f32[72,128]{1,0:T(8,128)S(1)} %diagonal_corners.1), channel_id=1, source_target_pairs={{0,15},{1,12},{2,13},{3,14},{4,11},{5,8},{6,9},{7,10},{8,7},{9,4},... | collective-permute-start | bytes 110600 | tf_op jit(solution)/shard_map/diagonal_corners/ppermute | solution.py:605
  12.6 4.8 %collective-permute-start.4 = (f32[80,128]{1,0:T(8,128)S(1)}, f32[80,128]{1,0:T(8,128)S(1)}, u32[]{:S(2)}, u32[]{:S(2)}) collective-permute-start(f32[80,128]{1,0:T(8,128)S(1)} %relay_low_corners.1), channel_id=1, source_target_pairs={{0,12},{4,8},{8,4},{12,0},{1,13},{5,9},{9,5},{13,1},{2,14},{6,10},... | collective-permute-start | bytes 122888 | tf_op jit(solution)/shard_map/relay_low_corners/ppermute | solution.py:619
  15.7 1.7 %collective-permute-start.6 = (f32[144,128]{1,0:T(8,128)S(1)}, f32[144,128]{1,0:T(8,128)S(1)}, u32[]{:S(2)}, u32[]{:S(2)}) collective-permute-start(f32[144,128]{1,0:T(8,128)S(1)} %relay_corners.1), channel_id=1, source_target_pairs={{0,4},{4,0},{8,12},{12,8},{1,5},{5,1},{9,13},{13,9},{2,6},{6,2},{1... | collective-permute-start | bytes 221192 | tf_op jit(solution)/shard_map/relay_corners/ppermute | solution.py:622
  19.2 3.9 %collective-permute-start.7 = (f32[64,128]{1,0:T(8,128)S(1)}, f32[64,128]{1,0:T(8,128)S(1)}, u32[]{:S(2)}, u32[]{:S(2)}) collective-permute-start(f32[64,128]{1,0:T(8,128)S(1)} %get-tuple-element.54), channel_id=1, source_target_pairs={{0,16},{16,0},{1,17},{17,1},{2,18},{18,2},{3,19},{19,3},{4,20},{20... | collective-permute-start | bytes 98312 | tf_op jit(solution)/shard_map/sum_angles/ppermute | solution.py:650

commit v19 on v18

--- a/solution.py
+++ b/solution.py
@@ -194,7 +194,7 @@
         pl.when(parity == value)(functools.partial(body, value))
 
 
-def pack_y_kernel(plan, fwd, adj, eps, e0, h0, e1, h1, coef, z_up, z_down, sems, scratch):
+def pack_y_kernel(plan, fwd, adj, eps, e0, h0, e1, h1, coef, z_up, sems, scratch):
     nx, ny = plan.nx, plan.ny
     own = (pl.ds(STEPS, nx), pl.ds(0, ny), slice(None))
     copies = [pltpu.make_async_copy(eps, coef.at[own], sems.at[0])]
@@ -217,13 +217,13 @@
         sweeps.both(1, range(nx), range(nx - 1), runs=(run,))
     state = State([e0, e1], [h0, h1], coef)
     pack(plan, plan.y_low, state, 0, ny, z_up, fold(plan, state, 0, scratch))
-    pack(plan, plan.y_high, state, 0, -ny, z_down)
-
-
-def pack_x_kernel(plan, e0, h0, e1, h1, coef, x_up, x_down, scratch):
+
+
+def pack_x_kernel(plan, e0, h0, e1, h1, coef, x_up, x_down, z_down, scratch):
     state = State([e0, e1], [h0, h1], coef)
     pack(plan, plan.x_low, state, plan.nx, 0, x_up, fold(plan, state, 1, scratch))
     pack(plan, plan.x_high, state, -plan.nx, 0, x_down)
+    pack(plan, plan.y_high, state, 0, -plan.ny, z_down)
 
 
 def pack_diagonal_kernel(plan, e0, h0, e1, h1, coef, after, diagonal):
@@ -556,35 +556,34 @@
 
     assert lax.axis_size("gx") % 2 == 0 and nx * ny % (groups * SUB) == 0
     with jax.named_scope("pack_y"):
-        *first, coef, z_up, z_down = pl.pallas_call(
+        *first, coef, z_up = pl.pallas_call(
             functools.partial(pack_y_kernel, plan),
             out_shape=(
                 *[array(12, wide, ring, depth)] * 4,
                 array(wide, ring, depth),
                 lines(plan.y_low.lines),
-                lines(plan.y_high.lines),
             ),
             in_specs=[HBM] * 3,
-            out_specs=[VMEM] * 7,
+            out_specs=[VMEM] * 6,
             scratch_shapes=[pltpu.SemaphoreType.DMA((25,)), pltpu.VMEM((24 * nx, depth), jnp.float32)],
             compiler_params=params(8),
         )(*(pltpu.with_memory_space_constraint(array, pltpu.HBM) for array in (forward_fields[0], adjoint_fields[0], permittivity)))
     e0, h0, e1, h1, coef = (state.reshape((-1, depth)) for state in (*first, coef))
     with jax.named_scope("send_y"):
         z_low = lax.ppermute(z_up, "gy", ring_pairs("gy", 1))
-        z_high = lax.ppermute(z_down, "gy", ring_pairs("gy", -1))
     with jax.named_scope("pack_x"):
-        x_up, x_down = pl.pallas_call(
+        x_up, x_down, z_down = pl.pallas_call(
             functools.partial(pack_x_kernel, plan),
-            out_shape=[lines(plan.x_low.lines), lines(plan.x_high.lines)],
+            out_shape=[lines(plan.x_low.lines), lines(plan.x_high.lines), lines(plan.y_high.lines)],
             in_specs=[VMEM] * 5,
-            out_specs=[VMEM] * 2,
+            out_specs=[VMEM] * 3,
             scratch_shapes=[pltpu.VMEM((24 * ny, depth), jnp.float32)],
             compiler_params=params(8),
             cost_estimate=cost(40 * 2**20),
         )(e0, h0, e1, h1, coef)
     with jax.named_scope("send_x"):
         x_low = lax.ppermute(x_up, "gx", ring_pairs("gx", 1))
+        z_high = lax.ppermute(z_down, "gy", ring_pairs("gy", -1))
         x_high = lax.ppermute(x_down, "gx", ring_pairs("gx", -1))
     with jax.named_scope("turns"):
         turns = pl.pallas_call(

time: 24 us -> 24 us (level)
  transfers between devices with their start and end apart: 8 -> 8, of which waited for: 4 -> 3; matrix products, arithmetic and copies ran while one was open for 0% -> 0% of each run, Pallas kernels for 13% -> 13%
where the time goes in v19:
time: 24 us; the launch traced here: 23.8 us
  starting transfers between devices  11.8 us (49%)
  Pallas kernels  7.54 us (31%)
  waiting for transfers between devices  3.08 us (13%)
  between operations  1.37 us (6%)
    ppermute x1, starting transfers between devices, shards(): z_low = lax.ppermute(z_up, 'gy', ring_pairs('gy', 1))  3.08 us
    ppermute x1, starting transfers between devices, shards(): z_high = lax.ppermute(z_down, 'gy', ring_pairs('gy', -1))  2.1 us
    pallas_call x1, Pallas kernels, shards(): pl.pallas_call(functools.partial(pack_y_kernel, plan), out_shape=(*[array...  1.95 us
    ppermute x1, starting transfers between devices, shards(): far_high = lax.ppermute(to_diagonal, ('gx', 'gy'), diagonal_pairs())  1.74 us
    pallas_call x1, Pallas kernels, shards(): pl.pallas_call(functools.partial(edges_kernel, plan, groups), out_shape=[...  1.74 us
    ppermute x1, starting transfers between devices, shards(): far_low = lax.ppermute(to_far, 'gx', far_pairs())  1.57 us
    ppermute x1, starting transfers between devices, shards(): lax.ppermute(part, 'angle', ring_pairs('angle', k + 1))  1.51 us
    ppermute x1, waiting for transfers between devices, shards(): z_high = lax.ppermute(z_down, 'gy', ring_pairs('gy', -1))  1.5 us
  transfers between devices with their start and end apart: 8, of which 3 were waited for; matrix products, arithmetic and copies ran while one was open for 0% of the time, Pallas kernels for 13%

profile of v19, /device:TPU:0, one launch (start us, length us, event | category | flops | bytes accessed | tf_op | source)
XLA Modules:
  0.0 23.8 jit_solution(13619385936130691599)
XLA Ops:
  0.6 1.9 %pack_y.1 = (f32[12,14,24,128]{3,2,1,0:T(8,128)S(1)}, f32[12,14,24,128]{3,2,1,0:T(8,128)S(1)}, f32[12,14,24,128]{3,2,1,0:T(8,128)S(1)}, f32[12,14,24,128]{3,2,1,...) custom-call(f32[12,8,16,128]{3,2,1,0:T(8,128)} %bitcast.33, f32[12,8,16,128]{3,2,1,0:T(8,128)} %bitcast.34, ...), custom_call_target="tpu_custom_call" | custom-call | tf_op jit(solution)/shard_map/pack_y/pallas_call | solution.py:559
  2.6 3.1 %collective-permute-start = (f32[360,128]{1,0:T(8,128)S(1)}, f32[360,128]{1,0:T(8,128)S(1)}, u32[]{:S(2)}, u32[]{:S(2)}) collective-permute-start(f32[360,128]{1,0:T(8,128)S(1)} %get-tuple-element.34), channel_id=1, source_target_pairs={{0,1},{1,2},{2,3},{3,0},{4,5},{5,6},{6,7},{7,4},{8,9},{9,10},{10,1... | collective-permute-start | bytes 552968 | tf_op jit(solution)/shard_map/send_y/ppermute | solution.py:573
  5.7 0.1 pack_x.1
  5.8 0.1 collective-permute-start.2
  5.9 2.1 %collective-permute-start.1 = (f32[304,128]{1,0:T(8,128)S(1)}, f32[304,128]{1,0:T(8,128)S(1)}, u32[]{:S(2)}, u32[]{:S(2)}) collective-permute-start(f32[304,128]{1,0:T(8,128)S(1)} %get-tuple-element.35), channel_id=1, source_target_pairs={{0,3},{1,0},{2,1},{3,2},{4,7},{5,4},{6,5},{7,6},{8,11},{9,8},{10,9... | collective-permute-start | bytes 466952 | tf_op jit(solution)/shard_map/send_x/ppermute | solution.py:586
  8.0 0.0 copy-start.2
  8.0 0.0 copy-start.3
  8.0 0.0 copy-start
  8.0 0.0 copy-start.1
  8.0 1.5 %collective-permute-start.3 = (f32[568,128]{1,0:T(8,128)S(1)}, f32[568,128]{1,0:T(8,128)S(1)}, u32[]{:S(2)}, u32[]{:S(2)}) collective-permute-start(f32[568,128]{1,0:T(8,128)S(1)} %get-tuple-element.46), channel_id=1, source_target_pairs={{0,12},{4,0},{8,4},{12,8},{1,13},{5,1},{9,5},{13,9},{2,14},{6,2},{... | collective-permute-start | bytes 872456 | tf_op jit(solution)/shard_map/send_x/ppermute | solution.py:587
  9.5 1.7 %collective-permute-start.5 = (f32[72,128]{1,0:T(8,128)S(1)}, f32[72,128]{1,0:T(8,128)S(1)}, u32[]{:S(2)}, u32[]{:S(2)}) collective-permute-start(f32[72,128]{1,0:T(8,128)S(1)} %diagonal_corners.1), channel_id=1, source_target_pairs={{0,15},{1,12},{2,13},{3,14},{4,11},{5,8},{6,9},{7,10},{8,7},{9,4},... | collective-permute-start | bytes 110600 | tf_op jit(solution)/shard_map/diagonal_corners/ppermute | solution.py:604
  11.8 0.0 copy-done.2
  11.9 0.0 copy-done.3
  11.9 0.6 %turns.1.refs_16_ = f32[24,128]{1,0:T(8,128)S(1)} custom-call(f32[2,2]{1,0:T(2,128)S(1)} %copy-done.2, s32[1]{0:T(128)S(6)} %copy.43.index, s32[4]{0:T(128)S(1)} %copy-done.3), custom_call_target="tpu_custom_call" | custom-call | tf_op jit(solution)/shard_map/turns/pallas_call | solution.py:589
  12.5 0.0 collective-permute-done.z_low.refs_0_.refs_14_
  12.5 1.6 %collective-permute-start.4 = (f32[80,128]{1,0:T(8,128)S(1)}, f32[80,128]{1,0:T(8,128)S(1)}, u32[]{:S(2)}, u32[]{:S(2)}) collective-permute-start(f32[80,128]{1,0:T(8,128)S(1)} %relay_low_corners.1), channel_id=1, source_target_pairs={{0,12},{4,8},{8,4},{12,0},{1,13},{5,9},{9,5},{13,1},{2,14},{6,10},... | collective-permute-start | bytes 122888 | tf_op jit(solution)/shard_map/relay_low_corners/ppermute | solution.py:618
  14.1 1.5 %collective-permute-done.1.z_high.refs_1_.refs_15_ = f32[304,128]{1,0:T(8,128)S(1)} collective-permute-done((f32[304,128]{1,0:T(8,128)S(1)}, f32[304,128]{1,0:T(8,128)S(1)}, u32[]{:S(2)}, u32[]{:S(2)}) %collective-permute-start.1) | collective-permute-done | bytes 155680 | tf_op jit(solution)/shard_map/send_x/ppermute | solution.py:586
  15.6 0.1 relay_corners.1
  15.7 0.3 %collective-permute-start.6 = (f32[144,128]{1,0:T(8,128)S(1)}, f32[144,128]{1,0:T(8,128)S(1)}, u32[]{:S(2)}, u32[]{:S(2)}) collective-permute-start(f32[144,128]{1,0:T(8,128)S(1)} %relay_corners.1), channel_id=1, source_target_pairs={{0,4},{4,0},{8,12},{12,8},{1,5},{5,1},{9,13},{13,9},{2,6},{6,2},{1... | collective-permute-start | bytes 221192 | tf_op jit(solution)/shard_map/relay_corners/ppermute | solution.py:621
  15.9 0.0 copy-done
  15.9 0.0 copy-done.1
  15.9 1.3 %middle.1 = (f32[4032,128]{1,0:T(8,128)S(1)}, f32[4032,128]{1,0:T(8,128)S(1)}, f32[4032,128]{1,0:T(8,128)S(1)}, f32[4032,128]{1,0:T(8,128)S(1)}, f32[4032,128]{1...) custom-call(f32[4032,128]{1,0:T(8,128)S(1)} %bitcast.16, ...), custom_call_target="tpu_custom_call", output_to_operand_aliasing={{0}: (0, {}), {4}: (1, {}), {1}: (2, {}), {5}: (3, {}), {8}... | custom-call | flops 1610612736 | bytes 1610612736 | tf_op jit(solution)/shard_map/middle/pallas_call | solution.py:628
  17.3 0.1 collective-permute-done.5.refs_12_
  17.4 0.0 collective-permute-done.4.refs_11_
  17.4 0.0 collective-permute-done.6.refs_13_
  17.4 0.0 collective-permute-done.3.refs_10_
  17.4 0.0 collective-permute-done.2.refs_9_
  17.4 1.7 %edges.1 = (f32[4032,128]{1,0:T(8,128)S(1)}, f32[4032,128]{1,0:T(8,128)S(1)}, f32[4032,128]{1,0:T(8,128)S(1)}, f32[4032,128]{1,0:T(8,128)S(1)}, f32[4032,128]{1,...) custom-call(f32[4032,128]{1,0:T(8,128)S(1)} %get-tuple-element.36.re, ...), custom_call_target="tpu_custom_call", output_to_operand_aliasing={{0}: (0, {}), {1}: (1, {}), {2}: (2, {}), {3}: (3, {}), {4}... | custom-call | tf_op jit(solution)/shard_map/edges/pallas_call | solution.py:639
  19.1 1.5 %collective-permute-start.7 = (f32[64,128]{1,0:T(8,128)S(1)}, f32[64,128]{1,0:T(8,128)S(1)}, u32[]{:S(2)}, u32[]{:S(2)}) collective-permute-start(f32[64,128]{1,0:T(8,128)S(1)} %get-tuple-element.54), channel_id=1, source_target_pairs={{0,16},{16,0},{1,17},{17,1},{2,18},{18,2},{3,19},{19,3},{4,20},{20... | collective-permute-start | bytes 98312 | tf_op jit(solution)/shard_map/sum_angles/ppermute | solution.py:649
  20.7 1.0 %write.1 = (f32[6,8,16,128]{3,2,1,0:T(8,128)}, f32[6,8,16,128]{3,2,1,0:T(8,128)}) custom-call(f32[6,8,16,128]{3,2,1,0:T(8,128)S(1)} %bitcast.29, f32[6,8,16,128]{3,2,1,0:T(8,128)S(1)} %bitcast.30), custom_call_target="tpu_custom_call" | custom-call | tf_op jit(solution)/shard_map/write/pallas_call | solution.py:658
  21.6 1.4 %collective-permute-done.7.refs_1_ = f32[64,128]{1,0:T(8,128)S(1)} collective-permute-done((f32[64,128]{1,0:T(8,128)S(1)}, f32[64,128]{1,0:T(8,128)S(1)}, u32[]{:S(2)}, u32[]{:S(2)}) %collective-permute-start.7) | collective-permute-done | bytes 32800 | tf_op jit(solution)/shard_map/sum_angles/ppermute | solution.py:649
  23.1 0.7 %sum_angles.1 = f32[128,64]{1,0:T(8,128)} custom-call(f32[64,128]{1,0:T(8,128)S(1)} %get-tuple-element.53.refs_0_, f32[64,128]{1,0:T(8,128)S(1)} %collective-permute-done.7.refs_1_), custom_call_target="tpu_custom_call" | custom-call | tf_op jit(solution)/shard_map/sum_angles/pallas_call | solution.py:650
  (2 shorter events, 0.0 us)
Async XLA Ops:
  2.6 9.9 %collective-permute-start = (f32[360,128]{1,0:T(8,128)S(1)}, f32[360,128]{1,0:T(8,128)S(1)}, u32[]{:S(2)}, u32[]{:S(2)}) collective-permute-start(f32[360,128]{1,0:T(8,128)S(1)} %get-tuple-element.34), channel_id=1, source_target_pairs={{0,1},{1,2},{2,3},{3,0},{4,5},{5,6},{6,7},{7,4},{8,9},{9,10},{10,1... | collective-permute-start | bytes 552968 | tf_op jit(solution)/shard_map/send_y/ppermute | solution.py:573
  5.8 11.6 %collective-permute-start.2 = (f32[608,128]{1,0:T(8,128)S(1)}, f32[608,128]{1,0:T(8,128)S(1)}, u32[]{:S(2)}, u32[]{:S(2)}) collective-permute-start(f32[608,128]{1,0:T(8,128)S(1)} %get-tuple-element.45.after), channel_id=1, source_target_pairs={{0,4},{4,8},{8,12},{12,0},{1,5},{5,9},{9,13},{13,1},{2,6},{6,10},{... | collective-permute-start | bytes 933896 | tf_op jit(solution)/shard_map/send_x/ppermute | solution.py:585
  5.9 9.7 %collective-permute-start.1 = (f32[304,128]{1,0:T(8,128)S(1)}, f32[304,128]{1,0:T(8,128)S(1)}, u32[]{:S(2)}, u32[]{:S(2)}) collective-permute-start(f32[304,128]{1,0:T(8,128)S(1)} %get-tuple-element.35), channel_id=1, source_target_pairs={{0,3},{1,0},{2,1},{3,2},{4,7},{5,4},{6,5},{7,6},{8,11},{9,8},{10,9... | collective-permute-start | bytes 466952 | tf_op jit(solution)/shard_map/send_x/ppermute | solution.py:586
  8.0 3.9 %copy-start.2 = (f32[2,2]{1,0:T(2,128)S(1)}, f32[2,2]{1,0:T(2,128)}, u32[]{:S(2)}) copy-start(f32[2,2]{1,0:T(2,128)} %table.1) | copy-start | bytes 52
  8.0 3.9 %copy-start.3 = (s32[4]{0:T(128)S(1)}, s32[4]{0:T(128)}, u32[]{:S(2)}) copy-start(s32[4]{0:T(128)} %tiles.1) | copy-start | bytes 52
  8.0 8.0 %copy-start = (f32[1,6,8,16,128]{4,3,2,1,0:T(8,128)S(1)}, f32[1,6,8,16,128]{4,3,2,1,0:T(8,128)}, u32[]{:S(2)}) copy-start(f32[1,6,8,16,128]{4,3,2,1,0:T(8,128)} %param.10) | copy-start | bytes 1179652
  8.0 8.0 %copy-start.1 = (f32[1,6,8,16,128]{4,3,2,1,0:T(8,128)S(1)}, f32[1,6,8,16,128]{4,3,2,1,0:T(8,128)}, u32[]{:S(2)}) copy-start(f32[1,6,8,16,128]{4,3,2,1,0:T(8,128)} %param.11) | copy-start | bytes 1179652
  8.0 9.4 %collective-permute-start.3 = (f32[568,128]{1,0:T(8,128)S(1)}, f32[568,128]{1,0:T(8,128)S(1)}, u32[]{:S(2)}, u32[]{:S(2)}) collective-permute-start(f32[568,128]{1,0:T(8,128)S(1)} %get-tuple-element.46), channel_id=1, source_target_pairs={{0,12},{4,0},{8,4},{12,8},{1,13},{5,1},{9,5},{13,9},{2,14},{6,2},{... | collective-permute-start | bytes 872456 | tf_op jit(solution)/shard_map/send_x/ppermute | solution.py:587
  9.5 7.9 %collective-permute-start.5 = (f32[72,128]{1,0:T(8,128)S(1)}, f32[72,128]{1,0:T(8,128)S(1)}, u32[]{:S(2)}, u32[]{:S(2)}) collective-permute-start(f32[72,128]{1,0:T(8,128)S(1)} %diagonal_corners.1), channel_id=1, source_target_pairs={{0,15},{1,12},{2,13},{3,14},{4,11},{5,8},{6,9},{7,10},{8,7},{9,4},... | collective-permute-start | bytes 110600 | tf_op jit(solution)/shard_map/diagonal_corners/ppermute | solution.py:604
  12.5 4.8 %collective-permute-start.4 = (f32[80,128]{1,0:T(8,128)S(1)}, f32[80,128]{1,0:T(8,128)S(1)}, u32[]{:S(2)}, u32[]{:S(2)}) collective-permute-start(f32[80,128]{1,0:T(8,128)S(1)} %relay_low_corners.1), channel_id=1, source_target_pairs={{0,12},{4,8},{8,4},{12,0},{1,13},{5,9},{9,5},{13,1},{2,14},{6,10},... | collective-permute-start | bytes 122888 | tf_op jit(solution)/shard_map/relay_low_corners/ppermute | solution.py:618
  15.7 1.7 %collective-permute-start.6 = (f32[144,128]{1,0:T(8,128)S(1)}, f32[144,128]{1,0:T(8,128)S(1)}, u32[]{:S(2)}, u32[]{:S(2)}) collective-permute-start(f32[144,128]{1,0:T(8,128)S(1)} %relay_corners.1), channel_id=1, source_target_pairs={{0,4},{4,0},{8,12},{12,8},{1,5},{5,1},{9,13},{13,9},{2,6},{6,2},{1... | collective-permute-start | bytes 221192 | tf_op jit(solution)/shard_map/relay_corners/ppermute | solution.py:621
  19.1 3.9 %collective-permute-start.7 = (f32[64,128]{1,0:T(8,128)S(1)}, f32[64,128]{1,0:T(8,128)S(1)}, u32[]{:S(2)}, u32[]{:S(2)}) collective-permute-start(f32[64,128]{1,0:T(8,128)S(1)} %get-tuple-element.54), channel_id=1, source_target_pairs={{0,16},{16,0},{1,17},{17,1},{2,18},{18,2},{3,19},{19,3},{4,20},{20... | collective-permute-start | bytes 98312 | tf_op jit(solution)/shard_map/sum_angles/ppermute | solution.py:649
